TPU v7x, 32 devices: a whole 2x2x4 slice. The times are simulated.
32 devices in a mesh: seq: 2 (over core), expert: 4 (over y, x), tensor: 4 (over z).
Axes of the slice: x: 2, y: 2, z: 4, core: 2. Of those that a mesh axis runs over, the one named last changes fastest.
Arguments:
- tokens: bfloat16 [1024, 4096], P(('seq', 'expert'), 'tensor'), may hold values from -100 to 100
- routes: int32 [1024, 2], P(('seq', 'expert')), may hold values from 0 to 3, all different within a row; in each aligned block of 128 rows (0 to 127, 128 to 255, ...) at most 128 rows name the same one
- route_weights: float32 [1024, 2], P(('seq', 'expert')), may hold values from 0.1 to 0.9
- norm_gain: float32 [4096], P('tensor'), may hold values from 0.1 to 1.9
- final_gain: float32 [4096], P('tensor'), may hold values from 0.1 to 1.9
- w_gate: bfloat16 [4, 4096, 14336], P('expert', None, ('seq', 'tensor')), may hold values from -0.09375 to 0.09375
- w_up: bfloat16 [4, 4096, 14336], P('expert', None, ('seq', 'tensor')), may hold values from -0.09375 to 0.09375
- w_down: bfloat16 [4, 14336, 4096], P('expert', ('seq', 'tensor')), may hold values from -0.09375 to 0.09375
- head_weight: bfloat16 [4096, 32000], P(None, ('expert', 'tensor')), may hold values from -100 to 100
- targets: int32 [1024], P('seq'), may hold values from 0 to 31999
Outputs:
- loss: float32 [1024], P(('seq', 'expert', 'tensor'))
Inputs may be any that keep to these rules, and one draw needn't show every extreme that they name: Within each aligned block of 128 rows no expert is named by more than 128 routes, a bound that some block reaches; the two experts of a row differ.
All inputs are finite; a program needn't handle non-finite values.
Results may differ from a plain program's by a relative error of at most 0.00365.
Values may be sent and summed in bfloat16 or wider, within the bound.
No kernel may reach another device: no remote copies, remote signals or barrier semaphores. Data moves between devices by JAX's collectives and lax.ppermute only.
A program may use at most 192 MiB of HBM per device.

v0:
```python
import jax
import jax.numpy as jnp
from jax import lax
from jax.sharding import PartitionSpec as P

epsilon = 1e-05


def joined(part, axis, combine):
    gathered = jax.tree.map(lambda a: lax.all_gather(a, axis), part)

    def take(source):
        return jax.tree.map(lambda a: lax.dynamic_index_in_dim(a, source, 0, False), gathered)

    return lax.fori_loop(
        1, lax.axis_size(axis), lambda source, state: combine(state, take(source)), take(0)
    )


def combine_totals(left_terms, right_terms):
    row_top = jnp.maximum(left_terms[0], right_terms[0])
    row_total = left_terms[1] * jnp.exp(left_terms[0] - row_top) + right_terms[1] * jnp.exp(
        right_terms[0] - row_top
    )
    return (row_top, row_total, left_terms[2] + right_terms[2])


def on_device(
    tokens, routes, route_weights, norm_gain, final_gain, w_gate, w_up, w_down, head_weight, targets
):
    tok_rows, slice_width = tokens.shape
    n_seq = lax.axis_size("seq")
    n_expert = lax.axis_size("expert")
    n_tensor = lax.axis_size("tensor")
    full_width = slice_width * n_tensor
    experts = w_gate.shape[0] * n_expert
    capacity = 4 * tok_rows // experts
    slots_all = experts * capacity
    hidden_part = w_gate.shape[2]
    vocab_part = head_weight.shape[1]
    token_float = tokens.astype(jnp.float32)
    first_squares = lax.psum(jnp.sum(token_float * token_float, axis=1), "tensor")
    normed = (
        token_float * lax.rsqrt(first_squares / full_width + epsilon)[:, None] * norm_gain[None, :]
    ).astype(jnp.bfloat16)
    expert_ids = jnp.arange(experts, dtype=jnp.int32)
    onehot = (routes.reshape(-1)[:, None] == expert_ids[None, :]).astype(jnp.int32)
    earlier = jnp.cumsum(onehot, axis=0) - onehot
    slot_index = jnp.sum(earlier * onehot, axis=1).reshape(tok_rows, 2)
    place_index = routes * capacity + slot_index
    positions = jnp.arange(slots_all, dtype=jnp.int32)
    first_hit = place_index[None, :, 0] == positions[:, None]
    second_hit = place_index[None, :, 1] == positions[:, None]
    dispatch = (first_hit | second_hit).astype(jnp.bfloat16)
    outgoing = (
        jnp.dot(dispatch, normed, preferred_element_type=jnp.float32)
        .astype(jnp.bfloat16)
        .reshape(experts, capacity, slice_width)
    )
    incoming = lax.all_to_all(outgoing, "expert", split_axis=0, concat_axis=0, tiled=True)
    gate_local = w_gate[0]
    up_local = w_up[0]
    down_local = w_down[0]
    zero_acc = jnp.zeros((n_seq, slots_all, hidden_part), jnp.float32)

    def add_rows(carry_in, row_block, seq_index, row_start):
        gate_rows = lax.dynamic_slice_in_dim(gate_local, row_start, row_block.shape[1], 0)
        up_rows = lax.dynamic_slice_in_dim(up_local, row_start, row_block.shape[1], 0)
        gate_part = jnp.dot(row_block, gate_rows, preferred_element_type=jnp.float32)
        up_part = jnp.dot(row_block, up_rows, preferred_element_type=jnp.float32)
        gate_acc = lax.dynamic_update_index_in_dim(
            carry_in[0],
            lax.dynamic_index_in_dim(carry_in[0], seq_index, 0, False) + gate_part,
            seq_index,
            0,
        )
        up_acc = lax.dynamic_update_index_in_dim(
            carry_in[1],
            lax.dynamic_index_in_dim(carry_in[1], seq_index, 0, False) + up_part,
            seq_index,
            0,
        )
        return (gate_acc, up_acc)

    shard_piece = lax.all_gather(incoming[None], ("seq", "tensor"), axis=0, tiled=True)

    def add_piece(step_index, running):
        row_block = lax.dynamic_index_in_dim(shard_piece, step_index, 0, False).reshape(
            slots_all, slice_width
        )
        return add_rows(
            running, row_block, step_index // n_tensor, step_index % n_tensor * slice_width
        )

    gate_sum, up_sum = lax.fori_loop(0, shard_piece.shape[0], add_piece, (zero_acc, zero_acc))
    hidden = (jax.nn.silu(gate_sum) * up_sum).astype(jnp.bfloat16)

    def one_block(block_index):
        seq_index = block_index // n_tensor
        column_start = block_index % n_tensor * slice_width
        hidden_rows = lax.dynamic_index_in_dim(hidden, seq_index, 0, False)
        down_cols = lax.dynamic_slice_in_dim(down_local, column_start, slice_width, 1)
        return jnp.dot(hidden_rows, down_cols, preferred_element_type=jnp.float32)

    blocks = lax.map(
        one_block,
        jnp.arange(lax.axis_size(("seq", "tensor")) * slots_all // slots_all, dtype=jnp.int32),
    )
    expert_out = lax.psum_scatter(
        blocks.reshape(lax.axis_size(("seq", "tensor")) * slots_all, slice_width),
        ("seq", "tensor"),
        scatter_dimension=0,
        tiled=True,
    )
    outgoing_back = expert_out.astype(jnp.bfloat16).reshape(experts, capacity, slice_width)
    returned = lax.all_to_all(outgoing_back, "expert", split_axis=0, concat_axis=0, tiled=True)
    combine_matrix = route_weights[:, 0:1] * (place_index[:, 0:1] == positions[None, :]).astype(
        jnp.float32
    )
    combine_matrix = combine_matrix + route_weights[:, 1:2] * (
        place_index[:, 1:2] == positions[None, :]
    ).astype(jnp.float32)
    mixed_rows = jnp.dot(
        combine_matrix,
        returned.reshape(slots_all, slice_width).astype(jnp.float32),
        precision=lax.Precision.HIGHEST,
    )
    residual = (token_float + mixed_rows).astype(jnp.bfloat16)
    residual_float = residual.astype(jnp.float32)
    second_squares = lax.psum(jnp.sum(residual_float * residual_float, axis=1), "tensor")
    final_rows = (
        residual_float
        * lax.rsqrt(second_squares / full_width + epsilon)[:, None]
        * final_gain[None, :]
    ).astype(jnp.bfloat16)
    zero_logits = jnp.zeros((n_expert, tok_rows, vocab_part), jnp.float32)
    fold_shard_piece = lax.all_gather(final_rows[None], ("expert", "tensor"), axis=0, tiled=True)

    def add_piece(step_index, running):
        expert_index = step_index // n_tensor
        row_start = step_index % n_tensor * slice_width
        row_block = lax.dynamic_index_in_dim(fold_shard_piece, step_index, 0, False)
        head_rows = lax.dynamic_slice_in_dim(head_weight, row_start, slice_width, 0)
        partial_logits = jnp.dot(row_block, head_rows, preferred_element_type=jnp.float32)
        return lax.dynamic_update_index_in_dim(
            running,
            lax.dynamic_index_in_dim(running, expert_index, 0, False) + partial_logits,
            expert_index,
            0,
        )

    logits = lax.fori_loop(0, fold_shard_piece.shape[0], add_piece, zero_logits)
    logits = logits.reshape(n_expert * tok_rows, vocab_part)
    vocab_start = (lax.axis_index("expert") * n_tensor + lax.axis_index("tensor")) * vocab_part
    local_top = jnp.max(logits, axis=1)
    local_total = jnp.sum(jnp.exp(logits - local_top[:, None]), axis=1)
    target_hit = targets[:, None] - vocab_start == jnp.arange(vocab_part, dtype=jnp.int32)[None, :]
    target_logit = jnp.sum(jnp.where(target_hit, logits, jnp.zeros_like(logits)), axis=1)
    own_rows = tok_rows // n_tensor
    row_top, row_total, row_target = joined(
        (local_top, local_total, target_logit), ("expert", "tensor"), combine_totals
    )
    loss_all = row_top + jnp.log(row_total) - row_target
    own_start = lax.axis_index("expert") * tok_rows + lax.axis_index("tensor") * own_rows
    return lax.dynamic_slice_in_dim(loss_all, own_start, own_rows)


def solution(mesh):
    return jax.shard_map(
        on_device,
        mesh=mesh,
        in_specs=(
            P(("seq", "expert"), "tensor"),
            P(("seq", "expert"), None),
            P(("seq", "expert"), None),
            P("tensor"),
            P("tensor"),
            P("expert", None, ("seq", "tensor")),
            P("expert", None, ("seq", "tensor")),
            P("expert", ("seq", "tensor"), None),
            P(None, ("expert", "tensor")),
            P("seq"),
        ),
        out_specs=P(("seq", "expert", "tensor")),
        check_vma=False,
    )
```

profile of v0, /device:TPU:0, one launch (start us, length us, event | category | flops | bytes accessed | tf_op | source)
XLA Modules:
  0.0 1030.5 jit_solution(18191108443773237769)
XLA Ops:
  11.3 13.5 %psum.14 = f32[128]{0:T(128)S(1)} all-reduce(f32[128]{0:T(128)S(1)} %fusion.35), channel_id=1, replica_groups=mesh['seq'=2,'expert'=4,'tensor'=4] {'tensor'}, use_global_device_ids=true, to_apply=%region_4.5 | all-reduce | flops 128 | bytes 1024 | tf_op jit(solution)/shard_map/psum | solution.py:42
  26.2 15.7 %all_to_all.10 = bf16[4,128,1024]{2,1,0:T(8,128)(2,1)} all-to-all(bf16[4,128,1024]{2,1,0:T(8,128)(2,1)S(1)} %bitcast.124), channel_id=1, replica_groups=mesh['seq'=2,'expert'=4,'tensor'=4] {'expert'}, dimensions={0} | all-to-all | bytes 2097152 | tf_op jit(solution)/shard_map/all_to_all | solution.py:60
  42.0 78.8 %all-gather.8.cloned.1.call-done = bf16[32,128,1024]{2,1,0:T(8,128)(2,1)} async-done(((bf16[4,128,1024]{2,1,0:T(8,128)(2,1)}), bf16[32,128,1024]{2,1,0:T(8,128)(2,1)}) %all-gather.8.cloned.1.call-update) | async-done | bytes 8388624 | tf_op jit(solution)/shard_map/all_gather | solution.py:85
  127.7 168.3 %while.63 = (s32[]{:T(128)}, f32[2,512,1792]{2,1,0:T(8,128)}, f32[2,512,1792]{2,1,0:T(8,128)}, bf16[8,4,128,1024]{3,2,1,0:T(8,128)(2,1)}, bf16[4096,1792]{1,0:T(...) while((s32[]{:T(128)}, f32[2,512,1792]{2,1,0:T(8,128)}, ...), condition=%wide.region_6.7_spmd, body=%wide.region_5.6_spmd.sunk | while | flops 3759931392 | bytes 55574904 | solution.py:95
  127.7 6.6 constant_dynamic-slice_fusion.12
  135.6 7.1 bitcast_dynamic-update-slice_fusion.7
  156.6 7.1 bitcast_dynamic-update-slice_fusion.7
  177.7 7.2 bitcast_dynamic-update-slice_fusion.7
  198.7 7.1 bitcast_dynamic-update-slice_fusion.7
  211.8 6.6 constant_dynamic-slice_fusion.12
  219.8 7.2 bitcast_dynamic-update-slice_fusion.7
  240.8 7.2 bitcast_dynamic-update-slice_fusion.7
  261.8 7.2 bitcast_dynamic-update-slice_fusion.7
  282.9 7.2 bitcast_dynamic-update-slice_fusion.7
  296.0 7.6 multiply_convert_fusion
  303.6 75.6 %while.64 = (s32[]{:T(128)}, f32[8,512,1024]{2,1,0:T(8,128)}, s32[8]{0:T(128)S(1)}, bf16[2,512,1792]{2,1,0:T(8,128)(2,1)}, bf16[1792,4096]{1,0:T(8,128)(2,1)}, /...) while((s32[]{:T(128)}, f32[8,512,1024]{2,1,0:T(8,128)}, ...), condition=%wide.region_8.9_spmd, body=%wide.region_7.8_spmd.sunk | while | flops 1879048192 | bytes 7603100 | solution.py:105
  379.2 323.8 %reduce-scatter.2.cloned.1.call-done = f32[512,1024]{1,0:T(8,128)} async-done(((f32[4096,1024]{1,0:T(8,128)}), f32[512,1024]{1,0:T(8,128)}) %reduce-scatter.2.cloned.1.call-update) | async-done | bytes 2097168 | tf_op jit(solution)/shard_map/reduce_scatter | solution.py:109
  709.4 14.2 %all-to-all-done.1 = bf16[4,128,1024]{2,1,0:T(8,128)(2,1)S(1)} async-done(((bf16[4,128,1024]{2,1,0:T(8,128)(2,1)}), bf16[4,128,1024]{2,1,0:T(8,128)(2,1)S(1)}, u32[]{:S(2)}, u32[]{:S(2)}) %all-to-all-start.1) | async-done | bytes 1048608 | tf_op jit(solution)/shard_map/all_to_all | solution.py:116
  724.3 11.6 %psum.15 = f32[128]{0:T(128)S(1)} all-reduce(f32[128]{0:T(128)S(1)} %get-tuple-element.585), channel_id=1, replica_groups=mesh['seq'=2,'expert'=4,'tensor'=4] {'tensor'}, use_global_device_ids=true, to_apply=%region_11.12 | all-reduce | flops 128 | bytes 1024 | tf_op jit(solution)/shard_map/psum | solution.py:130
  736.8 73.3 %all-gather.10.cloned.1.call-done = bf16[2048,1024]{1,0:T(8,128)(2,1)} async-done(((bf16[128,1024]{1,0:T(8,128)(2,1)}), bf16[2048,1024]{1,0:T(8,128)(2,1)}) %all-gather.10.cloned.1.call-update) | async-done | bytes 4194320 | tf_op jit(solution)/shard_map/all_gather | solution.py:137
  812.3 92.2 %while.65 = (s32[]{:T(128)}, f32[4,128,2000]{1,2,0:T(8,128)}, bf16[16,128,1024]{2,1,0:T(8,128)(2,1)}, bf16[4096,2000]{0,1:T(8,128)(2,1)}, s32[]{:T(128)}, /*inde...) while((s32[]{:T(128)}, f32[4,128,2000]{1,2,0:T(8,128)}, ...), condition=%wide.region_13.14_spmd, body=%wide.region_12.13_spmd.sunk | while | flops 524544032 | bytes 8454980 | solution.py:152
  910.1 38.5 %all-gather.3 = f32[16,1,512]{2,1,0:T(1,128)S(1)} all-gather(f32[1,1,512]{2,1,0:T(1,128)S(1)} %bitcast.139), channel_id=1, replica_groups=mesh['seq'=2,'expert'=4,'tensor'=4] {'expert','tensor'}, dimensions={0}, use_global_device_ids=true | all-gather | bytes 34816 | tf_op jit(solution)/shard_map/all_gather | solution.py:10
  948.6 35.7 %all-gather.4 = f32[16,1,512]{2,1,0:T(1,128)S(1)} all-gather(f32[1,1,512]{2,1,0:T(1,128)S(1)} %bitcast.138), channel_id=1, replica_groups=mesh['seq'=2,'expert'=4,'tensor'=4] {'expert','tensor'}, dimensions={0}, use_global_device_ids=true | all-gather | bytes 34816 | tf_op jit(solution)/shard_map/all_gather | solution.py:10
  984.3 37.7 %all-gather.2 = f32[16,1,512]{2,1,0:T(1,128)S(1)} all-gather(f32[1,1,512]{2,1,0:T(1,128)S(1)} %bitcast.137), channel_id=1, replica_groups=mesh['seq'=2,'expert'=4,'tensor'=4] {'expert','tensor'}, dimensions={0}, use_global_device_ids=true | all-gather | bytes 34816 | tf_op jit(solution)/shard_map/all_gather | solution.py:10
  (202 shorter events, 274.7 us)
Async XLA Ops:
  6.5 114.3 %all-gather.8.cloned.1.call-start = ((), (), s32[]{:S(2)}) async-start(), calls=%async_computation.4 | async-start | bytes 9437184 | tf_op jit(solution)/shard_map/all_gather | solution.py:85
  41.9 661.1 %reduce-scatter.2.cloned.1.call-start = ((), (), s32[]{:S(2)}) async-start(), calls=%async_computation.3 | async-start | bytes 18874368 | tf_op jit(solution)/shard_map/reduce_scatter | solution.py:109
  135.6 7.2 copy-start
  156.6 7.2 copy-start
  177.7 7.2 copy-start
  198.7 7.2 copy-start
  219.7 7.2 copy-start
  240.8 7.2 copy-start
  261.8 7.2 copy-start
  282.9 7.2 copy-start
  379.2 330.3 %copy-start.4 = (f32[128,2]{0,1:T(2,128)S(1)}, f32[128,2]{0,1:T(2,128)}, u32[]{:S(2)}) copy-start(f32[128,2]{0,1:T(2,128)} %param.20) | copy-start | bytes 3076
  379.2 344.4 %copy-start.1 = (bf16[128,1024]{1,0:T(8,128)(2,1)S(1)}, bf16[128,1024]{1,0:T(8,128)(2,1)}, u32[]{:S(2)}) copy-start(bf16[128,1024]{1,0:T(8,128)(2,1)} %param.18) | copy-start | bytes 786436
  379.2 356.8 %copy-start.2 = (f32[1024]{0:T(1024)S(1)}, f32[1024]{0:T(1024)}, u32[]{:S(2)}) copy-start(f32[1024]{0:T(1024)} %param.22) | copy-start | bytes 12292
  379.2 357.6 %copy-start.3 = (s32[512]{0:T(512)S(1)}, s32[512]{0:T(512)}, u32[]{:S(2)}) copy-start(s32[512]{0:T(512)} %param.27) | copy-start | bytes 6148
  705.8 17.8 %all-to-all-start.1 = ((bf16[4,128,1024]{2,1,0:T(8,128)(2,1)}), bf16[4,128,1024]{2,1,0:T(8,128)(2,1)S(1)}, u32[]{:S(2)}, u32[]{:S(2)}) async-start(bf16[4,128,1024]{2,1,0:T(8,128)(2,1)} %bitcast.26), calls=%async_computation.2 | async-start | bytes 2097152 | tf_op jit(solution)/shard_map/all_to_all | solution.py:116
  709.4 100.7 %all-gather.10.cloned.1.call-start = ((), (), s32[]{:S(2)}) async-start(), calls=%async_computation.5 | async-start | bytes 4456448 | tf_op jit(solution)/shard_map/all_gather | solution.py:137
Sparse Core Ops, SparseCore 0:
  42.0 78.7 all-gather.7
  379.3 323.6 reduce-scatter.1
  736.9 73.1 all-gather.9
where the time goes:
time: 1030 us
  waiting for transfers between devices  490 us (48%)
  matrix products  227 us (22%)
  blocking collectives  153 us (15%)
  local copies, waits for them, and re-layouts  101 us (10%)
  loops' own time  23.1 us (2%)
  other arithmetic  20.4 us (2%)
  between operations  13.2 us (1%)
    reduce_scatter x1, waiting for transfers between devices, on_device(): lax.psum_scatter(blocks.reshape(lax.axis_size(('seq', 'tensor')) * slots_...  324 us
    all_gather x3, blocking collectives, joined(): gathered = jax.tree.map(lambda a: lax.all_gather(a, axis), part)  112 us
    all_gather x1, waiting for transfers between devices, on_device(): lax.all_gather(incoming[None], ('seq', 'tensor'), axis=0, tiled=True)  78.8 us
    all_gather x1, waiting for transfers between devices, on_device(): lax.all_gather(final_rows[None], ('expert', 'tensor'), axis=0, tiled=True)  73.3 us
    dot_general x16, matrix products, add_piece(): jnp.dot(row_block, head_rows, preferred_element_type=jnp.float32)  71.5 us
    dot_general x8, matrix products, add_rows(): up_part = jnp.dot(row_block, up_rows, preferred_element_type=jnp.float32)  57.3 us
    dynamic_slice x8, local copies, waits for them, and re-layouts, add_rows(): lax.dynamic_index_in_dim(carry_in[1], seq_index, 0, False) + up_part  52.9 us
    dot_general x8, matrix products, one_block(): return jnp.dot(hidden_rows, down_cols, preferred_element_type=jnp.float32)  48 us
  transfers between devices with their start and end apart: 4, of which 4 were waited for; matrix products, arithmetic and copies ran while one was open for 0% of the time, Pallas kernels for 0%

commit v1 on v0

v1 whole, which is shorter than its diff:
```python
import functools

import jax
import jax.numpy as jnp
from jax import lax
from jax.experimental import pallas as pl
from jax.experimental.pallas import tpu as pltpu
from jax.sharding import PartitionSpec as P

epsilon = 1e-05
LANES = 128
VMEM_BYTES = 56 * 1024 * 1024
MIB = 1024 * 1024


def params(limit=VMEM_BYTES):
    return pltpu.CompilerParams(vmem_limit_bytes=limit)


def whole():
    return pl.BlockSpec(memory_space=pltpu.VMEM)


def scalars():
    return pl.BlockSpec(memory_space=pltpu.SMEM)


def anywhere():
    return pl.BlockSpec(memory_space=pl.ANY)


def swap(x, axis, distance):
    size = lax.axis_size(axis)
    return lax.ppermute(x, axis, [(i, i ^ distance) for i in range(size)])


def gather_near(x, axis):
    return [x] + [swap(x, axis, d) for d in range(1, lax.axis_size(axis))]


def gather_plane(x, axis, first):
    if lax.axis_size(axis) != 4:
        return gather_near(x, axis)
    second = 3 - first
    near = swap(x, axis, first)
    side = swap(x, axis, second)
    far = swap(side, axis, first)
    pieces = {0: x, first: near, second: side, 3: far}
    return [pieces[d] for d in range(4)]


def norm_kernel(own_rows, where, *refs):
    count = (len(refs) - 3) // 2
    slices, gains = refs[:count], refs[count : 2 * count]
    small_ref, rows_ref, raw_ref = refs[2 * count :]
    rows, width = slices[0].shape
    full_width = width * count
    total = jnp.zeros((rows, 1), jnp.float32)
    for piece in slices:
        value = piece[...].astype(jnp.float32)
        total = total + jnp.sum(value * value, axis=1, keepdims=True)
    scale = lax.rsqrt(total / full_width + epsilon)
    start = pl.multiple_of(where[count], own_rows)
    for d in range(count):
        columns = pl.ds(pl.multiple_of(where[d], width), width)
        value = slices[d][...].astype(jnp.float32)
        rows_ref[:, columns] = (value * scale * gains[d][...]).astype(jnp.bfloat16)
        raw_ref[:, columns] = slices[d][pl.ds(start, own_rows), :]
    rows_ref[:, full_width:] = small_ref[...]


def norm_rows(where, slices, gains, small, own_rows):
    rows, width = slices[0].shape
    full_width = width * len(slices)
    return pl.pallas_call(
        functools.partial(norm_kernel, own_rows),
        out_shape=(
            jax.ShapeDtypeStruct((rows, full_width + LANES), jnp.bfloat16),
            jax.ShapeDtypeStruct((own_rows, full_width), jnp.bfloat16),
        ),
        in_specs=[scalars()] + [whole()] * (2 * len(slices) + 1),
        out_specs=(whole(), whole()),
        compiler_params=params(),
        cost_estimate=pl.CostEstimate(
            flops=6 * rows * full_width, bytes_accessed=4 * rows * full_width, transcendentals=rows
        ),
        name="norm_rows",
    )(where, *slices, *gains, small)


def hidden_kernel(pieces, full_width, where, *refs):
    piece_refs = refs[:pieces]
    gate_ref, up_ref, out_ref, rows_scr, weight_scr, sems = refs[pieces:]

    @pl.when(pl.program_id(0) == 0)
    def _():
        copies = []
        start = 0
        for i in range(pieces):
            count = piece_refs[i].shape[0]
            copies.append(
                pltpu.make_async_copy(
                    piece_refs[i], rows_scr.at[pl.ds(start, count), :], sems.at[i]
                )
            )
            start += count
        for copy in copies:
            copy.start()
        for copy in copies:
            copy.wait()
        small = rows_scr[:, full_width:].astype(jnp.float32)
        lane = lax.broadcasted_iota(jnp.int32, small.shape, 1)
        first = where[0] * 3
        mine = (lane >= first) & (lane < first + 3)
        weight = jnp.sum(jnp.where(mine, small, 0.0), axis=1, keepdims=True)
        weight_scr[...] = jnp.broadcast_to(weight, weight_scr.shape)

    rows = rows_scr[:, :full_width]
    gate = jnp.dot(rows, gate_ref[0], preferred_element_type=jnp.float32)
    up = jnp.dot(rows, up_ref[0], preferred_element_type=jnp.float32)
    hidden = gate / (1.0 + jnp.exp(-gate)) * up * weight_scr[:, :1]
    out_ref[...] = hidden.astype(jnp.bfloat16)


def hidden_rows(where, pieces, w_gate, w_up):
    rows = sum(p.shape[0] for p in pieces)
    full_width, hidden = w_gate.shape[1:]
    tile = 256 if hidden % 256 == 0 else hidden
    weight_spec = pl.BlockSpec((1, full_width, tile), lambda i: (0, 0, i))
    return pl.pallas_call(
        functools.partial(hidden_kernel, len(pieces), full_width),
        out_shape=jax.ShapeDtypeStruct((rows, hidden), jnp.bfloat16),
        grid=(hidden // tile,),
        in_specs=[scalars()] + [anywhere()] * len(pieces) + [weight_spec, weight_spec],
        out_specs=pl.BlockSpec((rows, tile), lambda i: (0, i)),
        scratch_shapes=[
            pltpu.VMEM((rows, full_width + LANES), jnp.bfloat16),
            pltpu.VMEM((rows, LANES), jnp.float32),
            pltpu.SemaphoreType.DMA((len(pieces),)),
        ],
        compiler_params=params(),
        cost_estimate=pl.CostEstimate(
            flops=4 * rows * full_width * hidden,
            bytes_accessed=4 * full_width * hidden + 2 * rows * (full_width + hidden),
            transcendentals=rows * hidden,
        ),
        name="hidden_rows",
    )(where, *pieces, w_gate, w_up)


def down_kernel(hidden_ref, down_ref, *outs):
    out = jnp.dot(hidden_ref[...], down_ref[0], preferred_element_type=jnp.float32)
    part = out.shape[0] // len(outs)
    for i in range(len(outs)):
        outs[i][...] = out[i * part : (i + 1) * part].astype(jnp.bfloat16)


def down_rows(hidden, w_down, parts):
    rows, depth = hidden.shape
    full_width = w_down.shape[2]
    tile = 512 if full_width % 512 == 0 else full_width
    shape = jax.ShapeDtypeStruct((rows // parts, full_width), jnp.bfloat16)
    return pl.pallas_call(
        down_kernel,
        out_shape=(shape,) * parts,
        grid=(full_width // tile,),
        in_specs=[
            pl.BlockSpec((rows, depth), lambda i: (0, 0)),
            pl.BlockSpec((1, depth, tile), lambda i: (0, 0, i)),
        ],
        out_specs=(pl.BlockSpec((rows // parts, tile), lambda i: (0, i)),) * parts,
        compiler_params=params(),
        cost_estimate=pl.CostEstimate(
            flops=2 * rows * depth * full_width,
            bytes_accessed=2 * depth * full_width + 2 * rows * (depth + full_width),
            transcendentals=0,
        ),
        name="down_rows",
    )(hidden, w_down)


def final_kernel(where, parts, raw_ref, *refs):
    gains, out_ref = refs[:-1], refs[-1]
    width = gains[0].shape[1]
    residual = raw_ref[...].astype(jnp.float32)
    mixed = parts[0][...].astype(jnp.float32)
    for part in parts[1:]:
        mixed = mixed + part[...].astype(jnp.float32)
    residual = (residual + mixed).astype(jnp.bfloat16).astype(jnp.float32)
    total = jnp.sum(residual * residual, axis=1, keepdims=True)
    scale = lax.rsqrt(total / residual.shape[1] + epsilon)
    out_ref[...] = (residual * scale).astype(jnp.float32)
    for d in range(len(gains)):
        columns = pl.ds(pl.multiple_of(where[d], width), width)
        out_ref[:, columns] = out_ref[:, columns] * gains[d][...]


def final_rows(where, parts, raw, gains):
    rows, full_width = raw.shape

    def body(where_ref, *refs):
        final_kernel(where_ref, refs[: len(parts)], refs[len(parts)], *refs[len(parts) + 1 :])

    return pl.pallas_call(
        body,
        out_shape=jax.ShapeDtypeStruct((rows, full_width), jnp.float32),
        in_specs=[scalars()] + [whole()] * (len(parts) + 1 + len(gains)),
        out_specs=whole(),
        compiler_params=params(),
        cost_estimate=pl.CostEstimate(
            flops=8 * rows * full_width, bytes_accessed=14 * rows * full_width, transcendentals=rows
        ),
        name="final_rows",
    )(where, *parts, raw, *gains).astype(jnp.bfloat16)


def head_kernel(pieces, vocab_part, tile, *refs):
    piece_refs = refs[:pieces]
    head_ref, target_ref, out_ref, rows_scr, top_scr, total_scr, hit_scr, sems = refs[pieces:]
    step = pl.program_id(0)

    @pl.when(step == 0)
    def _():
        copies = []
        start = 0
        for i in range(pieces):
            count = piece_refs[i].shape[0]
            copies.append(
                pltpu.make_async_copy(
                    piece_refs[i], rows_scr.at[pl.ds(start, count), :], sems.at[i]
                )
            )
            start += count
        for copy in copies:
            copy.start()
        for copy in copies:
            copy.wait()
        top_scr[...] = jnp.full(top_scr.shape, -jnp.inf, jnp.float32)
        total_scr[...] = jnp.zeros(total_scr.shape, jnp.float32)
        hit_scr[...] = jnp.zeros(hit_scr.shape, jnp.float32)

    logits = jnp.dot(rows_scr[...], head_ref[...], preferred_element_type=jnp.float32)
    column = lax.broadcasted_iota(jnp.int32, logits.shape, 1) + step * tile
    logits = jnp.where(column < vocab_part, logits, -jnp.inf)
    old_top = top_scr[:, :1]
    top = jnp.maximum(old_top, jnp.max(logits, axis=1, keepdims=True))
    total = total_scr[:, :1] * jnp.exp(old_top - top) + jnp.sum(
        jnp.exp(logits - top), axis=1, keepdims=True
    )
    hit = (column == target_ref[:, :1]) & (column < vocab_part)
    target = hit_scr[:, :1] + jnp.sum(jnp.where(hit, logits, 0.0), axis=1, keepdims=True)
    top_scr[...] = jnp.broadcast_to(top, top_scr.shape)
    total_scr[...] = jnp.broadcast_to(total, total_scr.shape)
    hit_scr[...] = jnp.broadcast_to(target, hit_scr.shape)

    @pl.when(step == pl.num_programs(0) - 1)
    def _():
        lane = lax.broadcasted_iota(jnp.int32, out_ref.shape, 1)
        out_ref[...] = jnp.where(
            lane == 0, top_scr[...], jnp.where(lane == 1, total_scr[...], hit_scr[...])
        )


def head_terms(pieces, head_weight, targets):
    rows = sum(p.shape[0] for p in pieces)
    full_width, vocab_part = head_weight.shape
    tile = 512
    return pl.pallas_call(
        functools.partial(head_kernel, len(pieces), vocab_part, tile),
        out_shape=jax.ShapeDtypeStruct((rows, LANES), jnp.float32),
        grid=(pl.cdiv(vocab_part, tile),),
        in_specs=[anywhere()] * len(pieces)
        + [
            pl.BlockSpec((full_width, tile), lambda i: (0, i)),
            pl.BlockSpec((rows, 1), lambda i: (0, 0)),
        ],
        out_specs=pl.BlockSpec((rows, LANES), lambda i: (0, 0)),
        scratch_shapes=[
            pltpu.VMEM((rows, full_width), jnp.bfloat16),
            pltpu.VMEM((rows, LANES), jnp.float32),
            pltpu.VMEM((rows, LANES), jnp.float32),
            pltpu.VMEM((rows, LANES), jnp.float32),
            pltpu.SemaphoreType.DMA((len(pieces),)),
        ],
        compiler_params=params(),
        cost_estimate=pl.CostEstimate(
            flops=2 * rows * full_width * vocab_part,
            bytes_accessed=2 * full_width * (vocab_part + rows),
            transcendentals=rows * vocab_part,
        ),
        name="head_terms",
    )(*pieces, head_weight, targets)


def join_terms(parts):
    top = functools.reduce(jnp.maximum, [p[..., 0] for p in parts])
    total = sum(p[..., 1] * jnp.exp(p[..., 0] - top) for p in parts)
    target = sum(p[..., 2] for p in parts)
    return jnp.stack([top, total, target], axis=-1)


def flip(x, axis, index):
    size = x.shape[axis]
    bit = 1
    while bit < size:
        shape = x.shape[:axis] + (size // (2 * bit), 2, bit) + x.shape[axis + 1 :]
        turned = jnp.flip(x.reshape(shape), axis + 1).reshape(x.shape)
        x = jnp.where((index & bit) != 0, turned, x)
        bit *= 2
    return x


def route_columns(routes, route_weights, experts):
    ids = jnp.arange(experts, dtype=jnp.int32)
    weight = jnp.zeros((routes.shape[0], experts), jnp.float32)
    for j in range(routes.shape[1]):
        weight = weight + jnp.where(routes[:, j : j + 1] == ids, route_weights[:, j : j + 1], 0.0)
    high = lax.reduce_precision(weight, 8, 7)
    middle = lax.reduce_precision(weight - high, 8, 7)
    low = weight - high - middle
    parts = jnp.stack([high, middle, low], axis=-1).reshape(routes.shape[0], 3 * experts)
    parts = jnp.pad(parts, ((0, 0), (0, LANES - 3 * experts)))
    return parts.astype(jnp.bfloat16)


def on_device(
    tokens, routes, route_weights, norm_gain, final_gain, w_gate, w_up, w_down, head_weight, targets
):
    tok_rows, width = tokens.shape
    n_expert = lax.axis_size("expert")
    n_tensor = lax.axis_size("tensor")
    my_expert = lax.axis_index("expert")
    my_tensor = lax.axis_index("tensor")
    experts = w_gate.shape[0] * n_expert
    full_width = width * n_tensor
    own = tok_rows // n_tensor
    splits = 2 if own % 32 == 0 else 1
    sub = own // splits
    rows = sub * n_tensor
    vocab_part = head_weight.shape[1]
    f32 = jnp.float32

    near = jnp.arange(n_tensor, dtype=jnp.int32) ^ my_tensor
    where = jnp.concatenate([near * width, (my_tensor * sub)[None]]).astype(jnp.int32)
    mine = my_expert.astype(jnp.int32)[None]

    def part_of(x, h):
        return x.reshape((n_tensor, splits, sub) + x.shape[1:])[:, h].reshape(
            (rows,) + x.shape[1:]
        )

    small = route_columns(routes, route_weights, experts)
    gains = gather_near(jnp.stack([norm_gain, final_gain]), "tensor")
    norm_gains = [g[0:1] for g in gains]
    final_gains = [g[1:2] for g in gains]

    pieces, raws = [], []
    for h in range(splits):
        slices = gather_near(part_of(tokens, h), "tensor")
        normed, raw = norm_rows(where, slices, norm_gains, part_of(small, h), sub)
        plane = gather_plane(normed, "expert", 1 + h % 2)
        other = [swap(p, "seq", 1) for p in plane]
        pieces.append(plane + other)
        raws.append(raw)

    finals = []
    for h in range(splits):
        hidden = hidden_rows(mine, pieces[h], w_gate, w_up)
        kept, sent = down_rows(hidden, w_down, 2)
        got = swap(sent, "seq", 1)
        kept = kept.reshape(n_expert, rows, full_width)
        got = got.reshape(n_expert, rows, full_width)

        def both(d):
            return kept[d].astype(f32) + got[d].astype(f32)

        if n_expert == 4:
            first = 1 + h % 2
            second = 3 - first
            sending = jnp.stack([both(first), both(3)]).astype(jnp.bfloat16)
            arrived = swap(sending, "expert", first)
            passing = (both(second) + arrived[1].astype(f32)).astype(jnp.bfloat16)
            last = swap(passing, "expert", second)
            total = both(0) + arrived[0].astype(f32) + last.astype(f32)
        else:
            total = both(0)
            for d in range(1, n_expert):
                total = total + swap(both(d).astype(jnp.bfloat16), "expert", d).astype(f32)
        total = total.astype(jnp.bfloat16).reshape(n_tensor, sub, full_width)

        parts = [lax.dynamic_index_in_dim(total, my_tensor, 0, False)]
        for d in range(1, n_tensor):
            out = lax.dynamic_index_in_dim(total, my_tensor ^ d, 0, False)
            parts.append(swap(out, "tensor", d))
        finals.append(final_rows(where, parts, raws[h], final_gains))

    start = (my_expert * n_tensor + my_tensor) * vocab_part
    local = (targets - start).astype(jnp.int32).reshape(n_expert, n_tensor, splits, sub)
    local = flip(flip(local, 0, my_expert), 1, my_tensor)
    terms = []
    for h in range(splits):
        column = jnp.concatenate(gather_near(finals[h], "tensor"), axis=0)
        plane = gather_plane(column, "expert", 1 + h % 2)
        terms.append(
            head_terms(plane, head_weight, local[:, :, h].reshape(-1, 1)).reshape(
                n_expert, n_tensor, sub, LANES
            )[..., :3]
        )
    terms = jnp.stack(terms, axis=2)
    joined = join_terms(
        [terms[:, 0]] + [swap(terms[:, d], "tensor", d) for d in range(1, n_tensor)]
    )
    joined = join_terms(
        [joined[0]] + [swap(joined[d], "expert", d) for d in range(1, n_expert)]
    )
    return (joined[..., 0] + jnp.log(joined[..., 1]) - joined[..., 2]).reshape(own)


def solution(mesh):
    return jax.shard_map(
        on_device,
        mesh=mesh,
        in_specs=(
            P(("seq", "expert"), "tensor"),
            P(("seq", "expert"), None),
            P(("seq", "expert"), None),
            P("tensor"),
            P("tensor"),
            P("expert", None, ("seq", "tensor")),
            P("expert", None, ("seq", "tensor")),
            P("expert", ("seq", "tensor"), None),
            P(None, ("expert", "tensor")),
            P("seq"),
        ),
        out_specs=P(("seq", "expert", "tensor")),
        check_vma=False,
    )
```

time: 1030 us -> 323 us (0.31)
  waiting for transfers between devices: 490 us -> 99.6 us
  matrix products: 227 us -> 0 us
  blocking collectives: 153 us -> 0 us
  Pallas kernels: 0 us -> 105 us
  local copies, waits for them, and re-layouts: 101 us -> 40.8 us
  starting transfers between devices: 3.68 us -> 63 us
  loops' own time: 23.1 us -> 0 us
  between operations: 13.2 us -> 0.58 us
    reduce_scatter x1 -> x0, waiting for transfers between devices: 324 us -> none  [on_device(): lax.psum_scatter(blocks.reshape(lax.axis_size(('seq', 'tensor')) * slots_...]
    dot_general x42 -> x0, matrix products: 227 us -> none  [the longest x16 71.5 us: add_piece(): jnp.dot(row_block, head_rows, preferred_element_type=jnp.float32)]
    all_gather x2 -> x0, waiting for transfers between devices: 152 us -> none  [the longest x1 78.8 us: on_device(): lax.all_gather(incoming[None], ('seq', 'tensor'), axis=0, tiled=True)]
    all_gather x3 -> x0, blocking collectives: 112 us -> none  [joined(): gathered = jax.tree.map(lambda a: lax.all_gather(a, axis), part)]
    pallas_call x0 -> x10, Pallas kernels: none -> 105 us  [the longest x2 45.3 us: hidden_rows(): pl.pallas_call(functools.partial(hidden_kernel, len(pieces), full_width),...]
    ppermute x0 -> x53, waiting for transfers between devices: none -> 99.6 us  [swap(): return lax.ppermute(x, axis, [(i, i ^ distance) for i in range(size)])]
    dynamic_slice x74 -> x0, local copies, waits for them, and re-layouts: 90 us -> none  [the longest x8 52.9 us: add_rows(): lax.dynamic_index_in_dim(carry_in[1], seq_index, 0, False) + up_part]
    ppermute x0 -> x53, starting transfers between devices: none -> 63 us  [swap(): return lax.ppermute(x, axis, [(i, i ^ distance) for i in range(size)])]
  transfers between devices with their start and end apart: 4 -> 53, of which waited for: 4 -> 22; matrix products, arithmetic and copies ran while one was open for 0% -> 13% of each run, Pallas kernels for 0% -> 28%
where the time goes in v1:
time: 323 us; the launch traced here: 322 us
  Pallas kernels  105 us (33%)
  waiting for transfers between devices  99.6 us (31%)
  starting transfers between devices  63 us (20%)
  local copies, waits for them, and re-layouts  40.8 us (13%)
  other arithmetic  12.4 us (4%)
    ppermute x53, waiting for transfers between devices, swap(): return lax.ppermute(x, axis, [(i, i ^ distance) for i in range(size)])  99.6 us
    ppermute x53, starting transfers between devices, swap(): return lax.ppermute(x, axis, [(i, i ^ distance) for i in range(size)])  63 us
    pallas_call x2, Pallas kernels, hidden_rows(): pl.pallas_call(functools.partial(hidden_kernel, len(pieces), full_width),...  45.3 us
    unnamed x76, local copies, waits for them, and re-layouts  31.6 us
    pallas_call x2, Pallas kernels, down_rows(): pl.pallas_call(down_kernel, out_shape=(shape,) * parts, grid=(full_width...  27.5 us
    pallas_call x2, Pallas kernels, head_terms(): pl.pallas_call(functools.partial(head_kernel, len(pieces), vocab_part, ti...  24.1 us
  transfers between devices with their start and end apart: 53, of which 22 were waited for; matrix products, arithmetic and copies ran while one was open for 13% of the time, Pallas kernels for 28%

profile of v1, /device:TPU:0, one launch (start us, length us, event | category | flops | bytes accessed | tf_op | source)
XLA Modules:
  0.0 321.9 jit_solution(7687564858193119415)
XLA Ops:
  0.7 5.1 %collective-permute-start.5 = (f32[2,1024]{1,0:T(2,128)S(1)}, f32[2,1024]{1,0:T(2,128)S(1)}, u32[]{:S(2)}, u32[]{:S(2)}) collective-permute-start(f32[2,1024]{1,0:T(2,128)S(1)} %pad_maximum_fusion.6), channel_id=1, source_target_pairs={{0,3},{1,2},{2,1},{3,0},{4,7},{5,6},{6,5},{7,4},{8,11},{9,10},{10,... | collective-permute-start | bytes 24584 | tf_op jit(solution)/shard_map/ppermute | solution.py:34
  7.5 3.8 %collective-permute-start.2 = (bf16[64,1024]{1,0:T(8,128)(2,1)S(1)}, bf16[64,1024]{1,0:T(8,128)(2,1)S(1)}, u32[]{:S(2)}, u32[]{:S(2)}) collective-permute-start(bf16[64,1024]{1,0:T(8,128)(2,1)S(1)} %bitcast.146), channel_id=1, source_target_pairs={{0,3},{1,2},{2,1},{3,0},{4,7},{5,6},{6,5},{7,4},{8,11},{9,10},{10,... | collective-permute-start | bytes 393224 | tf_op jit(solution)/shard_map/ppermute | solution.py:34
  16.7 5.0 %collective-permute-done.1.refs_2_ = bf16[64,1024]{1,0:T(8,128)(2,1)S(1)} collective-permute-done((bf16[64,1024]{1,0:T(8,128)(2,1)S(1)}, bf16[64,1024]{1,0:T(8,128)(2,1)S(1)}, u32[]{:S(2)}, u32[]{:S(2)}) %collective-permute-start.1) | collective-permute-done | bytes 131104 | tf_op jit(solution)/shard_map/ppermute | solution.py:34
  28.3 2.4 collective-permute-start.25
  30.8 3.8 %collective-permute-done.27.refs_3_ = bf16[64,1024]{1,0:T(8,128)(2,1)S(1)} collective-permute-done((bf16[64,1024]{1,0:T(8,128)(2,1)S(1)}, bf16[64,1024]{1,0:T(8,128)(2,1)S(1)}, u32[]{:S(2)}, u32[]{:S(2)}) %collective-permute-start.27) | collective-permute-done | bytes 131104 | tf_op jit(solution)/shard_map/ppermute | solution.py:34
  36.1 2.7 collective-permute-done.26.refs_2_
  44.3 3.4 %collective-permute-done.6.refs_1_ = bf16[64,4224]{1,0:T(8,128)(2,1)S(1)} collective-permute-done((bf16[64,4224]{1,0:T(8,128)(2,1)}, bf16[64,4224]{1,0:T(8,128)(2,1)S(1)}, u32[]{:S(2)}, u32[]{:S(2)}) %collective-permute-start.6) | collective-permute-done | bytes 540704 | tf_op jit(solution)/shard_map/ppermute | solution.py:34
  47.7 11.6 %collective-permute-done.28.refs_1_ = bf16[64,4224]{1,0:T(8,128)(2,1)S(1)} collective-permute-done((bf16[64,4224]{1,0:T(8,128)(2,1)}, bf16[64,4224]{1,0:T(8,128)(2,1)S(1)}, u32[]{:S(2)}, u32[]{:S(2)}) %collective-permute-start.28) | collective-permute-done | bytes 540704 | tf_op jit(solution)/shard_map/ppermute | solution.py:34
  59.8 9.2 %collective-permute-done.8.refs_3_ = bf16[64,4224]{1,0:T(8,128)(2,1)} collective-permute-done((bf16[64,4224]{1,0:T(8,128)(2,1)S(1)}, bf16[64,4224]{1,0:T(8,128)(2,1)}, u32[]{:S(2)}, u32[]{:S(2)}) %collective-permute-start.8) | collective-permute-done | bytes 540704 | tf_op jit(solution)/shard_map/ppermute | solution.py:34
  71.2 22.7 %hidden_rows.2.hidden_ref = bf16[512,1792]{1,0:T(8,128)(2,1)} custom-call(s32[1]{0:T(128)} %bitcast.1.where, bf16[64,4224]{1,0:T(8,128)(2,1)} %get-tuple-element.13.refs_0_, bf16[64,4224]{1,0:T(8,128)(2,1)} %copy-done.29, bf16[64,4224]{1,0:T(8,128)(2,1)} %copy-done.26, bf16[64,4224]{1,0:T(8,128)(2,1)} %collective-permute-done.8.refs_3_, ...), custom_call_target="tpu_custom_call" | custom-call | flops 15032385536 | bytes 35389440 | tf_op jit(solution)/shard_map/hidden_rows/pallas_call | solution.py:130
  94.0 13.7 %down_rows.2 = (bf16[256,4096]{1,0:T(8,128)(2,1)}, bf16[256,4096]{1,0:T(8,128)(2,1)}) custom-call(bf16[512,1792]{1,0:T(8,128)(2,1)} %hidden_rows.2.hidden_ref, bf16[1,1792,4096]{2,1,0:T(8,128)(2,1)} %down_ref.3), custom_call_target="tpu_custom_call" | custom-call | flops 7516192768 | bytes 20709376 | tf_op jit(solution)/shard_map/down_rows/pallas_call | solution.py:163
  109.8 22.6 %hidden_rows.3.hidden_ref = bf16[512,1792]{1,0:T(8,128)(2,1)} custom-call(s32[1]{0:T(128)} %bitcast.1.where, bf16[64,4224]{1,0:T(8,128)(2,1)} %get-tuple-element.17.refs_0_, bf16[64,4224]{1,0:T(8,128)(2,1)} %copy-done.28, bf16[64,4224]{1,0:T(8,128)(2,1)} %copy-done.30, bf16[64,4224]{1,0:T(8,128)(2,1)} %copy-done.31, bf16[64,4224]{1,0:T(8,128)(2,1)} %copy-done.32, ...), custom_call_target="tpu_custom_call" | custom-call | flops 15032385536 | bytes 35389440 | tf_op jit(solution)/shard_map/hidden_rows/pallas_call | solution.py:130
  132.3 13.8 %down_rows.3 = (bf16[256,4096]{1,0:T(8,128)(2,1)}, bf16[256,4096]{1,0:T(8,128)(2,1)}) custom-call(bf16[512,1792]{1,0:T(8,128)(2,1)} %hidden_rows.3.hidden_ref, bf16[1,1792,4096]{2,1,0:T(8,128)(2,1)} %down_ref.3), custom_call_target="tpu_custom_call" | custom-call | flops 7516192768 | bytes 20709376 | tf_op jit(solution)/shard_map/down_rows/pallas_call | solution.py:163
  152.8 20.9 %collective-permute-done.14 = bf16[2,64,4096]{2,1,0:T(8,128)(2,1)} collective-permute-done((bf16[2,64,4096]{2,1,0:T(8,128)(2,1)}, bf16[2,64,4096]{2,1,0:T(8,128)(2,1)}, u32[]{:S(2)}, u32[]{:S(2)}) %collective-permute-start.14) | collective-permute-done | bytes 1048608 | tf_op jit(solution)/shard_map/ppermute | solution.py:34
  175.7 2.8 collective-permute-done.36
  181.3 7.9 %collective-permute-done.15 = bf16[64,4096]{1,0:T(8,128)(2,1)S(1)} collective-permute-done((bf16[64,4096]{1,0:T(8,128)(2,1)S(1)}, bf16[64,4096]{1,0:T(8,128)(2,1)S(1)}, u32[]{:S(2)}, u32[]{:S(2)}) %collective-permute-start.15) | collective-permute-done | bytes 524320 | tf_op jit(solution)/shard_map/ppermute | solution.py:34
  200.5 7.7 %collective-permute-start.38 = (bf16[16,4096]{1,0:T(8,128)(2,1)S(1)}, bf16[16,4096]{1,0:T(8,128)(2,1)S(1)}, u32[]{:S(2)}, u32[]{:S(2)}) collective-permute-start(bf16[16,4096]{1,0:T(8,128)(2,1)S(1)} %get-tuple-element.35), channel_id=1, source_target_pairs={{0,1},{1,0},{2,3},{3,2},{4,5},{5,4},{6,7},{7,6},{8,9},{9,8},{10,11... | collective-permute-start | bytes 393224 | tf_op jit(solution)/shard_map/ppermute | solution.py:34
  208.2 3.9 %collective-permute-done.17.refs_2_ = bf16[16,4096]{1,0:T(8,128)(2,1)S(1)} collective-permute-done((bf16[16,4096]{1,0:T(8,128)(2,1)S(1)}, bf16[16,4096]{1,0:T(8,128)(2,1)S(1)}, u32[]{:S(2)}, u32[]{:S(2)}) %collective-permute-start.17) | collective-permute-done | bytes 131104 | tf_op jit(solution)/shard_map/ppermute | solution.py:34
  228.7 6.2 %collective-permute-done.20 = bf16[16,4096]{1,0:T(8,128)(2,1)S(1)} collective-permute-done((bf16[16,4096]{1,0:T(8,128)(2,1)S(1)}, bf16[16,4096]{1,0:T(8,128)(2,1)S(1)}, u32[]{:S(2)}, u32[]{:S(2)}) %collective-permute-start.20) | collective-permute-done | bytes 131104 | tf_op jit(solution)/shard_map/ppermute | solution.py:34
  235.5 4.0 %collective-permute-done.42 = bf16[16,4096]{1,0:T(8,128)(2,1)S(1)} collective-permute-done((bf16[16,4096]{1,0:T(8,128)(2,1)S(1)}, bf16[16,4096]{1,0:T(8,128)(2,1)S(1)}, u32[]{:S(2)}, u32[]{:S(2)}) %collective-permute-start.42) | collective-permute-done | bytes 131104 | tf_op jit(solution)/shard_map/ppermute | solution.py:34
  246.8 7.7 %collective-permute-done.44.refs_1_ = bf16[64,4096]{1,0:T(8,128)(2,1)S(1)} collective-permute-done((bf16[64,4096]{1,0:T(8,128)(2,1)S(1)}, bf16[64,4096]{1,0:T(8,128)(2,1)S(1)}, u32[]{:S(2)}, u32[]{:S(2)}) %collective-permute-start.44) | collective-permute-done | bytes 524320 | tf_op jit(solution)/shard_map/ppermute | solution.py:34
  256.7 22.6 %copy.107.refs_4_ = bf16[4096,2000]{1,0:T(8,128)(2,1)} copy(bf16[4096,2000]{0,1:T(8,128)(2,1)} %param.18) | data formatting | bytes 32768000 | tf_op args[8]
  280.1 12.0 %head_terms.2 = f32[256,128]{1,0:T(8,128)} custom-call(bf16[64,4096]{1,0:T(8,128)(2,1)} %copy-done.5, bf16[64,4096]{1,0:T(8,128)(2,1)} %copy-done.9, bf16[64,4096]{1,0:T(8,128)(2,1)} %copy-done.7, bf16[64,4096]{1,0:T(8,128)(2,1)} %collective-permute-done.24.refs_3_, bf16[4096,2000]{1,0:T(8,128)(2,1)} %copy.107.refs_4_, s32[256,1]{1,0:T(8,128)} %reshape_squeeze.24.refs_5_), custom_call_target="tpu_custom_call" | custom-call | flops 4194304000 | bytes 18481152 | tf_op jit(solution)/shard_map/head_terms/pallas_call | solution.py:268
  294.1 12.0 %head_terms.3 = f32[256,128]{1,0:T(8,128)} custom-call(bf16[64,4096]{1,0:T(8,128)(2,1)} %copy-done.6, bf16[64,4096]{1,0:T(8,128)(2,1)} %copy-done.8, bf16[64,4096]{1,0:T(8,128)(2,1)} %copy-done.10, bf16[64,4096]{1,0:T(8,128)(2,1)} %collective-permute-done.46.refs_3_, bf16[4096,2000]{1,0:T(8,128)(2,1)} %copy.107.refs_4_, s32[256,1]{1,0:T(8,128)} %reshape_squeeze.25.refs_5_), custom_call_target="tpu_custom_call" | custom-call | flops 4194304000 | bytes 18481152 | tf_op jit(solution)/shard_map/head_terms/pallas_call | solution.py:268
  (237 shorter events, 93.8 us)
Async XLA Ops:
  24.8 18.4 %collective-permute-start.7 = (bf16[64,4224]{1,0:T(8,128)(2,1)}, bf16[64,4224]{1,0:T(8,128)(2,1)S(1)}, u32[]{:S(2)}, u32[]{:S(2)}) collective-permute-start(bf16[64,4224]{1,0:T(8,128)(2,1)} %get-tuple-element.13.refs_0_), channel_id=1, source_target_pairs={{0,8},{4,12},{8,0},{12,4},{1,9},{5,13},{9,1},{13,5},{2,10},{6,14},... | collective-permute-start | bytes 1622024 | tf_op jit(solution)/shard_map/ppermute | solution.py:34
  41.7 17.5 %collective-permute-start.28 = (bf16[64,4224]{1,0:T(8,128)(2,1)}, bf16[64,4224]{1,0:T(8,128)(2,1)S(1)}, u32[]{:S(2)}, u32[]{:S(2)}) collective-permute-start(bf16[64,4224]{1,0:T(8,128)(2,1)} %get-tuple-element.17.refs_0_), channel_id=1, source_target_pairs={{0,4},{4,0},{8,12},{12,8},{1,5},{5,1},{9,13},{13,9},{2,6},{6,2},{1... | collective-permute-start | bytes 1622024 | tf_op jit(solution)/shard_map/ppermute | solution.py:34
  43.2 25.7 %collective-permute-start.8 = (bf16[64,4224]{1,0:T(8,128)(2,1)S(1)}, bf16[64,4224]{1,0:T(8,128)(2,1)}, u32[]{:S(2)}, u32[]{:S(2)}) collective-permute-start(bf16[64,4224]{1,0:T(8,128)(2,1)S(1)} %collective-permute-done.7.refs_2_), channel_id=1, source_target_pairs={{0,4},{4,0},{8,12},{12,8},{1,5},{5,1},{9,13},{13,9},{2,6},{6,2},{1... | collective-permute-start | bytes 1622024 | tf_op jit(solution)/shard_map/ppermute | solution.py:34
  43.8 25.2 %collective-permute-start.29 = (bf16[64,4224]{1,0:T(8,128)(2,1)}, bf16[64,4224]{1,0:T(8,128)(2,1)S(1)}, u32[]{:S(2)}, u32[]{:S(2)}) collective-permute-start(bf16[64,4224]{1,0:T(8,128)(2,1)} %get-tuple-element.17.refs_0_), channel_id=1, source_target_pairs={{0,8},{4,12},{8,0},{12,4},{1,9},{5,13},{9,1},{13,5},{2,10},{6,14},... | collective-permute-start | bytes 1622024 | tf_op jit(solution)/shard_map/ppermute | solution.py:34
  44.3 25.2 %collective-permute-start.11 = (bf16[64,4224]{1,0:T(8,128)(2,1)S(1)}, bf16[64,4224]{1,0:T(8,128)(2,1)}, u32[]{:S(2)}, u32[]{:S(2)}) collective-permute-start(bf16[64,4224]{1,0:T(8,128)(2,1)S(1)} %collective-permute-done.7.refs_2_), channel_id=1, source_target_pairs={{0,16},{16,0},{1,17},{17,1},{2,18},{18,2},{3,19},{19,3},{4,20},{20... | collective-permute-start | bytes 1622024 | tf_op jit(solution)/shard_map/ppermute | solution.py:34
  47.7 21.9 %collective-permute-start.10 = (bf16[64,4224]{1,0:T(8,128)(2,1)S(1)}, bf16[64,4224]{1,0:T(8,128)(2,1)}, u32[]{:S(2)}, u32[]{:S(2)}) collective-permute-start(bf16[64,4224]{1,0:T(8,128)(2,1)S(1)} %collective-permute-done.6.refs_1_), channel_id=1, source_target_pairs={{0,16},{16,0},{1,17},{17,1},{2,18},{18,2},{3,19},{19,3},{4,20},{20... | collective-permute-start | bytes 1622024 | tf_op jit(solution)/shard_map/ppermute | solution.py:34
  69.0 38.8 %collective-permute-start.31 = (bf16[64,4224]{1,0:T(8,128)(2,1)}, bf16[64,4224]{1,0:T(8,128)(2,1)S(1)}, u32[]{:S(2)}, u32[]{:S(2)}) collective-permute-start(bf16[64,4224]{1,0:T(8,128)(2,1)} %get-tuple-element.17.refs_0_), channel_id=1, source_target_pairs={{0,16},{16,0},{1,17},{17,1},{2,18},{18,2},{3,19},{19,3},{4,20},{20... | collective-permute-start | bytes 1622024 | tf_op jit(solution)/shard_map/ppermute | solution.py:34
  69.5 38.3 %collective-permute-start.32 = (bf16[64,4224]{1,0:T(8,128)(2,1)S(1)}, bf16[64,4224]{1,0:T(8,128)(2,1)S(1)}, u32[]{:S(2)}, u32[]{:S(2)}) collective-permute-start(bf16[64,4224]{1,0:T(8,128)(2,1)S(1)} %collective-permute-done.28.refs_1_), channel_id=1, source_target_pairs={{0,16},{16,0},{1,17},{17,1},{2,18},{18,2},{3,19},{19,3},{4,20},{20... | collective-permute-start | bytes 1622024 | tf_op jit(solution)/shard_map/ppermute | solution.py:34
  69.5 38.2 %collective-permute-start.33 = (bf16[64,4224]{1,0:T(8,128)(2,1)S(1)}, bf16[64,4224]{1,0:T(8,128)(2,1)S(1)}, u32[]{:S(2)}, u32[]{:S(2)}) collective-permute-start(bf16[64,4224]{1,0:T(8,128)(2,1)S(1)} %collective-permute-done.29.refs_2_), channel_id=1, source_target_pairs={{0,16},{16,0},{1,17},{17,1},{2,18},{18,2},{3,19},{19,3},{4,20},{20... | collective-permute-start | bytes 1622024 | tf_op jit(solution)/shard_map/ppermute | solution.py:34
  70.0 37.8 %collective-permute-start.34 = (bf16[64,4224]{1,0:T(8,128)(2,1)S(1)}, bf16[64,4224]{1,0:T(8,128)(2,1)S(1)}, u32[]{:S(2)}, u32[]{:S(2)}) collective-permute-start(bf16[64,4224]{1,0:T(8,128)(2,1)S(1)} %collective-permute-done.30.refs_3_), channel_id=1, source_target_pairs={{0,16},{16,0},{1,17},{17,1},{2,18},{18,2},{3,19},{19,3},{4,20},{20... | collective-permute-start | bytes 1622024 | tf_op jit(solution)/shard_map/ppermute | solution.py:34
  107.6 38.9 %collective-permute-start.13 = (bf16[256,4096]{1,0:T(8,128)(2,1)}, bf16[256,4096]{1,0:T(8,128)(2,1)S(1)}, u32[]{:S(2)}, u32[]{:S(2)}) collective-permute-start(bf16[256,4096]{1,0:T(8,128)(2,1)} %get-tuple-element.15), channel_id=1, source_target_pairs={{0,16},{16,0},{1,17},{17,1},{2,18},{18,2},{3,19},{19,3},{4,20},{20... | collective-permute-start | bytes 6291464 | tf_op jit(solution)/shard_map/ppermute | solution.py:34
  148.2 25.5 %collective-permute-start.14 = (bf16[2,64,4096]{2,1,0:T(8,128)(2,1)}, bf16[2,64,4096]{2,1,0:T(8,128)(2,1)}, u32[]{:S(2)}, u32[]{:S(2)}) collective-permute-start(bf16[2,64,4096]{2,1,0:T(8,128)(2,1)} %pad_maximum_fusion), channel_id=1, source_target_pairs={{0,4},{4,0},{8,12},{12,8},{1,5},{5,1},{9,13},{13,9},{2,6},{6,2},{1... | collective-permute-start | bytes 3145736 | tf_op jit(solution)/shard_map/ppermute | solution.py:34
  152.3 26.2 %collective-permute-start.36 = (bf16[2,64,4096]{2,1,0:T(8,128)(2,1)}, bf16[2,64,4096]{2,1,0:T(8,128)(2,1)S(1)}, u32[]{:S(2)}, u32[]{:S(2)}) collective-permute-start(bf16[2,64,4096]{2,1,0:T(8,128)(2,1)} %pad_maximum_fusion.1), channel_id=1, source_target_pairs={{0,8},{4,12},{8,0},{12,4},{1,9},{5,13},{9,1},{13,5},{2,10},{6,14},... | collective-permute-start | bytes 3145736 | tf_op jit(solution)/shard_map/ppermute | solution.py:34
  193.3 18.7 %collective-permute-start.17 = (bf16[16,4096]{1,0:T(8,128)(2,1)S(1)}, bf16[16,4096]{1,0:T(8,128)(2,1)S(1)}, u32[]{:S(2)}, u32[]{:S(2)}) collective-permute-start(bf16[16,4096]{1,0:T(8,128)(2,1)S(1)} %get-tuple-element.30), channel_id=1, source_target_pairs={{0,2},{1,3},{2,0},{3,1},{4,6},{5,7},{6,4},{7,5},{8,10},{9,11},{10,... | collective-permute-start | bytes 393224 | tf_op jit(solution)/shard_map/ppermute | solution.py:34
  195.0 17.0 %collective-permute-start.16 = (bf16[16,4096]{1,0:T(8,128)(2,1)S(1)}, bf16[16,4096]{1,0:T(8,128)(2,1)S(1)}, u32[]{:S(2)}, u32[]{:S(2)}) collective-permute-start(bf16[16,4096]{1,0:T(8,128)(2,1)S(1)} %get-tuple-element.31), channel_id=1, source_target_pairs={{0,1},{1,0},{2,3},{3,2},{4,5},{5,4},{6,7},{7,6},{8,9},{9,8},{10,11... | collective-permute-start | bytes 393224 | tf_op jit(solution)/shard_map/ppermute | solution.py:34
  197.7 20.1 %collective-permute-start.40 = (bf16[16,4096]{1,0:T(8,128)(2,1)S(1)}, bf16[16,4096]{1,0:T(8,128)(2,1)S(1)}, u32[]{:S(2)}, u32[]{:S(2)}) collective-permute-start(bf16[16,4096]{1,0:T(8,128)(2,1)S(1)} %get-tuple-element.33), channel_id=1, source_target_pairs={{0,3},{1,2},{2,1},{3,0},{4,7},{5,6},{6,5},{7,4},{8,11},{9,10},{10,... | collective-permute-start | bytes 393224 | tf_op jit(solution)/shard_map/ppermute | solution.py:34
  199.7 20.8 %collective-permute-start.39 = (bf16[16,4096]{1,0:T(8,128)(2,1)S(1)}, bf16[16,4096]{1,0:T(8,128)(2,1)S(1)}, u32[]{:S(2)}, u32[]{:S(2)}) collective-permute-start(bf16[16,4096]{1,0:T(8,128)(2,1)S(1)} %get-tuple-element.34), channel_id=1, source_target_pairs={{0,2},{1,3},{2,0},{3,1},{4,6},{5,7},{6,4},{7,5},{8,10},{9,11},{10,... | collective-permute-start | bytes 393224 | tf_op jit(solution)/shard_map/ppermute | solution.py:34
  200.5 20.0 %collective-permute-start.38 = (bf16[16,4096]{1,0:T(8,128)(2,1)S(1)}, bf16[16,4096]{1,0:T(8,128)(2,1)S(1)}, u32[]{:S(2)}, u32[]{:S(2)}) collective-permute-start(bf16[16,4096]{1,0:T(8,128)(2,1)S(1)} %get-tuple-element.35), channel_id=1, source_target_pairs={{0,1},{1,0},{2,3},{3,2},{4,5},{5,4},{6,7},{7,6},{8,9},{9,8},{10,11... | collective-permute-start | bytes 393224 | tf_op jit(solution)/shard_map/ppermute | solution.py:34
  217.8 17.1 %collective-permute-start.20 = (bf16[16,4096]{1,0:T(8,128)(2,1)S(1)}, bf16[16,4096]{1,0:T(8,128)(2,1)S(1)}, u32[]{:S(2)}, u32[]{:S(2)}) collective-permute-start(bf16[16,4096]{1,0:T(8,128)(2,1)S(1)} %convert_element_type.132), channel_id=1, source_target_pairs={{0,2},{1,3},{2,0},{3,1},{4,6},{5,7},{6,4},{7,5},{8,10},{9,11},{10,... | collective-permute-start | bytes 393224 | tf_op jit(solution)/shard_map/ppermute | solution.py:34
  217.8 17.1 %collective-permute-start.19 = (bf16[16,4096]{1,0:T(8,128)(2,1)S(1)}, bf16[16,4096]{1,0:T(8,128)(2,1)S(1)}, u32[]{:S(2)}, u32[]{:S(2)}) collective-permute-start(bf16[16,4096]{1,0:T(8,128)(2,1)S(1)} %convert_element_type.132), channel_id=1, source_target_pairs={{0,1},{1,0},{2,3},{3,2},{4,5},{5,4},{6,7},{7,6},{8,9},{9,8},{10,11... | collective-permute-start | bytes 393224 | tf_op jit(solution)/shard_map/ppermute | solution.py:34
  241.5 37.8 %collective-permute-start.22 = (bf16[64,4096]{1,0:T(8,128)(2,1)S(1)}, bf16[64,4096]{1,0:T(8,128)(2,1)S(1)}, u32[]{:S(2)}, u32[]{:S(2)}) collective-permute-start(bf16[64,4096]{1,0:T(8,128)(2,1)S(1)} %pad_maximum_fusion.2.refs_0_), channel_id=1, source_target_pairs={{0,4},{4,0},{8,12},{12,8},{1,5},{5,1},{9,13},{13,9},{2,6},{6,2},{1... | collective-permute-start | bytes 1572872 | tf_op jit(solution)/shard_map/ppermute | solution.py:34
  244.2 35.1 %collective-permute-start.24 = (bf16[64,4096]{1,0:T(8,128)(2,1)S(1)}, bf16[64,4096]{1,0:T(8,128)(2,1)}, u32[]{:S(2)}, u32[]{:S(2)}) collective-permute-start(bf16[64,4096]{1,0:T(8,128)(2,1)S(1)} %collective-permute-done.23.refs_2_), channel_id=1, source_target_pairs={{0,4},{4,0},{8,12},{12,8},{1,5},{5,1},{9,13},{13,9},{2,6},{6,2},{1... | collective-permute-start | bytes 1572872 | tf_op jit(solution)/shard_map/ppermute | solution.py:34
  246.2 47.0 %collective-permute-start.45 = (bf16[64,4096]{1,0:T(8,128)(2,1)S(1)}, bf16[64,4096]{1,0:T(8,128)(2,1)S(1)}, u32[]{:S(2)}, u32[]{:S(2)}) collective-permute-start(bf16[64,4096]{1,0:T(8,128)(2,1)S(1)} %pad_maximum_fusion.3.refs_0_), channel_id=1, source_target_pairs={{0,8},{4,12},{8,0},{12,4},{1,9},{5,13},{9,1},{13,5},{2,10},{6,14},... | collective-permute-start | bytes 1572872 | tf_op jit(solution)/shard_map/ppermute | solution.py:34
  254.5 38.7 %collective-permute-start.46 = (bf16[64,4096]{1,0:T(8,128)(2,1)S(1)}, bf16[64,4096]{1,0:T(8,128)(2,1)}, u32[]{:S(2)}, u32[]{:S(2)}) collective-permute-start(bf16[64,4096]{1,0:T(8,128)(2,1)S(1)} %collective-permute-done.44.refs_1_), channel_id=1, source_target_pairs={{0,8},{4,12},{8,0},{12,4},{1,9},{5,13},{9,1},{13,5},{2,10},{6,14},... | collective-permute-start | bytes 1572872 | tf_op jit(solution)/shard_map/ppermute | solution.py:34
  (65 other events, 730.9 us)

commit v2 on v1

v2 whole, which is shorter than its diff:
```python
import functools

import jax
import jax.numpy as jnp
from jax import lax
from jax.experimental import pallas as pl
from jax.experimental.pallas import tpu as pltpu
from jax.sharding import PartitionSpec as P

epsilon = 1e-05
LANES = 128
VMEM_BYTES = 56 * 1024 * 1024


def params(limit=VMEM_BYTES):
    return pltpu.CompilerParams(vmem_limit_bytes=limit)


def whole():
    return pl.BlockSpec(memory_space=pltpu.VMEM)


def anywhere():
    return pl.BlockSpec(memory_space=pl.ANY)


def swap(x, axis, distance):
    size = lax.axis_size(axis)
    return lax.ppermute(x, axis, [(i, i ^ distance) for i in range(size)])


def gather_near(x, axis):
    return [x] + [swap(x, axis, d) for d in range(1, lax.axis_size(axis))]


def gather_plane(x, axis):
    if lax.axis_size(axis) != 4:
        return gather_near(x, axis)
    half = x.shape[0] // 2
    one, two = swap(x, axis, 1), swap(x, axis, 2)
    return [x, one, two, swap(two[:half], axis, 1), swap(one[half:], axis, 2)]


def load_pieces(piece_refs, scratch, sems):
    copies = []
    start = 0
    for i in range(len(piece_refs)):
        count = piece_refs[i].shape[0]
        copies.append(
            pltpu.make_async_copy(piece_refs[i], scratch.at[pl.ds(start, count), :], sems.at[i])
        )
        start += count
    for copy in copies:
        copy.start()
    for copy in copies:
        copy.wait()


def norm_kernel(splits, part, count, *refs):
    slices, gains = refs[:count], refs[count : 2 * count]
    routes_ref, weights_ref = refs[2 * count : 2 * count + 2]
    rows_ref, raw_ref = refs[-2:]
    rows, width = slices[0].shape
    full_width = width * count
    own_rows = rows // count
    me = lax.axis_index("tensor")
    total = jnp.zeros((rows, 1), jnp.float32)
    for piece in slices:
        value = piece[...].astype(jnp.float32)
        total = total + jnp.sum(value * value, axis=1, keepdims=True)
    scale = lax.rsqrt(total / full_width + epsilon)
    start = pl.multiple_of(me * own_rows, own_rows)
    for d in range(count):
        columns = pl.ds(pl.multiple_of((me ^ d) * width, width), width)
        value = slices[d][...].astype(jnp.float32)
        rows_ref[:, columns] = (value * scale * gains[d][0:1, :]).astype(jnp.bfloat16)
        raw_ref[:, columns] = slices[d][pl.ds(start, own_rows), :]
    lane = lax.broadcasted_iota(jnp.int32, (own_rows, LANES), 1)
    expert = lane // 3
    kind = lane - expert * 3
    for i in range(count):
        block = pl.ds((i * splits + part) * own_rows, own_rows)
        weight = jnp.zeros((own_rows, LANES), jnp.float32)
        for j in range(routes_ref.shape[1]):
            named = routes_ref[block, j : j + 1] == expert
            weight = weight + jnp.where(named, weights_ref[block, j : j + 1], 0.0)
        high = weight.astype(jnp.bfloat16).astype(jnp.float32)
        middle = (weight - high).astype(jnp.bfloat16).astype(jnp.float32)
        low = weight - high - middle
        value = jnp.where(kind == 0, high, jnp.where(kind == 1, middle, low))
        rows_ref[i * own_rows : (i + 1) * own_rows, full_width:] = value.astype(jnp.bfloat16)


def norm_rows(slices, gains, routes, route_weights, splits, part, after):
    rows, width = slices[0].shape
    count = len(slices)
    full_width = width * count
    return pl.pallas_call(
        functools.partial(norm_kernel, splits, part, count),
        out_shape=(
            jax.ShapeDtypeStruct((rows, full_width + LANES), jnp.bfloat16),
            jax.ShapeDtypeStruct((rows // count, full_width), jnp.bfloat16),
        ),
        in_specs=[whole()] * (2 * count + 2) + [anywhere()] * len(after),
        out_specs=(whole(), whole()),
        compiler_params=params(),
        cost_estimate=pl.CostEstimate(
            flops=6 * rows * full_width, bytes_accessed=4 * rows * full_width, transcendentals=rows
        ),
        name="norm_rows",
    )(*slices, *gains, routes, route_weights, *after)


def hidden_kernel(pieces, streams, after, *refs):
    piece_refs = refs[:pieces]
    gate_refs = refs[pieces : pieces + streams]
    up_refs = refs[pieces + streams : pieces + 2 * streams]
    out_ref, rows_scr, weight_scr, sems = refs[pieces + 2 * streams + after :]
    depth = gate_refs[0].shape[1]

    @pl.when(pl.program_id(0) == 0)
    def _():
        load_pieces(piece_refs, rows_scr, sems)
        small = rows_scr[:, depth * streams :].astype(jnp.float32)
        lane = lax.broadcasted_iota(jnp.int32, small.shape, 1)
        first = lax.axis_index("expert") * 3
        mine = (lane >= first) & (lane < first + 3)
        weight = jnp.sum(jnp.where(mine, small, 0.0), axis=1, keepdims=True)
        weight_scr[...] = jnp.broadcast_to(0.5 * weight, weight_scr.shape)

    def product(refs):
        total = None
        for i in range(streams):
            rows = rows_scr[:, i * depth : (i + 1) * depth]
            term = jnp.dot(rows, refs[i][0], preferred_element_type=jnp.float32)
            total = term if total is None else total + term
        return total

    gate = product(gate_refs)
    up = product(up_refs)
    hidden = gate * (1.0 + jnp.tanh(0.5 * gate)) * up * weight_scr[:, :1]
    out_ref[...] = hidden.astype(jnp.bfloat16)


def hidden_rows(pieces, w_gate, w_up, after):
    rows = sum(p.shape[0] for p in pieces)
    full_width, hidden = w_gate.shape[1:]
    tile = 256 if hidden % 256 == 0 else hidden
    streams = 2
    depth = full_width // streams
    weight_specs = [
        pl.BlockSpec((1, depth, tile), lambda i, part=part: (0, part, i)) for part in range(streams)
    ]
    return pl.pallas_call(
        functools.partial(hidden_kernel, len(pieces), streams, len(after)),
        out_shape=jax.ShapeDtypeStruct((rows, hidden), jnp.bfloat16),
        grid=(hidden // tile,),
        in_specs=[anywhere()] * len(pieces) + weight_specs * 2 + [anywhere()] * len(after),
        out_specs=pl.BlockSpec((rows, tile), lambda i: (0, i)),
        scratch_shapes=[
            pltpu.VMEM((rows, full_width + LANES), jnp.bfloat16),
            pltpu.VMEM((rows, LANES), jnp.float32),
            pltpu.SemaphoreType.DMA((len(pieces),)),
        ],
        compiler_params=params(),
        cost_estimate=pl.CostEstimate(
            flops=4 * rows * full_width * hidden,
            bytes_accessed=4 * full_width * hidden + 2 * rows * (full_width + hidden),
            transcendentals=rows * hidden,
        ),
        name="hidden_rows",
    )(*pieces, *[w_gate] * streams, *[w_up] * streams, *after)


def down_kernel(streams, after, hidden_ref, *refs):
    outs = refs[streams + after :]
    part = hidden_ref.shape[0] // len(outs)
    for j in range(streams):
        out = jnp.dot(hidden_ref[...], refs[j][0], preferred_element_type=jnp.float32)
        columns = slice(j * out.shape[1], (j + 1) * out.shape[1])
        for i in range(len(outs)):
            outs[i][:, columns] = out[i * part : (i + 1) * part].astype(jnp.bfloat16)


def down_rows(hidden, w_down, parts, after):
    rows, depth = hidden.shape
    full_width = w_down.shape[2]
    tile = 512 if full_width % 512 == 0 else full_width
    streams = 2
    narrow = tile // streams
    shape = jax.ShapeDtypeStruct((rows // parts, full_width), jnp.bfloat16)
    return pl.pallas_call(
        functools.partial(down_kernel, streams, len(after)),
        out_shape=(shape,) * parts,
        grid=(full_width // tile,),
        in_specs=[pl.BlockSpec((rows, depth), lambda i: (0, 0))]
        + [
            pl.BlockSpec((1, depth, narrow), lambda i, part=part: (0, 0, streams * i + part))
            for part in range(streams)
        ]
        + [anywhere()] * len(after),
        out_specs=(pl.BlockSpec((rows // parts, tile), lambda i: (0, i)),) * parts,
        compiler_params=params(),
        cost_estimate=pl.CostEstimate(
            flops=2 * rows * depth * full_width,
            bytes_accessed=2 * depth * full_width + 2 * rows * (depth + full_width),
            transcendentals=0,
        ),
        name="down_rows",
    )(hidden, *[w_down] * streams, *after)


def final_kernel(parts, gains_count, *refs):
    part_refs, raw_ref = refs[:parts], refs[parts]
    gains = refs[parts + 1 : parts + 1 + gains_count]
    out_ref, work = refs[parts + 1 + gains_count :]
    width = gains[0].shape[1]
    me = lax.axis_index("tensor")
    mixed = part_refs[0][...].astype(jnp.float32)
    for part in part_refs[1:]:
        mixed = mixed + part[...].astype(jnp.float32)
    residual = raw_ref[...].astype(jnp.float32) + mixed
    residual = residual.astype(jnp.bfloat16).astype(jnp.float32)
    total = jnp.sum(residual * residual, axis=1, keepdims=True)
    scale = lax.rsqrt(total / residual.shape[1] + epsilon)
    work[...] = residual * scale
    for d in range(gains_count):
        columns = pl.ds(pl.multiple_of((me ^ d) * width, width), width)
        out_ref[:, columns] = (work[:, columns] * gains[d][1:2, :]).astype(jnp.bfloat16)


def final_rows(parts, raw, gains):
    rows, full_width = raw.shape
    return pl.pallas_call(
        functools.partial(final_kernel, len(parts), len(gains)),
        out_shape=jax.ShapeDtypeStruct((rows, full_width), jnp.bfloat16),
        in_specs=[whole()] * (len(parts) + 1 + len(gains)),
        out_specs=whole(),
        scratch_shapes=[pltpu.VMEM((rows, full_width), jnp.float32)],
        compiler_params=params(),
        cost_estimate=pl.CostEstimate(
            flops=8 * rows * full_width, bytes_accessed=12 * rows * full_width, transcendentals=rows
        ),
        name="final_rows",
    )(*parts, raw, *gains)


def head_kernel(pieces, *refs):
    piece_refs = refs[:pieces]
    head_ref, target_ref, out_ref, rows_scr, sems = refs[pieces:]
    step = pl.program_id(0)
    tile = head_ref.shape[0]

    @pl.when(step == 0)
    def _():
        load_pieces(piece_refs, rows_scr, sems)
        lane = lax.broadcasted_iota(jnp.int32, out_ref.shape, 0)
        out_ref[...] = jnp.where(lane == 0, -jnp.inf, 0.0)

    logits = lax.dot_general(
        head_ref[...],
        rows_scr[...],
        (((1,), (1,)), ((), ())),
        preferred_element_type=jnp.float32,
    )
    word = lax.broadcasted_iota(jnp.int32, logits.shape, 0) + step * tile
    old_top, old_total = out_ref[0:1, :], out_ref[1:2, :]
    top = jnp.maximum(old_top, jnp.max(logits, axis=0, keepdims=True))
    out_ref[0:1, :] = top
    out_ref[1:2, :] = old_total * jnp.exp(old_top - top) + jnp.sum(
        jnp.exp(logits - top), axis=0, keepdims=True
    )
    hit = word == target_ref[...]
    out_ref[2:3, :] += jnp.sum(jnp.where(hit, logits, 0.0), axis=0, keepdims=True)


def head_terms(pieces, head_rows, targets):
    rows = sum(p.shape[0] for p in pieces)
    vocab_part, full_width = head_rows.shape
    tile = 400 if vocab_part % 400 == 0 else vocab_part
    return pl.pallas_call(
        functools.partial(head_kernel, len(pieces)),
        out_shape=jax.ShapeDtypeStruct((8, rows), jnp.float32),
        grid=(vocab_part // tile,),
        in_specs=[anywhere()] * len(pieces)
        + [
            pl.BlockSpec((tile, full_width), lambda i: (i, 0)),
            pl.BlockSpec((1, rows), lambda i: (0, 0)),
        ],
        out_specs=pl.BlockSpec((8, rows), lambda i: (0, 0)),
        scratch_shapes=[
            pltpu.VMEM((rows, full_width), jnp.bfloat16),
            pltpu.SemaphoreType.DMA((len(pieces),)),
        ],
        compiler_params=params(),
        cost_estimate=pl.CostEstimate(
            flops=2 * rows * full_width * vocab_part,
            bytes_accessed=2 * full_width * (vocab_part + rows),
            transcendentals=rows * vocab_part,
        ),
        name="head_terms",
    )(*pieces, head_rows, targets)


def join_terms(parts):
    top = functools.reduce(jnp.maximum, [p[0] for p in parts])
    total = sum(p[1] * jnp.exp(p[0] - top) for p in parts)
    target = sum(p[2] for p in parts)
    return jnp.stack([top, total, target])


def flip(x, axis, index):
    size = x.shape[axis]
    bit = 1
    while bit < size:
        shape = x.shape[:axis] + (size // (2 * bit), 2, bit) + x.shape[axis + 1 :]
        turned = jnp.flip(x.reshape(shape), axis + 1).reshape(x.shape)
        x = jnp.where((index & bit) != 0, turned, x)
        bit *= 2
    return x


def sum_plane(kept, got):
    f32, b16 = jnp.float32, jnp.bfloat16
    count, rows = kept.shape[:2]

    def both(d, part=slice(None)):
        return kept[d, part].astype(f32) + got[d, part].astype(f32)

    if count != 4:
        total = both(0)
        for d in range(1, count):
            total = total + swap(both(d).astype(b16), "expert", d).astype(f32)
        return total.astype(b16), []
    upper, lower = slice(0, rows // 2), slice(rows // 2, rows)
    one = jnp.stack([both(1, upper), both(3, upper)]).astype(b16)
    two = jnp.stack([both(2, lower), both(3, lower)]).astype(b16)
    from_one, from_two = swap(one, "expert", 1), swap(two, "expert", 2)
    pass_two = (both(2, upper) + from_one[1].astype(f32)).astype(b16)
    pass_one = (both(1, lower) + from_two[1].astype(f32)).astype(b16)
    last_two, last_one = swap(pass_two, "expert", 2), swap(pass_one, "expert", 1)
    total = jnp.concatenate(
        [
            both(0, upper) + from_one[0].astype(f32) + last_two.astype(f32),
            both(0, lower) + from_two[0].astype(f32) + last_one.astype(f32),
        ]
    )
    return total.astype(b16), [one, two, pass_one, pass_two]


def on_device(
    tokens, routes, route_weights, norm_gain, final_gain, w_gate, w_up, w_down, head_weight, targets
):
    tok_rows, width = tokens.shape
    n_expert = lax.axis_size("expert")
    n_tensor = lax.axis_size("tensor")
    my_expert = lax.axis_index("expert")
    my_tensor = lax.axis_index("tensor")
    full_width = width * n_tensor
    own = tok_rows // n_tensor
    splits = 2 if own % 32 == 0 else 1
    sub = own // splits
    rows = sub * n_tensor
    vocab_part = head_weight.shape[1]

    parts = tokens.reshape(n_tensor, splits, sub, width)
    slices = [gather_near(parts[:, h].reshape(rows, width), "tensor") for h in range(splits)]
    gains = gather_near(jnp.stack([norm_gain, final_gain]), "tensor")
    pieces, raws = [], []
    after = []
    for h in range(splits):
        normed, raw = norm_rows(slices[h], gains, routes, route_weights, splits, h, after)
        plane = gather_plane(normed, "expert")
        pieces.append(plane + [swap(p, "seq", 1) for p in plane])
        raws.append(raw)
        after = plane[1:3]

    finals = []
    sent = [[], []]
    for h in range(splits):
        hidden = hidden_rows(pieces[h], w_gate, w_up, sent[0])
        kept, other = down_rows(hidden, w_down, 2, sent[1])
        got = swap(other, "seq", 1)
        shape = (n_expert, rows, full_width)
        total, moved = sum_plane(kept.reshape(shape), got.reshape(shape))
        sent = [moved[:2], moved[2:]]
        total = total.reshape(n_tensor, sub, full_width)
        mine = [lax.dynamic_index_in_dim(total, my_tensor, 0, False)]
        for d in range(1, n_tensor):
            out = lax.dynamic_index_in_dim(total, my_tensor ^ d, 0, False)
            mine.append(swap(out, "tensor", d))
        finals.append(final_rows(mine, raws[h], gains))

    start = (my_expert * n_tensor + my_tensor) * vocab_part
    local = (targets - start).astype(jnp.int32).reshape(n_expert, n_tensor, splits, sub)
    local = flip(flip(local, 0, my_expert), 1, my_tensor)
    head_rows = head_weight.T
    terms = []
    for h in range(splits):
        column = jnp.concatenate(gather_near(finals[h], "tensor"), axis=0)
        plane = gather_plane(column, "expert")
        term = head_terms(plane, head_rows, local[:, :, h].reshape(1, -1))
        terms.append(term[:3].reshape(3, n_expert, n_tensor, sub))
    terms = jnp.stack(terms, axis=3)
    joined = join_terms(
        [terms[:, :, 0]] + [swap(terms[:, :, d], "tensor", d) for d in range(1, n_tensor)]
    )
    joined = join_terms(
        [joined[:, 0]] + [swap(joined[:, d], "expert", d) for d in range(1, n_expert)]
    )
    return (joined[0] + jnp.log(joined[1]) - joined[2]).reshape(own)


def solution(mesh):
    return jax.shard_map(
        on_device,
        mesh=mesh,
        in_specs=(
            P(("seq", "expert"), "tensor"),
            P(("seq", "expert"), None),
            P(("seq", "expert"), None),
            P("tensor"),
            P("tensor"),
            P("expert", None, ("seq", "tensor")),
            P("expert", None, ("seq", "tensor")),
            P("expert", ("seq", "tensor"), None),
            P(None, ("expert", "tensor")),
            P("seq"),
        ),
        out_specs=P(("seq", "expert", "tensor")),
        check_vma=False,
    )
```

time: 323 us -> 318 us (0.985)
  local copies, waits for them, and re-layouts: 40.8 us -> 19.8 us
  waiting for transfers between devices: 99.6 us -> 110 us
  starting transfers between devices: 63 us -> 70.1 us
    unnamed x76 -> x106, local copies, waits for them, and re-layouts: 31.6 us -> 9.79 us
    ppermute x53 -> x63, waiting for transfers between devices: 99.6 us -> 110 us  [swap(): return lax.ppermute(x, axis, [(i, i ^ distance) for i in range(size)])]
    ppermute x53 -> x63, starting transfers between devices: 63 us -> 70.1 us  [swap(): return lax.ppermute(x, axis, [(i, i ^ distance) for i in range(size)])]
    convert_element_type x6 -> x2, other arithmetic: 7.31 us -> 3.32 us  [sum_plane(): pass_two = (both(2, upper) + from_one[1].astype(f32)).astype(b16)]
  transfers between devices with their start and end apart: 53 -> 63, of which waited for: 22 -> 31; matrix products, arithmetic and copies ran while one was open for 13% -> 6% of each run, Pallas kernels for 28% -> 13%
where the time goes in v2:
time: 318 us; the launch traced here: 316 us
  waiting for transfers between devices  110 us (35%)
  Pallas kernels  104 us (33%)
  starting transfers between devices  70.1 us (22%)
  local copies, waits for them, and re-layouts  19.8 us (6%)
  other arithmetic  11.6 us (4%)
    ppermute x63, waiting for transfers between devices, swap(): return lax.ppermute(x, axis, [(i, i ^ distance) for i in range(size)])  110 us
    ppermute x63, starting transfers between devices, swap(): return lax.ppermute(x, axis, [(i, i ^ distance) for i in range(size)])  70.1 us
    pallas_call x2, Pallas kernels, hidden_rows(): pl.pallas_call(functools.partial(hidden_kernel, len(pieces), streams, len...  45 us
    pallas_call x2, Pallas kernels, down_rows(): pl.pallas_call(functools.partial(down_kernel, streams, len(after)), out_s...  27.2 us
    pallas_call x2, Pallas kernels, head_terms(): pl.pallas_call(functools.partial(head_kernel, len(pieces)), out_shape=jax...  23.3 us
    unnamed x106, local copies, waits for them, and re-layouts  9.79 us
  transfers between devices with their start and end apart: 63, of which 31 were waited for; matrix products, arithmetic and copies ran while one was open for 6% of the time, Pallas kernels for 13%

profile of v2, /device:TPU:0, one launch (start us, length us, event | category | flops | bytes accessed | tf_op | source)
XLA Modules:
  0.0 316.3 jit_solution(16275172897829920474)
XLA Ops:
  1.0 3.1 collective-permute-start
  4.1 2.6 collective-permute-start.1
  8.4 3.5 %collective-permute-start.4 = (f32[2,1024]{1,0:T(2,128)S(1)}, f32[2,1024]{1,0:T(2,128)S(1)}, u32[]{:S(2)}, u32[]{:S(2)}) collective-permute-start(f32[2,1024]{1,0:T(2,128)S(1)} %pad_maximum_fusion.8.refs_4_.refs_5_), channel_id=1, source_target_pairs={{0,2},{1,3},{2,0},{3,1},{4,6},{5,7},{6,4},{7,5},{8,10},{9,11},{10,... | collective-permute-start | bytes 24584 | tf_op jit(solution)/shard_map/ppermute | solution.py:29
  25.7 9.8 %collective-permute-done.7.refs_2_.refs_11_ = bf16[64,4224]{1,0:T(8,128)(2,1)S(1)} collective-permute-done((bf16[64,4224]{1,0:T(8,128)(2,1)}, bf16[64,4224]{1,0:T(8,128)(2,1)S(1)}, u32[]{:S(2)}, u32[]{:S(2)}) %collective-permute-start.7) | collective-permute-done | bytes 540704 | tf_op jit(solution)/shard_map/ppermute | solution.py:29
  39.2 3.3 %collective-permute-done.8.refs_3_ = bf16[32,4224]{1,0:T(8,128)(2,1)S(1)} collective-permute-done((bf16[32,4224]{1,0:T(8,128)(2,1)S(1)}, bf16[32,4224]{1,0:T(8,128)(2,1)S(1)}, u32[]{:S(2)}, u32[]{:S(2)}) %collective-permute-start.8) | collective-permute-done | bytes 270368 | tf_op jit(solution)/shard_map/ppermute | solution.py:29
  42.5 4.3 %collective-permute-done.9.refs_4_ = bf16[32,4224]{1,0:T(8,128)(2,1)S(1)} collective-permute-done((bf16[32,4224]{1,0:T(8,128)(2,1)S(1)}, bf16[32,4224]{1,0:T(8,128)(2,1)S(1)}, u32[]{:S(2)}, u32[]{:S(2)}) %collective-permute-start.9) | collective-permute-done | bytes 270368 | tf_op jit(solution)/shard_map/ppermute | solution.py:29
  49.1 22.5 %hidden_rows.2.hidden_ref = bf16[512,1792]{1,0:T(8,128)(2,1)} custom-call(bf16[64,4224]{1,0:T(8,128)(2,1)} %get-tuple-element.13.refs_0_, bf16[64,4224]{1,0:T(8,128)(2,1)} %copy-done.1, bf16[64,4224]{1,0:T(8,128)(2,1)} %copy-done, bf16[32,4224]{1,0:T(8,128)(2,1)} %copy-done.30, bf16[32,4224]{1,0:T(8,128)(2,1)} %copy-done.31, bf16[64,4224]{1,0:T(8,128)(2,1)} %copy-done.19, ...), custom_call_target="tpu_custom_call" | custom-call | flops 15032385536 | bytes 35389440 | tf_op jit(solution)/shard_map/hidden_rows/pallas_call | solution.py:154
  71.6 13.6 %down_rows.2 = (bf16[256,4096]{1,0:T(8,128)(2,1)}, bf16[256,4096]{1,0:T(8,128)(2,1)}) custom-call(bf16[512,1792]{1,0:T(8,128)(2,1)} %hidden_rows.2.hidden_ref, bf16[1,1792,4096]{2,1,0:T(8,128)(2,1)} %refs_1_.3, bf16[1,1792,4096]{2,1,0:T(8,128)(2,1)} %refs_1_.3), custom_call_target="tpu_custom_call" | custom-call | flops 7516192768 | bytes 20709376 | tf_op jit(solution)/shard_map/down_rows/pallas_call | solution.py:192
  89.8 3.7 %collective-permute-done.30.refs_1_ = bf16[64,1024]{1,0:T(8,128)(2,1)S(1)} collective-permute-done((bf16[64,1024]{1,0:T(8,128)(2,1)S(1)}, bf16[64,1024]{1,0:T(8,128)(2,1)S(1)}, u32[]{:S(2)}, u32[]{:S(2)}) %collective-permute-start.30) | collective-permute-done | bytes 131104 | tf_op jit(solution)/shard_map/ppermute | solution.py:29
  93.5 5.5 %collective-permute-done.31.refs_2_ = bf16[64,1024]{1,0:T(8,128)(2,1)S(1)} collective-permute-done((bf16[64,1024]{1,0:T(8,128)(2,1)S(1)}, bf16[64,1024]{1,0:T(8,128)(2,1)S(1)}, u32[]{:S(2)}, u32[]{:S(2)}) %collective-permute-start.31) | collective-permute-done | bytes 131104 | tf_op jit(solution)/shard_map/ppermute | solution.py:29
  104.4 10.4 %collective-permute-done.34.refs_2_ = bf16[64,4224]{1,0:T(8,128)(2,1)S(1)} collective-permute-done((bf16[64,4224]{1,0:T(8,128)(2,1)}, bf16[64,4224]{1,0:T(8,128)(2,1)S(1)}, u32[]{:S(2)}, u32[]{:S(2)}) %collective-permute-start.34) | collective-permute-done | bytes 540704 | tf_op jit(solution)/shard_map/ppermute | solution.py:29
  118.1 3.5 %collective-permute-done.35.refs_3_ = bf16[32,4224]{1,0:T(8,128)(2,1)S(1)} collective-permute-done((bf16[32,4224]{1,0:T(8,128)(2,1)S(1)}, bf16[32,4224]{1,0:T(8,128)(2,1)S(1)}, u32[]{:S(2)}, u32[]{:S(2)}) %collective-permute-start.35) | collective-permute-done | bytes 270368 | tf_op jit(solution)/shard_map/ppermute | solution.py:29
  129.0 22.5 %hidden_rows.3.hidden_ref = bf16[512,1792]{1,0:T(8,128)(2,1)} custom-call(bf16[64,4224]{1,0:T(8,128)(2,1)} %get-tuple-element.17.refs_0_, bf16[64,4224]{1,0:T(8,128)(2,1)} %copy-done.10, bf16[64,4224]{1,0:T(8,128)(2,1)} %copy-done.9, bf16[32,4224]{1,0:T(8,128)(2,1)} %copy-done.26, bf16[32,4224]{1,0:T(8,128)(2,1)} %copy-done.27, bf16[64,4224]{1,0:T(8,128)(2,1)} %copy-done.17, ...), custom_call_target="tpu_custom_call" | custom-call | flops 15032385536 | bytes 35389440 | tf_op jit(solution)/shard_map/hidden_rows/pallas_call | solution.py:154
  153.6 13.6 %down_rows.3 = (bf16[256,4096]{1,0:T(8,128)(2,1)}, bf16[256,4096]{1,0:T(8,128)(2,1)}) custom-call(bf16[512,1792]{1,0:T(8,128)(2,1)} %hidden_rows.3.hidden_ref, bf16[1,1792,4096]{2,1,0:T(8,128)(2,1)} %refs_1_.3, bf16[1,1792,4096]{2,1,0:T(8,128)(2,1)} %refs_1_.3, bf16[32,4096]{1,0:T(8,128)(2,1)} %get-tuple-element.36.refs_2_, ...), custom_call_target="tpu_custom_call" | custom-call | flops 7516192768 | bytes 20709376 | tf_op jit(solution)/shard_map/down_rows/pallas_call | solution.py:192
  178.2 9.6 %collective-permute-done.45 = bf16[2,32,4096]{2,1,0:T(8,128)(2,1)S(1)} collective-permute-done((bf16[2,32,4096]{2,1,0:T(8,128)(2,1)S(1)}, bf16[2,32,4096]{2,1,0:T(8,128)(2,1)S(1)}, u32[]{:S(2)}, u32[]{:S(2)}) %collective-permute-start.45) | collective-permute-done | bytes 524320 | tf_op jit(solution)/shard_map/ppermute | solution.py:29
  201.7 3.9 %collective-permute-done.21.refs_2_ = bf16[16,4096]{1,0:T(8,128)(2,1)S(1)} collective-permute-done((bf16[16,4096]{1,0:T(8,128)(2,1)S(1)}, bf16[16,4096]{1,0:T(8,128)(2,1)S(1)}, u32[]{:S(2)}, u32[]{:S(2)}) %collective-permute-start.21) | collective-permute-done | bytes 131104 | tf_op jit(solution)/shard_map/ppermute | solution.py:29
  216.2 17.5 %collective-permute-done.48.refs_2_ = bf16[16,4096]{1,0:T(8,128)(2,1)S(1)} collective-permute-done((bf16[16,4096]{1,0:T(8,128)(2,1)S(1)}, bf16[16,4096]{1,0:T(8,128)(2,1)S(1)}, u32[]{:S(2)}, u32[]{:S(2)}) %collective-permute-start.48) | collective-permute-done | bytes 131104 | tf_op jit(solution)/shard_map/ppermute | solution.py:29
  243.9 6.8 %collective-permute-done.51 = bf16[16,4096]{1,0:T(8,128)(2,1)S(1)} collective-permute-done((bf16[16,4096]{1,0:T(8,128)(2,1)}, bf16[16,4096]{1,0:T(8,128)(2,1)S(1)}, u32[]{:S(2)}, u32[]{:S(2)}) %collective-permute-start.51) | collective-permute-done | bytes 131104 | tf_op jit(solution)/shard_map/ppermute | solution.py:29
  253.8 2.9 collective-permute-done.27.refs_2_
  261.7 6.2 %collective-permute-done.54.refs_2_ = bf16[64,4096]{1,0:T(8,128)(2,1)S(1)} collective-permute-done((bf16[64,4096]{1,0:T(8,128)(2,1)S(1)}, bf16[64,4096]{1,0:T(8,128)(2,1)S(1)}, u32[]{:S(2)}, u32[]{:S(2)}) %collective-permute-start.54) | collective-permute-done | bytes 524320 | tf_op jit(solution)/shard_map/ppermute | solution.py:29
  271.5 3.3 %collective-permute-done.28.refs_3_ = bf16[32,4096]{1,0:T(8,128)(2,1)S(1)} collective-permute-done((bf16[32,4096]{1,0:T(8,128)(2,1)}, bf16[32,4096]{1,0:T(8,128)(2,1)S(1)}, u32[]{:S(2)}, u32[]{:S(2)}) %collective-permute-start.28) | collective-permute-done | bytes 262176 | tf_op jit(solution)/shard_map/ppermute | solution.py:29
  275.6 11.6 %head_terms.2 = f32[8,256]{1,0:T(8,128)} custom-call(bf16[64,4096]{1,0:T(8,128)(2,1)} %copy-done.7, bf16[64,4096]{1,0:T(8,128)(2,1)} %copy-done.13, bf16[64,4096]{1,0:T(8,128)(2,1)} %copy-done.11, bf16[32,4096]{1,0:T(8,128)(2,1)} %copy-done.34, bf16[32,4096]{1,0:T(8,128)(2,1)} %collective-permute-done.29.refs_4_, bf16[2000,4096]{1,0:T(8,128)(2,1)} %bitcast.98, ...), custom_call_target="tpu_custom_call" | custom-call | flops 4194304000 | bytes 18481152 | tf_op jit(solution)/shard_map/head_terms/pallas_call | solution.py:281
  288.1 11.7 %head_terms.3 = f32[8,256]{1,0:T(8,128)} custom-call(bf16[64,4096]{1,0:T(8,128)(2,1)} %copy-done.8, bf16[64,4096]{1,0:T(8,128)(2,1)} %copy-done.14, bf16[64,4096]{1,0:T(8,128)(2,1)} %copy-done.12, bf16[32,4096]{1,0:T(8,128)(2,1)} %collective-permute-done.55.refs_3_, bf16[32,4096]{1,0:T(8,128)(2,1)} %collective-permute-done.56.refs_4_, ...), custom_call_target="tpu_custom_call" | custom-call | flops 4194304000 | bytes 18481152 | tf_op jit(solution)/shard_map/head_terms/pallas_call | solution.py:281
  305.8 2.7 collective-permute-done.59
  (289 shorter events, 117.4 us)
Async XLA Ops:
  1.0 18.0 %collective-permute-start = (bf16[64,1024]{1,0:T(8,128)(2,1)S(1)}, bf16[64,1024]{1,0:T(8,128)(2,1)S(1)}, u32[]{:S(2)}, u32[]{:S(2)}) collective-permute-start(bf16[64,1024]{1,0:T(8,128)(2,1)S(1)} %bitcast.115), channel_id=1, source_target_pairs={{0,1},{1,0},{2,3},{3,2},{4,5},{5,4},{6,7},{7,6},{8,9},{9,8},{10,11... | collective-permute-start | bytes 393224 | tf_op jit(solution)/shard_map/ppermute | solution.py:29
  4.1 15.0 %collective-permute-start.1 = (bf16[64,1024]{1,0:T(8,128)(2,1)S(1)}, bf16[64,1024]{1,0:T(8,128)(2,1)S(1)}, u32[]{:S(2)}, u32[]{:S(2)}) collective-permute-start(bf16[64,1024]{1,0:T(8,128)(2,1)S(1)} %bitcast.116), channel_id=1, source_target_pairs={{0,2},{1,3},{2,0},{3,1},{4,6},{5,7},{6,4},{7,5},{8,10},{9,11},{10,... | collective-permute-start | bytes 393224 | tf_op jit(solution)/shard_map/ppermute | solution.py:29
  24.2 13.5 %collective-permute-start.6 = (bf16[64,4224]{1,0:T(8,128)(2,1)}, bf16[64,4224]{1,0:T(8,128)(2,1)S(1)}, u32[]{:S(2)}, u32[]{:S(2)}) collective-permute-start(bf16[64,4224]{1,0:T(8,128)(2,1)} %get-tuple-element.13.refs_0_), channel_id=1, source_target_pairs={{0,4},{4,0},{8,12},{12,8},{1,5},{5,1},{9,13},{13,9},{2,6},{6,2},{1... | collective-permute-start | bytes 1622024 | tf_op jit(solution)/shard_map/ppermute | solution.py:29
  25.7 21.1 %collective-permute-start.10 = (bf16[64,4224]{1,0:T(8,128)(2,1)}, bf16[64,4224]{1,0:T(8,128)(2,1)S(1)}, u32[]{:S(2)}, u32[]{:S(2)}) collective-permute-start(bf16[64,4224]{1,0:T(8,128)(2,1)} %get-tuple-element.13.refs_0_), channel_id=1, source_target_pairs={{0,16},{16,0},{1,17},{17,1},{2,18},{18,2},{3,19},{19,3},{4,20},{20... | collective-permute-start | bytes 1622024 | tf_op jit(solution)/shard_map/ppermute | solution.py:29
  85.3 38.4 %collective-permute-start.15 = (bf16[256,4096]{1,0:T(8,128)(2,1)}, bf16[256,4096]{1,0:T(8,128)(2,1)S(1)}, u32[]{:S(2)}, u32[]{:S(2)}) collective-permute-start(bf16[256,4096]{1,0:T(8,128)(2,1)} %get-tuple-element.15), channel_id=1, source_target_pairs={{0,16},{16,0},{1,17},{17,1},{2,18},{18,2},{3,19},{19,3},{4,20},{20... | collective-permute-start | bytes 6291464 | tf_op jit(solution)/shard_map/ppermute | solution.py:29
  103.7 13.5 %collective-permute-start.33 = (bf16[64,4224]{1,0:T(8,128)(2,1)}, bf16[64,4224]{1,0:T(8,128)(2,1)S(1)}, u32[]{:S(2)}, u32[]{:S(2)}) collective-permute-start(bf16[64,4224]{1,0:T(8,128)(2,1)} %get-tuple-element.17.refs_0_), channel_id=1, source_target_pairs={{0,4},{4,0},{8,12},{12,8},{1,5},{5,1},{9,13},{13,9},{2,6},{6,2},{1... | collective-permute-start | bytes 1622024 | tf_op jit(solution)/shard_map/ppermute | solution.py:29
  124.7 26.8 %collective-permute-start.18 = (bf16[2,32,4096]{2,1,0:T(8,128)(2,1)S(1)}, bf16[2,32,4096]{2,1,0:T(8,128)(2,1)S(1)}, u32[]{:S(2)}, u32[]{:S(2)}) collective-permute-start(bf16[2,32,4096]{2,1,0:T(8,128)(2,1)S(1)} %pad_maximum_fusion.1.refs_15_), channel_id=1, source_target_pairs={{0,8},{4,12},{8,0},{12,4},{1,9},{5,13},{9,1},{13,5},{2,10},{6,14},... | collective-permute-start | bytes 1572872 | tf_op jit(solution)/shard_map/ppermute | solution.py:29
  125.2 26.3 %collective-permute-start.16 = (bf16[2,32,4096]{2,1,0:T(8,128)(2,1)S(1)}, bf16[2,32,4096]{2,1,0:T(8,128)(2,1)}, u32[]{:S(2)}, u32[]{:S(2)}) collective-permute-start(bf16[2,32,4096]{2,1,0:T(8,128)(2,1)S(1)} %pad_maximum_fusion.refs_14_), channel_id=1, source_target_pairs={{0,4},{4,0},{8,12},{12,8},{1,5},{5,1},{9,13},{13,9},{2,6},{6,2},{1... | collective-permute-start | bytes 1572872 | tf_op jit(solution)/shard_map/ppermute | solution.py:29
  173.7 14.2 %collective-permute-start.45 = (bf16[2,32,4096]{2,1,0:T(8,128)(2,1)S(1)}, bf16[2,32,4096]{2,1,0:T(8,128)(2,1)S(1)}, u32[]{:S(2)}, u32[]{:S(2)}) collective-permute-start(bf16[2,32,4096]{2,1,0:T(8,128)(2,1)S(1)} %pad_maximum_fusion.5), channel_id=1, source_target_pairs={{0,8},{4,12},{8,0},{12,4},{1,9},{5,13},{9,1},{13,5},{2,10},{6,14},... | collective-permute-start | bytes 1572872 | tf_op jit(solution)/shard_map/ppermute | solution.py:29
  174.3 13.8 %collective-permute-start.43 = (bf16[2,32,4096]{2,1,0:T(8,128)(2,1)S(1)}, bf16[2,32,4096]{2,1,0:T(8,128)(2,1)S(1)}, u32[]{:S(2)}, u32[]{:S(2)}) collective-permute-start(bf16[2,32,4096]{2,1,0:T(8,128)(2,1)S(1)} %pad_maximum_fusion.4), channel_id=1, source_target_pairs={{0,4},{4,0},{8,12},{12,8},{1,5},{5,1},{9,13},{13,9},{2,6},{6,2},{1... | collective-permute-start | bytes 1572872 | tf_op jit(solution)/shard_map/ppermute | solution.py:29
  199.8 14.9 %collective-permute-start.47 = (bf16[16,4096]{1,0:T(8,128)(2,1)S(1)}, bf16[16,4096]{1,0:T(8,128)(2,1)S(1)}, u32[]{:S(2)}, u32[]{:S(2)}) collective-permute-start(bf16[16,4096]{1,0:T(8,128)(2,1)S(1)} %get-tuple-element.47), channel_id=1, source_target_pairs={{0,1},{1,0},{2,3},{3,2},{4,5},{5,4},{6,7},{7,6},{8,9},{9,8},{10,11... | collective-permute-start | bytes 393224 | tf_op jit(solution)/shard_map/ppermute | solution.py:29
  208.4 30.9 %collective-permute-start.23 = (bf16[16,4096]{1,0:T(8,128)(2,1)}, bf16[16,4096]{1,0:T(8,128)(2,1)S(1)}, u32[]{:S(2)}, u32[]{:S(2)}) collective-permute-start(bf16[16,4096]{1,0:T(8,128)(2,1)} %final_rows.2), channel_id=1, source_target_pairs={{0,1},{1,0},{2,3},{3,2},{4,5},{5,4},{6,7},{7,6},{8,9},{9,8},{10,11... | collective-permute-start | bytes 393224 | tf_op jit(solution)/shard_map/ppermute | solution.py:29
  210.3 30.5 %collective-permute-start.24 = (bf16[16,4096]{1,0:T(8,128)(2,1)}, bf16[16,4096]{1,0:T(8,128)(2,1)S(1)}, u32[]{:S(2)}, u32[]{:S(2)}) collective-permute-start(bf16[16,4096]{1,0:T(8,128)(2,1)} %final_rows.2), channel_id=1, source_target_pairs={{0,2},{1,3},{2,0},{3,1},{4,6},{5,7},{6,4},{7,5},{8,10},{9,11},{10,... | collective-permute-start | bytes 393224 | tf_op jit(solution)/shard_map/ppermute | solution.py:29
  211.2 29.6 %collective-permute-start.25 = (bf16[16,4096]{1,0:T(8,128)(2,1)}, bf16[16,4096]{1,0:T(8,128)(2,1)S(1)}, u32[]{:S(2)}, u32[]{:S(2)}) collective-permute-start(bf16[16,4096]{1,0:T(8,128)(2,1)} %final_rows.2), channel_id=1, source_target_pairs={{0,3},{1,2},{2,1},{3,0},{4,7},{5,6},{6,5},{7,4},{8,11},{9,10},{10,... | collective-permute-start | bytes 393224 | tf_op jit(solution)/shard_map/ppermute | solution.py:29
  212.8 20.9 %collective-permute-start.48 = (bf16[16,4096]{1,0:T(8,128)(2,1)S(1)}, bf16[16,4096]{1,0:T(8,128)(2,1)S(1)}, u32[]{:S(2)}, u32[]{:S(2)}) collective-permute-start(bf16[16,4096]{1,0:T(8,128)(2,1)S(1)} %get-tuple-element.46), channel_id=1, source_target_pairs={{0,2},{1,3},{2,0},{3,1},{4,6},{5,7},{6,4},{7,5},{8,10},{9,11},{10,... | collective-permute-start | bytes 393224 | tf_op jit(solution)/shard_map/ppermute | solution.py:29
  214.7 19.0 %collective-permute-start.49 = (bf16[16,4096]{1,0:T(8,128)(2,1)S(1)}, bf16[16,4096]{1,0:T(8,128)(2,1)S(1)}, u32[]{:S(2)}, u32[]{:S(2)}) collective-permute-start(bf16[16,4096]{1,0:T(8,128)(2,1)S(1)} %get-tuple-element.45), channel_id=1, source_target_pairs={{0,3},{1,2},{2,1},{3,0},{4,7},{5,6},{6,5},{7,4},{8,11},{9,10},{10,... | collective-permute-start | bytes 393224 | tf_op jit(solution)/shard_map/ppermute | solution.py:29
  241.8 14.9 %collective-permute-start.27 = (bf16[64,4096]{1,0:T(8,128)(2,1)S(1)}, bf16[64,4096]{1,0:T(8,128)(2,1)S(1)}, u32[]{:S(2)}, u32[]{:S(2)}) collective-permute-start(bf16[64,4096]{1,0:T(8,128)(2,1)S(1)} %pad_maximum_fusion.3.refs_0_), channel_id=1, source_target_pairs={{0,8},{4,12},{8,0},{12,4},{1,9},{5,13},{9,1},{13,5},{2,10},{6,14},... | collective-permute-start | bytes 1572872 | tf_op jit(solution)/shard_map/ppermute | solution.py:29
  243.1 15.6 %collective-permute-start.26 = (bf16[64,4096]{1,0:T(8,128)(2,1)S(1)}, bf16[64,4096]{1,0:T(8,128)(2,1)S(1)}, u32[]{:S(2)}, u32[]{:S(2)}) collective-permute-start(bf16[64,4096]{1,0:T(8,128)(2,1)S(1)} %pad_maximum_fusion.3.refs_0_), channel_id=1, source_target_pairs={{0,4},{4,0},{8,12},{12,8},{1,5},{5,1},{9,13},{13,9},{2,6},{6,2},{1... | collective-permute-start | bytes 1572872 | tf_op jit(solution)/shard_map/ppermute | solution.py:29
  251.6 16.3 %collective-permute-start.54 = (bf16[64,4096]{1,0:T(8,128)(2,1)S(1)}, bf16[64,4096]{1,0:T(8,128)(2,1)S(1)}, u32[]{:S(2)}, u32[]{:S(2)}) collective-permute-start(bf16[64,4096]{1,0:T(8,128)(2,1)S(1)} %pad_maximum_fusion.7.refs_0_), channel_id=1, source_target_pairs={{0,8},{4,12},{8,0},{12,4},{1,9},{5,13},{9,1},{13,5},{2,10},{6,14},... | collective-permute-start | bytes 1572872 | tf_op jit(solution)/shard_map/ppermute | solution.py:29
  252.9 17.1 %collective-permute-start.53 = (bf16[64,4096]{1,0:T(8,128)(2,1)S(1)}, bf16[64,4096]{1,0:T(8,128)(2,1)S(1)}, u32[]{:S(2)}, u32[]{:S(2)}) collective-permute-start(bf16[64,4096]{1,0:T(8,128)(2,1)S(1)} %pad_maximum_fusion.7.refs_0_), channel_id=1, source_target_pairs={{0,4},{4,0},{8,12},{12,8},{1,5},{5,1},{9,13},{13,9},{2,6},{6,2},{1... | collective-permute-start | bytes 1572872 | tf_op jit(solution)/shard_map/ppermute | solution.py:29
  257.5 17.4 %collective-permute-start.28 = (bf16[32,4096]{1,0:T(8,128)(2,1)}, bf16[32,4096]{1,0:T(8,128)(2,1)S(1)}, u32[]{:S(2)}, u32[]{:S(2)}) collective-permute-start(bf16[32,4096]{1,0:T(8,128)(2,1)} %slice.384), channel_id=1, source_target_pairs={{0,4},{4,0},{8,12},{12,8},{1,5},{5,1},{9,13},{13,9},{2,6},{6,2},{1... | collective-permute-start | bytes 786440 | tf_op jit(solution)/shard_map/ppermute | solution.py:29
  259.6 15.3 %collective-permute-start.29 = (bf16[32,4096]{1,0:T(8,128)(2,1)}, bf16[32,4096]{1,0:T(8,128)(2,1)}, u32[]{:S(2)}, u32[]{:S(2)}) collective-permute-start(bf16[32,4096]{1,0:T(8,128)(2,1)} %slice.385), channel_id=1, source_target_pairs={{0,8},{4,12},{8,0},{12,4},{1,9},{5,13},{9,1},{13,5},{2,10},{6,14},... | collective-permute-start | bytes 786440 | tf_op jit(solution)/shard_map/ppermute | solution.py:29
  268.7 19.3 %collective-permute-start.55 = (bf16[32,4096]{1,0:T(8,128)(2,1)}, bf16[32,4096]{1,0:T(8,128)(2,1)}, u32[]{:S(2)}, u32[]{:S(2)}) collective-permute-start(bf16[32,4096]{1,0:T(8,128)(2,1)} %slice.411), channel_id=1, source_target_pairs={{0,4},{4,0},{8,12},{12,8},{1,5},{5,1},{9,13},{13,9},{2,6},{6,2},{1... | collective-permute-start | bytes 786440 | tf_op jit(solution)/shard_map/ppermute | solution.py:29
  270.8 17.3 %collective-permute-start.56 = (bf16[32,4096]{1,0:T(8,128)(2,1)}, bf16[32,4096]{1,0:T(8,128)(2,1)}, u32[]{:S(2)}, u32[]{:S(2)}) collective-permute-start(bf16[32,4096]{1,0:T(8,128)(2,1)} %slice.412), channel_id=1, source_target_pairs={{0,8},{4,12},{8,0},{12,4},{1,9},{5,13},{9,1},{13,5},{2,10},{6,14},... | collective-permute-start | bytes 786440 | tf_op jit(solution)/shard_map/ppermute | solution.py:29
  (91 other events, 815.2 us)

commit v3 on v2

--- a/solution.py
+++ b/solution.py
@@ -9,6 +9,8 @@
 
 epsilon = 1e-05
 LANES = 128
+LARGEST = 512
+MIB = 1024 * 1024
 VMEM_BYTES = 56 * 1024 * 1024
 
 
@@ -56,24 +58,37 @@
         copy.wait()
 
 
+def split_three(x):
+    high = lax.reduce_precision(x, 8, 7)
+    middle = lax.reduce_precision(x - high, 8, 7)
+    return jnp.stack([high, middle, x - high - middle])
+
+
+def gain_row(ref, index):
+    tail = ref[ref.shape[0] - 16 :, :].astype(jnp.float32)
+    first = 3 * index
+    return tail[first : first + 1] + tail[first + 1 : first + 2] + tail[first + 2 : first + 3]
+
+
 def norm_kernel(splits, part, count, *refs):
     slices, gains = refs[:count], refs[count : 2 * count]
     routes_ref, weights_ref = refs[2 * count : 2 * count + 2]
     rows_ref, raw_ref = refs[-2:]
-    rows, width = slices[0].shape
+    rows = rows_ref.shape[0]
+    width = slices[0].shape[1]
     full_width = width * count
     own_rows = rows // count
     me = lax.axis_index("tensor")
     total = jnp.zeros((rows, 1), jnp.float32)
     for piece in slices:
-        value = piece[...].astype(jnp.float32)
+        value = piece[:rows, :].astype(jnp.float32)
         total = total + jnp.sum(value * value, axis=1, keepdims=True)
     scale = lax.rsqrt(total / full_width + epsilon)
     start = pl.multiple_of(me * own_rows, own_rows)
     for d in range(count):
         columns = pl.ds(pl.multiple_of((me ^ d) * width, width), width)
-        value = slices[d][...].astype(jnp.float32)
-        rows_ref[:, columns] = (value * scale * gains[d][0:1, :]).astype(jnp.bfloat16)
+        value = slices[d][:rows, :].astype(jnp.float32)
+        rows_ref[:, columns] = (value * scale * gain_row(gains[d], 0)).astype(jnp.bfloat16)
         raw_ref[:, columns] = slices[d][pl.ds(start, own_rows), :]
     lane = lax.broadcasted_iota(jnp.int32, (own_rows, LANES), 1)
     expert = lane // 3
@@ -91,8 +106,8 @@
         rows_ref[i * own_rows : (i + 1) * own_rows, full_width:] = value.astype(jnp.bfloat16)
 
 
-def norm_rows(slices, gains, routes, route_weights, splits, part, after):
-    rows, width = slices[0].shape
+def norm_rows(slices, gains, routes, route_weights, splits, part, rows, after):
+    width = slices[0].shape[1]
     count = len(slices)
     full_width = width * count
     return pl.pallas_call(
@@ -103,7 +118,7 @@
         ),
         in_specs=[whole()] * (2 * count + 2) + [anywhere()] * len(after),
         out_specs=(whole(), whole()),
-        compiler_params=params(),
+        compiler_params=params(6 * MIB),
         cost_estimate=pl.CostEstimate(
             flops=6 * rows * full_width, bytes_accessed=4 * rows * full_width, transcendentals=rows
         ),
@@ -111,103 +126,133 @@
     )(*slices, *gains, routes, route_weights, *after)
 
 
-def hidden_kernel(pieces, streams, after, *refs):
+def stage_kernel(source_ref, target_ref, sem):
+    copy = pltpu.make_async_copy(source_ref, target_ref, sem)
+    copy.start()
+    copy.wait()
+
+
+def stage(weight):
+    return pl.pallas_call(
+        stage_kernel,
+        out_shape=pltpu.VMEM(weight.shape, weight.dtype),
+        in_specs=[anywhere()],
+        out_specs=anywhere(),
+        scratch_shapes=[pltpu.SemaphoreType.DMA],
+        compiler_params=params(MIB),
+        cost_estimate=pl.CostEstimate(
+            flops=0, bytes_accessed=4 * weight.size, transcendentals=0
+        ),
+        name="stage",
+    )(pltpu.with_memory_space_constraint(weight, pltpu.HBM))
+
+
+def hidden_kernel(pieces, after, tile, *refs):
     piece_refs = refs[:pieces]
-    gate_refs = refs[pieces : pieces + streams]
-    up_refs = refs[pieces + streams : pieces + 2 * streams]
-    out_ref, rows_scr, weight_scr, sems = refs[pieces + 2 * streams + after :]
-    depth = gate_refs[0].shape[1]
-
-    @pl.when(pl.program_id(0) == 0)
-    def _():
-        load_pieces(piece_refs, rows_scr, sems)
-        small = rows_scr[:, depth * streams :].astype(jnp.float32)
-        lane = lax.broadcasted_iota(jnp.int32, small.shape, 1)
-        first = lax.axis_index("expert") * 3
-        mine = (lane >= first) & (lane < first + 3)
-        weight = jnp.sum(jnp.where(mine, small, 0.0), axis=1, keepdims=True)
-        weight_scr[...] = jnp.broadcast_to(0.5 * weight, weight_scr.shape)
-
-    def product(refs):
-        total = None
-        for i in range(streams):
-            rows = rows_scr[:, i * depth : (i + 1) * depth]
-            term = jnp.dot(rows, refs[i][0], preferred_element_type=jnp.float32)
-            total = term if total is None else total + term
-        return total
-
-    gate = product(gate_refs)
-    up = product(up_refs)
-    hidden = gate * (1.0 + jnp.tanh(0.5 * gate)) * up * weight_scr[:, :1]
-    out_ref[...] = hidden.astype(jnp.bfloat16)
+    gate_ref, up_ref = refs[pieces : pieces + 2]
+    out_ref, rows_scr, weight_scr, gate_scr, sems, gate_sems = refs[pieces + 2 + after :]
+    full_width, hidden_part = gate_ref.shape[1:]
+    steps = hidden_part // tile
+
+    def columns(i):
+        return pl.ds(pl.multiple_of(i * tile, tile), tile)
+
+    def fetch(i):
+        slot = lax.rem(i, 2)
+        return pltpu.make_async_copy(
+            gate_ref.at[0, :, columns(i)], gate_scr.at[slot], gate_sems.at[slot]
+        )
+
+    fetch(0).start()
+    load_pieces(piece_refs, rows_scr, sems)
+    small = rows_scr[:, full_width:].astype(jnp.float32)
+    lane = lax.broadcasted_iota(jnp.int32, small.shape, 1)
+    first = lax.axis_index("expert") * 3
+    mine = (lane >= first) & (lane < first + 3)
+    weight = jnp.sum(jnp.where(mine, small, 0.0), axis=1, keepdims=True)
+    weight_scr[...] = jnp.broadcast_to(0.5 * weight, weight_scr.shape)
+
+    @pl.loop(0, steps)
+    def _(i):
+        @pl.when(i + 1 < steps)
+        def _():
+            fetch(i + 1).start()
+
+        rows = rows_scr[:, :full_width]
+        up = jnp.dot(rows, up_ref[0, :, columns(i)], preferred_element_type=jnp.float32)
+        fetch(i).wait()
+        gate_block = gate_scr[lax.rem(i, 2)]
+        gate = jnp.dot(rows, gate_block, preferred_element_type=jnp.float32)
+        hidden = gate * (1.0 + jnp.tanh(0.5 * gate)) * up * weight_scr[:, :1]
+        out_ref[:, columns(i)] = hidden.astype(jnp.bfloat16)
 
 
 def hidden_rows(pieces, w_gate, w_up, after):
     rows = sum(p.shape[0] for p in pieces)
     full_width, hidden = w_gate.shape[1:]
-    tile = 256 if hidden % 256 == 0 else hidden
-    streams = 2
-    depth = full_width // streams
-    weight_specs = [
-        pl.BlockSpec((1, depth, tile), lambda i, part=part: (0, part, i)) for part in range(streams)
-    ]
-    return pl.pallas_call(
-        functools.partial(hidden_kernel, len(pieces), streams, len(after)),
+    tile = next(t for t in (256, 128, hidden) if hidden % t == 0)
+    return pl.pallas_call(
+        functools.partial(hidden_kernel, len(pieces), len(after), tile),
         out_shape=jax.ShapeDtypeStruct((rows, hidden), jnp.bfloat16),
-        grid=(hidden // tile,),
-        in_specs=[anywhere()] * len(pieces) + weight_specs * 2 + [anywhere()] * len(after),
-        out_specs=pl.BlockSpec((rows, tile), lambda i: (0, i)),
+        in_specs=[anywhere()] * (len(pieces) + 1) + [whole()] + [anywhere()] * len(after),
+        out_specs=whole(),
         scratch_shapes=[
             pltpu.VMEM((rows, full_width + LANES), jnp.bfloat16),
             pltpu.VMEM((rows, LANES), jnp.float32),
+            pltpu.VMEM((2, full_width, tile), jnp.bfloat16),
             pltpu.SemaphoreType.DMA((len(pieces),)),
+            pltpu.SemaphoreType.DMA((2,)),
         ],
-        compiler_params=params(),
+        compiler_params=params((8 + rows // 64) * MIB),
         cost_estimate=pl.CostEstimate(
             flops=4 * rows * full_width * hidden,
-            bytes_accessed=4 * full_width * hidden + 2 * rows * (full_width + hidden),
+            bytes_accessed=2 * rows * (full_width + hidden),
             transcendentals=rows * hidden,
         ),
         name="hidden_rows",
-    )(*pieces, *[w_gate] * streams, *[w_up] * streams, *after)
-
-
-def down_kernel(streams, after, hidden_ref, *refs):
-    outs = refs[streams + after :]
-    part = hidden_ref.shape[0] // len(outs)
-    for j in range(streams):
-        out = jnp.dot(hidden_ref[...], refs[j][0], preferred_element_type=jnp.float32)
-        columns = slice(j * out.shape[1], (j + 1) * out.shape[1])
-        for i in range(len(outs)):
-            outs[i][:, columns] = out[i * part : (i + 1) * part].astype(jnp.bfloat16)
-
-
-def down_rows(hidden, w_down, parts, after):
-    rows, depth = hidden.shape
-    full_width = w_down.shape[2]
+    )(*pieces, w_gate, w_up, *after)
+
+
+def down_kernel(start, hidden_ref, down_ref, *refs):
+    out_ref = refs[-1]
+    full_width = out_ref.shape[1]
     tile = 512 if full_width % 512 == 0 else full_width
-    streams = 2
-    narrow = tile // streams
-    shape = jax.ShapeDtypeStruct((rows // parts, full_width), jnp.bfloat16)
-    return pl.pallas_call(
-        functools.partial(down_kernel, streams, len(after)),
-        out_shape=(shape,) * parts,
-        grid=(full_width // tile,),
-        in_specs=[pl.BlockSpec((rows, depth), lambda i: (0, 0))]
-        + [
-            pl.BlockSpec((1, depth, narrow), lambda i, part=part: (0, 0, streams * i + part))
-            for part in range(streams)
-        ]
-        + [anywhere()] * len(after),
-        out_specs=(pl.BlockSpec((rows // parts, tile), lambda i: (0, i)),) * parts,
-        compiler_params=params(),
+
+    @pl.loop(0, full_width // tile)
+    def _(i):
+        columns = pl.ds(pl.multiple_of(i * tile, tile), tile)
+        rows = hidden_ref[start : start + out_ref.shape[0], :]
+        out = jnp.dot(rows, down_ref[0, :, columns], preferred_element_type=jnp.float32)
+        out_ref[:, columns] = out.astype(jnp.bfloat16)
+
+
+def down_rows(hidden, w_down, start, rows, after):
+    depth, full_width = w_down.shape[1:]
+    return pl.pallas_call(
+        functools.partial(down_kernel, start),
+        out_shape=jax.ShapeDtypeStruct((rows, full_width), jnp.bfloat16),
+        in_specs=[whole()] * 2 + [anywhere()] * len(after),
+        out_specs=whole(),
+        compiler_params=params((4 + rows // 64) * MIB),
         cost_estimate=pl.CostEstimate(
             flops=2 * rows * depth * full_width,
-            bytes_accessed=2 * depth * full_width + 2 * rows * (depth + full_width),
+            bytes_accessed=2 * rows * (depth + full_width),
             transcendentals=0,
         ),
         name="down_rows",
-    )(hidden, *[w_down] * streams, *after)
+    )(hidden, w_down, *after)
+
+
+def many_rows(pieces, w_gate, w_up, w_down):
+    outs = []
+    while pieces:
+        count = 1
+        while count < len(pieces) and sum(p.shape[0] for p in pieces[: count + 1]) <= LARGEST:
+            count += 1
+        hidden = hidden_rows(pieces[:count], w_gate, w_up, [])
+        outs.append(down_rows(hidden, w_down, 0, hidden.shape[0], []))
+        pieces = pieces[count:]
+    return jnp.concatenate(outs)
 
 
 def final_kernel(parts, gains_count, *refs):
@@ -226,7 +271,7 @@
     work[...] = residual * scale
     for d in range(gains_count):
         columns = pl.ds(pl.multiple_of((me ^ d) * width, width), width)
-        out_ref[:, columns] = (work[:, columns] * gains[d][1:2, :]).astype(jnp.bfloat16)
+        out_ref[:, columns] = (work[:, columns] * gain_row(gains[d], 1)).astype(jnp.bfloat16)
 
 
 def final_rows(parts, raw, gains):
@@ -237,7 +282,7 @@
         in_specs=[whole()] * (len(parts) + 1 + len(gains)),
         out_specs=whole(),
         scratch_shapes=[pltpu.VMEM((rows, full_width), jnp.float32)],
-        compiler_params=params(),
+        compiler_params=params(6 * MIB),
         cost_estimate=pl.CostEstimate(
             flops=8 * rows * full_width, bytes_accessed=12 * rows * full_width, transcendentals=rows
         ),
@@ -248,54 +293,48 @@
 def head_kernel(pieces, *refs):
     piece_refs = refs[:pieces]
     head_ref, target_ref, out_ref, rows_scr, sems = refs[pieces:]
-    step = pl.program_id(0)
-    tile = head_ref.shape[0]
-
-    @pl.when(step == 0)
-    def _():
-        load_pieces(piece_refs, rows_scr, sems)
-        lane = lax.broadcasted_iota(jnp.int32, out_ref.shape, 0)
-        out_ref[...] = jnp.where(lane == 0, -jnp.inf, 0.0)
-
-    logits = lax.dot_general(
-        head_ref[...],
-        rows_scr[...],
-        (((1,), (1,)), ((), ())),
-        preferred_element_type=jnp.float32,
-    )
-    word = lax.broadcasted_iota(jnp.int32, logits.shape, 0) + step * tile
-    old_top, old_total = out_ref[0:1, :], out_ref[1:2, :]
-    top = jnp.maximum(old_top, jnp.max(logits, axis=0, keepdims=True))
-    out_ref[0:1, :] = top
-    out_ref[1:2, :] = old_total * jnp.exp(old_top - top) + jnp.sum(
-        jnp.exp(logits - top), axis=0, keepdims=True
-    )
-    hit = word == target_ref[...]
-    out_ref[2:3, :] += jnp.sum(jnp.where(hit, logits, 0.0), axis=0, keepdims=True)
+    vocab_part = head_ref.shape[0]
+    tile = 400 if vocab_part % 400 == 0 else vocab_part
+    load_pieces(piece_refs, rows_scr, sems)
+    lane = lax.broadcasted_iota(jnp.int32, out_ref.shape, 0)
+    out_ref[...] = jnp.where(lane == 0, -jnp.inf, 0.0)
+
+    @pl.loop(0, vocab_part // tile)
+    def _(i):
+        start = pl.multiple_of(i * tile, tile)
+        logits = lax.dot_general(
+            head_ref[pl.ds(start, tile), :],
+            rows_scr[...],
+            (((1,), (1,)), ((), ())),
+            preferred_element_type=jnp.float32,
+        )
+        word = lax.broadcasted_iota(jnp.int32, logits.shape, 0) + start
+        old_top, old_total = out_ref[0:1, :], out_ref[1:2, :]
+        top = jnp.maximum(old_top, jnp.max(logits, axis=0, keepdims=True))
+        out_ref[0:1, :] = top
+        out_ref[1:2, :] = old_total * jnp.exp(old_top - top) + jnp.sum(
+            jnp.exp(logits - top), axis=0, keepdims=True
+        )
+        hit = word == target_ref[...]
+        out_ref[2:3, :] += jnp.sum(jnp.where(hit, logits, 0.0), axis=0, keepdims=True)
 
 
 def head_terms(pieces, head_rows, targets):
     rows = sum(p.shape[0] for p in pieces)
     vocab_part, full_width = head_rows.shape
-    tile = 400 if vocab_part % 400 == 0 else vocab_part
     return pl.pallas_call(
         functools.partial(head_kernel, len(pieces)),
         out_shape=jax.ShapeDtypeStruct((8, rows), jnp.float32),
-        grid=(vocab_part // tile,),
-        in_specs=[anywhere()] * len(pieces)
-        + [
-            pl.BlockSpec((tile, full_width), lambda i: (i, 0)),
-            pl.BlockSpec((1, rows), lambda i: (0, 0)),
-        ],
-        out_specs=pl.BlockSpec((8, rows), lambda i: (0, 0)),
+        in_specs=[anywhere()] * len(pieces) + [whole()] * 2,
+        out_specs=whole(),
         scratch_shapes=[
             pltpu.VMEM((rows, full_width), jnp.bfloat16),
             pltpu.SemaphoreType.DMA((len(pieces),)),
         ],
-        compiler_params=params(),
+        compiler_params=params((6 + rows // 64) * MIB),
         cost_estimate=pl.CostEstimate(
             flops=2 * rows * full_width * vocab_part,
-            bytes_accessed=2 * full_width * (vocab_part + rows),
+            bytes_accessed=2 * full_width * rows,
             transcendentals=rows * vocab_part,
         ),
         name="head_terms",
@@ -364,26 +403,49 @@
     vocab_part = head_weight.shape[1]
 
     parts = tokens.reshape(n_tensor, splits, sub, width)
-    slices = [gather_near(parts[:, h].reshape(rows, width), "tensor") for h in range(splits)]
-    gains = gather_near(jnp.stack([norm_gain, final_gain]), "tensor")
-    pieces, raws = [], []
+    rider = jnp.concatenate([split_three(norm_gain), split_three(final_gain)])
+    rider = jnp.pad(rider, ((0, 16 - rider.shape[0]), (0, 0))).astype(jnp.bfloat16)
+    slices = []
+    for h in range(splits):
+        part = parts[:, h].reshape(rows, width)
+        slices.append(
+            gather_near(part if h else jnp.concatenate([part, rider]), "tensor")
+        )
+    gains = slices[0]
+    planes, raws = [], []
     after = []
     for h in range(splits):
-        normed, raw = norm_rows(slices[h], gains, routes, route_weights, splits, h, after)
+        normed, raw = norm_rows(slices[h], gains, routes, route_weights, splits, h, rows, after)
         plane = gather_plane(normed, "expert")
-        pieces.append(plane + [swap(p, "seq", 1) for p in plane])
+        planes.append(plane)
         raws.append(raw)
         after = plane[1:3]
 
+    w_gate = pltpu.with_memory_space_constraint(w_gate, pltpu.HBM)
+    staged = stage(w_up)
     finals = []
-    sent = [[], []]
+    begun, moved = [], []
+    last = None
     for h in range(splits):
-        hidden = hidden_rows(pieces[h], w_gate, w_up, sent[0])
-        kept, other = down_rows(hidden, w_down, 2, sent[1])
+        nearer, later = [], []
+        if h + 1 < splits:
+            nearer, later = planes[h + 1][:1], planes[h + 1][1:3]
+        away = [swap(p, "seq", 1) for p in planes[h]]
+        if 2 * n_expert * rows <= LARGEST:
+            hidden = hidden_rows(planes[h] + away, w_gate, w_up if h else staged, begun + nearer)
+            hidden = pltpu.with_memory_space_constraint(hidden, pltpu.VMEM)
+            half = hidden.shape[0] // 2
+            other = down_rows(hidden, w_down, half, half, moved + later)
+            kept = down_rows(hidden, w_down, 0, half, [] if last is None else [last])
+        else:
+            kept, other = many_rows(planes[h], w_gate, w_up, w_down), many_rows(
+                away, w_gate, w_up, w_down
+            )
         got = swap(other, "seq", 1)
         shape = (n_expert, rows, full_width)
-        total, moved = sum_plane(kept.reshape(shape), got.reshape(shape))
-        sent = [moved[:2], moved[2:]]
+        total, sums = sum_plane(kept.reshape(shape), got.reshape(shape))
+        begun, moved = sums[:2], sums[2:]
+        last = total
         total = total.reshape(n_tensor, sub, full_width)
         mine = [lax.dynamic_index_in_dim(total, my_tensor, 0, False)]
         for d in range(1, n_tensor):
@@ -394,7 +456,7 @@
     start = (my_expert * n_tensor + my_tensor) * vocab_part
     local = (targets - start).astype(jnp.int32).reshape(n_expert, n_tensor, splits, sub)
     local = flip(flip(local, 0, my_expert), 1, my_tensor)
-    head_rows = head_weight.T
+    head_rows = pltpu.with_memory_space_constraint(head_weight.T, pltpu.VMEM)
     terms = []
     for h in range(splits):
         column = jnp.concatenate(gather_near(finals[h], "tensor"), axis=0)

time: 318 us -> 305 us (0.959)
  waiting for transfers between devices: 110 us -> 92.2 us
  local copies, waits for them, and re-layouts: 19.8 us -> 30.2 us
  starting transfers between devices: 70.1 us -> 64.8 us
    pallas_call x4 -> x7, Pallas kernels: 72.2 us -> 92.5 us  [the longest x2 66.3 us: hidden_rows(): pl.pallas_call(functools.partial(hidden_kernel, len(pieces), len(after),...]
    ppermute x63 -> x60, waiting for transfers between devices: 110 us -> 92.2 us  [swap(): return lax.ppermute(x, axis, [(i, i ^ distance) for i in range(size)])]
    unnamed x106 -> x38, local copies, waits for them, and re-layouts: 9.79 us -> 19.8 us
    pallas_call x2, Pallas kernels: 23.3 us -> 13.6 us  [head_terms(): pl.pallas_call(functools.partial(head_kernel, len(pieces)), out_shape=jax...]
    ppermute x63 -> x60, starting transfers between devices: 70.1 us -> 64.8 us  [swap(): return lax.ppermute(x, axis, [(i, i ^ distance) for i in range(size)])]
    pallas_call x2, Pallas kernels: 4.63 us -> 0.68 us  [norm_rows(): pl.pallas_call(functools.partial(norm_kernel, splits, part, count), out_s...]
    pallas_call x2, Pallas kernels: 4.13 us -> 0.45 us  [final_rows(): pl.pallas_call(functools.partial(final_kernel, len(parts), len(gains)), o...]
  transfers between devices with their start and end apart: 63 -> 60, of which waited for: 31 -> 25; matrix products, arithmetic and copies ran while one was open for 6% -> 5% of each run, Pallas kernels for 13% -> 29%
where the time goes in v3:
time: 305 us; the launch traced here: 304 us
  Pallas kernels  107 us (35%)
  waiting for transfers between devices  92.2 us (30%)
  starting transfers between devices  64.8 us (21%)
  local copies, waits for them, and re-layouts  30.2 us (10%)
  other arithmetic  8.85 us (3%)
    ppermute x60, waiting for transfers between devices, swap(): return lax.ppermute(x, axis, [(i, i ^ distance) for i in range(size)])  92.2 us
    pallas_call x2, Pallas kernels, hidden_rows(): pl.pallas_call(functools.partial(hidden_kernel, len(pieces), len(after),...  66.3 us
    ppermute x60, starting transfers between devices, swap(): return lax.ppermute(x, axis, [(i, i ^ distance) for i in range(size)])  64.8 us
    pallas_call x4, Pallas kernels, down_rows(): pl.pallas_call(functools.partial(down_kernel, start), out_shape=jax.Shape...  21.1 us
    unnamed x38, local copies, waits for them, and re-layouts  19.8 us
    pallas_call x2, Pallas kernels, head_terms(): pl.pallas_call(functools.partial(head_kernel, len(pieces)), out_shape=jax...  13.6 us
  transfers between devices with their start and end apart: 60, of which 25 were waited for; matrix products, arithmetic and copies ran while one was open for 5% of the time, Pallas kernels for 29%

profile of v3, /device:TPU:0, one launch (start us, length us, event | category | flops | bytes accessed | tf_op | source)
XLA Modules:
  0.0 303.9 jit_solution(14766241821497538148)
XLA Ops:
  12.3 8.4 %collective-permute-done.1.refs_2_.refs_6_.refs_7_ = bf16[80,1024]{1,0:T(8,128)(2,1)S(1)} collective-permute-done((bf16[80,1024]{1,0:T(8,128)(2,1)S(1)}, bf16[80,1024]{1,0:T(8,128)(2,1)S(1)}, u32[]{:S(2)}, u32[]{:S(2)}) %collective-permute-start.1) | collective-permute-done | bytes 163872 | tf_op jit(solution)/shard_map/ppermute | solution.py:31
  29.2 3.4 %collective-permute-done.4.refs_11_.refs_2_ = bf16[64,4224]{1,0:T(8,128)(2,1)S(1)} collective-permute-done((bf16[64,4224]{1,0:T(8,128)(2,1)S(1)}, bf16[64,4224]{1,0:T(8,128)(2,1)S(1)}, u32[]{:S(2)}, u32[]{:S(2)}) %collective-permute-start.4) | collective-permute-done | bytes 540704 | tf_op jit(solution)/shard_map/ppermute | solution.py:31
  38.4 3.2 %collective-permute-done.5.refs_3_ = bf16[32,4224]{1,0:T(8,128)(2,1)S(1)} collective-permute-done((bf16[32,4224]{1,0:T(8,128)(2,1)S(1)}, bf16[32,4224]{1,0:T(8,128)(2,1)S(1)}, u32[]{:S(2)}, u32[]{:S(2)}) %collective-permute-start.5) | collective-permute-done | bytes 270368 | tf_op jit(solution)/shard_map/ppermute | solution.py:31
  41.6 5.2 %collective-permute-done.6.refs_4_ = bf16[32,4224]{1,0:T(8,128)(2,1)S(1)} collective-permute-done((bf16[32,4224]{1,0:T(8,128)(2,1)S(1)}, bf16[32,4224]{1,0:T(8,128)(2,1)S(1)}, u32[]{:S(2)}, u32[]{:S(2)}) %collective-permute-start.6) | collective-permute-done | bytes 270368 | tf_op jit(solution)/shard_map/ppermute | solution.py:31
  46.8 5.2 %stage.1.refs_11_ = bf16[1,4096,1792]{2,1,0:T(8,128)(2,1)S(1)} custom-call(bf16[1,4096,1792]{2,1,0:T(8,128)(2,1)} %refs_11_.1), custom_call_target="tpu_custom_call" | custom-call | bytes 29360128 | tf_op jit(solution)/shard_map/stage/pallas_call | solution.py:136
  53.6 33.1 %hidden_rows.2.hidden_ref = bf16[512,1792]{1,0:T(8,128)(2,1)S(1)} custom-call(bf16[64,4224]{1,0:T(8,128)(2,1)S(1)} %get-tuple-element.9.refs_0_, bf16[64,4224]{1,0:T(8,128)(2,1)S(1)} %collective-permute-done.3.refs_10_.refs_1_, bf16[64,4224]{1,0:T(8,128)(2,1)S(1)} %collective-permute-done.4.refs_11_.refs_2_, ...), custom_call_target="tpu_custom_call" | custom-call | flops 15032385536 | bytes 6029312 | tf_op jit(solution)/shard_map/hidden_rows/pallas_call | solution.py:194
  86.8 5.2 %down_rows.5 = bf16[256,4096]{1,0:T(8,128)(2,1)S(1)} custom-call(bf16[512,1792]{1,0:T(8,128)(2,1)S(1)} %hidden_rows.2.hidden_ref, bf16[1,1792,4096]{2,1,0:T(8,128)(2,1)S(1)} %bitcast.93, bf16[64,4224]{1,0:T(8,128)(2,1)S(1)} %collective-permute-done.15.refs_0_.refs_1_, bf16[64,4224]{1,0:T(8,128)(2,1)S(1)} %collective-permute-done.16.refs_1_.refs_2_), custom_call_target="tpu_custom_call" | custom-call | flops 3758096384 | bytes 3014656 | tf_op jit(solution)/shard_map/down_rows/pallas_call | solution.py:231
  95.8 5.2 %down_rows.4 = bf16[256,4096]{1,0:T(8,128)(2,1)S(1)} custom-call(bf16[512,1792]{1,0:T(8,128)(2,1)S(1)} %hidden_rows.2.hidden_ref, bf16[1,1792,4096]{2,1,0:T(8,128)(2,1)S(1)} %bitcast.93), custom_call_target="tpu_custom_call" | custom-call | flops 3758096384 | bytes 3014656 | tf_op jit(solution)/shard_map/down_rows/pallas_call | solution.py:231
  105.5 5.2 %copy-done.2 = bf16[1,4096,1792]{2,1,0:T(8,128)(2,1)S(1)} copy-done((bf16[1,4096,1792]{2,1,0:T(8,128)(2,1)S(1)}, bf16[1,4096,1792]{2,1,0:T(8,128)(2,1)}, u32[]{:S(2)}) %copy-start.2) | copy-done | bytes 14680088
  110.7 33.1 %hidden_rows.3.hidden_ref = bf16[512,1792]{1,0:T(8,128)(2,1)S(1)} custom-call(bf16[64,4224]{1,0:T(8,128)(2,1)S(1)} %get-tuple-element.10.refs_12_.refs_0_, bf16[64,4224]{1,0:T(8,128)(2,1)S(1)} %collective-permute-done.15.refs_0_.refs_1_, bf16[64,4224]{1,0:T(8,128)(2,1)S(1)} %collective-permute-done.16.refs_1_.refs_2_, ...), custom_call_target="tpu_custom_call" | custom-call | flops 15032385536 | bytes 6029312 | tf_op jit(solution)/shard_map/hidden_rows/pallas_call | solution.py:194
  144.0 5.2 %down_rows.7 = bf16[256,4096]{1,0:T(8,128)(2,1)S(1)} custom-call(bf16[512,1792]{1,0:T(8,128)(2,1)S(1)} %hidden_rows.3.hidden_ref, bf16[1,1792,4096]{2,1,0:T(8,128)(2,1)S(1)} %bitcast.93, bf16[32,4096]{1,0:T(8,128)(2,1)S(1)} %get-tuple-element.28.refs_0_, bf16[32,4096]{1,0:T(8,128)(2,1)S(1)} %get-tuple-element.27.refs_1_), custom_call_target="tpu_custom_call" | custom-call | flops 3758096384 | bytes 3014656 | tf_op jit(solution)/shard_map/down_rows/pallas_call | solution.py:231
  151.5 6.6 %collective-permute-done.19 = bf16[32,4096]{1,0:T(8,128)(2,1)S(1)} collective-permute-done((bf16[32,4096]{1,0:T(8,128)(2,1)S(1)}, bf16[32,4096]{1,0:T(8,128)(2,1)S(1)}, u32[]{:S(2)}, u32[]{:S(2)}) %collective-permute-start.19) | collective-permute-done | bytes 262176 | tf_op jit(solution)/shard_map/ppermute | solution.py:31
  159.1 5.4 %down_rows.6 = bf16[256,4096]{1,0:T(8,128)(2,1)S(1)} custom-call(bf16[512,1792]{1,0:T(8,128)(2,1)S(1)} %hidden_rows.3.hidden_ref, bf16[1,1792,4096]{2,1,0:T(8,128)(2,1)S(1)} %bitcast.93, bf16[64,4096]{1,0:T(8,128)(2,1)S(1)} %maximum_convert_fusion.refs_0_), custom_call_target="tpu_custom_call" | custom-call | flops 3758096384 | bytes 3014656 | tf_op jit(solution)/shard_map/down_rows/pallas_call | solution.py:231
  172.3 7.2 %collective-permute-done.42 = bf16[2,32,4096]{2,1,0:T(8,128)(2,1)} collective-permute-done((bf16[2,32,4096]{2,1,0:T(8,128)(2,1)}, bf16[2,32,4096]{2,1,0:T(8,128)(2,1)}, u32[]{:S(2)}, u32[]{:S(2)}) %collective-permute-start.42) | collective-permute-done | bytes 524320 | tf_op jit(solution)/shard_map/ppermute | solution.py:31
  208.2 16.9 %collective-permute-done.45.refs_2_ = bf16[16,4096]{1,0:T(8,128)(2,1)S(1)} collective-permute-done((bf16[16,4096]{1,0:T(8,128)(2,1)S(1)}, bf16[16,4096]{1,0:T(8,128)(2,1)S(1)}, u32[]{:S(2)}, u32[]{:S(2)}) %collective-permute-start.45) | collective-permute-done | bytes 131104 | tf_op jit(solution)/shard_map/ppermute | solution.py:31
  231.9 7.5 %collective-permute-done.48 = bf16[16,4096]{1,0:T(8,128)(2,1)S(1)} collective-permute-done((bf16[16,4096]{1,0:T(8,128)(2,1)S(1)}, bf16[16,4096]{1,0:T(8,128)(2,1)S(1)}, u32[]{:S(2)}, u32[]{:S(2)}) %collective-permute-start.48) | collective-permute-done | bytes 131104 | tf_op jit(solution)/shard_map/ppermute | solution.py:31
  241.5 3.3 %collective-permute-done.29.refs_2_ = bf16[64,4096]{1,0:T(8,128)(2,1)S(1)} collective-permute-done((bf16[64,4096]{1,0:T(8,128)(2,1)S(1)}, bf16[64,4096]{1,0:T(8,128)(2,1)S(1)}, u32[]{:S(2)}, u32[]{:S(2)}) %collective-permute-start.29) | collective-permute-done | bytes 524320 | tf_op jit(solution)/shard_map/ppermute | solution.py:31
  249.2 6.9 %collective-permute-done.51.refs_2_ = bf16[64,4096]{1,0:T(8,128)(2,1)S(1)} collective-permute-done((bf16[64,4096]{1,0:T(8,128)(2,1)S(1)}, bf16[64,4096]{1,0:T(8,128)(2,1)S(1)}, u32[]{:S(2)}, u32[]{:S(2)}) %collective-permute-start.51) | collective-permute-done | bytes 524320 | tf_op jit(solution)/shard_map/ppermute | solution.py:31
  259.5 3.6 %collective-permute-done.30.refs_3_ = bf16[32,4096]{1,0:T(8,128)(2,1)S(1)} collective-permute-done((bf16[32,4096]{1,0:T(8,128)(2,1)}, bf16[32,4096]{1,0:T(8,128)(2,1)S(1)}, u32[]{:S(2)}, u32[]{:S(2)}) %collective-permute-start.30) | collective-permute-done | bytes 262176 | tf_op jit(solution)/shard_map/ppermute | solution.py:31
  263.1 5.7 %copy-done = bf16[4096,2000]{0,1:T(8,128)(2,1)S(1)} copy-done((bf16[4096,2000]{0,1:T(8,128)(2,1)S(1)}, bf16[4096,2000]{0,1:T(8,128)(2,1)}, u32[]{:S(2)}) %copy-start) | copy-done | bytes 16384024
  268.7 6.8 %head_terms.2 = f32[8,256]{1,0:T(8,128)S(1)} custom-call(bf16[64,4096]{1,0:T(8,128)(2,1)S(1)} %pad_maximum_fusion.2.refs_0_, bf16[64,4096]{1,0:T(8,128)(2,1)S(1)} %collective-permute-done.28.refs_1_, bf16[64,4096]{1,0:T(8,128)(2,1)S(1)} %collective-permute-done.29.refs_2_, bf16[32,4096]{1,0:T(8,128)(2,1)S(1)} %collective-permute-done.30.refs_3_, ...), custom_call_target="tpu_custom_call" | custom-call | flops 4194304000 | bytes 2097152 | tf_op jit(solution)/shard_map/head_terms/pallas_call | solution.py:325
  275.7 5.6 %copy-done.1 = bf16[4096,2000]{0,1:T(8,128)(2,1)S(1)} copy-done((bf16[4096,2000]{0,1:T(8,128)(2,1)S(1)}, bf16[4096,2000]{0,1:T(8,128)(2,1)}, u32[]{:S(2)}) %copy-start.1) | copy-done | bytes 16384024
  281.3 6.8 %head_terms.3 = f32[8,256]{1,0:T(8,128)S(1)} custom-call(bf16[64,4096]{1,0:T(8,128)(2,1)S(1)} %pad_maximum_fusion.6.refs_0_, bf16[64,4096]{1,0:T(8,128)(2,1)S(1)} %collective-permute-done.50.refs_1_, bf16[64,4096]{1,0:T(8,128)(2,1)S(1)} %collective-permute-done.51.refs_2_, bf16[32,4096]{1,0:T(8,128)(2,1)} %collective-permute-done.52.refs_3_, ...), custom_call_target="tpu_custom_call" | custom-call | flops 4194304000 | bytes 2097152 | tf_op jit(solution)/shard_map/head_terms/pallas_call | solution.py:325
  293.3 3.3 %collective-permute-done.56 = f32[3,4,2,16]{3,2,1,0:T(2,128)S(1)} collective-permute-done((f32[3,4,2,16]{3,2,1,0:T(2,128)S(1)}, f32[3,4,2,16]{3,2,1,0:T(2,128)S(1)}, u32[]{:S(2)}, u32[]{:S(2)}) %collective-permute-start.56) | collective-permute-done | bytes 1568 | tf_op jit(solution)/shard_map/ppermute | solution.py:31
  (228 shorter events, 105.1 us)
Async XLA Ops:
  5.6 15.0 %collective-permute-start.1 = (bf16[80,1024]{1,0:T(8,128)(2,1)S(1)}, bf16[80,1024]{1,0:T(8,128)(2,1)S(1)}, u32[]{:S(2)}, u32[]{:S(2)}) collective-permute-start(bf16[80,1024]{1,0:T(8,128)(2,1)S(1)} %fusion.7.refs_0_.refs_4_.refs_5_), channel_id=1, source_target_pairs={{0,2},{1,3},{2,0},{3,1},{4,6},{5,7},{6,4},{7,5},{8,10},{9,11},{10,... | collective-permute-start | bytes 491528 | tf_op jit(solution)/shard_map/ppermute | solution.py:31
  32.6 19.8 %collective-permute-start.7 = (bf16[64,4224]{1,0:T(8,128)(2,1)S(1)}, bf16[64,4224]{1,0:T(8,128)(2,1)S(1)}, u32[]{:S(2)}, u32[]{:S(2)}) collective-permute-start(bf16[64,4224]{1,0:T(8,128)(2,1)S(1)} %get-tuple-element.9.refs_0_), channel_id=1, source_target_pairs={{0,16},{16,0},{1,17},{17,1},{2,18},{18,2},{3,19},{19,3},{4,20},{20... | collective-permute-start | bytes 1622024 | tf_op jit(solution)/shard_map/ppermute | solution.py:31
  35.4 17.6 %collective-permute-start.8 = (bf16[64,4224]{1,0:T(8,128)(2,1)S(1)}, bf16[64,4224]{1,0:T(8,128)(2,1)S(1)}, u32[]{:S(2)}, u32[]{:S(2)}) collective-permute-start(bf16[64,4224]{1,0:T(8,128)(2,1)S(1)} %collective-permute-done.3.refs_10_.refs_1_), channel_id=1, source_target_pairs={{0,16},{16,0},{1,17},{17,1},{2,18},{18,2},{3,19},{19,3},{4,20},{20... | collective-permute-start | bytes 1622024 | tf_op jit(solution)/shard_map/ppermute | solution.py:31
  37.9 15.6 %collective-permute-start.9 = (bf16[64,4224]{1,0:T(8,128)(2,1)S(1)}, bf16[64,4224]{1,0:T(8,128)(2,1)S(1)}, u32[]{:S(2)}, u32[]{:S(2)}) collective-permute-start(bf16[64,4224]{1,0:T(8,128)(2,1)S(1)} %collective-permute-done.4.refs_11_.refs_2_), channel_id=1, source_target_pairs={{0,16},{16,0},{1,17},{17,1},{2,18},{18,2},{3,19},{19,3},{4,20},{20... | collective-permute-start | bytes 1622024 | tf_op jit(solution)/shard_map/ppermute | solution.py:31
  52.4 34.3 %collective-permute-start.15 = (bf16[64,4224]{1,0:T(8,128)(2,1)S(1)}, bf16[64,4224]{1,0:T(8,128)(2,1)S(1)}, u32[]{:S(2)}, u32[]{:S(2)}) collective-permute-start(bf16[64,4224]{1,0:T(8,128)(2,1)S(1)} %get-tuple-element.10.refs_12_.refs_0_), channel_id=1, source_target_pairs={{0,4},{4,0},{8,12},{12,8},{1,5},{5,1},{9,13},{13,9},{2,6},{6,2},{1... | collective-permute-start | bytes 1622024 | tf_op jit(solution)/shard_map/ppermute | solution.py:31
  53.0 33.7 %collective-permute-start.16 = (bf16[64,4224]{1,0:T(8,128)(2,1)S(1)}, bf16[64,4224]{1,0:T(8,128)(2,1)S(1)}, u32[]{:S(2)}, u32[]{:S(2)}) collective-permute-start(bf16[64,4224]{1,0:T(8,128)(2,1)S(1)} %get-tuple-element.10.refs_12_.refs_0_), channel_id=1, source_target_pairs={{0,8},{4,12},{8,0},{12,4},{1,9},{5,13},{9,1},{13,5},{2,10},{6,14},... | collective-permute-start | bytes 1622024 | tf_op jit(solution)/shard_map/ppermute | solution.py:31
  103.3 40.4 %collective-permute-start.20 = (bf16[2,32,4096]{2,1,0:T(8,128)(2,1)S(1)}, bf16[2,32,4096]{2,1,0:T(8,128)(2,1)S(1)}, u32[]{:S(2)}, u32[]{:S(2)}) collective-permute-start(bf16[2,32,4096]{2,1,0:T(8,128)(2,1)S(1)} %pad_maximum_fusion.1.refs_13_), channel_id=1, source_target_pairs={{0,8},{4,12},{8,0},{12,4},{1,9},{5,13},{9,1},{13,5},{2,10},{6,14},... | collective-permute-start | bytes 1572872 | tf_op jit(solution)/shard_map/ppermute | solution.py:31
  104.9 38.9 %collective-permute-start.18 = (bf16[2,32,4096]{2,1,0:T(8,128)(2,1)S(1)}, bf16[2,32,4096]{2,1,0:T(8,128)(2,1)S(1)}, u32[]{:S(2)}, u32[]{:S(2)}) collective-permute-start(bf16[2,32,4096]{2,1,0:T(8,128)(2,1)S(1)} %pad_maximum_fusion.refs_12_), channel_id=1, source_target_pairs={{0,4},{4,0},{8,12},{12,8},{1,5},{5,1},{9,13},{13,9},{2,6},{6,2},{1... | collective-permute-start | bytes 1572872 | tf_op jit(solution)/shard_map/ppermute | solution.py:31
  149.2 15.3 %collective-permute-start.39 = (bf16[256,4096]{1,0:T(8,128)(2,1)S(1)}, bf16[256,4096]{1,0:T(8,128)(2,1)S(1)}, u32[]{:S(2)}, u32[]{:S(2)}) collective-permute-start(bf16[256,4096]{1,0:T(8,128)(2,1)S(1)} %down_rows.7), channel_id=1, source_target_pairs={{0,16},{16,0},{1,17},{17,1},{2,18},{18,2},{3,19},{19,3},{4,20},{20... | collective-permute-start | bytes 6291464 | tf_op jit(solution)/shard_map/ppermute | solution.py:31
  166.0 13.5 %collective-permute-start.42 = (bf16[2,32,4096]{2,1,0:T(8,128)(2,1)}, bf16[2,32,4096]{2,1,0:T(8,128)(2,1)}, u32[]{:S(2)}, u32[]{:S(2)}) collective-permute-start(bf16[2,32,4096]{2,1,0:T(8,128)(2,1)} %pad_maximum_fusion.4), channel_id=1, source_target_pairs={{0,8},{4,12},{8,0},{12,4},{1,9},{5,13},{9,1},{13,5},{2,10},{6,14},... | collective-permute-start | bytes 1572872 | tf_op jit(solution)/shard_map/ppermute | solution.py:31
  191.5 14.9 %collective-permute-start.44 = (bf16[16,4096]{1,0:T(8,128)(2,1)S(1)}, bf16[16,4096]{1,0:T(8,128)(2,1)S(1)}, u32[]{:S(2)}, u32[]{:S(2)}) collective-permute-start(bf16[16,4096]{1,0:T(8,128)(2,1)S(1)} %get-tuple-element.39), channel_id=1, source_target_pairs={{0,1},{1,0},{2,3},{3,2},{4,5},{5,4},{6,7},{7,6},{8,9},{9,8},{10,11... | collective-permute-start | bytes 393224 | tf_op jit(solution)/shard_map/ppermute | solution.py:31
  199.9 28.5 %collective-permute-start.25 = (bf16[16,4096]{1,0:T(8,128)(2,1)S(1)}, bf16[16,4096]{1,0:T(8,128)(2,1)S(1)}, u32[]{:S(2)}, u32[]{:S(2)}) collective-permute-start(bf16[16,4096]{1,0:T(8,128)(2,1)S(1)} %final_rows.2), channel_id=1, source_target_pairs={{0,1},{1,0},{2,3},{3,2},{4,5},{5,4},{6,7},{7,6},{8,9},{9,8},{10,11... | collective-permute-start | bytes 393224 | tf_op jit(solution)/shard_map/ppermute | solution.py:31
  201.7 28.1 %collective-permute-start.26 = (bf16[16,4096]{1,0:T(8,128)(2,1)S(1)}, bf16[16,4096]{1,0:T(8,128)(2,1)S(1)}, u32[]{:S(2)}, u32[]{:S(2)}) collective-permute-start(bf16[16,4096]{1,0:T(8,128)(2,1)S(1)} %final_rows.2), channel_id=1, source_target_pairs={{0,2},{1,3},{2,0},{3,1},{4,6},{5,7},{6,4},{7,5},{8,10},{9,11},{10,... | collective-permute-start | bytes 393224 | tf_op jit(solution)/shard_map/ppermute | solution.py:31
  203.0 26.9 %collective-permute-start.27 = (bf16[16,4096]{1,0:T(8,128)(2,1)S(1)}, bf16[16,4096]{1,0:T(8,128)(2,1)S(1)}, u32[]{:S(2)}, u32[]{:S(2)}) collective-permute-start(bf16[16,4096]{1,0:T(8,128)(2,1)S(1)} %final_rows.2), channel_id=1, source_target_pairs={{0,3},{1,2},{2,1},{3,0},{4,7},{5,6},{6,5},{7,4},{8,11},{9,10},{10,... | collective-permute-start | bytes 393224 | tf_op jit(solution)/shard_map/ppermute | solution.py:31
  204.4 20.8 %collective-permute-start.45 = (bf16[16,4096]{1,0:T(8,128)(2,1)S(1)}, bf16[16,4096]{1,0:T(8,128)(2,1)S(1)}, u32[]{:S(2)}, u32[]{:S(2)}) collective-permute-start(bf16[16,4096]{1,0:T(8,128)(2,1)S(1)} %get-tuple-element.38), channel_id=1, source_target_pairs={{0,2},{1,3},{2,0},{3,1},{4,6},{5,7},{6,4},{7,5},{8,10},{9,11},{10,... | collective-permute-start | bytes 393224 | tf_op jit(solution)/shard_map/ppermute | solution.py:31
  206.4 18.8 %collective-permute-start.46 = (bf16[16,4096]{1,0:T(8,128)(2,1)S(1)}, bf16[16,4096]{1,0:T(8,128)(2,1)S(1)}, u32[]{:S(2)}, u32[]{:S(2)}) collective-permute-start(bf16[16,4096]{1,0:T(8,128)(2,1)S(1)} %get-tuple-element.37), channel_id=1, source_target_pairs={{0,3},{1,2},{2,1},{3,0},{4,7},{5,6},{6,5},{7,4},{8,11},{9,10},{10,... | collective-permute-start | bytes 393224 | tf_op jit(solution)/shard_map/ppermute | solution.py:31
  229.9 14.9 %collective-permute-start.29 = (bf16[64,4096]{1,0:T(8,128)(2,1)S(1)}, bf16[64,4096]{1,0:T(8,128)(2,1)S(1)}, u32[]{:S(2)}, u32[]{:S(2)}) collective-permute-start(bf16[64,4096]{1,0:T(8,128)(2,1)S(1)} %pad_maximum_fusion.2.refs_0_), channel_id=1, source_target_pairs={{0,8},{4,12},{8,0},{12,4},{1,9},{5,13},{9,1},{13,5},{2,10},{6,14},... | collective-permute-start | bytes 1572872 | tf_op jit(solution)/shard_map/ppermute | solution.py:31
  231.4 15.1 %collective-permute-start.28 = (bf16[64,4096]{1,0:T(8,128)(2,1)S(1)}, bf16[64,4096]{1,0:T(8,128)(2,1)S(1)}, u32[]{:S(2)}, u32[]{:S(2)}) collective-permute-start(bf16[64,4096]{1,0:T(8,128)(2,1)S(1)} %pad_maximum_fusion.2.refs_0_), channel_id=1, source_target_pairs={{0,4},{4,0},{8,12},{12,8},{1,5},{5,1},{9,13},{13,9},{2,6},{6,2},{1... | collective-permute-start | bytes 1572872 | tf_op jit(solution)/shard_map/ppermute | solution.py:31
  239.5 16.6 %collective-permute-start.51 = (bf16[64,4096]{1,0:T(8,128)(2,1)S(1)}, bf16[64,4096]{1,0:T(8,128)(2,1)S(1)}, u32[]{:S(2)}, u32[]{:S(2)}) collective-permute-start(bf16[64,4096]{1,0:T(8,128)(2,1)S(1)} %pad_maximum_fusion.6.refs_0_), channel_id=1, source_target_pairs={{0,8},{4,12},{8,0},{12,4},{1,9},{5,13},{9,1},{13,5},{2,10},{6,14},... | collective-permute-start | bytes 1572872 | tf_op jit(solution)/shard_map/ppermute | solution.py:31
  240.9 16.9 %collective-permute-start.50 = (bf16[64,4096]{1,0:T(8,128)(2,1)S(1)}, bf16[64,4096]{1,0:T(8,128)(2,1)S(1)}, u32[]{:S(2)}, u32[]{:S(2)}) collective-permute-start(bf16[64,4096]{1,0:T(8,128)(2,1)S(1)} %pad_maximum_fusion.6.refs_0_), channel_id=1, source_target_pairs={{0,4},{4,0},{8,12},{12,8},{1,5},{5,1},{9,13},{13,9},{2,6},{6,2},{1... | collective-permute-start | bytes 1572872 | tf_op jit(solution)/shard_map/ppermute | solution.py:31
  245.6 17.5 %collective-permute-start.30 = (bf16[32,4096]{1,0:T(8,128)(2,1)}, bf16[32,4096]{1,0:T(8,128)(2,1)S(1)}, u32[]{:S(2)}, u32[]{:S(2)}) collective-permute-start(bf16[32,4096]{1,0:T(8,128)(2,1)} %slice.385), channel_id=1, source_target_pairs={{0,4},{4,0},{8,12},{12,8},{1,5},{5,1},{9,13},{13,9},{2,6},{6,2},{1... | collective-permute-start | bytes 786440 | tf_op jit(solution)/shard_map/ppermute | solution.py:31
  247.2 15.9 %collective-permute-start.31 = (bf16[32,4096]{1,0:T(8,128)(2,1)}, bf16[32,4096]{1,0:T(8,128)(2,1)}, u32[]{:S(2)}, u32[]{:S(2)}) collective-permute-start(bf16[32,4096]{1,0:T(8,128)(2,1)} %slice.386), channel_id=1, source_target_pairs={{0,8},{4,12},{8,0},{12,4},{1,9},{5,13},{9,1},{13,5},{2,10},{6,14},... | collective-permute-start | bytes 786440 | tf_op jit(solution)/shard_map/ppermute | solution.py:31
  256.8 18.8 %collective-permute-start.52 = (bf16[32,4096]{1,0:T(8,128)(2,1)}, bf16[32,4096]{1,0:T(8,128)(2,1)}, u32[]{:S(2)}, u32[]{:S(2)}) collective-permute-start(bf16[32,4096]{1,0:T(8,128)(2,1)} %slice.411), channel_id=1, source_target_pairs={{0,4},{4,0},{8,12},{12,8},{1,5},{5,1},{9,13},{13,9},{2,6},{6,2},{1... | collective-permute-start | bytes 786440 | tf_op jit(solution)/shard_map/ppermute | solution.py:31
  258.5 17.2 %collective-permute-start.53 = (bf16[32,4096]{1,0:T(8,128)(2,1)}, bf16[32,4096]{1,0:T(8,128)(2,1)}, u32[]{:S(2)}, u32[]{:S(2)}) collective-permute-start(bf16[32,4096]{1,0:T(8,128)(2,1)} %slice.412), channel_id=1, source_target_pairs={{0,8},{4,12},{8,0},{12,4},{1,9},{5,13},{9,1},{13,5},{2,10},{6,14},... | collective-permute-start | bytes 786440 | tf_op jit(solution)/shard_map/ppermute | solution.py:31
  (54 other events, 611.4 us)

commit v4 on v3

--- a/solution.py
+++ b/solution.py
@@ -126,112 +126,120 @@
     )(*slices, *gains, routes, route_weights, *after)
 
 
-def stage_kernel(source_ref, target_ref, sem):
-    copy = pltpu.make_async_copy(source_ref, target_ref, sem)
-    copy.start()
-    copy.wait()
-
-
-def stage(weight):
-    return pl.pallas_call(
-        stage_kernel,
-        out_shape=pltpu.VMEM(weight.shape, weight.dtype),
-        in_specs=[anywhere()],
-        out_specs=anywhere(),
-        scratch_shapes=[pltpu.SemaphoreType.DMA],
-        compiler_params=params(MIB),
-        cost_estimate=pl.CostEstimate(
-            flops=0, bytes_accessed=4 * weight.size, transcendentals=0
-        ),
-        name="stage",
-    )(pltpu.with_memory_space_constraint(weight, pltpu.HBM))
-
-
-def hidden_kernel(pieces, after, tile, *refs):
+def hidden_kernel(pieces, after, tile, first, steps, *refs):
     piece_refs = refs[:pieces]
-    gate_ref, up_ref = refs[pieces : pieces + 2]
-    out_ref, rows_scr, weight_scr, gate_scr, sems, gate_sems = refs[pieces + 2 + after :]
-    full_width, hidden_part = gate_ref.shape[1:]
-    steps = hidden_part // tile
-
-    def columns(i):
-        return pl.ds(pl.multiple_of(i * tile, tile), tile)
-
-    def fetch(i):
+    weight_refs = refs[pieces : pieces + 2]
+    out_ref, rows_scr, route_scr, weight_scr, sems, weight_sems = refs[pieces + 2 + after :]
+    full_width = weight_scr.shape[2]
+
+    def fetch(i, act):
         slot = lax.rem(i, 2)
-        return pltpu.make_async_copy(
-            gate_ref.at[0, :, columns(i)], gate_scr.at[slot], gate_sems.at[slot]
-        )
-
-    fetch(0).start()
+        columns = pl.ds(pl.multiple_of((first + i) * tile, tile), tile)
+        for j in range(2):
+            act(
+                pltpu.make_async_copy(
+                    weight_refs[j].at[0, :, columns],
+                    weight_scr.at[j, slot],
+                    weight_sems.at[j, slot],
+                )
+            )
+
+    fetch(0, lambda copy: copy.start())
     load_pieces(piece_refs, rows_scr, sems)
     small = rows_scr[:, full_width:].astype(jnp.float32)
     lane = lax.broadcasted_iota(jnp.int32, small.shape, 1)
-    first = lax.axis_index("expert") * 3
-    mine = (lane >= first) & (lane < first + 3)
+    start = lax.axis_index("expert") * 3
+    mine = (lane >= start) & (lane < start + 3)
     weight = jnp.sum(jnp.where(mine, small, 0.0), axis=1, keepdims=True)
-    weight_scr[...] = jnp.broadcast_to(0.5 * weight, weight_scr.shape)
+    route_scr[...] = jnp.broadcast_to(0.5 * weight, route_scr.shape)
 
     @pl.loop(0, steps)
     def _(i):
+        fetch(i, lambda copy: copy.wait())
+
         @pl.when(i + 1 < steps)
         def _():
-            fetch(i + 1).start()
-
+            fetch(i + 1, lambda copy: copy.start())
+
+        slot = lax.rem(i, 2)
         rows = rows_scr[:, :full_width]
-        up = jnp.dot(rows, up_ref[0, :, columns(i)], preferred_element_type=jnp.float32)
-        fetch(i).wait()
-        gate_block = gate_scr[lax.rem(i, 2)]
-        gate = jnp.dot(rows, gate_block, preferred_element_type=jnp.float32)
-        hidden = gate * (1.0 + jnp.tanh(0.5 * gate)) * up * weight_scr[:, :1]
-        out_ref[:, columns(i)] = hidden.astype(jnp.bfloat16)
-
-
-def hidden_rows(pieces, w_gate, w_up, after):
+        gate = jnp.dot(rows, weight_scr[0, slot], preferred_element_type=jnp.float32)
+        up = jnp.dot(rows, weight_scr[1, slot], preferred_element_type=jnp.float32)
+        hidden = gate * (1.0 + jnp.tanh(0.5 * gate)) * up * route_scr[:, :1]
+        columns = pl.ds(pl.multiple_of(i * tile, tile), tile)
+        out_ref[:, columns] = hidden.astype(jnp.bfloat16)
+
+
+def tile_of(weight):
+    hidden = weight.shape[2]
+    return next(t for t in (256, 128, hidden) if hidden % t == 0)
+
+
+def hidden_rows(pieces, w_gate, w_up, after, first, steps, tile):
     rows = sum(p.shape[0] for p in pieces)
-    full_width, hidden = w_gate.shape[1:]
-    tile = next(t for t in (256, 128, hidden) if hidden % t == 0)
+    full_width = w_gate.shape[1]
+    hidden = steps * tile
     return pl.pallas_call(
-        functools.partial(hidden_kernel, len(pieces), len(after), tile),
+        functools.partial(hidden_kernel, len(pieces), len(after), tile, first, steps),
         out_shape=jax.ShapeDtypeStruct((rows, hidden), jnp.bfloat16),
-        in_specs=[anywhere()] * (len(pieces) + 1) + [whole()] + [anywhere()] * len(after),
+        in_specs=[anywhere()] * (len(pieces) + 2 + len(after)),
         out_specs=whole(),
         scratch_shapes=[
             pltpu.VMEM((rows, full_width + LANES), jnp.bfloat16),
             pltpu.VMEM((rows, LANES), jnp.float32),
-            pltpu.VMEM((2, full_width, tile), jnp.bfloat16),
+            pltpu.VMEM((2, 2, full_width, tile), jnp.bfloat16),
             pltpu.SemaphoreType.DMA((len(pieces),)),
-            pltpu.SemaphoreType.DMA((2,)),
+            pltpu.SemaphoreType.DMA((2, 2)),
         ],
-        compiler_params=params((8 + rows // 64) * MIB),
+        compiler_params=params((14 + rows // 64) * MIB),
         cost_estimate=pl.CostEstimate(
             flops=4 * rows * full_width * hidden,
-            bytes_accessed=2 * rows * (full_width + hidden),
+            bytes_accessed=4 * full_width * hidden + 2 * rows * (full_width + hidden),
             transcendentals=rows * hidden,
         ),
         name="hidden_rows",
     )(*pieces, w_gate, w_up, *after)
 
 
-def down_kernel(start, hidden_ref, down_ref, *refs):
-    out_ref = refs[-1]
+def hidden_dots(pieces, w_gate, w_up):
+    full_width = w_gate.shape[1]
+    joined = jnp.concatenate(pieces)
+    rows = joined[:, :full_width]
+    small = joined[:, full_width:].astype(jnp.float32)
+    lane = jnp.arange(LANES, dtype=jnp.int32)
+    start = lax.axis_index("expert") * 3
+    weight = jnp.sum(jnp.where((lane >= start) & (lane < start + 3), small, 0.0), axis=1)
+    gate = jnp.dot(rows, w_gate[0], preferred_element_type=jnp.float32)
+    up = jnp.dot(rows, w_up[0], preferred_element_type=jnp.float32)
+    return (jax.nn.silu(gate) * up * weight[:, None]).astype(jnp.bfloat16)
+
+
+def down_kernel(start, count, *refs):
+    hidden_refs, down_ref, out_ref = refs[:count], refs[count], refs[-1]
     full_width = out_ref.shape[1]
     tile = 512 if full_width % 512 == 0 else full_width
 
     @pl.loop(0, full_width // tile)
     def _(i):
         columns = pl.ds(pl.multiple_of(i * tile, tile), tile)
-        rows = hidden_ref[start : start + out_ref.shape[0], :]
-        out = jnp.dot(rows, down_ref[0, :, columns], preferred_element_type=jnp.float32)
+        out = None
+        depth = 0
+        for hidden_ref in hidden_refs:
+            rows = hidden_ref[start : start + out_ref.shape[0], :]
+            block = down_ref[0, depth : depth + rows.shape[1], columns]
+            term = jnp.dot(rows, block, preferred_element_type=jnp.float32)
+            out = term if out is None else out + term
+            depth += rows.shape[1]
         out_ref[:, columns] = out.astype(jnp.bfloat16)
 
 
 def down_rows(hidden, w_down, start, rows, after):
     depth, full_width = w_down.shape[1:]
+    hidden = [pltpu.with_memory_space_constraint(part, pltpu.VMEM) for part in hidden]
     return pl.pallas_call(
-        functools.partial(down_kernel, start),
+        functools.partial(down_kernel, start, len(hidden)),
         out_shape=jax.ShapeDtypeStruct((rows, full_width), jnp.bfloat16),
-        in_specs=[whole()] * 2 + [anywhere()] * len(after),
+        in_specs=[whole()] * (len(hidden) + 1) + [anywhere()] * len(after),
         out_specs=whole(),
         compiler_params=params((4 + rows // 64) * MIB),
         cost_estimate=pl.CostEstimate(
@@ -240,17 +248,19 @@
             transcendentals=0,
         ),
         name="down_rows",
-    )(hidden, w_down, *after)
+    )(*hidden, w_down, *after)
 
 
 def many_rows(pieces, w_gate, w_up, w_down):
     outs = []
+    tile = tile_of(w_gate)
+    steps = w_gate.shape[2] // tile
     while pieces:
         count = 1
         while count < len(pieces) and sum(p.shape[0] for p in pieces[: count + 1]) <= LARGEST:
             count += 1
-        hidden = hidden_rows(pieces[:count], w_gate, w_up, [])
-        outs.append(down_rows(hidden, w_down, 0, hidden.shape[0], []))
+        hidden = hidden_rows(pieces[:count], w_gate, w_up, [], 0, steps, tile)
+        outs.append(down_rows([hidden], w_down, 0, hidden.shape[0], []))
         pieces = pieces[count:]
     return jnp.concatenate(outs)
 
@@ -290,25 +300,35 @@
     )(*parts, raw, *gains)
 
 
-def head_kernel(pieces, *refs):
+def head_kernel(pieces, tile, *refs):
     piece_refs = refs[:pieces]
-    head_ref, target_ref, out_ref, rows_scr, sems = refs[pieces:]
-    vocab_part = head_ref.shape[0]
-    tile = 400 if vocab_part % 400 == 0 else vocab_part
+    head_ref, target_ref, out_ref, rows_scr, head_scr, sems, head_sems = refs[pieces:]
+    steps = head_ref.shape[0] // tile
+
+    def fetch(i):
+        return pltpu.make_async_copy(
+            head_ref.at[pl.ds(pl.multiple_of(i * tile, tile), tile), :],
+            head_scr.at[i],
+            head_sems.at[i],
+        )
+
+    fetch(0).start()
     load_pieces(piece_refs, rows_scr, sems)
+    for i in range(1, steps):
+        fetch(i).start()
     lane = lax.broadcasted_iota(jnp.int32, out_ref.shape, 0)
     out_ref[...] = jnp.where(lane == 0, -jnp.inf, 0.0)
 
-    @pl.loop(0, vocab_part // tile)
+    @pl.loop(0, steps)
     def _(i):
-        start = pl.multiple_of(i * tile, tile)
+        fetch(i).wait()
         logits = lax.dot_general(
-            head_ref[pl.ds(start, tile), :],
+            head_scr[i],
             rows_scr[...],
             (((1,), (1,)), ((), ())),
             preferred_element_type=jnp.float32,
         )
-        word = lax.broadcasted_iota(jnp.int32, logits.shape, 0) + start
+        word = lax.broadcasted_iota(jnp.int32, logits.shape, 0) + i * tile
         old_top, old_total = out_ref[0:1, :], out_ref[1:2, :]
         top = jnp.maximum(old_top, jnp.max(logits, axis=0, keepdims=True))
         out_ref[0:1, :] = top
@@ -322,19 +342,22 @@
 def head_terms(pieces, head_rows, targets):
     rows = sum(p.shape[0] for p in pieces)
     vocab_part, full_width = head_rows.shape
+    tile = next(t for t in (400, 200, 80, 8, vocab_part) if vocab_part % t == 0)
     return pl.pallas_call(
-        functools.partial(head_kernel, len(pieces)),
+        functools.partial(head_kernel, len(pieces), tile),
         out_shape=jax.ShapeDtypeStruct((8, rows), jnp.float32),
-        in_specs=[anywhere()] * len(pieces) + [whole()] * 2,
+        in_specs=[anywhere()] * (len(pieces) + 1) + [whole()],
         out_specs=whole(),
         scratch_shapes=[
             pltpu.VMEM((rows, full_width), jnp.bfloat16),
+            pltpu.VMEM((vocab_part // tile, tile, full_width), jnp.bfloat16),
             pltpu.SemaphoreType.DMA((len(pieces),)),
+            pltpu.SemaphoreType.DMA((vocab_part // tile,)),
         ],
-        compiler_params=params((6 + rows // 64) * MIB),
+        compiler_params=params((22 + rows // 64) * MIB),
         cost_estimate=pl.CostEstimate(
             flops=2 * rows * full_width * vocab_part,
-            bytes_accessed=2 * full_width * rows,
+            bytes_accessed=2 * full_width * (vocab_part + rows),
             transcendentals=rows * vocab_part,
         ),
         name="head_terms",
@@ -421,22 +444,27 @@
         raws.append(raw)
         after = plane[1:3]
 
-    w_gate = pltpu.with_memory_space_constraint(w_gate, pltpu.HBM)
-    staged = stage(w_up)
     finals = []
     begun, moved = [], []
     last = None
     for h in range(splits):
-        nearer, later = [], []
-        if h + 1 < splits:
-            nearer, later = planes[h + 1][:1], planes[h + 1][1:3]
+        later = planes[h + 1][1:3] if h + 1 < splits else []
         away = [swap(p, "seq", 1) for p in planes[h]]
         if 2 * n_expert * rows <= LARGEST:
-            hidden = hidden_rows(planes[h] + away, w_gate, w_up if h else staged, begun + nearer)
-            hidden = pltpu.with_memory_space_constraint(hidden, pltpu.VMEM)
-            half = hidden.shape[0] // 2
-            other = down_rows(hidden, w_down, half, half, moved + later)
-            kept = down_rows(hidden, w_down, 0, half, [] if last is None else [last])
+            half = n_expert * rows
+            everything = planes[h] + away
+            if h == 0:
+                hidden = [hidden_dots(everything, w_gate, w_up)]
+            else:
+                tile = tile_of(w_gate)
+                steps = w_gate.shape[2] // tile
+                cut = (steps + 1) // 2
+                hidden = [
+                    hidden_rows(everything, w_gate, w_up, begun, 0, cut, tile),
+                    hidden_rows(everything, w_gate, w_up, moved, cut, steps - cut, tile),
+                ]
+            other = down_rows(hidden, w_down, half, half, later + ([] if last is None else [last]))
+            kept = down_rows(hidden, w_down, 0, half, [])
         else:
             kept, other = many_rows(planes[h], w_gate, w_up, w_down), many_rows(
                 away, w_gate, w_up, w_down
@@ -456,7 +484,7 @@
     start = (my_expert * n_tensor + my_tensor) * vocab_part
     local = (targets - start).astype(jnp.int32).reshape(n_expert, n_tensor, splits, sub)
     local = flip(flip(local, 0, my_expert), 1, my_tensor)
-    head_rows = pltpu.with_memory_space_constraint(head_weight.T, pltpu.VMEM)
+    head_rows = pltpu.with_memory_space_constraint(head_weight.T, pltpu.HBM)
     terms = []
     for h in range(splits):
         column = jnp.concatenate(gather_near(finals[h], "tensor"), axis=0)

time: 305 us -> 280 us (0.918)
  Pallas kernels: 107 us -> 59.9 us
  matrix products: 0 us -> 26.4 us
  starting transfers between devices: 64.8 us -> 78 us
  local copies, waits for them, and re-layouts: 30.2 us -> 17.1 us
  waiting for transfers between devices: 92.2 us -> 86.5 us
    pallas_call x2, Pallas kernels: 66.3 us -> 20.8 us  [hidden_rows(): pl.pallas_call(functools.partial(hidden_kernel, len(pieces), len(after),...]
    dot_general x0 -> x2, matrix products: none -> 26.4 us  [the longest x1 13.7 us: hidden_dots(): up = jnp.dot(rows, w_up[0], preferred_element_type=jnp.float32)]
    ppermute x60, starting transfers between devices: 64.8 us -> 78 us  [swap(): return lax.ppermute(x, axis, [(i, i ^ distance) for i in range(size)])]
    unnamed x38 -> x55, local copies, waits for them, and re-layouts: 19.8 us -> 7.33 us
    ppermute x60, waiting for transfers between devices: 92.2 us -> 86.5 us  [swap(): return lax.ppermute(x, axis, [(i, i ^ distance) for i in range(size)])]
    pallas_call x7 -> x6, Pallas kernels: 39.9 us -> 38 us  [the longest x4 20.9 us: down_rows(): pl.pallas_call(functools.partial(down_kernel, start, len(hidden)), out_sh...]
  transfers between devices with their start and end apart: 60 -> 60, of which waited for: 25 -> 24; matrix products, arithmetic and copies ran while one was open for 5% -> 15% of each run, Pallas kernels for 29% -> 15%
where the time goes in v4:
time: 280 us; the launch traced here: 279 us
  waiting for transfers between devices  86.5 us (31%)
  starting transfers between devices  78 us (28%)
  Pallas kernels  59.9 us (21%)
  matrix products  26.4 us (9%)
  local copies, waits for them, and re-layouts  17.1 us (6%)
  other arithmetic  10.1 us (4%)
    ppermute x60, waiting for transfers between devices, swap(): return lax.ppermute(x, axis, [(i, i ^ distance) for i in range(size)])  86.5 us
    ppermute x60, starting transfers between devices, swap(): return lax.ppermute(x, axis, [(i, i ^ distance) for i in range(size)])  78 us
    pallas_call x4, Pallas kernels, down_rows(): pl.pallas_call(functools.partial(down_kernel, start, len(hidden)), out_sh...  20.9 us
    pallas_call x2, Pallas kernels, hidden_rows(): pl.pallas_call(functools.partial(hidden_kernel, len(pieces), len(after),...  20.8 us
    pallas_call x2, Pallas kernels, head_terms(): pl.pallas_call(functools.partial(head_kernel, len(pieces), tile), out_sha...  17.1 us
    dot_general x1, matrix products, hidden_dots(): up = jnp.dot(rows, w_up[0], preferred_element_type=jnp.float32)  13.7 us
    dot_general x1, matrix products, hidden_dots(): gate = jnp.dot(rows, w_gate[0], preferred_element_type=jnp.float32)  12.7 us
    unnamed x55, local copies, waits for them, and re-layouts  7.33 us
  transfers between devices with their start and end apart: 60, of which 24 were waited for; matrix products, arithmetic and copies ran while one was open for 15% of the time, Pallas kernels for 15%

profile of v4, /device:TPU:0, one launch (start us, length us, event | category | flops | bytes accessed | tf_op | source)
XLA Modules:
  0.0 278.8 jit_solution(4709326668221832045)
XLA Ops:
  2.5 3.1 %collective-permute-start = (bf16[80,1024]{1,0:T(8,128)(2,1)S(1)}, bf16[80,1024]{1,0:T(8,128)(2,1)S(1)}, u32[]{:S(2)}, u32[]{:S(2)}) collective-permute-start(bf16[80,1024]{1,0:T(8,128)(2,1)S(1)} %fusion.13.refs_0_.refs_4_.refs_5_), channel_id=1, source_target_pairs={{0,1},{1,0},{2,3},{3,2},{4,5},{5,4},{6,7},{7,6},{8,9},{9,8},{10,11... | collective-permute-start | bytes 491528 | tf_op jit(solution)/shard_map/ppermute | solution.py:31
  5.6 2.6 collective-permute-start.1
  9.1 3.5 %collective-permute-start.13 = (bf16[64,1024]{1,0:T(8,128)(2,1)S(1)}, bf16[64,1024]{1,0:T(8,128)(2,1)S(1)}, u32[]{:S(2)}, u32[]{:S(2)}) collective-permute-start(bf16[64,1024]{1,0:T(8,128)(2,1)S(1)} %bitcast.112), channel_id=1, source_target_pairs={{0,2},{1,3},{2,0},{3,1},{4,6},{5,7},{6,4},{7,5},{8,10},{9,11},{10,... | collective-permute-start | bytes 393224 | tf_op jit(solution)/shard_map/ppermute | solution.py:31
  14.2 4.0 %collective-permute-start.14 = (bf16[64,1024]{1,0:T(8,128)(2,1)S(1)}, bf16[64,1024]{1,0:T(8,128)(2,1)S(1)}, u32[]{:S(2)}, u32[]{:S(2)}) collective-permute-start(bf16[64,1024]{1,0:T(8,128)(2,1)S(1)} %bitcast.113), channel_id=1, source_target_pairs={{0,3},{1,2},{2,1},{3,0},{4,7},{5,6},{6,5},{7,4},{8,11},{9,10},{10,... | collective-permute-start | bytes 393224 | tf_op jit(solution)/shard_map/ppermute | solution.py:31
  24.2 8.4 %collective-permute-done.13.refs_2_ = bf16[64,1024]{1,0:T(8,128)(2,1)S(1)} collective-permute-done((bf16[64,1024]{1,0:T(8,128)(2,1)S(1)}, bf16[64,1024]{1,0:T(8,128)(2,1)S(1)}, u32[]{:S(2)}, u32[]{:S(2)}) %collective-permute-start.13) | collective-permute-done | bytes 131104 | tf_op jit(solution)/shard_map/ppermute | solution.py:31
  38.6 11.8 %collective-permute-done.5 = bf16[32,4224]{1,0:T(8,128)(2,1)S(1)} collective-permute-done((bf16[32,4224]{1,0:T(8,128)(2,1)S(1)}, bf16[32,4224]{1,0:T(8,128)(2,1)S(1)}, u32[]{:S(2)}, u32[]{:S(2)}) %collective-permute-start.5) | collective-permute-done | bytes 270368 | tf_op jit(solution)/shard_map/ppermute | solution.py:31
  54.0 12.7 %fusion.2 = f32[512,1792]{1,0:T(8,128)S(1)} fusion(bf16[1,4096,1792]{2,1,0:T(8,128)(2,1)} %refs_10_.3, bf16[512,4224]{1,0:T(8,128)(2,1)S(1)} %constant_dynamic-update-slice_fusion), kind=kOutput, calls=%fused_computation.2 | convolution fusion | flops 7516192768 | bytes 22544384 | tf_op jit(solution)/shard_map/dot_general | solution.py:212
  66.9 13.7 %multiply_convert_fusion.refs_0_ = bf16[512,1792]{1,0:T(8,128)(2,1)S(1)} fusion(f32[512,1792]{1,0:T(8,128)S(1)} %fusion.2, f32[512]{0:T(512)S(1)} %select_reduce_fusion, bf16[1,4096,1792]{2,1,0:T(8,128)(2,1)} %refs_11_.3, bf16[512,4224]{1,0:T(8,128)(2,1)} %copy-done.11), kind=kOutput, calls=%fused_computation.6 | convolution fusion | flops 7522615296 | bytes 24381440 | tf_op jit(solution)/shard_map/dot_general | solution.py:213
  80.6 5.2 %down_rows.5 = bf16[256,4096]{1,0:T(8,128)(2,1)S(1)} custom-call(bf16[512,1792]{1,0:T(8,128)(2,1)S(1)} %multiply_convert_fusion.refs_0_, bf16[1,1792,4096]{2,1,0:T(8,128)(2,1)S(1)} %bitcast.101, bf16[64,4224]{1,0:T(8,128)(2,1)S(1)} %collective-permute-done.15.refs_2_.refs_1_, bf16[64,4224]{1,0:T(8,128)(2,1)S(1)} %collective-permute-done.16.refs_3_.refs_2_), custom_call_target="tpu_custom_call" | custom-call | flops 3758096384 | bytes 3014656 | tf_op jit(solution)/shard_map/down_rows/pallas_call | solution.py:239
  89.2 5.2 %down_rows.4 = bf16[256,4096]{1,0:T(8,128)(2,1)S(1)} custom-call(bf16[512,1792]{1,0:T(8,128)(2,1)S(1)} %multiply_convert_fusion.refs_0_, bf16[1,1792,4096]{2,1,0:T(8,128)(2,1)S(1)} %bitcast.101), custom_call_target="tpu_custom_call" | custom-call | flops 3758096384 | bytes 3014656 | tf_op jit(solution)/shard_map/down_rows/pallas_call | solution.py:239
  99.5 11.6 %hidden_rows.2.refs_0_ = bf16[512,1024]{1,0:T(8,128)(2,1)S(1)} custom-call(bf16[64,4224]{1,0:T(8,128)(2,1)S(1)} %copy-done.1, bf16[64,4224]{1,0:T(8,128)(2,1)S(1)} %collective-permute-done.15.refs_2_.refs_1_, bf16[64,4224]{1,0:T(8,128)(2,1)S(1)} %collective-permute-done.16.refs_3_.refs_2_, bf16[32,4224]{1,0:T(8,128)(2,1)S(1)} %collective-permute-done.32.refs_3_, ...), custom_call_target="tpu_custom_call" | custom-call | flops 8589934592 | bytes 22020096 | tf_op jit(solution)/shard_map/hidden_rows/pallas_call | solution.py:182
  114.2 9.2 %hidden_rows.3.refs_1_ = bf16[512,768]{1,0:T(8,128)(2,1)S(1)} custom-call(bf16[64,4224]{1,0:T(8,128)(2,1)S(1)} %copy-done.1, bf16[64,4224]{1,0:T(8,128)(2,1)S(1)} %collective-permute-done.15.refs_2_.refs_1_, bf16[64,4224]{1,0:T(8,128)(2,1)S(1)} %collective-permute-done.16.refs_3_.refs_2_, bf16[32,4224]{1,0:T(8,128)(2,1)S(1)} %collective-permute-done.32.refs_3_, ...), custom_call_target="tpu_custom_call" | custom-call | flops 6442450944 | bytes 17563648 | tf_op jit(solution)/shard_map/hidden_rows/pallas_call | solution.py:182
  123.7 5.2 %down_rows.7 = bf16[256,4096]{1,0:T(8,128)(2,1)S(1)} custom-call(bf16[512,1024]{1,0:T(8,128)(2,1)S(1)} %hidden_rows.2.refs_0_, bf16[512,768]{1,0:T(8,128)(2,1)S(1)} %hidden_rows.3.refs_1_, bf16[1,1792,4096]{2,1,0:T(8,128)(2,1)S(1)} %bitcast.101, bf16[64,4096]{1,0:T(8,128)(2,1)S(1)} %maximum_convert_fusion.refs_3_), custom_call_target="tpu_custom_call" | custom-call | flops 3758096384 | bytes 3014656 | tf_op jit(solution)/shard_map/down_rows/pallas_call | solution.py:239
  129.0 5.2 %down_rows.6 = bf16[256,4096]{1,0:T(8,128)(2,1)S(1)} custom-call(bf16[512,1024]{1,0:T(8,128)(2,1)S(1)} %hidden_rows.2.refs_0_, bf16[512,768]{1,0:T(8,128)(2,1)S(1)} %hidden_rows.3.refs_1_, bf16[1,1792,4096]{2,1,0:T(8,128)(2,1)S(1)} %bitcast.101), custom_call_target="tpu_custom_call" | custom-call | flops 3758096384 | bytes 3014656 | tf_op jit(solution)/shard_map/down_rows/pallas_call | solution.py:239
  142.5 8.8 %collective-permute-done.42 = bf16[2,32,4096]{2,1,0:T(8,128)(2,1)} collective-permute-done((bf16[2,32,4096]{2,1,0:T(8,128)(2,1)}, bf16[2,32,4096]{2,1,0:T(8,128)(2,1)}, u32[]{:S(2)}, u32[]{:S(2)}) %collective-permute-start.42) | collective-permute-done | bytes 524320 | tf_op jit(solution)/shard_map/ppermute | solution.py:31
  157.2 8.8 %collective-permute-start.22 = (bf16[16,4096]{1,0:T(8,128)(2,1)}, bf16[16,4096]{1,0:T(8,128)(2,1)S(1)}, u32[]{:S(2)}, u32[]{:S(2)}) collective-permute-start(bf16[16,4096]{1,0:T(8,128)(2,1)} %get-tuple-element.35), channel_id=1, source_target_pairs={{0,1},{1,0},{2,3},{3,2},{4,5},{5,4},{6,7},{7,6},{8,9},{9,8},{10,11... | collective-permute-start | bytes 393224 | tf_op jit(solution)/shard_map/ppermute | solution.py:31
  173.7 4.7 %collective-permute-done.23.refs_2_ = bf16[16,4096]{1,0:T(8,128)(2,1)S(1)} collective-permute-done((bf16[16,4096]{1,0:T(8,128)(2,1)}, bf16[16,4096]{1,0:T(8,128)(2,1)S(1)}, u32[]{:S(2)}, u32[]{:S(2)}) %collective-permute-start.23) | collective-permute-done | bytes 131104 | tf_op jit(solution)/shard_map/ppermute | solution.py:31
  191.3 16.4 %collective-permute-done.45.refs_2_ = bf16[16,4096]{1,0:T(8,128)(2,1)S(1)} collective-permute-done((bf16[16,4096]{1,0:T(8,128)(2,1)S(1)}, bf16[16,4096]{1,0:T(8,128)(2,1)S(1)}, u32[]{:S(2)}, u32[]{:S(2)}) %collective-permute-start.45) | collective-permute-done | bytes 131104 | tf_op jit(solution)/shard_map/ppermute | solution.py:31
  214.7 7.4 %collective-permute-done.48 = bf16[16,4096]{1,0:T(8,128)(2,1)S(1)} collective-permute-done((bf16[16,4096]{1,0:T(8,128)(2,1)S(1)}, bf16[16,4096]{1,0:T(8,128)(2,1)S(1)}, u32[]{:S(2)}, u32[]{:S(2)}) %collective-permute-start.48) | collective-permute-done | bytes 131104 | tf_op jit(solution)/shard_map/ppermute | solution.py:31
  232.0 6.7 %collective-permute-done.51.refs_2_ = bf16[64,4096]{1,0:T(8,128)(2,1)S(1)} collective-permute-done((bf16[64,4096]{1,0:T(8,128)(2,1)S(1)}, bf16[64,4096]{1,0:T(8,128)(2,1)S(1)}, u32[]{:S(2)}, u32[]{:S(2)}) %collective-permute-start.51) | collective-permute-done | bytes 524320 | tf_op jit(solution)/shard_map/ppermute | solution.py:31
  242.2 3.1 %collective-permute-done.30.refs_3_ = bf16[32,4096]{1,0:T(8,128)(2,1)S(1)} collective-permute-done((bf16[32,4096]{1,0:T(8,128)(2,1)}, bf16[32,4096]{1,0:T(8,128)(2,1)S(1)}, u32[]{:S(2)}, u32[]{:S(2)}) %collective-permute-start.30) | collective-permute-done | bytes 262176 | tf_op jit(solution)/shard_map/ppermute | solution.py:31
  245.3 8.5 %head_terms.2 = f32[8,256]{1,0:T(8,128)S(1)} custom-call(bf16[64,4096]{1,0:T(8,128)(2,1)S(1)} %pad_maximum_fusion.2.refs_0_, bf16[64,4096]{1,0:T(8,128)(2,1)S(1)} %collective-permute-done.28.refs_1_, bf16[64,4096]{1,0:T(8,128)(2,1)S(1)} %collective-permute-done.29.refs_2_, bf16[32,4096]{1,0:T(8,128)(2,1)S(1)} %collective-permute-done.30.refs_3_, ...), custom_call_target="tpu_custom_call" | custom-call | flops 4194304000 | bytes 18481152 | tf_op jit(solution)/shard_map/head_terms/pallas_call | solution.py:346
  254.0 8.6 %head_terms.3 = f32[8,256]{1,0:T(8,128)S(1)} custom-call(bf16[64,4096]{1,0:T(8,128)(2,1)S(1)} %pad_maximum_fusion.6.refs_0_, bf16[64,4096]{1,0:T(8,128)(2,1)S(1)} %collective-permute-done.50.refs_1_, bf16[64,4096]{1,0:T(8,128)(2,1)S(1)} %collective-permute-done.51.refs_2_, bf16[32,4096]{1,0:T(8,128)(2,1)} %collective-permute-done.52.refs_3_, ...), custom_call_target="tpu_custom_call" | custom-call | flops 4194304000 | bytes 18481152 | tf_op jit(solution)/shard_map/head_terms/pallas_call | solution.py:346
  267.7 3.3 %collective-permute-done.56 = f32[3,4,2,16]{3,2,1,0:T(2,128)S(1)} collective-permute-done((f32[3,4,2,16]{3,2,1,0:T(2,128)S(1)}, f32[3,4,2,16]{3,2,1,0:T(2,128)S(1)}, u32[]{:S(2)}, u32[]{:S(2)}) %collective-permute-start.56) | collective-permute-done | bytes 1568 | tf_op jit(solution)/shard_map/ppermute | solution.py:31
  (250 shorter events, 100.4 us)
Async XLA Ops:
  5.6 15.0 %collective-permute-start.1 = (bf16[80,1024]{1,0:T(8,128)(2,1)S(1)}, bf16[80,1024]{1,0:T(8,128)(2,1)S(1)}, u32[]{:S(2)}, u32[]{:S(2)}) collective-permute-start(bf16[80,1024]{1,0:T(8,128)(2,1)S(1)} %fusion.13.refs_0_.refs_4_.refs_5_), channel_id=1, source_target_pairs={{0,2},{1,3},{2,0},{3,1},{4,6},{5,7},{6,4},{7,5},{8,10},{9,11},{10,... | collective-permute-start | bytes 491528 | tf_op jit(solution)/shard_map/ppermute | solution.py:31
  8.2 15.9 %collective-permute-start.12 = (bf16[64,1024]{1,0:T(8,128)(2,1)S(1)}, bf16[64,1024]{1,0:T(8,128)(2,1)S(1)}, u32[]{:S(2)}, u32[]{:S(2)}) collective-permute-start(bf16[64,1024]{1,0:T(8,128)(2,1)S(1)} %bitcast.111), channel_id=1, source_target_pairs={{0,1},{1,0},{2,3},{3,2},{4,5},{5,4},{6,7},{7,6},{8,9},{9,8},{10,11... | collective-permute-start | bytes 393224 | tf_op jit(solution)/shard_map/ppermute | solution.py:31
  9.1 23.5 %collective-permute-start.13 = (bf16[64,1024]{1,0:T(8,128)(2,1)S(1)}, bf16[64,1024]{1,0:T(8,128)(2,1)S(1)}, u32[]{:S(2)}, u32[]{:S(2)}) collective-permute-start(bf16[64,1024]{1,0:T(8,128)(2,1)S(1)} %bitcast.112), channel_id=1, source_target_pairs={{0,2},{1,3},{2,0},{3,1},{4,6},{5,7},{6,4},{7,5},{8,10},{9,11},{10,... | collective-permute-start | bytes 393224 | tf_op jit(solution)/shard_map/ppermute | solution.py:31
  14.2 18.4 %collective-permute-start.14 = (bf16[64,1024]{1,0:T(8,128)(2,1)S(1)}, bf16[64,1024]{1,0:T(8,128)(2,1)S(1)}, u32[]{:S(2)}, u32[]{:S(2)}) collective-permute-start(bf16[64,1024]{1,0:T(8,128)(2,1)S(1)} %bitcast.113), channel_id=1, source_target_pairs={{0,3},{1,2},{2,1},{3,0},{4,7},{5,6},{6,5},{7,4},{8,11},{9,10},{10,... | collective-permute-start | bytes 393224 | tf_op jit(solution)/shard_map/ppermute | solution.py:31
  24.1 27.1 %collective-permute-start.7 = (bf16[64,4224]{1,0:T(8,128)(2,1)S(1)}, bf16[64,4224]{1,0:T(8,128)(2,1)S(1)}, u32[]{:S(2)}, u32[]{:S(2)}) collective-permute-start(bf16[64,4224]{1,0:T(8,128)(2,1)S(1)} %get-tuple-element.9), channel_id=1, source_target_pairs={{0,16},{16,0},{1,17},{17,1},{2,18},{18,2},{3,19},{19,3},{4,20},{20... | collective-permute-start | bytes 1622024 | tf_op jit(solution)/shard_map/ppermute | solution.py:31
  34.2 46.3 %collective-permute-start.15 = (bf16[64,4224]{1,0:T(8,128)(2,1)S(1)}, bf16[64,4224]{1,0:T(8,128)(2,1)S(1)}, u32[]{:S(2)}, u32[]{:S(2)}) collective-permute-start(bf16[64,4224]{1,0:T(8,128)(2,1)S(1)} %get-tuple-element.10.refs_0_), channel_id=1, source_target_pairs={{0,4},{4,0},{8,12},{12,8},{1,5},{5,1},{9,13},{13,9},{2,6},{6,2},{1... | collective-permute-start | bytes 1622024 | tf_op jit(solution)/shard_map/ppermute | solution.py:31
  34.8 45.8 %collective-permute-start.16 = (bf16[64,4224]{1,0:T(8,128)(2,1)S(1)}, bf16[64,4224]{1,0:T(8,128)(2,1)S(1)}, u32[]{:S(2)}, u32[]{:S(2)}) collective-permute-start(bf16[64,4224]{1,0:T(8,128)(2,1)S(1)} %get-tuple-element.10.refs_0_), channel_id=1, source_target_pairs={{0,8},{4,12},{8,0},{12,4},{1,9},{5,13},{9,1},{13,5},{2,10},{6,14},... | collective-permute-start | bytes 1622024 | tf_op jit(solution)/shard_map/ppermute | solution.py:31
  136.7 14.6 %collective-permute-start.42 = (bf16[2,32,4096]{2,1,0:T(8,128)(2,1)}, bf16[2,32,4096]{2,1,0:T(8,128)(2,1)}, u32[]{:S(2)}, u32[]{:S(2)}) collective-permute-start(bf16[2,32,4096]{2,1,0:T(8,128)(2,1)} %pad_maximum_fusion.4), channel_id=1, source_target_pairs={{0,8},{4,12},{8,0},{12,4},{1,9},{5,13},{9,1},{13,5},{2,10},{6,14},... | collective-permute-start | bytes 1572872 | tf_op jit(solution)/shard_map/ppermute | solution.py:31
  138.6 14.4 %collective-permute-start.40 = (bf16[2,32,4096]{2,1,0:T(8,128)(2,1)}, bf16[2,32,4096]{2,1,0:T(8,128)(2,1)}, u32[]{:S(2)}, u32[]{:S(2)}) collective-permute-start(bf16[2,32,4096]{2,1,0:T(8,128)(2,1)} %pad_maximum_fusion.3), channel_id=1, source_target_pairs={{0,4},{4,0},{8,12},{12,8},{1,5},{5,1},{9,13},{13,9},{2,6},{6,2},{1... | collective-permute-start | bytes 1572872 | tf_op jit(solution)/shard_map/ppermute | solution.py:31
  154.3 15.3 %collective-permute-start.41 = (bf16[32,4096]{1,0:T(8,128)(2,1)S(1)}, bf16[32,4096]{1,0:T(8,128)(2,1)S(1)}, u32[]{:S(2)}, u32[]{:S(2)}) collective-permute-start(bf16[32,4096]{1,0:T(8,128)(2,1)S(1)} %get-tuple-element.19), channel_id=1, source_target_pairs={{0,8},{4,12},{8,0},{12,4},{1,9},{5,13},{9,1},{13,5},{2,10},{6,14},... | collective-permute-start | bytes 786440 | tf_op jit(solution)/shard_map/ppermute | solution.py:31
  157.2 16.5 %collective-permute-start.22 = (bf16[16,4096]{1,0:T(8,128)(2,1)}, bf16[16,4096]{1,0:T(8,128)(2,1)S(1)}, u32[]{:S(2)}, u32[]{:S(2)}) collective-permute-start(bf16[16,4096]{1,0:T(8,128)(2,1)} %get-tuple-element.35), channel_id=1, source_target_pairs={{0,1},{1,0},{2,3},{3,2},{4,5},{5,4},{6,7},{7,6},{8,9},{9,8},{10,11... | collective-permute-start | bytes 393224 | tf_op jit(solution)/shard_map/ppermute | solution.py:31
  171.2 18.0 %collective-permute-start.44 = (bf16[16,4096]{1,0:T(8,128)(2,1)S(1)}, bf16[16,4096]{1,0:T(8,128)(2,1)S(1)}, u32[]{:S(2)}, u32[]{:S(2)}) collective-permute-start(bf16[16,4096]{1,0:T(8,128)(2,1)S(1)} %get-tuple-element.39), channel_id=1, source_target_pairs={{0,1},{1,0},{2,3},{3,2},{4,5},{5,4},{6,7},{7,6},{8,9},{9,8},{10,11... | collective-permute-start | bytes 393224 | tf_op jit(solution)/shard_map/ppermute | solution.py:31
  182.7 28.3 %collective-permute-start.25 = (bf16[16,4096]{1,0:T(8,128)(2,1)S(1)}, bf16[16,4096]{1,0:T(8,128)(2,1)S(1)}, u32[]{:S(2)}, u32[]{:S(2)}) collective-permute-start(bf16[16,4096]{1,0:T(8,128)(2,1)S(1)} %final_rows.2), channel_id=1, source_target_pairs={{0,1},{1,0},{2,3},{3,2},{4,5},{5,4},{6,7},{7,6},{8,9},{9,8},{10,11... | collective-permute-start | bytes 393224 | tf_op jit(solution)/shard_map/ppermute | solution.py:31
  184.7 27.7 %collective-permute-start.26 = (bf16[16,4096]{1,0:T(8,128)(2,1)S(1)}, bf16[16,4096]{1,0:T(8,128)(2,1)S(1)}, u32[]{:S(2)}, u32[]{:S(2)}) collective-permute-start(bf16[16,4096]{1,0:T(8,128)(2,1)S(1)} %final_rows.2), channel_id=1, source_target_pairs={{0,2},{1,3},{2,0},{3,1},{4,6},{5,7},{6,4},{7,5},{8,10},{9,11},{10,... | collective-permute-start | bytes 393224 | tf_op jit(solution)/shard_map/ppermute | solution.py:31
  186.3 26.1 %collective-permute-start.27 = (bf16[16,4096]{1,0:T(8,128)(2,1)S(1)}, bf16[16,4096]{1,0:T(8,128)(2,1)S(1)}, u32[]{:S(2)}, u32[]{:S(2)}) collective-permute-start(bf16[16,4096]{1,0:T(8,128)(2,1)S(1)} %final_rows.2), channel_id=1, source_target_pairs={{0,3},{1,2},{2,1},{3,0},{4,7},{5,6},{6,5},{7,4},{8,11},{9,10},{10,... | collective-permute-start | bytes 393224 | tf_op jit(solution)/shard_map/ppermute | solution.py:31
  187.2 20.5 %collective-permute-start.45 = (bf16[16,4096]{1,0:T(8,128)(2,1)S(1)}, bf16[16,4096]{1,0:T(8,128)(2,1)S(1)}, u32[]{:S(2)}, u32[]{:S(2)}) collective-permute-start(bf16[16,4096]{1,0:T(8,128)(2,1)S(1)} %get-tuple-element.38), channel_id=1, source_target_pairs={{0,2},{1,3},{2,0},{3,1},{4,6},{5,7},{6,4},{7,5},{8,10},{9,11},{10,... | collective-permute-start | bytes 393224 | tf_op jit(solution)/shard_map/ppermute | solution.py:31
  189.2 18.4 %collective-permute-start.46 = (bf16[16,4096]{1,0:T(8,128)(2,1)S(1)}, bf16[16,4096]{1,0:T(8,128)(2,1)S(1)}, u32[]{:S(2)}, u32[]{:S(2)}) collective-permute-start(bf16[16,4096]{1,0:T(8,128)(2,1)S(1)} %get-tuple-element.37), channel_id=1, source_target_pairs={{0,3},{1,2},{2,1},{3,0},{4,7},{5,6},{6,5},{7,4},{8,11},{9,10},{10,... | collective-permute-start | bytes 393224 | tf_op jit(solution)/shard_map/ppermute | solution.py:31
  212.5 14.9 %collective-permute-start.29 = (bf16[64,4096]{1,0:T(8,128)(2,1)S(1)}, bf16[64,4096]{1,0:T(8,128)(2,1)S(1)}, u32[]{:S(2)}, u32[]{:S(2)}) collective-permute-start(bf16[64,4096]{1,0:T(8,128)(2,1)S(1)} %pad_maximum_fusion.2.refs_0_), channel_id=1, source_target_pairs={{0,8},{4,12},{8,0},{12,4},{1,9},{5,13},{9,1},{13,5},{2,10},{6,14},... | collective-permute-start | bytes 1572872 | tf_op jit(solution)/shard_map/ppermute | solution.py:31
  213.6 15.6 %collective-permute-start.28 = (bf16[64,4096]{1,0:T(8,128)(2,1)S(1)}, bf16[64,4096]{1,0:T(8,128)(2,1)S(1)}, u32[]{:S(2)}, u32[]{:S(2)}) collective-permute-start(bf16[64,4096]{1,0:T(8,128)(2,1)S(1)} %pad_maximum_fusion.2.refs_0_), channel_id=1, source_target_pairs={{0,4},{4,0},{8,12},{12,8},{1,5},{5,1},{9,13},{13,9},{2,6},{6,2},{1... | collective-permute-start | bytes 1572872 | tf_op jit(solution)/shard_map/ppermute | solution.py:31
  222.1 16.5 %collective-permute-start.51 = (bf16[64,4096]{1,0:T(8,128)(2,1)S(1)}, bf16[64,4096]{1,0:T(8,128)(2,1)S(1)}, u32[]{:S(2)}, u32[]{:S(2)}) collective-permute-start(bf16[64,4096]{1,0:T(8,128)(2,1)S(1)} %pad_maximum_fusion.6.refs_0_), channel_id=1, source_target_pairs={{0,8},{4,12},{8,0},{12,4},{1,9},{5,13},{9,1},{13,5},{2,10},{6,14},... | collective-permute-start | bytes 1572872 | tf_op jit(solution)/shard_map/ppermute | solution.py:31
  223.2 17.2 %collective-permute-start.50 = (bf16[64,4096]{1,0:T(8,128)(2,1)S(1)}, bf16[64,4096]{1,0:T(8,128)(2,1)S(1)}, u32[]{:S(2)}, u32[]{:S(2)}) collective-permute-start(bf16[64,4096]{1,0:T(8,128)(2,1)S(1)} %pad_maximum_fusion.6.refs_0_), channel_id=1, source_target_pairs={{0,4},{4,0},{8,12},{12,8},{1,5},{5,1},{9,13},{13,9},{2,6},{6,2},{1... | collective-permute-start | bytes 1572872 | tf_op jit(solution)/shard_map/ppermute | solution.py:31
  228.1 17.2 %collective-permute-start.30 = (bf16[32,4096]{1,0:T(8,128)(2,1)}, bf16[32,4096]{1,0:T(8,128)(2,1)S(1)}, u32[]{:S(2)}, u32[]{:S(2)}) collective-permute-start(bf16[32,4096]{1,0:T(8,128)(2,1)} %slice.395), channel_id=1, source_target_pairs={{0,4},{4,0},{8,12},{12,8},{1,5},{5,1},{9,13},{13,9},{2,6},{6,2},{1... | collective-permute-start | bytes 786440 | tf_op jit(solution)/shard_map/ppermute | solution.py:31
  229.9 15.4 %collective-permute-start.31 = (bf16[32,4096]{1,0:T(8,128)(2,1)}, bf16[32,4096]{1,0:T(8,128)(2,1)}, u32[]{:S(2)}, u32[]{:S(2)}) collective-permute-start(bf16[32,4096]{1,0:T(8,128)(2,1)} %slice.396), channel_id=1, source_target_pairs={{0,8},{4,12},{8,0},{12,4},{1,9},{5,13},{9,1},{13,5},{2,10},{6,14},... | collective-permute-start | bytes 786440 | tf_op jit(solution)/shard_map/ppermute | solution.py:31
  239.4 14.6 %collective-permute-start.52 = (bf16[32,4096]{1,0:T(8,128)(2,1)}, bf16[32,4096]{1,0:T(8,128)(2,1)}, u32[]{:S(2)}, u32[]{:S(2)}) collective-permute-start(bf16[32,4096]{1,0:T(8,128)(2,1)} %slice.421), channel_id=1, source_target_pairs={{0,4},{4,0},{8,12},{12,8},{1,5},{5,1},{9,13},{13,9},{2,6},{6,2},{1... | collective-permute-start | bytes 786440 | tf_op jit(solution)/shard_map/ppermute | solution.py:31
  (58 other events, 593.2 us)

commit v5 on v4

--- a/solution.py
+++ b/solution.py
@@ -70,10 +70,17 @@
     return tail[first : first + 1] + tail[first + 1 : first + 2] + tail[first + 2 : first + 3]
 
 
-def norm_kernel(splits, part, count, *refs):
+def norm_kernel(splits, part, count, after, *refs):
     slices, gains = refs[:count], refs[count : 2 * count]
     routes_ref, weights_ref = refs[2 * count : 2 * count + 2]
-    rows_ref, raw_ref = refs[-2:]
+    rest = refs[2 * count + 2 + after :]
+    handing_on = len(rest) > 2
+    if handing_on:
+        next_ref, rows_ref, raw_ref, out_ref, sem = rest
+        copy = pltpu.make_async_copy(next_ref, out_ref, sem)
+        copy.start()
+    else:
+        rows_ref, raw_ref = rest
     rows = rows_ref.shape[0]
     width = slices[0].shape[1]
     full_width = width * count
@@ -104,26 +111,30 @@
         low = weight - high - middle
         value = jnp.where(kind == 0, high, jnp.where(kind == 1, middle, low))
         rows_ref[i * own_rows : (i + 1) * own_rows, full_width:] = value.astype(jnp.bfloat16)
-
-
-def norm_rows(slices, gains, routes, route_weights, splits, part, rows, after):
+    if handing_on:
+        copy.wait()
+
+
+def norm_rows(slices, gains, routes, route_weights, splits, part, rows, after, following):
     width = slices[0].shape[1]
     count = len(slices)
     full_width = width * count
     return pl.pallas_call(
-        functools.partial(norm_kernel, splits, part, count),
+        functools.partial(norm_kernel, splits, part, count, len(after)),
         out_shape=(
             jax.ShapeDtypeStruct((rows, full_width + LANES), jnp.bfloat16),
             jax.ShapeDtypeStruct((rows // count, full_width), jnp.bfloat16),
-        ),
-        in_specs=[whole()] * (2 * count + 2) + [anywhere()] * len(after),
-        out_specs=(whole(), whole()),
+        )
+        + tuple(jax.ShapeDtypeStruct(f.shape, f.dtype) for f in following),
+        in_specs=[whole()] * (2 * count + 2) + [anywhere()] * (len(after) + len(following)),
+        out_specs=(whole(), whole()) + (anywhere(),) * len(following),
+        scratch_shapes=[pltpu.SemaphoreType.DMA] * len(following),
         compiler_params=params(6 * MIB),
         cost_estimate=pl.CostEstimate(
             flops=6 * rows * full_width, bytes_accessed=4 * rows * full_width, transcendentals=rows
         ),
         name="norm_rows",
-    )(*slices, *gains, routes, route_weights, *after)
+    )(*slices, *gains, routes, route_weights, *after, *following)
 
 
 def hidden_kernel(pieces, after, tile, first, steps, *refs):
@@ -201,19 +212,6 @@
     )(*pieces, w_gate, w_up, *after)
 
 
-def hidden_dots(pieces, w_gate, w_up):
-    full_width = w_gate.shape[1]
-    joined = jnp.concatenate(pieces)
-    rows = joined[:, :full_width]
-    small = joined[:, full_width:].astype(jnp.float32)
-    lane = jnp.arange(LANES, dtype=jnp.int32)
-    start = lax.axis_index("expert") * 3
-    weight = jnp.sum(jnp.where((lane >= start) & (lane < start + 3), small, 0.0), axis=1)
-    gate = jnp.dot(rows, w_gate[0], preferred_element_type=jnp.float32)
-    up = jnp.dot(rows, w_up[0], preferred_element_type=jnp.float32)
-    return (jax.nn.silu(gate) * up * weight[:, None]).astype(jnp.bfloat16)
-
-
 def down_kernel(start, count, *refs):
     hidden_refs, down_ref, out_ref = refs[:count], refs[count], refs[-1]
     full_width = out_ref.shape[1]
@@ -265,45 +263,65 @@
     return jnp.concatenate(outs)
 
 
-def final_kernel(parts, gains_count, *refs):
-    part_refs, raw_ref = refs[:parts], refs[parts]
-    gains = refs[parts + 1 : parts + 1 + gains_count]
-    out_ref, work = refs[parts + 1 + gains_count :]
-    width = gains[0].shape[1]
+def final_kernel(parts, gains_count, after, *refs):
+    part_refs, gain_refs = refs[: parts + 1], refs[parts + 1 : parts + 1 + gains_count]
+    out_ref, rows_scr, gains_scr, work, sems = refs[parts + 1 + gains_count + after :]
+    width = gains_scr.shape[2]
     me = lax.axis_index("tensor")
-    mixed = part_refs[0][...].astype(jnp.float32)
-    for part in part_refs[1:]:
-        mixed = mixed + part[...].astype(jnp.float32)
-    residual = raw_ref[...].astype(jnp.float32) + mixed
+    copies = [
+        pltpu.make_async_copy(part_refs[i], rows_scr.at[i], sems.at[i]) for i in range(parts + 1)
+    ]
+    for d in range(gains_count):
+        tail = gain_refs[d].at[pl.ds(gain_refs[d].shape[0] - 16, 16), :]
+        copies.append(pltpu.make_async_copy(tail, gains_scr.at[d], sems.at[parts + 1 + d]))
+    for copy in copies:
+        copy.start()
+    for copy in copies:
+        copy.wait()
+    mixed = rows_scr[0].astype(jnp.float32)
+    for i in range(1, parts):
+        mixed = mixed + rows_scr[i].astype(jnp.float32)
+    residual = rows_scr[parts].astype(jnp.float32) + mixed
     residual = residual.astype(jnp.bfloat16).astype(jnp.float32)
     total = jnp.sum(residual * residual, axis=1, keepdims=True)
     scale = lax.rsqrt(total / residual.shape[1] + epsilon)
     work[...] = residual * scale
     for d in range(gains_count):
         columns = pl.ds(pl.multiple_of((me ^ d) * width, width), width)
-        out_ref[:, columns] = (work[:, columns] * gain_row(gains[d], 1)).astype(jnp.bfloat16)
-
-
-def final_rows(parts, raw, gains):
+        out_ref[:, columns] = (work[:, columns] * gain_row(gains_scr.at[d], 1)).astype(
+            jnp.bfloat16
+        )
+
+
+def final_rows(parts, raw, gains, after):
     rows, full_width = raw.shape
+    count = len(parts) + 1 + len(gains)
     return pl.pallas_call(
-        functools.partial(final_kernel, len(parts), len(gains)),
+        functools.partial(final_kernel, len(parts), len(gains), len(after)),
         out_shape=jax.ShapeDtypeStruct((rows, full_width), jnp.bfloat16),
-        in_specs=[whole()] * (len(parts) + 1 + len(gains)),
+        in_specs=[anywhere()] * (count + len(after)),
         out_specs=whole(),
-        scratch_shapes=[pltpu.VMEM((rows, full_width), jnp.float32)],
+        scratch_shapes=[
+            pltpu.VMEM((len(parts) + 1, rows, full_width), jnp.bfloat16),
+            pltpu.VMEM((len(gains), 16, gains[0].shape[1]), jnp.bfloat16),
+            pltpu.VMEM((rows, full_width), jnp.float32),
+            pltpu.SemaphoreType.DMA((count,)),
+        ],
         compiler_params=params(6 * MIB),
         cost_estimate=pl.CostEstimate(
             flops=8 * rows * full_width, bytes_accessed=12 * rows * full_width, transcendentals=rows
         ),
         name="final_rows",
-    )(*parts, raw, *gains)
-
-
-def head_kernel(pieces, tile, *refs):
+    )(*parts, raw, *gains, *after)
+
+
+def head_kernel(pieces, tile, sub, *refs):
     piece_refs = refs[:pieces]
     head_ref, target_ref, out_ref, rows_scr, head_scr, sems, head_sems = refs[pieces:]
-    steps = head_ref.shape[0] // tile
+    vocab_part = head_ref.shape[0]
+    steps = vocab_part // tile
+    my_expert, my_tensor = lax.axis_index("expert"), lax.axis_index("tensor")
+    n_tensor = lax.axis_size("tensor")
 
     def fetch(i):
         return pltpu.make_async_copy(
@@ -312,12 +330,28 @@
             head_sems.at[i],
         )
 
+    copies = []
+    for piece_ref in piece_refs:
+        for start in range(0, piece_ref.shape[0], sub):
+            far_expert, far_tensor = divmod(len(copies), n_tensor)
+            block = (my_expert ^ far_expert) * n_tensor + (my_tensor ^ far_tensor)
+            copies.append(
+                pltpu.make_async_copy(
+                    piece_ref.at[pl.ds(start, sub), :],
+                    rows_scr.at[pl.ds(pl.multiple_of(block * sub, sub), sub), :],
+                    sems.at[len(copies)],
+                )
+            )
     fetch(0).start()
-    load_pieces(piece_refs, rows_scr, sems)
+    for copy in copies:
+        copy.start()
     for i in range(1, steps):
         fetch(i).start()
+    for copy in copies:
+        copy.wait()
     lane = lax.broadcasted_iota(jnp.int32, out_ref.shape, 0)
     out_ref[...] = jnp.where(lane == 0, -jnp.inf, 0.0)
+    targets = target_ref[...] - (my_expert * n_tensor + my_tensor) * vocab_part
 
     @pl.loop(0, steps)
     def _(i):
@@ -335,23 +369,23 @@
         out_ref[1:2, :] = old_total * jnp.exp(old_top - top) + jnp.sum(
             jnp.exp(logits - top), axis=0, keepdims=True
         )
-        hit = word == target_ref[...]
+        hit = word == targets
         out_ref[2:3, :] += jnp.sum(jnp.where(hit, logits, 0.0), axis=0, keepdims=True)
 
 
-def head_terms(pieces, head_rows, targets):
+def head_terms(pieces, head_rows, targets, sub):
     rows = sum(p.shape[0] for p in pieces)
     vocab_part, full_width = head_rows.shape
     tile = next(t for t in (400, 200, 80, 8, vocab_part) if vocab_part % t == 0)
     return pl.pallas_call(
-        functools.partial(head_kernel, len(pieces), tile),
+        functools.partial(head_kernel, len(pieces), tile, sub),
         out_shape=jax.ShapeDtypeStruct((8, rows), jnp.float32),
         in_specs=[anywhere()] * (len(pieces) + 1) + [whole()],
         out_specs=whole(),
         scratch_shapes=[
             pltpu.VMEM((rows, full_width), jnp.bfloat16),
             pltpu.VMEM((vocab_part // tile, tile, full_width), jnp.bfloat16),
-            pltpu.SemaphoreType.DMA((len(pieces),)),
+            pltpu.SemaphoreType.DMA((rows // sub,)),
             pltpu.SemaphoreType.DMA((vocab_part // tile,)),
         ],
         compiler_params=params((22 + rows // 64) * MIB),
@@ -371,43 +405,112 @@
     return jnp.stack([top, total, target])
 
 
-def flip(x, axis, index):
-    size = x.shape[axis]
-    bit = 1
-    while bit < size:
-        shape = x.shape[:axis] + (size // (2 * bit), 2, bit) + x.shape[axis + 1 :]
-        turned = jnp.flip(x.reshape(shape), axis + 1).reshape(x.shape)
-        x = jnp.where((index & bit) != 0, turned, x)
-        bit *= 2
-    return x
-
-
-def sum_plane(kept, got):
+def join_axis(terms, axis, place, me):
+    def of(d):
+        return lax.dynamic_index_in_dim(terms, me ^ d, place, False)
+
+    return join_terms([of(0)] + [swap(of(d), axis, d) for d in range(1, lax.axis_size(axis))])
+
+
+def pack_kernel(kept_ref, got_ref, one_ref, two_ref, home_ref, side_ref):
+    rows = home_ref.shape[0]
+    half = rows // 2
+
+    def both(d, first):
+        block = slice(d * rows + first, d * rows + first + half)
+        return kept_ref[block, :].astype(jnp.float32) + got_ref[block, :].astype(jnp.float32)
+
+    one_ref[:half, :] = both(1, 0).astype(jnp.bfloat16)
+    one_ref[half:, :] = both(3, 0).astype(jnp.bfloat16)
+    two_ref[:half, :] = both(2, half).astype(jnp.bfloat16)
+    two_ref[half:, :] = both(3, half).astype(jnp.bfloat16)
+    home_ref[:half, :] = both(0, 0)
+    home_ref[half:, :] = both(0, half)
+    side_ref[0] = both(1, half)
+    side_ref[1] = both(2, 0)
+
+
+def pass_kernel(side_ref, one_ref, two_ref, *refs):
+    pass_one_ref, pass_two_ref = refs[-2:]
+    half = pass_one_ref.shape[0]
+    pass_one_ref[...] = (side_ref[0] + two_ref[half:, :].astype(jnp.float32)).astype(jnp.bfloat16)
+    pass_two_ref[...] = (side_ref[1] + one_ref[half:, :].astype(jnp.float32)).astype(jnp.bfloat16)
+
+
+def total_kernel(count, home_ref, one_ref, two_ref, last_one_ref, last_two_ref, *refs):
+    outs, work = refs[-count - 1 : -1], refs[-1]
+    half = last_one_ref.shape[0]
+    sub = outs[0].shape[0]
+    me = lax.axis_index("tensor")
+    upper = one_ref[:half, :].astype(jnp.float32) + last_two_ref[...].astype(jnp.float32)
+    lower = two_ref[:half, :].astype(jnp.float32) + last_one_ref[...].astype(jnp.float32)
+    work[:half, :] = home_ref[:half, :] + upper
+    work[half:, :] = home_ref[half:, :] + lower
+    for d in range(count):
+        block = pl.ds(pl.multiple_of((me ^ d) * sub, sub), sub)
+        outs[d][...] = work[block, :].astype(jnp.bfloat16)
+
+
+def small_call(kernel, name, inputs, after, outs, scratch, limit):
+    size = sum(x.size * x.dtype.itemsize for x in inputs)
+    return pl.pallas_call(
+        kernel,
+        out_shape=tuple(jax.ShapeDtypeStruct(*out) for out in outs),
+        in_specs=[whole()] * len(inputs) + [anywhere()] * len(after),
+        out_specs=(whole(),) * len(outs),
+        scratch_shapes=scratch,
+        compiler_params=params(limit),
+        cost_estimate=pl.CostEstimate(flops=size, bytes_accessed=2 * size, transcendentals=0),
+        name=name,
+    )(*inputs, *after)
+
+
+def sum_plane(kept, got, rows, after_pass, after_total):
     f32, b16 = jnp.float32, jnp.bfloat16
-    count, rows = kept.shape[:2]
-
-    def both(d, part=slice(None)):
-        return kept[d, part].astype(f32) + got[d, part].astype(f32)
-
-    if count != 4:
-        total = both(0)
-        for d in range(1, count):
-            total = total + swap(both(d).astype(b16), "expert", d).astype(f32)
-        return total.astype(b16), []
-    upper, lower = slice(0, rows // 2), slice(rows // 2, rows)
-    one = jnp.stack([both(1, upper), both(3, upper)]).astype(b16)
-    two = jnp.stack([both(2, lower), both(3, lower)]).astype(b16)
-    from_one, from_two = swap(one, "expert", 1), swap(two, "expert", 2)
-    pass_two = (both(2, upper) + from_one[1].astype(f32)).astype(b16)
-    pass_one = (both(1, lower) + from_two[1].astype(f32)).astype(b16)
-    last_two, last_one = swap(pass_two, "expert", 2), swap(pass_one, "expert", 1)
-    total = jnp.concatenate(
-        [
-            both(0, upper) + from_one[0].astype(f32) + last_two.astype(f32),
-            both(0, lower) + from_two[0].astype(f32) + last_one.astype(f32),
-        ]
-    )
-    return total.astype(b16), [one, two, pass_one, pass_two]
+    n_tensor = lax.axis_size("tensor")
+    count, full_width = kept.shape[0] // rows, kept.shape[1]
+    half = rows // 2
+    sub = rows // n_tensor
+    if count == 4 and half % 16 == 0 and sub % 16 == 0:
+        one, two, home, side = small_call(
+            pack_kernel,
+            "pack",
+            [kept, got],
+            [],
+            [((rows, full_width), b16)] * 2
+            + [((rows, full_width), f32), ((2, half, full_width), f32)],
+            [],
+            10 * MIB,
+        )
+        from_one, from_two = swap(one, "expert", 1), swap(two, "expert", 2)
+        pass_one, pass_two = small_call(
+            pass_kernel,
+            "pass_on",
+            [side, from_one, from_two],
+            after_pass,
+            [((half, full_width), b16)] * 2,
+            [],
+            6 * MIB,
+        )
+        last_one, last_two = swap(pass_one, "expert", 1), swap(pass_two, "expert", 2)
+        pieces = small_call(
+            functools.partial(total_kernel, n_tensor),
+            "total",
+            [home, from_one, from_two, last_one, last_two],
+            after_total,
+            [((sub, full_width), b16)] * n_tensor,
+            [pltpu.VMEM((rows, full_width), f32)],
+            8 * MIB,
+        )
+        return list(pieces), [one, two], [pass_one, pass_two]
+    both = (kept.astype(f32) + got.astype(f32)).reshape(count, rows, full_width)
+    total = both[0]
+    for d in range(1, count):
+        total = total + swap(both[d].astype(b16), "expert", d).astype(f32)
+    total = total.astype(b16).reshape(n_tensor, sub, full_width)
+    me = lax.axis_index("tensor")
+    pieces = [lax.dynamic_index_in_dim(total, me ^ d, 0, False) for d in range(n_tensor)]
+    return pieces, [], []
 
 
 def on_device(
@@ -423,81 +526,77 @@
     splits = 2 if own % 32 == 0 else 1
     sub = own // splits
     rows = sub * n_tensor
-    vocab_part = head_weight.shape[1]
 
     parts = tokens.reshape(n_tensor, splits, sub, width)
     rider = jnp.concatenate([split_three(norm_gain), split_three(final_gain)])
     rider = jnp.pad(rider, ((0, 16 - rider.shape[0]), (0, 0))).astype(jnp.bfloat16)
-    slices = []
-    for h in range(splits):
-        part = parts[:, h].reshape(rows, width)
-        slices.append(
-            gather_near(part if h else jnp.concatenate([part, rider]), "tensor")
-        )
-    gains = slices[0]
+    blocks = [parts[:, h].reshape(rows, width) for h in range(splits)]
+    gains = slices = gather_near(jnp.concatenate([blocks[0], rider]), "tensor")
     planes, raws = [], []
     after = []
     for h in range(splits):
-        normed, raw = norm_rows(slices[h], gains, routes, route_weights, splits, h, rows, after)
+        following = blocks[h + 1 : h + 2]
+        normed, raw, *block = norm_rows(
+            slices, gains, routes, route_weights, splits, h, rows, after, following
+        )
+        if block:
+            slices = gather_near(block[0], "tensor")
         plane = gather_plane(normed, "expert")
         planes.append(plane)
         raws.append(raw)
-        after = plane[1:3]
-
-    finals = []
-    begun, moved = [], []
-    last = None
+        after = plane[3:]
+
+    w_gate = pltpu.with_memory_space_constraint(w_gate, pltpu.HBM)
+    w_up = pltpu.with_memory_space_constraint(w_up, pltpu.HBM)
+    head_rows = pltpu.with_memory_space_constraint(head_weight.T, pltpu.HBM)
+    target_rows = targets.reshape(n_expert, n_tensor, splits, sub)
+    terms = []
+    steps = {}
     for h in range(splits):
         later = planes[h + 1][1:3] if h + 1 < splits else []
         away = [swap(p, "seq", 1) for p in planes[h]]
         if 2 * n_expert * rows <= LARGEST:
             half = n_expert * rows
             everything = planes[h] + away
-            if h == 0:
-                hidden = [hidden_dots(everything, w_gate, w_up)]
-            else:
-                tile = tile_of(w_gate)
-                steps = w_gate.shape[2] // tile
-                cut = (steps + 1) // 2
-                hidden = [
-                    hidden_rows(everything, w_gate, w_up, begun, 0, cut, tile),
-                    hidden_rows(everything, w_gate, w_up, moved, cut, steps - cut, tile),
-                ]
-            other = down_rows(hidden, w_down, half, half, later + ([] if last is None else [last]))
-            kept = down_rows(hidden, w_down, 0, half, [])
+            tile = tile_of(w_gate)
+            count = w_gate.shape[2] // tile
+            cuts = [0, (count + 1) // 2, count - 1, count] if h else [0, count]
+            ties = [steps.get(key, []) for key in ("packed", "passed", "totals")]
+            hidden = [
+                hidden_rows(
+                    everything, w_gate, w_up, ties[i], cuts[i], cuts[i + 1] - cuts[i], tile
+                )
+                for i in range(len(cuts) - 1)
+            ]
+            other = down_rows(hidden, w_down, half, half, later)
+            kept = down_rows(hidden, w_down, 0, half, steps.get("final", []))
         else:
             kept, other = many_rows(planes[h], w_gate, w_up, w_down), many_rows(
                 away, w_gate, w_up, w_down
             )
         got = swap(other, "seq", 1)
-        shape = (n_expert, rows, full_width)
-        total, sums = sum_plane(kept.reshape(shape), got.reshape(shape))
-        begun, moved = sums[:2], sums[2:]
-        last = total
-        total = total.reshape(n_tensor, sub, full_width)
-        mine = [lax.dynamic_index_in_dim(total, my_tensor, 0, False)]
-        for d in range(1, n_tensor):
-            out = lax.dynamic_index_in_dim(total, my_tensor ^ d, 0, False)
-            mine.append(swap(out, "tensor", d))
-        finals.append(final_rows(mine, raws[h], gains))
-
-    start = (my_expert * n_tensor + my_tensor) * vocab_part
-    local = (targets - start).astype(jnp.int32).reshape(n_expert, n_tensor, splits, sub)
-    local = flip(flip(local, 0, my_expert), 1, my_tensor)
-    head_rows = pltpu.with_memory_space_constraint(head_weight.T, pltpu.HBM)
-    terms = []
-    for h in range(splits):
-        column = jnp.concatenate(gather_near(finals[h], "tensor"), axis=0)
-        plane = gather_plane(column, "expert")
-        term = head_terms(plane, head_rows, local[:, :, h].reshape(1, -1))
+        totals, packed, passed = sum_plane(
+            kept, got, rows, steps.get("column", []), steps.get("near", [])
+        )
+        mine = totals[:1] + [swap(totals[d], "tensor", d) for d in range(1, n_tensor)]
+        final = final_rows(mine, raws[h], gains, steps.get("far", []))
+        column = gather_near(final, "tensor")
+        plane = gather_plane(jnp.concatenate(column, axis=0), "expert")
+        wanted = target_rows[:, :, h].reshape(1, -1)
+        term = head_terms(plane, head_rows, wanted, sub)
         terms.append(term[:3].reshape(3, n_expert, n_tensor, sub))
+        steps = {
+            "packed": packed,
+            "passed": passed,
+            "totals": totals,
+            "final": [final],
+            "column": column[1:],
+            "near": plane[1:3],
+            "far": plane[3:],
+        }
     terms = jnp.stack(terms, axis=3)
-    joined = join_terms(
-        [terms[:, :, 0]] + [swap(terms[:, :, d], "tensor", d) for d in range(1, n_tensor)]
-    )
-    joined = join_terms(
-        [joined[:, 0]] + [swap(joined[:, d], "expert", d) for d in range(1, n_expert)]
-    )
+    joined = join_axis(terms, "tensor", 2, my_tensor)
+    joined = join_axis(joined, "expert", 1, my_expert)
     return (joined[0] + jnp.log(joined[1]) - joined[2]).reshape(own)
 
 

time: 280 us -> 265 us (0.946)
  Pallas kernels: 59.9 us -> 92.3 us
  matrix products: 26.4 us -> 0 us
  starting transfers between devices: 78 us -> 67.1 us
  local copies, waits for them, and re-layouts: 17.1 us -> 6.73 us
  waiting for transfers between devices: 86.5 us -> 95.8 us
  other arithmetic: 10.1 us -> 2.11 us
    dot_general x2 -> x0, matrix products: 26.4 us -> none  [the longest x1 13.7 us: hidden_dots(): up = jnp.dot(rows, w_up[0], preferred_element_type=jnp.float32)]
    pallas_call x2 -> x4, Pallas kernels: 20.8 us -> 43.7 us  [hidden_rows(): pl.pallas_call(functools.partial(hidden_kernel, len(pieces), len(after),...]
    ppermute x60, starting transfers between devices: 78 us -> 67.1 us  [swap(): return lax.ppermute(x, axis, [(i, i ^ distance) for i in range(size)])]
    pallas_call x6 -> x12, Pallas kernels: 18.2 us -> 27.6 us  [the longest x2 22.5 us: head_terms(): pl.pallas_call(functools.partial(head_kernel, len(pieces), tile, sub), ou...]
    ppermute x60, waiting for transfers between devices: 86.5 us -> 95.8 us  [swap(): return lax.ppermute(x, axis, [(i, i ^ distance) for i in range(size)])]
    unnamed x55 -> x16, local copies, waits for them, and re-layouts: 7.33 us -> 2.55 us
    another operation x9 -> x4, other arithmetic: 5.16 us -> 1.47 us
  transfers between devices with their start and end apart: 60 -> 60, of which waited for: 24 -> 29; matrix products, arithmetic and copies ran while one was open for 15% -> 2% of each run, Pallas kernels for 15% -> 23%
where the time goes in v5:
time: 265 us
  waiting for transfers between devices  95.8 us (36%)
  Pallas kernels  92.3 us (35%)
  starting transfers between devices  67.1 us (25%)
  local copies, waits for them, and re-layouts  6.73 us (3%)
    ppermute x60, waiting for transfers between devices, swap(): return lax.ppermute(x, axis, [(i, i ^ distance) for i in range(size)])  95.8 us
    ppermute x60, starting transfers between devices, swap(): return lax.ppermute(x, axis, [(i, i ^ distance) for i in range(size)])  67.1 us
    pallas_call x4, Pallas kernels, hidden_rows(): pl.pallas_call(functools.partial(hidden_kernel, len(pieces), len(after),...  43.7 us
    pallas_call x2, Pallas kernels, head_terms(): pl.pallas_call(functools.partial(head_kernel, len(pieces), tile, sub), ou...  22.5 us
    pallas_call x4, Pallas kernels, down_rows(): pl.pallas_call(functools.partial(down_kernel, start, len(hidden)), out_sh...  21 us
  transfers between devices with their start and end apart: 60, of which 29 were waited for; matrix products, arithmetic and copies ran while one was open for 2% of the time, Pallas kernels for 23%

profile of v5, /device:TPU:0, one launch (start us, length us, event | category | flops | bytes accessed | tf_op | source)
XLA Modules:
  0.0 264.6 jit_solution(11143170973947897873)
XLA Ops:
  2.5 3.1 %collective-permute-start = (bf16[80,1024]{1,0:T(8,128)(2,1)S(1)}, bf16[80,1024]{1,0:T(8,128)(2,1)S(1)}, u32[]{:S(2)}, u32[]{:S(2)}) collective-permute-start(bf16[80,1024]{1,0:T(8,128)(2,1)S(1)} %fusion.1.refs_0_.refs_4_.refs_5_), channel_id=1, source_target_pairs={{0,1},{1,0},{2,3},{3,2},{4,5},{5,4},{6,7},{7,6},{8,9},{9,8},{10,11... | collective-permute-start | bytes 491528 | tf_op jit(solution)/shard_map/ppermute | solution.py:31
  12.3 8.4 %collective-permute-done.1.refs_2_.refs_6_.refs_7_ = bf16[80,1024]{1,0:T(8,128)(2,1)S(1)} collective-permute-done((bf16[80,1024]{1,0:T(8,128)(2,1)S(1)}, bf16[80,1024]{1,0:T(8,128)(2,1)S(1)}, u32[]{:S(2)}, u32[]{:S(2)}) %collective-permute-start.1) | collective-permute-done | bytes 163872 | tf_op jit(solution)/shard_map/ppermute | solution.py:31
  29.4 3.4 %collective-permute-done.4.refs_2_ = bf16[64,4224]{1,0:T(8,128)(2,1)S(1)} collective-permute-done((bf16[64,4224]{1,0:T(8,128)(2,1)S(1)}, bf16[64,4224]{1,0:T(8,128)(2,1)S(1)}, u32[]{:S(2)}, u32[]{:S(2)}) %collective-permute-start.4) | collective-permute-done | bytes 540704 | tf_op jit(solution)/shard_map/ppermute | solution.py:31
  38.6 3.2 %collective-permute-done.5.refs_3_.refs_10_ = bf16[32,4224]{1,0:T(8,128)(2,1)S(1)} collective-permute-done((bf16[32,4224]{1,0:T(8,128)(2,1)S(1)}, bf16[32,4224]{1,0:T(8,128)(2,1)S(1)}, u32[]{:S(2)}, u32[]{:S(2)}) %collective-permute-start.5) | collective-permute-done | bytes 270368 | tf_op jit(solution)/shard_map/ppermute | solution.py:31
  41.8 5.2 %collective-permute-done.6.refs_4_.refs_11_ = bf16[32,4224]{1,0:T(8,128)(2,1)S(1)} collective-permute-done((bf16[32,4224]{1,0:T(8,128)(2,1)S(1)}, bf16[32,4224]{1,0:T(8,128)(2,1)S(1)}, u32[]{:S(2)}, u32[]{:S(2)}) %collective-permute-start.6) | collective-permute-done | bytes 270368 | tf_op jit(solution)/shard_map/ppermute | solution.py:31
  48.5 20.2 %hidden_rows.4.refs_0_ = bf16[512,1792]{1,0:T(8,128)(2,1)S(1)} custom-call(bf16[64,4224]{1,0:T(8,128)(2,1)S(1)} %get-tuple-element.30.refs_0_, bf16[64,4224]{1,0:T(8,128)(2,1)S(1)} %collective-permute-done.3.refs_1_, bf16[64,4224]{1,0:T(8,128)(2,1)S(1)} %collective-permute-done.4.refs_2_, bf16[32,4224]{1,0:T(8,128)(2,1)S(1)} %collective-permute-done.5.refs_3_.refs_10_, ...), custom_call_target="tpu_custom_call" | custom-call | flops 15032385536 | bytes 35389440 | tf_op jit(solution)/shard_map/hidden_rows/pallas_call | solution.py:193
  68.8 5.2 %down_rows.5 = bf16[256,4096]{1,0:T(8,128)(2,1)S(1)} custom-call(bf16[512,1792]{1,0:T(8,128)(2,1)S(1)} %hidden_rows.4.refs_0_, bf16[1,1792,4096]{2,1,0:T(8,128)(2,1)S(1)} %bitcast.38, bf16[64,4224]{1,0:T(8,128)(2,1)S(1)} %collective-permute-done.15.refs_2_.refs_1_, bf16[64,4224]{1,0:T(8,128)(2,1)S(1)} %collective-permute-done.16.refs_3_.refs_2_), custom_call_target="tpu_custom_call" | custom-call | flops 3758096384 | bytes 3014656 | tf_op jit(solution)/shard_map/down_rows/pallas_call | solution.py:237
  77.1 5.9 %collective-permute-done.32.refs_3_ = bf16[32,4224]{1,0:T(8,128)(2,1)S(1)} collective-permute-done((bf16[32,4224]{1,0:T(8,128)(2,1)S(1)}, bf16[32,4224]{1,0:T(8,128)(2,1)S(1)}, u32[]{:S(2)}, u32[]{:S(2)}) %collective-permute-start.32) | collective-permute-done | bytes 270368 | tf_op jit(solution)/shard_map/ppermute | solution.py:31
  84.2 5.2 %down_rows.4.kept_ref = bf16[256,4096]{1,0:T(8,128)(2,1)S(1)} custom-call(bf16[512,1792]{1,0:T(8,128)(2,1)S(1)} %hidden_rows.4.refs_0_, bf16[1,1792,4096]{2,1,0:T(8,128)(2,1)S(1)} %bitcast.38), custom_call_target="tpu_custom_call" | custom-call | flops 3758096384 | bytes 3014656 | tf_op jit(solution)/shard_map/down_rows/pallas_call | solution.py:237
  92.1 11.7 %hidden_rows.5.refs_0_ = bf16[512,1024]{1,0:T(8,128)(2,1)S(1)} custom-call(bf16[64,4224]{1,0:T(8,128)(2,1)S(1)} %get-tuple-element.32.refs_0_, bf16[64,4224]{1,0:T(8,128)(2,1)S(1)} %collective-permute-done.15.refs_2_.refs_1_, bf16[64,4224]{1,0:T(8,128)(2,1)S(1)} %collective-permute-done.16.refs_3_.refs_2_, ...), custom_call_target="tpu_custom_call" | custom-call | flops 8589934592 | bytes 22020096 | tf_op jit(solution)/shard_map/hidden_rows/pallas_call | solution.py:193
  107.2 7.0 %hidden_rows.6.refs_1_ = bf16[512,512]{1,0:T(8,128)(2,1)S(1)} custom-call(bf16[64,4224]{1,0:T(8,128)(2,1)S(1)} %get-tuple-element.32.refs_0_, bf16[64,4224]{1,0:T(8,128)(2,1)S(1)} %collective-permute-done.15.refs_2_.refs_1_, bf16[64,4224]{1,0:T(8,128)(2,1)S(1)} %collective-permute-done.16.refs_3_.refs_2_, ...), custom_call_target="tpu_custom_call" | custom-call | flops 4294967296 | bytes 13107200 | tf_op jit(solution)/shard_map/hidden_rows/pallas_call | solution.py:193
  114.6 4.7 %hidden_rows.7.refs_2_ = bf16[512,256]{1,0:T(8,128)(2,1)S(1)} custom-call(bf16[64,4224]{1,0:T(8,128)(2,1)S(1)} %get-tuple-element.32.refs_0_, bf16[64,4224]{1,0:T(8,128)(2,1)S(1)} %collective-permute-done.15.refs_2_.refs_1_, bf16[64,4224]{1,0:T(8,128)(2,1)S(1)} %collective-permute-done.16.refs_3_.refs_2_, ...), custom_call_target="tpu_custom_call" | custom-call | flops 2147483648 | bytes 8650752 | tf_op jit(solution)/shard_map/hidden_rows/pallas_call | solution.py:193
  119.4 5.4 %down_rows.7 = bf16[256,4096]{1,0:T(8,128)(2,1)S(1)} custom-call(bf16[512,1024]{1,0:T(8,128)(2,1)S(1)} %hidden_rows.5.refs_0_, bf16[512,512]{1,0:T(8,128)(2,1)S(1)} %hidden_rows.6.refs_1_, bf16[512,256]{1,0:T(8,128)(2,1)S(1)} %hidden_rows.7.refs_2_, bf16[1,1792,4096]{2,1,0:T(8,128)(2,1)S(1)} %bitcast.38), custom_call_target="tpu_custom_call" | custom-call | flops 3758096384 | bytes 3014656 | tf_op jit(solution)/shard_map/down_rows/pallas_call | solution.py:237
  129.2 3.8 %collective-permute-done.22.refs_1_ = bf16[16,4096]{1,0:T(8,128)(2,1)S(1)} collective-permute-done((bf16[16,4096]{1,0:T(8,128)(2,1)S(1)}, bf16[16,4096]{1,0:T(8,128)(2,1)S(1)}, u32[]{:S(2)}, u32[]{:S(2)}) %collective-permute-start.22) | collective-permute-done | bytes 131104 | tf_op jit(solution)/shard_map/ppermute | solution.py:31
  133.0 6.4 %collective-permute-done.23.refs_2_ = bf16[16,4096]{1,0:T(8,128)(2,1)S(1)} collective-permute-done((bf16[16,4096]{1,0:T(8,128)(2,1)S(1)}, bf16[16,4096]{1,0:T(8,128)(2,1)S(1)}, u32[]{:S(2)}, u32[]{:S(2)}) %collective-permute-start.23) | collective-permute-done | bytes 131104 | tf_op jit(solution)/shard_map/ppermute | solution.py:31
  146.0 5.2 %down_rows.6.kept_ref = bf16[256,4096]{1,0:T(8,128)(2,1)S(1)} custom-call(bf16[512,1024]{1,0:T(8,128)(2,1)S(1)} %hidden_rows.5.refs_0_, bf16[512,512]{1,0:T(8,128)(2,1)S(1)} %hidden_rows.6.refs_1_, bf16[512,256]{1,0:T(8,128)(2,1)S(1)} %hidden_rows.7.refs_2_, bf16[1,1792,4096]{2,1,0:T(8,128)(2,1)S(1)} %bitcast.38, bf16[16,4096]{1,0:T(8,128)(2,1)S(1)} %final_rows.2.refs_4_), custom_call_target="tpu_custom_call" | custom-call | flops 3758096384 | bytes 3014656 | tf_op jit(solution)/shard_map/down_rows/pallas_call | solution.py:237
  157.6 9.0 %collective-permute-done.40.one_ref = bf16[64,4096]{1,0:T(8,128)(2,1)S(1)} collective-permute-done((bf16[64,4096]{1,0:T(8,128)(2,1)S(1)}, bf16[64,4096]{1,0:T(8,128)(2,1)S(1)}, u32[]{:S(2)}, u32[]{:S(2)}) %collective-permute-start.40) | collective-permute-done | bytes 524320 | tf_op jit(solution)/shard_map/ppermute | solution.py:31
  169.2 9.2 %collective-permute-done.29.refs_2_.refs_1_ = bf16[64,4096]{1,0:T(8,128)(2,1)S(1)} collective-permute-done((bf16[64,4096]{1,0:T(8,128)(2,1)S(1)}, bf16[64,4096]{1,0:T(8,128)(2,1)S(1)}, u32[]{:S(2)}, u32[]{:S(2)}) %collective-permute-start.29) | collective-permute-done | bytes 524320 | tf_op jit(solution)/shard_map/ppermute | solution.py:31
  189.5 3.3 %collective-permute-done.45.refs_2_ = bf16[16,4096]{1,0:T(8,128)(2,1)S(1)} collective-permute-done((bf16[16,4096]{1,0:T(8,128)(2,1)S(1)}, bf16[16,4096]{1,0:T(8,128)(2,1)S(1)}, u32[]{:S(2)}, u32[]{:S(2)}) %collective-permute-start.45) | collective-permute-done | bytes 131104 | tf_op jit(solution)/shard_map/ppermute | solution.py:31
  195.9 5.3 %collective-permute-start.47 = (bf16[16,4096]{1,0:T(8,128)(2,1)S(1)}, bf16[16,4096]{1,0:T(8,128)(2,1)S(1)}, u32[]{:S(2)}, u32[]{:S(2)}) collective-permute-start(bf16[16,4096]{1,0:T(8,128)(2,1)S(1)} %final_rows.3), channel_id=1, source_target_pairs={{0,1},{1,0},{2,3},{3,2},{4,5},{5,4},{6,7},{7,6},{8,9},{9,8},{10,11... | collective-permute-start | bytes 393224 | tf_op jit(solution)/shard_map/ppermute | solution.py:31
  207.1 3.0 %collective-permute-done.49 = bf16[16,4096]{1,0:T(8,128)(2,1)S(1)} collective-permute-done((bf16[16,4096]{1,0:T(8,128)(2,1)S(1)}, bf16[16,4096]{1,0:T(8,128)(2,1)S(1)}, u32[]{:S(2)}, u32[]{:S(2)}) %collective-permute-start.49) | collective-permute-done | bytes 131104 | tf_op jit(solution)/shard_map/ppermute | solution.py:31
  212.4 8.9 %collective-permute-done.51.refs_2_ = bf16[64,4096]{1,0:T(8,128)(2,1)S(1)} collective-permute-done((bf16[64,4096]{1,0:T(8,128)(2,1)S(1)}, bf16[64,4096]{1,0:T(8,128)(2,1)S(1)}, u32[]{:S(2)}, u32[]{:S(2)}) %collective-permute-start.51) | collective-permute-done | bytes 524320 | tf_op jit(solution)/shard_map/ppermute | solution.py:31
  225.4 9.6 %head_terms.2 = f32[8,256]{1,0:T(8,128)S(1)} custom-call(bf16[64,4096]{1,0:T(8,128)(2,1)S(1)} %pad_maximum_fusion.refs_0_, bf16[64,4096]{1,0:T(8,128)(2,1)S(1)} %collective-permute-done.28.refs_1_.refs_0_, bf16[64,4096]{1,0:T(8,128)(2,1)S(1)} %collective-permute-done.29.refs_2_.refs_1_, bf16[32,4096]{1,0:T(8,128)(2,1)S(1)} %collective-permute-done.30.refs_3_.refs_9_, ...), custom_call_target="tpu_custom_call" | custom-call | flops 4194304000 | bytes 18481152 | tf_op jit(solution)/shard_map/head_terms/pallas_call | solution.py:380
  235.2 12.9 %head_terms.3 = f32[8,256]{1,0:T(8,128)S(1)} custom-call(bf16[64,4096]{1,0:T(8,128)(2,1)S(1)} %pad_maximum_fusion.1.refs_0_, bf16[64,4096]{1,0:T(8,128)(2,1)S(1)} %collective-permute-done.50.refs_1_, bf16[64,4096]{1,0:T(8,128)(2,1)S(1)} %collective-permute-done.51.refs_2_, bf16[32,4096]{1,0:T(8,128)(2,1)} %collective-permute-done.52.refs_3_, ...), custom_call_target="tpu_custom_call" | custom-call | flops 4194304000 | bytes 18481152 | tf_op jit(solution)/shard_map/head_terms/pallas_call | solution.py:380
  (185 shorter events, 98.9 us)
Async XLA Ops:
  5.6 15.0 %collective-permute-start.1 = (bf16[80,1024]{1,0:T(8,128)(2,1)S(1)}, bf16[80,1024]{1,0:T(8,128)(2,1)S(1)}, u32[]{:S(2)}, u32[]{:S(2)}) collective-permute-start(bf16[80,1024]{1,0:T(8,128)(2,1)S(1)} %fusion.1.refs_0_.refs_4_.refs_5_), channel_id=1, source_target_pairs={{0,2},{1,3},{2,0},{3,1},{4,6},{5,7},{6,4},{7,5},{8,10},{9,11},{10,... | collective-permute-start | bytes 491528 | tf_op jit(solution)/shard_map/ppermute | solution.py:31
  8.2 12.5 %collective-permute-start.2 = (bf16[80,1024]{1,0:T(8,128)(2,1)S(1)}, bf16[80,1024]{1,0:T(8,128)(2,1)S(1)}, u32[]{:S(2)}, u32[]{:S(2)}) collective-permute-start(bf16[80,1024]{1,0:T(8,128)(2,1)S(1)} %fusion.1.refs_0_.refs_4_.refs_5_), channel_id=1, source_target_pairs={{0,3},{1,2},{2,1},{3,0},{4,7},{5,6},{6,5},{7,4},{8,11},{9,10},{10,... | collective-permute-start | bytes 491528 | tf_op jit(solution)/shard_map/ppermute | solution.py:31
  21.2 11.6 %collective-permute-start.4 = (bf16[64,4224]{1,0:T(8,128)(2,1)S(1)}, bf16[64,4224]{1,0:T(8,128)(2,1)S(1)}, u32[]{:S(2)}, u32[]{:S(2)}) collective-permute-start(bf16[64,4224]{1,0:T(8,128)(2,1)S(1)} %get-tuple-element.30.refs_0_), channel_id=1, source_target_pairs={{0,8},{4,12},{8,0},{12,4},{1,9},{5,13},{9,1},{13,5},{2,10},{6,14},... | collective-permute-start | bytes 1622024 | tf_op jit(solution)/shard_map/ppermute | solution.py:31
  32.8 14.5 %collective-permute-start.7 = (bf16[64,4224]{1,0:T(8,128)(2,1)S(1)}, bf16[64,4224]{1,0:T(8,128)(2,1)S(1)}, u32[]{:S(2)}, u32[]{:S(2)}) collective-permute-start(bf16[64,4224]{1,0:T(8,128)(2,1)S(1)} %get-tuple-element.30.refs_0_), channel_id=1, source_target_pairs={{0,16},{16,0},{1,17},{17,1},{2,18},{18,2},{3,19},{19,3},{4,20},{20... | collective-permute-start | bytes 1622024 | tf_op jit(solution)/shard_map/ppermute | solution.py:31
  35.5 12.4 %collective-permute-start.8 = (bf16[64,4224]{1,0:T(8,128)(2,1)S(1)}, bf16[64,4224]{1,0:T(8,128)(2,1)S(1)}, u32[]{:S(2)}, u32[]{:S(2)}) collective-permute-start(bf16[64,4224]{1,0:T(8,128)(2,1)S(1)} %collective-permute-done.3.refs_1_), channel_id=1, source_target_pairs={{0,16},{16,0},{1,17},{17,1},{2,18},{18,2},{3,19},{19,3},{4,20},{20... | collective-permute-start | bytes 1622024 | tf_op jit(solution)/shard_map/ppermute | solution.py:31
  47.4 21.3 %collective-permute-start.15 = (bf16[64,4224]{1,0:T(8,128)(2,1)S(1)}, bf16[64,4224]{1,0:T(8,128)(2,1)S(1)}, u32[]{:S(2)}, u32[]{:S(2)}) collective-permute-start(bf16[64,4224]{1,0:T(8,128)(2,1)S(1)} %get-tuple-element.32.refs_0_), channel_id=1, source_target_pairs={{0,4},{4,0},{8,12},{12,8},{1,5},{5,1},{9,13},{13,9},{2,6},{6,2},{1... | collective-permute-start | bytes 1622024 | tf_op jit(solution)/shard_map/ppermute | solution.py:31
  48.0 20.7 %collective-permute-start.16 = (bf16[64,4224]{1,0:T(8,128)(2,1)S(1)}, bf16[64,4224]{1,0:T(8,128)(2,1)S(1)}, u32[]{:S(2)}, u32[]{:S(2)}) collective-permute-start(bf16[64,4224]{1,0:T(8,128)(2,1)S(1)} %get-tuple-element.32.refs_0_), channel_id=1, source_target_pairs={{0,8},{4,12},{8,0},{12,4},{1,9},{5,13},{9,1},{13,5},{2,10},{6,14},... | collective-permute-start | bytes 1622024 | tf_op jit(solution)/shard_map/ppermute | solution.py:31
  76.6 13.3 %collective-permute-start.34 = (bf16[64,4224]{1,0:T(8,128)(2,1)S(1)}, bf16[64,4224]{1,0:T(8,128)(2,1)S(1)}, u32[]{:S(2)}, u32[]{:S(2)}) collective-permute-start(bf16[64,4224]{1,0:T(8,128)(2,1)S(1)} %get-tuple-element.32.refs_0_), channel_id=1, source_target_pairs={{0,16},{16,0},{1,17},{17,1},{2,18},{18,2},{3,19},{19,3},{4,20},{20... | collective-permute-start | bytes 1622024 | tf_op jit(solution)/shard_map/ppermute | solution.py:31
  76.6 15.4 %collective-permute-start.35 = (bf16[64,4224]{1,0:T(8,128)(2,1)S(1)}, bf16[64,4224]{1,0:T(8,128)(2,1)S(1)}, u32[]{:S(2)}, u32[]{:S(2)}) collective-permute-start(bf16[64,4224]{1,0:T(8,128)(2,1)S(1)} %collective-permute-done.15.refs_2_.refs_1_), channel_id=1, source_target_pairs={{0,16},{16,0},{1,17},{17,1},{2,18},{18,2},{3,19},{19,3},{4,20},{20... | collective-permute-start | bytes 1622024 | tf_op jit(solution)/shard_map/ppermute | solution.py:31
  89.9 13.9 %collective-permute-start.18 = (bf16[64,4096]{1,0:T(8,128)(2,1)S(1)}, bf16[64,4096]{1,0:T(8,128)(2,1)S(1)}, u32[]{:S(2)}, u32[]{:S(2)}) collective-permute-start(bf16[64,4096]{1,0:T(8,128)(2,1)S(1)} %get-tuple-element.34.refs_12_), channel_id=1, source_target_pairs={{0,4},{4,0},{8,12},{12,8},{1,5},{5,1},{9,13},{13,9},{2,6},{6,2},{1... | collective-permute-start | bytes 1572872 | tf_op jit(solution)/shard_map/ppermute | solution.py:31
  91.2 13.5 %collective-permute-start.19 = (bf16[64,4096]{1,0:T(8,128)(2,1)S(1)}, bf16[64,4096]{1,0:T(8,128)(2,1)S(1)}, u32[]{:S(2)}, u32[]{:S(2)}) collective-permute-start(bf16[64,4096]{1,0:T(8,128)(2,1)S(1)} %get-tuple-element.35.refs_13_), channel_id=1, source_target_pairs={{0,8},{4,12},{8,0},{12,4},{1,9},{5,13},{9,1},{13,5},{2,10},{6,14},... | collective-permute-start | bytes 1572872 | tf_op jit(solution)/shard_map/ppermute | solution.py:31
  124.7 26.4 %collective-permute-start.39 = (bf16[256,4096]{1,0:T(8,128)(2,1)S(1)}, bf16[256,4096]{1,0:T(8,128)(2,1)S(1)}, u32[]{:S(2)}, u32[]{:S(2)}) collective-permute-start(bf16[256,4096]{1,0:T(8,128)(2,1)S(1)} %down_rows.7), channel_id=1, source_target_pairs={{0,16},{16,0},{1,17},{17,1},{2,18},{18,2},{3,19},{19,3},{4,20},{20... | collective-permute-start | bytes 6291464 | tf_op jit(solution)/shard_map/ppermute | solution.py:31
  126.5 12.9 %collective-permute-start.23 = (bf16[16,4096]{1,0:T(8,128)(2,1)S(1)}, bf16[16,4096]{1,0:T(8,128)(2,1)S(1)}, u32[]{:S(2)}, u32[]{:S(2)}) collective-permute-start(bf16[16,4096]{1,0:T(8,128)(2,1)S(1)} %get-tuple-element.41.refs_14_), channel_id=1, source_target_pairs={{0,2},{1,3},{2,0},{3,1},{4,6},{5,7},{6,4},{7,5},{8,10},{9,11},{10,... | collective-permute-start | bytes 393224 | tf_op jit(solution)/shard_map/ppermute | solution.py:31
  127.7 11.6 %collective-permute-start.24 = (bf16[16,4096]{1,0:T(8,128)(2,1)S(1)}, bf16[16,4096]{1,0:T(8,128)(2,1)S(1)}, u32[]{:S(2)}, u32[]{:S(2)}) collective-permute-start(bf16[16,4096]{1,0:T(8,128)(2,1)S(1)} %get-tuple-element.42.refs_15_), channel_id=1, source_target_pairs={{0,3},{1,2},{2,1},{3,0},{4,7},{5,6},{6,5},{7,4},{8,11},{9,10},{10,... | collective-permute-start | bytes 393224 | tf_op jit(solution)/shard_map/ppermute | solution.py:31
  140.7 12.6 %collective-permute-start.25 = (bf16[16,4096]{1,0:T(8,128)(2,1)S(1)}, bf16[16,4096]{1,0:T(8,128)(2,1)S(1)}, u32[]{:S(2)}, u32[]{:S(2)}) collective-permute-start(bf16[16,4096]{1,0:T(8,128)(2,1)S(1)} %final_rows.2.refs_4_), channel_id=1, source_target_pairs={{0,1},{1,0},{2,3},{3,2},{4,5},{5,4},{6,7},{7,6},{8,9},{9,8},{10,11... | collective-permute-start | bytes 393224 | tf_op jit(solution)/shard_map/ppermute | solution.py:31
  143.4 12.4 %collective-permute-start.26 = (bf16[16,4096]{1,0:T(8,128)(2,1)S(1)}, bf16[16,4096]{1,0:T(8,128)(2,1)S(1)}, u32[]{:S(2)}, u32[]{:S(2)}) collective-permute-start(bf16[16,4096]{1,0:T(8,128)(2,1)S(1)} %final_rows.2.refs_4_), channel_id=1, source_target_pairs={{0,2},{1,3},{2,0},{3,1},{4,6},{5,7},{6,4},{7,5},{8,10},{9,11},{10,... | collective-permute-start | bytes 393224 | tf_op jit(solution)/shard_map/ppermute | solution.py:31
  151.6 14.9 %collective-permute-start.40 = (bf16[64,4096]{1,0:T(8,128)(2,1)S(1)}, bf16[64,4096]{1,0:T(8,128)(2,1)S(1)}, u32[]{:S(2)}, u32[]{:S(2)}) collective-permute-start(bf16[64,4096]{1,0:T(8,128)(2,1)S(1)} %get-tuple-element.45), channel_id=1, source_target_pairs={{0,4},{4,0},{8,12},{12,8},{1,5},{5,1},{9,13},{13,9},{2,6},{6,2},{1... | collective-permute-start | bytes 1572872 | tf_op jit(solution)/shard_map/ppermute | solution.py:31
  152.4 14.9 %collective-permute-start.41 = (bf16[64,4096]{1,0:T(8,128)(2,1)S(1)}, bf16[64,4096]{1,0:T(8,128)(2,1)S(1)}, u32[]{:S(2)}, u32[]{:S(2)}) collective-permute-start(bf16[64,4096]{1,0:T(8,128)(2,1)S(1)} %get-tuple-element.46), channel_id=1, source_target_pairs={{0,8},{4,12},{8,0},{12,4},{1,9},{5,13},{9,1},{13,5},{2,10},{6,14},... | collective-permute-start | bytes 1572872 | tf_op jit(solution)/shard_map/ppermute | solution.py:31
  155.8 22.6 %collective-permute-start.29 = (bf16[64,4096]{1,0:T(8,128)(2,1)S(1)}, bf16[64,4096]{1,0:T(8,128)(2,1)S(1)}, u32[]{:S(2)}, u32[]{:S(2)}) collective-permute-start(bf16[64,4096]{1,0:T(8,128)(2,1)S(1)} %pad_maximum_fusion.refs_0_), channel_id=1, source_target_pairs={{0,8},{4,12},{8,0},{12,4},{1,9},{5,13},{9,1},{13,5},{2,10},{6,14},... | collective-permute-start | bytes 1572872 | tf_op jit(solution)/shard_map/ppermute | solution.py:31
  156.4 23.5 %collective-permute-start.28 = (bf16[64,4096]{1,0:T(8,128)(2,1)S(1)}, bf16[64,4096]{1,0:T(8,128)(2,1)S(1)}, u32[]{:S(2)}, u32[]{:S(2)}) collective-permute-start(bf16[64,4096]{1,0:T(8,128)(2,1)S(1)} %pad_maximum_fusion.refs_0_), channel_id=1, source_target_pairs={{0,4},{4,0},{8,12},{12,8},{1,5},{5,1},{9,13},{13,9},{2,6},{6,2},{1... | collective-permute-start | bytes 1572872 | tf_op jit(solution)/shard_map/ppermute | solution.py:31
  167.3 16.1 %collective-permute-start.42 = (bf16[32,4096]{1,0:T(8,128)(2,1)S(1)}, bf16[32,4096]{1,0:T(8,128)(2,1)S(1)}, u32[]{:S(2)}, u32[]{:S(2)}) collective-permute-start(bf16[32,4096]{1,0:T(8,128)(2,1)S(1)} %get-tuple-element.48), channel_id=1, source_target_pairs={{0,4},{4,0},{8,12},{12,8},{1,5},{5,1},{9,13},{13,9},{2,6},{6,2},{1... | collective-permute-start | bytes 786440 | tf_op jit(solution)/shard_map/ppermute | solution.py:31
  168.7 15.4 %collective-permute-start.43 = (bf16[32,4096]{1,0:T(8,128)(2,1)S(1)}, bf16[32,4096]{1,0:T(8,128)(2,1)S(1)}, u32[]{:S(2)}, u32[]{:S(2)}) collective-permute-start(bf16[32,4096]{1,0:T(8,128)(2,1)S(1)} %get-tuple-element.49), channel_id=1, source_target_pairs={{0,8},{4,12},{8,0},{12,4},{1,9},{5,13},{9,1},{13,5},{2,10},{6,14},... | collective-permute-start | bytes 786440 | tf_op jit(solution)/shard_map/ppermute | solution.py:31
  222.1 13.1 %collective-permute-start.52 = (bf16[32,4096]{1,0:T(8,128)(2,1)}, bf16[32,4096]{1,0:T(8,128)(2,1)}, u32[]{:S(2)}, u32[]{:S(2)}) collective-permute-start(bf16[32,4096]{1,0:T(8,128)(2,1)} %slice.176), channel_id=1, source_target_pairs={{0,4},{4,0},{8,12},{12,8},{1,5},{5,1},{9,13},{13,9},{2,6},{6,2},{1... | collective-permute-start | bytes 786440 | tf_op jit(solution)/shard_map/ppermute | solution.py:31
  223.5 11.7 %collective-permute-start.53 = (bf16[32,4096]{1,0:T(8,128)(2,1)}, bf16[32,4096]{1,0:T(8,128)(2,1)}, u32[]{:S(2)}, u32[]{:S(2)}) collective-permute-start(bf16[32,4096]{1,0:T(8,128)(2,1)} %slice.177), channel_id=1, source_target_pairs={{0,8},{4,12},{8,0},{12,4},{1,9},{5,13},{9,1},{13,5},{2,10},{6,14},... | collective-permute-start | bytes 786440 | tf_op jit(solution)/shard_map/ppermute | solution.py:31
  (43 other events, 420.6 us)

commit v6 on v5

--- a/solution.py
+++ b/solution.py
@@ -35,15 +35,60 @@
     return [x] + [swap(x, axis, d) for d in range(1, lax.axis_size(axis))]
 
 
-def gather_plane(x, axis):
+def gather_plane(x, axis, after):
     if lax.axis_size(axis) != 4:
         return gather_near(x, axis)
     half = x.shape[0] // 2
     one, two = swap(x, axis, 1), swap(x, axis, 2)
-    return [x, one, two, swap(two[:half], axis, 1), swap(one[half:], axis, 2)]
-
-
-def load_pieces(piece_refs, scratch, sems):
+    upper, lower = move_rows([two, one], [(0, 0, half, 0, 0), (1, half, half, 1, 0)], after)
+    return [x, one, two, swap(upper, axis, 1), swap(lower, axis, 2)]
+
+
+def move_kernel(sources, targets, moves, *refs):
+    out_refs, sems = refs[-targets - 1 : -1], refs[-1]
+    copies = []
+    for i, (source, start, count, target, place) in enumerate(moves):
+        copies.append(
+            pltpu.make_async_copy(
+                refs[source].at[pl.ds(start, count), :],
+                out_refs[target].at[pl.ds(place, count), :],
+                sems.at[i],
+            )
+        )
+    for copy in copies:
+        copy.start()
+    for copy in copies:
+        copy.wait()
+
+
+def move_rows(arrays, moves, after):
+    targets = 1 + max(m[3] for m in moves)
+    sizes = [sum(m[2] for m in moves if m[3] == t) for t in range(targets)]
+    size = sum(sizes) * arrays[0].shape[1]
+    return pl.pallas_call(
+        functools.partial(move_kernel, len(arrays), targets, moves),
+        out_shape=tuple(
+            jax.ShapeDtypeStruct((rows, arrays[0].shape[1]), arrays[0].dtype) for rows in sizes
+        ),
+        in_specs=[anywhere()] * (len(arrays) + len(after)),
+        out_specs=(anywhere(),) * targets,
+        scratch_shapes=[pltpu.SemaphoreType.DMA((len(moves),))],
+        compiler_params=params(MIB),
+        cost_estimate=pl.CostEstimate(flops=0, bytes_accessed=4 * size, transcendentals=0),
+        name="move_rows",
+    )(*arrays, *after)
+
+
+def stack_rows(arrays, after):
+    moves = []
+    place = 0
+    for i, x in enumerate(arrays):
+        moves.append((i, 0, x.shape[0], 0, place))
+        place += x.shape[0]
+    return move_rows(arrays, moves, after)[0]
+
+
+def load_pieces(piece_refs, scratch, sems, then):
     copies = []
     start = 0
     for i in range(len(piece_refs)):
@@ -54,6 +99,7 @@
         start += count
     for copy in copies:
         copy.start()
+    then()
     for copy in copies:
         copy.wait()
 
@@ -155,8 +201,7 @@
                 )
             )
 
-    fetch(0, lambda copy: copy.start())
-    load_pieces(piece_refs, rows_scr, sems)
+    load_pieces(piece_refs, rows_scr, sems, lambda: fetch(0, lambda copy: copy.start()))
     small = rows_scr[:, full_width:].astype(jnp.float32)
     lane = lax.broadcasted_iota(jnp.int32, small.shape, 1)
     start = lax.axis_index("expert") * 3
@@ -342,13 +387,13 @@
                     sems.at[len(copies)],
                 )
             )
+    for copy in copies:
+        copy.start()
     fetch(0).start()
     for copy in copies:
-        copy.start()
+        copy.wait()
     for i in range(1, steps):
         fetch(i).start()
-    for copy in copies:
-        copy.wait()
     lane = lax.broadcasted_iota(jnp.int32, out_ref.shape, 0)
     out_ref[...] = jnp.where(lane == 0, -jnp.inf, 0.0)
     targets = target_ref[...] - (my_expert * n_tensor + my_tensor) * vocab_part
@@ -465,7 +510,7 @@
     )(*inputs, *after)
 
 
-def sum_plane(kept, got, rows, after_pass, after_total):
+def sum_plane(kept, got, rows, after_pass):
     f32, b16 = jnp.float32, jnp.bfloat16
     n_tensor = lax.axis_size("tensor")
     count, full_width = kept.shape[0] // rows, kept.shape[1]
@@ -497,7 +542,7 @@
             functools.partial(total_kernel, n_tensor),
             "total",
             [home, from_one, from_two, last_one, last_two],
-            after_total,
+            [],
             [((sub, full_width), b16)] * n_tensor,
             [pltpu.VMEM((rows, full_width), f32)],
             8 * MIB,
@@ -541,7 +586,7 @@
         )
         if block:
             slices = gather_near(block[0], "tensor")
-        plane = gather_plane(normed, "expert")
+        plane = gather_plane(normed, "expert", [])
         planes.append(plane)
         raws.append(raw)
         after = plane[3:]
@@ -551,49 +596,59 @@
     head_rows = pltpu.with_memory_space_constraint(head_weight.T, pltpu.HBM)
     target_rows = targets.reshape(n_expert, n_tensor, splits, sub)
     terms = []
-    steps = {}
+    before = {}
     for h in range(splits):
-        later = planes[h + 1][1:3] if h + 1 < splits else []
-        away = [swap(p, "seq", 1) for p in planes[h]]
+        far = planes[h][3:]
+        if before and len(far) == 2:
+            far = [stack_rows(far, before["kept"])]
+        away = [swap(p, "seq", 1) for p in planes[h][:3] + far]
         if 2 * n_expert * rows <= LARGEST:
             half = n_expert * rows
             everything = planes[h] + away
             tile = tile_of(w_gate)
             count = w_gate.shape[2] // tile
             cuts = [0, (count + 1) // 2, count - 1, count] if h else [0, count]
-            ties = [steps.get(key, []) for key in ("packed", "passed", "totals")]
+            ties = [before.get(key, []) for key in ("packed", "passed", "totals")]
             hidden = [
                 hidden_rows(
                     everything, w_gate, w_up, ties[i], cuts[i], cuts[i + 1] - cuts[i], tile
                 )
                 for i in range(len(cuts) - 1)
             ]
-            other = down_rows(hidden, w_down, half, half, later)
-            kept = down_rows(hidden, w_down, 0, half, steps.get("final", []))
+            later = planes[h + 1][1:3] if h + 1 < splits else []
+            other = down_rows(hidden, w_down, half, half, later + before.get("sums", []))
+            kept = down_rows(hidden, w_down, 0, half, before.get("final", []))
         else:
+            away = [swap(p, "seq", 1) for p in planes[h]]
             kept, other = many_rows(planes[h], w_gate, w_up, w_down), many_rows(
                 away, w_gate, w_up, w_down
             )
         got = swap(other, "seq", 1)
-        totals, packed, passed = sum_plane(
-            kept, got, rows, steps.get("column", []), steps.get("near", [])
-        )
-        mine = totals[:1] + [swap(totals[d], "tensor", d) for d in range(1, n_tensor)]
-        final = final_rows(mine, raws[h], gains, steps.get("far", []))
+        totals, packed, passed = sum_plane(kept, got, rows, before.get("column", []))
+        sums = [swap(totals[d], "tensor", d) for d in range(1, n_tensor)]
+        finals_near, finals_far = [], []
+        if before:
+            column = stack_rows([before["final"][0]] + before["column"], totals[:1])
+            plane = gather_plane(column, "expert", [])
+            finals_near, finals_far = plane[1:3], plane[3:]
+            wanted = target_rows[:, :, h - 1].reshape(1, -1)
+            terms.append(head_terms(plane, head_rows, wanted, sub))
+        final = final_rows(totals[:1] + sums, raws[h], gains, finals_near)
         column = gather_near(final, "tensor")
-        plane = gather_plane(jnp.concatenate(column, axis=0), "expert")
-        wanted = target_rows[:, :, h].reshape(1, -1)
-        term = head_terms(plane, head_rows, wanted, sub)
-        terms.append(term[:3].reshape(3, n_expert, n_tensor, sub))
-        steps = {
+        before = {
+            "kept": [kept],
             "packed": packed,
             "passed": passed,
             "totals": totals,
+            "sums": sums,
             "final": [final],
             "column": column[1:],
-            "near": plane[1:3],
-            "far": plane[3:],
         }
+    column = stack_rows(column, finals_far)
+    plane = gather_plane(column, "expert", terms[-1:])
+    wanted = target_rows[:, :, splits - 1].reshape(1, -1)
+    terms.append(head_terms(plane, head_rows, wanted, sub))
+    terms = [term[:3].reshape(3, n_expert, n_tensor, sub) for term in terms]
     terms = jnp.stack(terms, axis=3)
     joined = join_axis(terms, "tensor", 2, my_tensor)
     joined = join_axis(joined, "expert", 1, my_expert)

time: 265 us -> 241 us (0.909)
  waiting for transfers between devices: 95.8 us -> 74.3 us
  starting transfers between devices: 67.1 us -> 62.9 us
    ppermute x60 -> x59, waiting for transfers between devices: 95.8 us -> 74.3 us  [swap(): return lax.ppermute(x, axis, [(i, i ^ distance) for i in range(size)])]
    ppermute x60 -> x59, starting transfers between devices: 67.1 us -> 62.9 us  [swap(): return lax.ppermute(x, axis, [(i, i ^ distance) for i in range(size)])]
  transfers between devices with their start and end apart: 60 -> 59, of which waited for: 29 -> 28; matrix products, arithmetic and copies ran while one was open for 2% -> 1% of each run, Pallas kernels for 23% -> 29%
where the time goes in v6:
time: 241 us; the launch traced here: 240 us
  Pallas kernels  94.5 us (39%)
  waiting for transfers between devices  74.3 us (31%)
  starting transfers between devices  62.9 us (26%)
  local copies, waits for them, and re-layouts  6.14 us (3%)
    ppermute x59, waiting for transfers between devices, swap(): return lax.ppermute(x, axis, [(i, i ^ distance) for i in range(size)])  74.3 us
    ppermute x59, starting transfers between devices, swap(): return lax.ppermute(x, axis, [(i, i ^ distance) for i in range(size)])  62.9 us
    pallas_call x4, Pallas kernels, hidden_rows(): pl.pallas_call(functools.partial(hidden_kernel, len(pieces), len(after),...  45.2 us
    pallas_call x2, Pallas kernels, head_terms(): pl.pallas_call(functools.partial(head_kernel, len(pieces), tile, sub), ou...  21.5 us
    pallas_call x4, Pallas kernels, down_rows(): pl.pallas_call(functools.partial(down_kernel, start, len(hidden)), out_sh...  20.8 us
  transfers between devices with their start and end apart: 59, of which 28 were waited for; matrix products, arithmetic and copies ran while one was open for 1% of the time, Pallas kernels for 29%

profile of v6, /device:TPU:0, one launch (start us, length us, event | category | flops | bytes accessed | tf_op | source)
XLA Modules:
  0.0 240.5 jit_solution(1775973529248631764)
XLA Ops:
  2.5 3.1 %collective-permute-start = (bf16[80,1024]{1,0:T(8,128)(2,1)S(1)}, bf16[80,1024]{1,0:T(8,128)(2,1)S(1)}, u32[]{:S(2)}, u32[]{:S(2)}) collective-permute-start(bf16[80,1024]{1,0:T(8,128)(2,1)S(1)} %fusion.1.refs_0_.refs_4_.refs_5_), channel_id=1, source_target_pairs={{0,1},{1,0},{2,3},{3,2},{4,5},{5,4},{6,7},{7,6},{8,9},{9,8},{10,11... | collective-permute-start | bytes 491528 | tf_op jit(solution)/shard_map/ppermute | solution.py:31
  12.3 8.4 %collective-permute-done.1.refs_2_.refs_6_.refs_7_ = bf16[80,1024]{1,0:T(8,128)(2,1)S(1)} collective-permute-done((bf16[80,1024]{1,0:T(8,128)(2,1)S(1)}, bf16[80,1024]{1,0:T(8,128)(2,1)S(1)}, u32[]{:S(2)}, u32[]{:S(2)}) %collective-permute-start.1) | collective-permute-done | bytes 163872 | tf_op jit(solution)/shard_map/ppermute | solution.py:31
  24.3 2.6 %collective-permute-start.12 = (bf16[64,1024]{1,0:T(8,128)(2,1)S(1)}, bf16[64,1024]{1,0:T(8,128)(2,1)S(1)}, u32[]{:S(2)}, u32[]{:S(2)}) collective-permute-start(bf16[64,1024]{1,0:T(8,128)(2,1)S(1)} %get-tuple-element.41.refs_0_), channel_id=1, source_target_pairs={{0,1},{1,0},{2,3},{3,2},{4,5},{5,4},{6,7},{7,6},{8,9},{9,8},{10,11... | collective-permute-start | bytes 393224 | tf_op jit(solution)/shard_map/ppermute | solution.py:31
  29.4 3.4 %collective-permute-done.3.refs_1_ = bf16[64,4224]{1,0:T(8,128)(2,1)S(1)} collective-permute-done((bf16[64,4224]{1,0:T(8,128)(2,1)S(1)}, bf16[64,4224]{1,0:T(8,128)(2,1)S(1)}, u32[]{:S(2)}, u32[]{:S(2)}) %collective-permute-start.3) | collective-permute-done | bytes 540704 | tf_op jit(solution)/shard_map/ppermute | solution.py:31
  34.7 3.4 %collective-permute-done.13.refs_2_ = bf16[64,1024]{1,0:T(8,128)(2,1)S(1)} collective-permute-done((bf16[64,1024]{1,0:T(8,128)(2,1)S(1)}, bf16[64,1024]{1,0:T(8,128)(2,1)S(1)}, u32[]{:S(2)}, u32[]{:S(2)}) %collective-permute-start.13) | collective-permute-done | bytes 131104 | tf_op jit(solution)/shard_map/ppermute | solution.py:31
  38.6 3.2 %collective-permute-done.5.refs_3_.refs_10_ = bf16[32,4224]{1,0:T(8,128)(2,1)S(1)} collective-permute-done((bf16[32,4224]{1,0:T(8,128)(2,1)S(1)}, bf16[32,4224]{1,0:T(8,128)(2,1)S(1)}, u32[]{:S(2)}, u32[]{:S(2)}) %collective-permute-start.5) | collective-permute-done | bytes 270368 | tf_op jit(solution)/shard_map/ppermute | solution.py:31
  41.8 5.1 %collective-permute-done.6.refs_4_.refs_11_ = bf16[32,4224]{1,0:T(8,128)(2,1)S(1)} collective-permute-done((bf16[32,4224]{1,0:T(8,128)(2,1)S(1)}, bf16[32,4224]{1,0:T(8,128)(2,1)S(1)}, u32[]{:S(2)}, u32[]{:S(2)}) %collective-permute-start.6) | collective-permute-done | bytes 270368 | tf_op jit(solution)/shard_map/ppermute | solution.py:31
  48.5 20.4 %hidden_rows.4.refs_0_ = bf16[512,1792]{1,0:T(8,128)(2,1)S(1)} custom-call(bf16[64,4224]{1,0:T(8,128)(2,1)S(1)} %get-tuple-element.38.refs_0_, bf16[64,4224]{1,0:T(8,128)(2,1)S(1)} %collective-permute-done.3.refs_1_, bf16[64,4224]{1,0:T(8,128)(2,1)S(1)} %collective-permute-done.4.refs_0_.refs_2_, ...), custom_call_target="tpu_custom_call" | custom-call | flops 15032385536 | bytes 35389440 | tf_op jit(solution)/shard_map/hidden_rows/pallas_call | solution.py:238
  69.0 5.2 %down_rows.5 = bf16[256,4096]{1,0:T(8,128)(2,1)S(1)} custom-call(bf16[512,1792]{1,0:T(8,128)(2,1)S(1)} %hidden_rows.4.refs_0_, bf16[1,1792,4096]{2,1,0:T(8,128)(2,1)S(1)} %bitcast.38, bf16[64,4224]{1,0:T(8,128)(2,1)S(1)} %collective-permute-done.15.refs_2_.refs_1_, bf16[64,4224]{1,0:T(8,128)(2,1)S(1)} %collective-permute-done.16.refs_3_.refs_0_.refs_2_), custom_call_target="tpu_custom_call" | custom-call | flops 3758096384 | bytes 3014656 | tf_op jit(solution)/shard_map/down_rows/pallas_call | solution.py:282
  77.1 5.2 %down_rows.4.kept_ref.refs_2_ = bf16[256,4096]{1,0:T(8,128)(2,1)S(1)} custom-call(bf16[512,1792]{1,0:T(8,128)(2,1)S(1)} %hidden_rows.4.refs_0_, bf16[1,1792,4096]{2,1,0:T(8,128)(2,1)S(1)} %bitcast.38), custom_call_target="tpu_custom_call" | custom-call | flops 3758096384 | bytes 3014656 | tf_op jit(solution)/shard_map/down_rows/pallas_call | solution.py:282
  87.1 12.2 %hidden_rows.5.refs_0_ = bf16[512,1024]{1,0:T(8,128)(2,1)S(1)} custom-call(bf16[64,4224]{1,0:T(8,128)(2,1)S(1)} %get-tuple-element.42.refs_0_, bf16[64,4224]{1,0:T(8,128)(2,1)S(1)} %collective-permute-done.15.refs_2_.refs_1_, bf16[64,4224]{1,0:T(8,128)(2,1)S(1)} %collective-permute-done.16.refs_3_.refs_0_.refs_2_, ...), custom_call_target="tpu_custom_call" | custom-call | flops 8589934592 | bytes 22020096 | tf_op jit(solution)/shard_map/hidden_rows/pallas_call | solution.py:238
  102.5 7.5 %hidden_rows.6.refs_1_ = bf16[512,512]{1,0:T(8,128)(2,1)S(1)} custom-call(bf16[64,4224]{1,0:T(8,128)(2,1)S(1)} %get-tuple-element.42.refs_0_, bf16[64,4224]{1,0:T(8,128)(2,1)S(1)} %collective-permute-done.15.refs_2_.refs_1_, bf16[64,4224]{1,0:T(8,128)(2,1)S(1)} %collective-permute-done.16.refs_3_.refs_0_.refs_2_, ...), custom_call_target="tpu_custom_call" | custom-call | flops 4294967296 | bytes 13107200 | tf_op jit(solution)/shard_map/hidden_rows/pallas_call | solution.py:238
  114.8 5.1 %hidden_rows.7.refs_2_ = bf16[512,256]{1,0:T(8,128)(2,1)S(1)} custom-call(bf16[64,4224]{1,0:T(8,128)(2,1)S(1)} %get-tuple-element.42.refs_0_, bf16[64,4224]{1,0:T(8,128)(2,1)S(1)} %collective-permute-done.15.refs_2_.refs_1_, bf16[64,4224]{1,0:T(8,128)(2,1)S(1)} %collective-permute-done.16.refs_3_.refs_0_.refs_2_, ...), custom_call_target="tpu_custom_call" | custom-call | flops 2147483648 | bytes 8650752 | tf_op jit(solution)/shard_map/hidden_rows/pallas_call | solution.py:238
  120.0 3.8 %collective-permute-done.23.refs_2_.refs_5_ = bf16[16,4096]{1,0:T(8,128)(2,1)S(1)} collective-permute-done((bf16[16,4096]{1,0:T(8,128)(2,1)S(1)}, bf16[16,4096]{1,0:T(8,128)(2,1)S(1)}, u32[]{:S(2)}, u32[]{:S(2)}) %collective-permute-start.23) | collective-permute-done | bytes 131104 | tf_op jit(solution)/shard_map/ppermute | solution.py:31
  123.8 5.2 %down_rows.7 = bf16[256,4096]{1,0:T(8,128)(2,1)S(1)} custom-call(bf16[512,1024]{1,0:T(8,128)(2,1)S(1)} %hidden_rows.5.refs_0_, bf16[512,512]{1,0:T(8,128)(2,1)S(1)} %hidden_rows.6.refs_1_, bf16[512,256]{1,0:T(8,128)(2,1)S(1)} %hidden_rows.7.refs_2_, bf16[1,1792,4096]{2,1,0:T(8,128)(2,1)S(1)} %bitcast.38, ...), custom_call_target="tpu_custom_call" | custom-call | flops 3758096384 | bytes 3014656 | tf_op jit(solution)/shard_map/down_rows/pallas_call | solution.py:282
  130.4 5.2 %down_rows.6.kept_ref = bf16[256,4096]{1,0:T(8,128)(2,1)S(1)} custom-call(bf16[512,1024]{1,0:T(8,128)(2,1)S(1)} %hidden_rows.5.refs_0_, bf16[512,512]{1,0:T(8,128)(2,1)S(1)} %hidden_rows.6.refs_1_, bf16[512,256]{1,0:T(8,128)(2,1)S(1)} %hidden_rows.7.refs_2_, bf16[1,1792,4096]{2,1,0:T(8,128)(2,1)S(1)} %bitcast.38, bf16[16,4096]{1,0:T(8,128)(2,1)S(1)} %final_rows.2.refs_4_.refs_0_), custom_call_target="tpu_custom_call" | custom-call | flops 3758096384 | bytes 3014656 | tf_op jit(solution)/shard_map/down_rows/pallas_call | solution.py:282
  142.8 2.6 %collective-permute-done.25.refs_0_.refs_1_ = bf16[16,4096]{1,0:T(8,128)(2,1)S(1)} collective-permute-done((bf16[16,4096]{1,0:T(8,128)(2,1)S(1)}, bf16[16,4096]{1,0:T(8,128)(2,1)S(1)}, u32[]{:S(2)}, u32[]{:S(2)}) %collective-permute-start.25) | collective-permute-done | bytes 131104 | tf_op jit(solution)/shard_map/ppermute | solution.py:31
  145.5 7.8 %collective-permute-done.26.refs_1_.refs_2_ = bf16[16,4096]{1,0:T(8,128)(2,1)S(1)} collective-permute-done((bf16[16,4096]{1,0:T(8,128)(2,1)S(1)}, bf16[16,4096]{1,0:T(8,128)(2,1)S(1)}, u32[]{:S(2)}, u32[]{:S(2)}) %collective-permute-start.26) | collective-permute-done | bytes 131104 | tf_op jit(solution)/shard_map/ppermute | solution.py:31
  155.2 4.5 %collective-permute-done.37.last_one_ref = bf16[32,4096]{1,0:T(8,128)(2,1)S(1)} collective-permute-done((bf16[32,4096]{1,0:T(8,128)(2,1)S(1)}, bf16[32,4096]{1,0:T(8,128)(2,1)S(1)}, u32[]{:S(2)}, u32[]{:S(2)}) %collective-permute-start.37) | collective-permute-done | bytes 262176 | tf_op jit(solution)/shard_map/ppermute | solution.py:31
  169.0 3.4 %collective-permute-done.39.refs_1_.refs_9_ = bf16[64,4096]{1,0:T(8,128)(2,1)S(1)} collective-permute-done((bf16[64,4096]{1,0:T(8,128)(2,1)S(1)}, bf16[64,4096]{1,0:T(8,128)(2,1)S(1)}, u32[]{:S(2)}, u32[]{:S(2)}) %collective-permute-start.39) | collective-permute-done | bytes 524320 | tf_op jit(solution)/shard_map/ppermute | solution.py:31
  184.5 7.3 %collective-permute-done.47.refs_2_ = bf16[16,4096]{1,0:T(8,128)(2,1)S(1)} collective-permute-done((bf16[16,4096]{1,0:T(8,128)(2,1)S(1)}, bf16[16,4096]{1,0:T(8,128)(2,1)S(1)}, u32[]{:S(2)}, u32[]{:S(2)}) %collective-permute-start.47) | collective-permute-done | bytes 131104 | tf_op jit(solution)/shard_map/ppermute | solution.py:31
  196.6 10.7 %head_terms.2.refs_2_ = f32[8,256]{1,0:T(8,128)S(1)} custom-call(bf16[64,4096]{1,0:T(8,128)(2,1)S(1)} %move_rows.10.refs_0_, bf16[64,4096]{1,0:T(8,128)(2,1)S(1)} %collective-permute-done.39.refs_1_.refs_9_, bf16[64,4096]{1,0:T(8,128)(2,1)S(1)} %collective-permute-done.40.refs_0_.refs_2_.refs_10_, bf16[32,4096]{1,0:T(8,128)(2,1)S(1)} %copy-done.1, ...), custom_call_target="tpu_custom_call" | custom-call | flops 4194304000 | bytes 18481152 | tf_op jit(solution)/shard_map/head_terms/pallas_call | solution.py:425
  209.9 4.0 %collective-permute-done.51.refs_3_ = bf16[32,4096]{1,0:T(8,128)(2,1)S(1)} collective-permute-done((bf16[32,4096]{1,0:T(8,128)(2,1)S(1)}, bf16[32,4096]{1,0:T(8,128)(2,1)S(1)}, u32[]{:S(2)}, u32[]{:S(2)}) %collective-permute-start.51) | collective-permute-done | bytes 262176 | tf_op jit(solution)/shard_map/ppermute | solution.py:31
  215.3 10.7 %head_terms.3 = f32[8,256]{1,0:T(8,128)S(1)} custom-call(bf16[64,4096]{1,0:T(8,128)(2,1)S(1)} %move_rows.12.refs_0_, bf16[64,4096]{1,0:T(8,128)(2,1)S(1)} %collective-permute-done.49.refs_1_, bf16[64,4096]{1,0:T(8,128)(2,1)S(1)} %collective-permute-done.50.refs_0_.refs_2_, bf16[32,4096]{1,0:T(8,128)(2,1)S(1)} %collective-permute-done.51.refs_3_, ...), custom_call_target="tpu_custom_call" | custom-call | flops 4194304000 | bytes 18481152 | tf_op jit(solution)/shard_map/head_terms/pallas_call | solution.py:425
  (184 shorter events, 89.7 us)
Async XLA Ops:
  5.6 15.0 %collective-permute-start.1 = (bf16[80,1024]{1,0:T(8,128)(2,1)S(1)}, bf16[80,1024]{1,0:T(8,128)(2,1)S(1)}, u32[]{:S(2)}, u32[]{:S(2)}) collective-permute-start(bf16[80,1024]{1,0:T(8,128)(2,1)S(1)} %fusion.1.refs_0_.refs_4_.refs_5_), channel_id=1, source_target_pairs={{0,2},{1,3},{2,0},{3,1},{4,6},{5,7},{6,4},{7,5},{8,10},{9,11},{10,... | collective-permute-start | bytes 491528 | tf_op jit(solution)/shard_map/ppermute | solution.py:31
  8.2 12.5 %collective-permute-start.2 = (bf16[80,1024]{1,0:T(8,128)(2,1)S(1)}, bf16[80,1024]{1,0:T(8,128)(2,1)S(1)}, u32[]{:S(2)}, u32[]{:S(2)}) collective-permute-start(bf16[80,1024]{1,0:T(8,128)(2,1)S(1)} %fusion.1.refs_0_.refs_4_.refs_5_), channel_id=1, source_target_pairs={{0,3},{1,2},{2,1},{3,0},{4,7},{5,6},{6,5},{7,4},{8,11},{9,10},{10,... | collective-permute-start | bytes 491528 | tf_op jit(solution)/shard_map/ppermute | solution.py:31
  21.2 11.6 %collective-permute-start.3 = (bf16[64,4224]{1,0:T(8,128)(2,1)S(1)}, bf16[64,4224]{1,0:T(8,128)(2,1)S(1)}, u32[]{:S(2)}, u32[]{:S(2)}) collective-permute-start(bf16[64,4224]{1,0:T(8,128)(2,1)S(1)} %get-tuple-element.38.refs_0_), channel_id=1, source_target_pairs={{0,4},{4,0},{8,12},{12,8},{1,5},{5,1},{9,13},{13,9},{2,6},{6,2},{1... | collective-permute-start | bytes 1622024 | tf_op jit(solution)/shard_map/ppermute | solution.py:31
  22.7 11.3 %collective-permute-start.4 = (bf16[64,4224]{1,0:T(8,128)(2,1)S(1)}, bf16[64,4224]{1,0:T(8,128)(2,1)S(1)}, u32[]{:S(2)}, u32[]{:S(2)}) collective-permute-start(bf16[64,4224]{1,0:T(8,128)(2,1)S(1)} %get-tuple-element.38.refs_0_), channel_id=1, source_target_pairs={{0,8},{4,12},{8,0},{12,4},{1,9},{5,13},{9,1},{13,5},{2,10},{6,14},... | collective-permute-start | bytes 1622024 | tf_op jit(solution)/shard_map/ppermute | solution.py:31
  26.9 11.2 %collective-permute-start.13 = (bf16[64,1024]{1,0:T(8,128)(2,1)S(1)}, bf16[64,1024]{1,0:T(8,128)(2,1)S(1)}, u32[]{:S(2)}, u32[]{:S(2)}) collective-permute-start(bf16[64,1024]{1,0:T(8,128)(2,1)S(1)} %get-tuple-element.41.refs_0_), channel_id=1, source_target_pairs={{0,2},{1,3},{2,0},{3,1},{4,6},{5,7},{6,4},{7,5},{8,10},{9,11},{10,... | collective-permute-start | bytes 393224 | tf_op jit(solution)/shard_map/ppermute | solution.py:31
  32.8 14.5 %collective-permute-start.7 = (bf16[64,4224]{1,0:T(8,128)(2,1)S(1)}, bf16[64,4224]{1,0:T(8,128)(2,1)S(1)}, u32[]{:S(2)}, u32[]{:S(2)}) collective-permute-start(bf16[64,4224]{1,0:T(8,128)(2,1)S(1)} %get-tuple-element.38.refs_0_), channel_id=1, source_target_pairs={{0,16},{16,0},{1,17},{17,1},{2,18},{18,2},{3,19},{19,3},{4,20},{20... | collective-permute-start | bytes 1622024 | tf_op jit(solution)/shard_map/ppermute | solution.py:31
  34.7 13.3 %collective-permute-start.8 = (bf16[64,4224]{1,0:T(8,128)(2,1)S(1)}, bf16[64,4224]{1,0:T(8,128)(2,1)S(1)}, u32[]{:S(2)}, u32[]{:S(2)}) collective-permute-start(bf16[64,4224]{1,0:T(8,128)(2,1)S(1)} %collective-permute-done.3.refs_1_), channel_id=1, source_target_pairs={{0,16},{16,0},{1,17},{17,1},{2,18},{18,2},{3,19},{19,3},{4,20},{20... | collective-permute-start | bytes 1622024 | tf_op jit(solution)/shard_map/ppermute | solution.py:31
  47.4 21.6 %collective-permute-start.15 = (bf16[64,4224]{1,0:T(8,128)(2,1)S(1)}, bf16[64,4224]{1,0:T(8,128)(2,1)S(1)}, u32[]{:S(2)}, u32[]{:S(2)}) collective-permute-start(bf16[64,4224]{1,0:T(8,128)(2,1)S(1)} %get-tuple-element.42.refs_0_), channel_id=1, source_target_pairs={{0,4},{4,0},{8,12},{12,8},{1,5},{5,1},{9,13},{13,9},{2,6},{6,2},{1... | collective-permute-start | bytes 1622024 | tf_op jit(solution)/shard_map/ppermute | solution.py:31
  48.0 21.0 %collective-permute-start.16 = (bf16[64,4224]{1,0:T(8,128)(2,1)S(1)}, bf16[64,4224]{1,0:T(8,128)(2,1)S(1)}, u32[]{:S(2)}, u32[]{:S(2)}) collective-permute-start(bf16[64,4224]{1,0:T(8,128)(2,1)S(1)} %get-tuple-element.42.refs_0_), channel_id=1, source_target_pairs={{0,8},{4,12},{8,0},{12,4},{1,9},{5,13},{9,1},{13,5},{2,10},{6,14},... | collective-permute-start | bytes 1622024 | tf_op jit(solution)/shard_map/ppermute | solution.py:31
  74.7 11.5 %collective-permute-start.30 = (bf16[64,4224]{1,0:T(8,128)(2,1)S(1)}, bf16[64,4224]{1,0:T(8,128)(2,1)S(1)}, u32[]{:S(2)}, u32[]{:S(2)}) collective-permute-start(bf16[64,4224]{1,0:T(8,128)(2,1)S(1)} %get-tuple-element.42.refs_0_), channel_id=1, source_target_pairs={{0,16},{16,0},{1,17},{17,1},{2,18},{18,2},{3,19},{19,3},{4,20},{20... | collective-permute-start | bytes 1622024 | tf_op jit(solution)/shard_map/ppermute | solution.py:31
  84.8 14.5 %collective-permute-start.18 = (bf16[64,4096]{1,0:T(8,128)(2,1)S(1)}, bf16[64,4096]{1,0:T(8,128)(2,1)S(1)}, u32[]{:S(2)}, u32[]{:S(2)}) collective-permute-start(bf16[64,4096]{1,0:T(8,128)(2,1)S(1)} %get-tuple-element.44.refs_11_), channel_id=1, source_target_pairs={{0,4},{4,0},{8,12},{12,8},{1,5},{5,1},{9,13},{13,9},{2,6},{6,2},{1... | collective-permute-start | bytes 1572872 | tf_op jit(solution)/shard_map/ppermute | solution.py:31
  86.2 14.0 %collective-permute-start.19 = (bf16[64,4096]{1,0:T(8,128)(2,1)S(1)}, bf16[64,4096]{1,0:T(8,128)(2,1)S(1)}, u32[]{:S(2)}, u32[]{:S(2)}) collective-permute-start(bf16[64,4096]{1,0:T(8,128)(2,1)S(1)} %get-tuple-element.45.refs_12_), channel_id=1, source_target_pairs={{0,8},{4,12},{8,0},{12,4},{1,9},{5,13},{9,1},{13,5},{2,10},{6,14},... | collective-permute-start | bytes 1572872 | tf_op jit(solution)/shard_map/ppermute | solution.py:31
  111.9 11.9 %collective-permute-start.23 = (bf16[16,4096]{1,0:T(8,128)(2,1)S(1)}, bf16[16,4096]{1,0:T(8,128)(2,1)S(1)}, u32[]{:S(2)}, u32[]{:S(2)}) collective-permute-start(bf16[16,4096]{1,0:T(8,128)(2,1)S(1)} %get-tuple-element.51.refs_13_), channel_id=1, source_target_pairs={{0,2},{1,3},{2,0},{3,1},{4,6},{5,7},{6,4},{7,5},{8,10},{9,11},{10,... | collective-permute-start | bytes 393224 | tf_op jit(solution)/shard_map/ppermute | solution.py:31
  136.1 17.2 %collective-permute-start.35 = (bf16[64,4096]{1,0:T(8,128)(2,1)S(1)}, bf16[64,4096]{1,0:T(8,128)(2,1)S(1)}, u32[]{:S(2)}, u32[]{:S(2)}) collective-permute-start(bf16[64,4096]{1,0:T(8,128)(2,1)S(1)} %get-tuple-element.57), channel_id=1, source_target_pairs={{0,4},{4,0},{8,12},{12,8},{1,5},{5,1},{9,13},{13,9},{2,6},{6,2},{1... | collective-permute-start | bytes 1572872 | tf_op jit(solution)/shard_map/ppermute | solution.py:31
  137.1 16.2 %collective-permute-start.36 = (bf16[64,4096]{1,0:T(8,128)(2,1)S(1)}, bf16[64,4096]{1,0:T(8,128)(2,1)S(1)}, u32[]{:S(2)}, u32[]{:S(2)}) collective-permute-start(bf16[64,4096]{1,0:T(8,128)(2,1)S(1)} %get-tuple-element.58), channel_id=1, source_target_pairs={{0,8},{4,12},{8,0},{12,4},{1,9},{5,13},{9,1},{13,5},{2,10},{6,14},... | collective-permute-start | bytes 1572872 | tf_op jit(solution)/shard_map/ppermute | solution.py:31
  140.3 12.9 %collective-permute-start.26 = (bf16[16,4096]{1,0:T(8,128)(2,1)S(1)}, bf16[16,4096]{1,0:T(8,128)(2,1)S(1)}, u32[]{:S(2)}, u32[]{:S(2)}) collective-permute-start(bf16[16,4096]{1,0:T(8,128)(2,1)S(1)} %final_rows.2.refs_4_.refs_0_), channel_id=1, source_target_pairs={{0,2},{1,3},{2,0},{3,1},{4,6},{5,7},{6,4},{7,5},{8,10},{9,11},{10,... | collective-permute-start | bytes 393224 | tf_op jit(solution)/shard_map/ppermute | solution.py:31
  141.4 11.9 %collective-permute-start.27 = (bf16[16,4096]{1,0:T(8,128)(2,1)S(1)}, bf16[16,4096]{1,0:T(8,128)(2,1)S(1)}, u32[]{:S(2)}, u32[]{:S(2)}) collective-permute-start(bf16[16,4096]{1,0:T(8,128)(2,1)S(1)} %final_rows.2.refs_4_.refs_0_), channel_id=1, source_target_pairs={{0,3},{1,2},{2,1},{3,0},{4,7},{5,6},{6,5},{7,4},{8,11},{9,10},{10,... | collective-permute-start | bytes 393224 | tf_op jit(solution)/shard_map/ppermute | solution.py:31
  162.9 11.7 %collective-permute-start.40 = (bf16[64,4096]{1,0:T(8,128)(2,1)S(1)}, bf16[64,4096]{1,0:T(8,128)(2,1)S(1)}, u32[]{:S(2)}, u32[]{:S(2)}) collective-permute-start(bf16[64,4096]{1,0:T(8,128)(2,1)S(1)} %move_rows.10.refs_0_), channel_id=1, source_target_pairs={{0,8},{4,12},{8,0},{12,4},{1,9},{5,13},{9,1},{13,5},{2,10},{6,14},... | collective-permute-start | bytes 1572872 | tf_op jit(solution)/shard_map/ppermute | solution.py:31
  163.7 12.3 %collective-permute-start.43 = (bf16[16,4096]{1,0:T(8,128)(2,1)S(1)}, bf16[16,4096]{1,0:T(8,128)(2,1)S(1)}, u32[]{:S(2)}, u32[]{:S(2)}) collective-permute-start(bf16[16,4096]{1,0:T(8,128)(2,1)S(1)} %get-tuple-element.65), channel_id=1, source_target_pairs={{0,1},{1,0},{2,3},{3,2},{4,5},{5,4},{6,7},{7,6},{8,9},{9,8},{10,11... | collective-permute-start | bytes 393224 | tf_op jit(solution)/shard_map/ppermute | solution.py:31
  174.7 17.1 %collective-permute-start.41 = (bf16[32,4096]{1,0:T(8,128)(2,1)S(1)}, bf16[32,4096]{1,0:T(8,128)(2,1)S(1)}, u32[]{:S(2)}, u32[]{:S(2)}) collective-permute-start(bf16[32,4096]{1,0:T(8,128)(2,1)S(1)} %get-tuple-element.63), channel_id=1, source_target_pairs={{0,4},{4,0},{8,12},{12,8},{1,5},{5,1},{9,13},{13,9},{2,6},{6,2},{1... | collective-permute-start | bytes 786440 | tf_op jit(solution)/shard_map/ppermute | solution.py:31
  175.0 16.8 %collective-permute-start.42 = (bf16[32,4096]{1,0:T(8,128)(2,1)S(1)}, bf16[32,4096]{1,0:T(8,128)(2,1)S(1)}, u32[]{:S(2)}, u32[]{:S(2)}) collective-permute-start(bf16[32,4096]{1,0:T(8,128)(2,1)S(1)} %get-tuple-element.64), channel_id=1, source_target_pairs={{0,8},{4,12},{8,0},{12,4},{1,9},{5,13},{9,1},{13,5},{2,10},{6,14},... | collective-permute-start | bytes 786440 | tf_op jit(solution)/shard_map/ppermute | solution.py:31
  180.1 11.6 %collective-permute-start.47 = (bf16[16,4096]{1,0:T(8,128)(2,1)S(1)}, bf16[16,4096]{1,0:T(8,128)(2,1)S(1)}, u32[]{:S(2)}, u32[]{:S(2)}) collective-permute-start(bf16[16,4096]{1,0:T(8,128)(2,1)S(1)} %final_rows.3.refs_0_), channel_id=1, source_target_pairs={{0,2},{1,3},{2,0},{3,1},{4,6},{5,7},{6,4},{7,5},{8,10},{9,11},{10,... | collective-permute-start | bytes 393224 | tf_op jit(solution)/shard_map/ppermute | solution.py:31
  192.5 14.8 %collective-permute-start.49 = (bf16[64,4096]{1,0:T(8,128)(2,1)S(1)}, bf16[64,4096]{1,0:T(8,128)(2,1)S(1)}, u32[]{:S(2)}, u32[]{:S(2)}) collective-permute-start(bf16[64,4096]{1,0:T(8,128)(2,1)S(1)} %move_rows.12.refs_0_), channel_id=1, source_target_pairs={{0,4},{4,0},{8,12},{12,8},{1,5},{5,1},{9,13},{13,9},{2,6},{6,2},{1... | collective-permute-start | bytes 1572872 | tf_op jit(solution)/shard_map/ppermute | solution.py:31
  193.8 13.6 %collective-permute-start.50 = (bf16[64,4096]{1,0:T(8,128)(2,1)S(1)}, bf16[64,4096]{1,0:T(8,128)(2,1)S(1)}, u32[]{:S(2)}, u32[]{:S(2)}) collective-permute-start(bf16[64,4096]{1,0:T(8,128)(2,1)S(1)} %move_rows.12.refs_0_), channel_id=1, source_target_pairs={{0,8},{4,12},{8,0},{12,4},{1,9},{5,13},{9,1},{13,5},{2,10},{6,14},... | collective-permute-start | bytes 1572872 | tf_op jit(solution)/shard_map/ppermute | solution.py:31
  (44 other events, 366.3 us)

commit v7 on v6

--- a/solution.py
+++ b/solution.py
@@ -37,11 +37,11 @@
 
 def gather_plane(x, axis, after):
     if lax.axis_size(axis) != 4:
-        return gather_near(x, axis)
+        return gather_near(x, axis), []
     half = x.shape[0] // 2
     one, two = swap(x, axis, 1), swap(x, axis, 2)
     upper, lower = move_rows([two, one], [(0, 0, half, 0, 0), (1, half, half, 1, 0)], after)
-    return [x, one, two, swap(upper, axis, 1), swap(lower, axis, 2)]
+    return [x, one, two, swap(upper, axis, 1), swap(lower, axis, 2)], [upper, lower]
 
 
 def move_kernel(sources, targets, moves, *refs):
@@ -88,7 +88,7 @@
     return move_rows(arrays, moves, after)[0]
 
 
-def load_pieces(piece_refs, scratch, sems, then):
+def load_pieces(piece_refs, scratch, sems):
     copies = []
     start = 0
     for i in range(len(piece_refs)):
@@ -99,34 +99,51 @@
         start += count
     for copy in copies:
         copy.start()
-    then()
     for copy in copies:
         copy.wait()
 
 
-def split_three(x):
-    high = lax.reduce_precision(x, 8, 7)
-    middle = lax.reduce_precision(x - high, 8, 7)
-    return jnp.stack([high, middle, x - high - middle])
-
-
-def gain_row(ref, index):
-    tail = ref[ref.shape[0] - 16 :, :].astype(jnp.float32)
-    first = 3 * index
-    return tail[first : first + 1] + tail[first + 1 : first + 2] + tail[first + 2 : first + 3]
+def begin_kernel(count, tokens_ref, norm_ref, final_ref, *block_refs):
+    splits = len(block_refs)
+    own_rows = tokens_ref.shape[0] // (count * splits)
+    for i in range(count):
+        for h in range(splits):
+            start = (i * splits + h) * own_rows
+            block_refs[h][i * own_rows : (i + 1) * own_rows, :] = tokens_ref[
+                start : start + own_rows, :
+            ]
+    lines = []
+    for gain_ref in (norm_ref, final_ref):
+        gain = gain_ref[...]
+        high = gain.astype(jnp.bfloat16).astype(jnp.float32)
+        middle = (gain - high).astype(jnp.bfloat16).astype(jnp.float32)
+        lines += [high, middle, gain - high - middle]
+    lines.append(jnp.zeros((2, lines[0].shape[1]), jnp.float32))
+    block_refs[0][count * own_rows :, :] = jnp.concatenate(lines).astype(jnp.bfloat16)
+
+
+def begin(tokens, norm_gain, final_gain, count, splits):
+    rows, width = tokens.shape
+    sizes = [rows // splits + (0 if h else 8) for h in range(splits)]
+    return small_call(
+        functools.partial(begin_kernel, count),
+        "begin",
+        [tokens, norm_gain.reshape(1, width), final_gain.reshape(1, width)],
+        [],
+        [((size, width), jnp.bfloat16) for size in sizes],
+        [],
+        4 * MIB,
+    )
 
 
 def norm_kernel(splits, part, count, after, *refs):
-    slices, gains = refs[:count], refs[count : 2 * count]
-    routes_ref, weights_ref = refs[2 * count : 2 * count + 2]
-    rest = refs[2 * count + 2 + after :]
-    handing_on = len(rest) > 2
-    if handing_on:
-        next_ref, rows_ref, raw_ref, out_ref, sem = rest
-        copy = pltpu.make_async_copy(next_ref, out_ref, sem)
-        copy.start()
-    else:
-        rows_ref, raw_ref = rest
+    slices = refs[:count]
+    routes_ref, weights_ref = refs[count : count + 2]
+    rest = list(refs[count + 2 :])
+    gains_in = rest.pop(0) if part else None
+    rest = rest[after:]
+    rows_ref, raw_ref = rest[:2]
+    gains_ref = gains_in if part else rest[2]
     rows = rows_ref.shape[0]
     width = slices[0].shape[1]
     full_width = width * count
@@ -140,8 +157,12 @@
     start = pl.multiple_of(me * own_rows, own_rows)
     for d in range(count):
         columns = pl.ds(pl.multiple_of((me ^ d) * width, width), width)
+        if not part:
+            tail = slices[d][rows:, :].astype(jnp.float32)
+            gains_ref[0:1, columns] = tail[0:1] + tail[1:2] + tail[2:3]
+            gains_ref[1:2, columns] = tail[3:4] + tail[4:5] + tail[5:6]
         value = slices[d][:rows, :].astype(jnp.float32)
-        rows_ref[:, columns] = (value * scale * gain_row(gains[d], 0)).astype(jnp.bfloat16)
+        rows_ref[:, columns] = (value * scale * gains_ref[0:1, columns]).astype(jnp.bfloat16)
         raw_ref[:, columns] = slices[d][pl.ds(start, own_rows), :]
     lane = lax.broadcasted_iota(jnp.int32, (own_rows, LANES), 1)
     expert = lane // 3
@@ -157,36 +178,35 @@
         low = weight - high - middle
         value = jnp.where(kind == 0, high, jnp.where(kind == 1, middle, low))
         rows_ref[i * own_rows : (i + 1) * own_rows, full_width:] = value.astype(jnp.bfloat16)
-    if handing_on:
-        copy.wait()
-
-
-def norm_rows(slices, gains, routes, route_weights, splits, part, rows, after, following):
+
+
+def norm_rows(slices, gains, routes, route_weights, splits, part, rows, after):
     width = slices[0].shape[1]
     count = len(slices)
     full_width = width * count
+    gains = gains if part else []
+    made = [] if part else [jax.ShapeDtypeStruct((8, full_width), jnp.float32)]
     return pl.pallas_call(
         functools.partial(norm_kernel, splits, part, count, len(after)),
         out_shape=(
             jax.ShapeDtypeStruct((rows, full_width + LANES), jnp.bfloat16),
             jax.ShapeDtypeStruct((rows // count, full_width), jnp.bfloat16),
-        )
-        + tuple(jax.ShapeDtypeStruct(f.shape, f.dtype) for f in following),
-        in_specs=[whole()] * (2 * count + 2) + [anywhere()] * (len(after) + len(following)),
-        out_specs=(whole(), whole()) + (anywhere(),) * len(following),
-        scratch_shapes=[pltpu.SemaphoreType.DMA] * len(following),
+            *made,
+        ),
+        in_specs=[whole()] * (count + 2 + len(gains)) + [anywhere()] * len(after),
+        out_specs=(whole(),) * (2 + len(made)),
         compiler_params=params(6 * MIB),
         cost_estimate=pl.CostEstimate(
             flops=6 * rows * full_width, bytes_accessed=4 * rows * full_width, transcendentals=rows
         ),
         name="norm_rows",
-    )(*slices, *gains, routes, route_weights, *after, *following)
+    )(*slices, routes, route_weights, *gains, *after)
 
 
 def hidden_kernel(pieces, after, tile, first, steps, *refs):
     piece_refs = refs[:pieces]
     weight_refs = refs[pieces : pieces + 2]
-    out_ref, rows_scr, route_scr, weight_scr, sems, weight_sems = refs[pieces + 2 + after :]
+    out_ref, rows_scr, route_scr, weight_scr, work, sems, weight_sems = refs[pieces + 2 + after :]
     full_width = weight_scr.shape[2]
 
     def fetch(i, act):
@@ -201,29 +221,49 @@
                 )
             )
 
-    load_pieces(piece_refs, rows_scr, sems, lambda: fetch(0, lambda copy: copy.start()))
-    small = rows_scr[:, full_width:].astype(jnp.float32)
-    lane = lax.broadcasted_iota(jnp.int32, small.shape, 1)
-    start = lax.axis_index("expert") * 3
-    mine = (lane >= start) & (lane < start + 3)
-    weight = jnp.sum(jnp.where(mine, small, 0.0), axis=1, keepdims=True)
-    route_scr[...] = jnp.broadcast_to(0.5 * weight, route_scr.shape)
-
-    @pl.loop(0, steps)
-    def _(i):
-        fetch(i, lambda copy: copy.wait())
-
-        @pl.when(i + 1 < steps)
-        def _():
-            fetch(i + 1, lambda copy: copy.start())
-
+    def start(copy):
+        copy.start()
+
+    def wait(copy):
+        copy.wait()
+
+    def dots(i):
+        rows = rows_scr[:, :full_width]
         slot = lax.rem(i, 2)
-        rows = rows_scr[:, :full_width]
-        gate = jnp.dot(rows, weight_scr[0, slot], preferred_element_type=jnp.float32)
-        up = jnp.dot(rows, weight_scr[1, slot], preferred_element_type=jnp.float32)
+        for j in range(2):
+            work[j] = jnp.dot(rows, weight_scr[j, slot], preferred_element_type=jnp.float32)
+
+    def finish(i):
+        gate, up = work[0], work[1]
         hidden = gate * (1.0 + jnp.tanh(0.5 * gate)) * up * route_scr[:, :1]
         columns = pl.ds(pl.multiple_of(i * tile, tile), tile)
         out_ref[:, columns] = hidden.astype(jnp.bfloat16)
+
+    fetch(0, start)
+    load_pieces(piece_refs, rows_scr, sems)
+    small = rows_scr[:, full_width:].astype(jnp.float32)
+    lane = lax.broadcasted_iota(jnp.int32, small.shape, 1)
+    place = lax.axis_index("expert") * 3
+    mine = (lane >= place) & (lane < place + 3)
+    weight = jnp.sum(jnp.where(mine, small, 0.0), axis=1, keepdims=True)
+    route_scr[...] = jnp.broadcast_to(0.5 * weight, route_scr.shape)
+    fetch(0, wait)
+    if steps > 1:
+        fetch(1, start)
+    dots(0)
+
+    @pl.loop(1, steps)
+    def _(i):
+        fetch(i, wait)
+
+        @pl.when(i + 1 < steps)
+        def _():
+            fetch(i + 1, start)
+
+        finish(i - 1)
+        dots(i)
+
+    finish(steps - 1)
 
 
 def tile_of(weight):
@@ -244,6 +284,7 @@
             pltpu.VMEM((rows, full_width + LANES), jnp.bfloat16),
             pltpu.VMEM((rows, LANES), jnp.float32),
             pltpu.VMEM((2, 2, full_width, tile), jnp.bfloat16),
+            pltpu.VMEM((2, rows, tile), jnp.float32),
             pltpu.SemaphoreType.DMA((len(pieces),)),
             pltpu.SemaphoreType.DMA((2, 2)),
         ],
@@ -262,7 +303,7 @@
     full_width = out_ref.shape[1]
     tile = 512 if full_width % 512 == 0 else full_width
 
-    @pl.loop(0, full_width // tile)
+    @pl.loop(0, full_width // tile, unroll=True)
     def _(i):
         columns = pl.ds(pl.multiple_of(i * tile, tile), tile)
         out = None
@@ -308,17 +349,13 @@
     return jnp.concatenate(outs)
 
 
-def final_kernel(parts, gains_count, after, *refs):
-    part_refs, gain_refs = refs[: parts + 1], refs[parts + 1 : parts + 1 + gains_count]
-    out_ref, rows_scr, gains_scr, work, sems = refs[parts + 1 + gains_count + after :]
-    width = gains_scr.shape[2]
-    me = lax.axis_index("tensor")
+def final_kernel(parts, *refs):
+    part_refs = refs[: parts + 2]
+    out_ref, rows_scr, gains_scr, sems = refs[-4:]
+    targets = [rows_scr.at[i] for i in range(parts + 1)] + [gains_scr]
     copies = [
-        pltpu.make_async_copy(part_refs[i], rows_scr.at[i], sems.at[i]) for i in range(parts + 1)
+        pltpu.make_async_copy(part_refs[i], targets[i], sems.at[i]) for i in range(parts + 2)
     ]
-    for d in range(gains_count):
-        tail = gain_refs[d].at[pl.ds(gain_refs[d].shape[0] - 16, 16), :]
-        copies.append(pltpu.make_async_copy(tail, gains_scr.at[d], sems.at[parts + 1 + d]))
     for copy in copies:
         copy.start()
     for copy in copies:
@@ -330,34 +367,27 @@
     residual = residual.astype(jnp.bfloat16).astype(jnp.float32)
     total = jnp.sum(residual * residual, axis=1, keepdims=True)
     scale = lax.rsqrt(total / residual.shape[1] + epsilon)
-    work[...] = residual * scale
-    for d in range(gains_count):
-        columns = pl.ds(pl.multiple_of((me ^ d) * width, width), width)
-        out_ref[:, columns] = (work[:, columns] * gain_row(gains_scr.at[d], 1)).astype(
-            jnp.bfloat16
-        )
+    out_ref[...] = (residual * scale * gains_scr[1:2, :]).astype(jnp.bfloat16)
 
 
 def final_rows(parts, raw, gains, after):
     rows, full_width = raw.shape
-    count = len(parts) + 1 + len(gains)
     return pl.pallas_call(
-        functools.partial(final_kernel, len(parts), len(gains), len(after)),
+        functools.partial(final_kernel, len(parts)),
         out_shape=jax.ShapeDtypeStruct((rows, full_width), jnp.bfloat16),
-        in_specs=[anywhere()] * (count + len(after)),
+        in_specs=[anywhere()] * (len(parts) + 2 + len(after)),
         out_specs=whole(),
         scratch_shapes=[
             pltpu.VMEM((len(parts) + 1, rows, full_width), jnp.bfloat16),
-            pltpu.VMEM((len(gains), 16, gains[0].shape[1]), jnp.bfloat16),
-            pltpu.VMEM((rows, full_width), jnp.float32),
-            pltpu.SemaphoreType.DMA((count,)),
+            pltpu.VMEM(gains.shape, jnp.float32),
+            pltpu.SemaphoreType.DMA((len(parts) + 2,)),
         ],
         compiler_params=params(6 * MIB),
         cost_estimate=pl.CostEstimate(
             flops=8 * rows * full_width, bytes_accessed=12 * rows * full_width, transcendentals=rows
         ),
         name="final_rows",
-    )(*parts, raw, *gains, *after)
+    )(*parts, raw, gains, *after)
 
 
 def head_kernel(pieces, tile, sub, *refs):
@@ -387,13 +417,15 @@
                     sems.at[len(copies)],
                 )
             )
+    ahead = min(2, steps)
+    for i in range(1):
+        fetch(i).start()
     for copy in copies:
         copy.start()
-    fetch(0).start()
+    for i in range(1, ahead):
+        fetch(i).start()
     for copy in copies:
         copy.wait()
-    for i in range(1, steps):
-        fetch(i).start()
     lane = lax.broadcasted_iota(jnp.int32, out_ref.shape, 0)
     out_ref[...] = jnp.where(lane == 0, -jnp.inf, 0.0)
     targets = target_ref[...] - (my_expert * n_tensor + my_tensor) * vocab_part
@@ -401,6 +433,11 @@
     @pl.loop(0, steps)
     def _(i):
         fetch(i).wait()
+
+        @pl.when(i + ahead < steps)
+        def _():
+            fetch(i + ahead).start()
+
         logits = lax.dot_general(
             head_scr[i],
             rows_scr[...],
@@ -572,21 +609,18 @@
     sub = own // splits
     rows = sub * n_tensor
 
-    parts = tokens.reshape(n_tensor, splits, sub, width)
-    rider = jnp.concatenate([split_three(norm_gain), split_three(final_gain)])
-    rider = jnp.pad(rider, ((0, 16 - rider.shape[0]), (0, 0))).astype(jnp.bfloat16)
-    blocks = [parts[:, h].reshape(rows, width) for h in range(splits)]
-    gains = slices = gather_near(jnp.concatenate([blocks[0], rider]), "tensor")
+    blocks = begin(tokens, norm_gain, final_gain, n_tensor, splits)
+    slices = [gather_near(block, "tensor") for block in blocks]
+    gains = None
     planes, raws = [], []
     after = []
     for h in range(splits):
-        following = blocks[h + 1 : h + 2]
-        normed, raw, *block = norm_rows(
-            slices, gains, routes, route_weights, splits, h, rows, after, following
-        )
-        if block:
-            slices = gather_near(block[0], "tensor")
-        plane = gather_plane(normed, "expert", [])
+        normed, raw, *made = norm_rows(
+            slices[h], [gains], routes, route_weights, splits, h, rows, after
+        )
+        if made:
+            gains = made[0]
+        plane, _ = gather_plane(normed, "expert", [])
         planes.append(plane)
         raws.append(raw)
         after = plane[3:]
@@ -598,11 +632,11 @@
     terms = []
     before = {}
     for h in range(splits):
-        far = planes[h][3:]
-        if before and len(far) == 2:
-            far = [stack_rows(far, before["kept"])]
-        away = [swap(p, "seq", 1) for p in planes[h][:3] + far]
         if 2 * n_expert * rows <= LARGEST:
+            nearer = stack_rows(planes[h][:3], [] if before else sum((p[1:] for p in slices[1:2]), []))
+            away = [swap(nearer, "seq", 1)]
+            if planes[h][3:]:
+                away.append(swap(stack_rows(planes[h][3:], before.get("kept", [])), "seq", 1))
             half = n_expert * rows
             everything = planes[h] + away
             tile = tile_of(w_gate)
@@ -626,14 +660,13 @@
         got = swap(other, "seq", 1)
         totals, packed, passed = sum_plane(kept, got, rows, before.get("column", []))
         sums = [swap(totals[d], "tensor", d) for d in range(1, n_tensor)]
-        finals_near, finals_far = [], []
+        cut = []
         if before:
             column = stack_rows([before["final"][0]] + before["column"], totals[:1])
-            plane = gather_plane(column, "expert", [])
-            finals_near, finals_far = plane[1:3], plane[3:]
+            plane, cut = gather_plane(column, "expert", [])
             wanted = target_rows[:, :, h - 1].reshape(1, -1)
             terms.append(head_terms(plane, head_rows, wanted, sub))
-        final = final_rows(totals[:1] + sums, raws[h], gains, finals_near)
+        final = final_rows(totals[:1] + sums, raws[h], gains, [])
         column = gather_near(final, "tensor")
         before = {
             "kept": [kept],
@@ -644,8 +677,8 @@
             "final": [final],
             "column": column[1:],
         }
-    column = stack_rows(column, finals_far)
-    plane = gather_plane(column, "expert", terms[-1:])
+    column = stack_rows(column, cut)
+    plane, _ = gather_plane(column, "expert", terms[-1:])
     wanted = target_rows[:, :, splits - 1].reshape(1, -1)
     terms.append(head_terms(plane, head_rows, wanted, sub))
     terms = [term[:3].reshape(3, n_expert, n_tensor, sub) for term in terms]

time: 241 us -> 234 us (0.971)
  Pallas kernels: 94.5 us -> 86.1 us
    pallas_call x4, Pallas kernels: 20.8 us -> 15.8 us  [down_rows(): pl.pallas_call(functools.partial(down_kernel, start, len(hidden)), out_sh...]
    pallas_call x2, Pallas kernels: 21.5 us -> 19.1 us  [head_terms(): pl.pallas_call(functools.partial(head_kernel, len(pieces), tile, sub), ou...]
    ppermute x59 -> x54, waiting for transfers between devices: 74.3 us -> 76.7 us  [swap(): return lax.ppermute(x, axis, [(i, i ^ distance) for i in range(size)])]
    ppermute x59 -> x54, starting transfers between devices: 62.9 us -> 64.4 us  [swap(): return lax.ppermute(x, axis, [(i, i ^ distance) for i in range(size)])]
  transfers between devices with their start and end apart: 59 -> 54, of which waited for: 28 -> 25; matrix products, arithmetic and copies ran while one was open for 1% -> 1% of each run, Pallas kernels for 29% -> 28%
where the time goes in v7:
time: 234 us
  Pallas kernels  86.1 us (37%)
  waiting for transfers between devices  76.7 us (33%)
  starting transfers between devices  64.4 us (28%)
  local copies, waits for them, and re-layouts  5.48 us (2%)
    ppermute x54, waiting for transfers between devices, swap(): return lax.ppermute(x, axis, [(i, i ^ distance) for i in range(size)])  76.7 us
    ppermute x54, starting transfers between devices, swap(): return lax.ppermute(x, axis, [(i, i ^ distance) for i in range(size)])  64.4 us
    pallas_call x4, Pallas kernels, hidden_rows(): pl.pallas_call(functools.partial(hidden_kernel, len(pieces), len(after),...  43 us
    pallas_call x2, Pallas kernels, head_terms(): pl.pallas_call(functools.partial(head_kernel, len(pieces), tile, sub), ou...  19.1 us
    pallas_call x4, Pallas kernels, down_rows(): pl.pallas_call(functools.partial(down_kernel, start, len(hidden)), out_sh...  15.8 us
  transfers between devices with their start and end apart: 54, of which 25 were waited for; matrix products, arithmetic and copies ran while one was open for 1% of the time, Pallas kernels for 28%

profile of v7, /device:TPU:0, one launch (start us, length us, event | category | flops | bytes accessed | tf_op | source)
XLA Modules:
  0.0 233.8 jit_solution(3494789531878134875)
XLA Ops:
  2.4 3.1 %collective-permute-start = (bf16[72,1024]{1,0:T(8,128)(2,1)S(1)}, bf16[72,1024]{1,0:T(8,128)(2,1)S(1)}, u32[]{:S(2)}, u32[]{:S(2)}) collective-permute-start(bf16[72,1024]{1,0:T(8,128)(2,1)S(1)} %get-tuple-element.40.refs_0_), channel_id=1, source_target_pairs={{0,1},{1,0},{2,3},{3,2},{4,5},{5,4},{6,7},{7,6},{8,9},{9,8},{10,11... | collective-permute-start | bytes 442376 | tf_op jit(solution)/shard_map/ppermute | solution.py:31
  5.5 2.6 %collective-permute-start.1 = (bf16[72,1024]{1,0:T(8,128)(2,1)S(1)}, bf16[72,1024]{1,0:T(8,128)(2,1)S(1)}, u32[]{:S(2)}, u32[]{:S(2)}) collective-permute-start(bf16[72,1024]{1,0:T(8,128)(2,1)S(1)} %get-tuple-element.40.refs_0_), channel_id=1, source_target_pairs={{0,2},{1,3},{2,0},{3,1},{4,6},{5,7},{6,4},{7,5},{8,10},{9,11},{10,... | collective-permute-start | bytes 442376 | tf_op jit(solution)/shard_map/ppermute | solution.py:31
  11.3 8.1 %collective-permute-done.1.refs_2_ = bf16[72,1024]{1,0:T(8,128)(2,1)S(1)} collective-permute-done((bf16[72,1024]{1,0:T(8,128)(2,1)S(1)}, bf16[72,1024]{1,0:T(8,128)(2,1)S(1)}, u32[]{:S(2)}, u32[]{:S(2)}) %collective-permute-start.1) | collective-permute-done | bytes 147488 | tf_op jit(solution)/shard_map/ppermute | solution.py:31
  29.3 7.0 %collective-permute-done.8.refs_4_.refs_2_ = bf16[64,1024]{1,0:T(8,128)(2,1)S(1)} collective-permute-done((bf16[64,1024]{1,0:T(8,128)(2,1)S(1)}, bf16[64,1024]{1,0:T(8,128)(2,1)S(1)}, u32[]{:S(2)}, u32[]{:S(2)}) %collective-permute-start.8) | collective-permute-done | bytes 131104 | tf_op jit(solution)/shard_map/ppermute | solution.py:31
  37.9 7.8 %collective-permute-done.5.refs_0_.refs_3_.refs_7_ = bf16[32,4224]{1,0:T(8,128)(2,1)S(1)} collective-permute-done((bf16[32,4224]{1,0:T(8,128)(2,1)S(1)}, bf16[32,4224]{1,0:T(8,128)(2,1)S(1)}, u32[]{:S(2)}, u32[]{:S(2)}) %collective-permute-start.5) | collective-permute-done | bytes 270368 | tf_op jit(solution)/shard_map/ppermute | solution.py:31
  48.6 19.5 %hidden_rows.4.refs_0_ = bf16[512,1792]{1,0:T(8,128)(2,1)S(1)} custom-call(bf16[64,4224]{1,0:T(8,128)(2,1)S(1)} %get-tuple-element.41.refs_0_, bf16[64,4224]{1,0:T(8,128)(2,1)S(1)} %collective-permute-done.3.refs_1_, bf16[64,4224]{1,0:T(8,128)(2,1)S(1)} %collective-permute-done.4.refs_0_.refs_2_, ...), custom_call_target="tpu_custom_call" | custom-call | flops 15032385536 | bytes 35389440 | tf_op jit(solution)/shard_map/hidden_rows/pallas_call | solution.py:278
  68.2 3.9 %down_rows.5 = bf16[256,4096]{1,0:T(8,128)(2,1)S(1)} custom-call(bf16[512,1792]{1,0:T(8,128)(2,1)S(1)} %hidden_rows.4.refs_0_, bf16[1,1792,4096]{2,1,0:T(8,128)(2,1)S(1)} %bitcast.33, bf16[64,4224]{1,0:T(8,128)(2,1)S(1)} %collective-permute-done.12.refs_2_.refs_1_, bf16[64,4224]{1,0:T(8,128)(2,1)S(1)} %collective-permute-done.13.refs_3_.refs_0_.refs_2_), custom_call_target="tpu_custom_call" | custom-call | flops 3758096384 | bytes 3014656 | tf_op jit(solution)/shard_map/down_rows/pallas_call | solution.py:323
  75.2 3.9 %down_rows.4.kept_ref.refs_2_ = bf16[256,4096]{1,0:T(8,128)(2,1)S(1)} custom-call(bf16[512,1792]{1,0:T(8,128)(2,1)S(1)} %hidden_rows.4.refs_0_, bf16[1,1792,4096]{2,1,0:T(8,128)(2,1)S(1)} %bitcast.33), custom_call_target="tpu_custom_call" | custom-call | flops 3758096384 | bytes 3014656 | tf_op jit(solution)/shard_map/down_rows/pallas_call | solution.py:323
  79.2 2.8 %collective-permute-done.25.refs_0_.refs_3_ = bf16[32,4224]{1,0:T(8,128)(2,1)S(1)} collective-permute-done((bf16[32,4224]{1,0:T(8,128)(2,1)S(1)}, bf16[32,4224]{1,0:T(8,128)(2,1)S(1)}, u32[]{:S(2)}, u32[]{:S(2)}) %collective-permute-start.25) | collective-permute-done | bytes 270368 | tf_op jit(solution)/shard_map/ppermute | solution.py:31
  85.5 11.8 %hidden_rows.5.refs_0_ = bf16[512,1024]{1,0:T(8,128)(2,1)S(1)} custom-call(bf16[64,4224]{1,0:T(8,128)(2,1)S(1)} %get-tuple-element.46.refs_0_, bf16[64,4224]{1,0:T(8,128)(2,1)S(1)} %collective-permute-done.12.refs_2_.refs_1_, bf16[64,4224]{1,0:T(8,128)(2,1)S(1)} %collective-permute-done.13.refs_3_.refs_0_.refs_2_, ...), custom_call_target="tpu_custom_call" | custom-call | flops 8589934592 | bytes 22020096 | tf_op jit(solution)/shard_map/hidden_rows/pallas_call | solution.py:278
  100.7 7.0 %hidden_rows.6.refs_1_ = bf16[512,512]{1,0:T(8,128)(2,1)S(1)} custom-call(bf16[64,4224]{1,0:T(8,128)(2,1)S(1)} %get-tuple-element.46.refs_0_, bf16[64,4224]{1,0:T(8,128)(2,1)S(1)} %collective-permute-done.12.refs_2_.refs_1_, bf16[64,4224]{1,0:T(8,128)(2,1)S(1)} %collective-permute-done.13.refs_3_.refs_0_.refs_2_, ...), custom_call_target="tpu_custom_call" | custom-call | flops 4294967296 | bytes 13107200 | tf_op jit(solution)/shard_map/hidden_rows/pallas_call | solution.py:278
  112.6 4.7 %hidden_rows.7.refs_2_ = bf16[512,256]{1,0:T(8,128)(2,1)S(1)} custom-call(bf16[64,4224]{1,0:T(8,128)(2,1)S(1)} %get-tuple-element.46.refs_0_, bf16[64,4224]{1,0:T(8,128)(2,1)S(1)} %collective-permute-done.12.refs_2_.refs_1_, bf16[64,4224]{1,0:T(8,128)(2,1)S(1)} %collective-permute-done.13.refs_3_.refs_0_.refs_2_, ...), custom_call_target="tpu_custom_call" | custom-call | flops 2147483648 | bytes 8650752 | tf_op jit(solution)/shard_map/hidden_rows/pallas_call | solution.py:278
  117.3 4.6 %collective-permute-done.20.refs_2_.refs_5_ = bf16[16,4096]{1,0:T(8,128)(2,1)S(1)} collective-permute-done((bf16[16,4096]{1,0:T(8,128)(2,1)S(1)}, bf16[16,4096]{1,0:T(8,128)(2,1)S(1)}, u32[]{:S(2)}, u32[]{:S(2)}) %collective-permute-start.20) | collective-permute-done | bytes 131104 | tf_op jit(solution)/shard_map/ppermute | solution.py:31
  122.0 3.9 %down_rows.7 = bf16[256,4096]{1,0:T(8,128)(2,1)S(1)} custom-call(bf16[512,1024]{1,0:T(8,128)(2,1)S(1)} %hidden_rows.5.refs_0_, bf16[512,512]{1,0:T(8,128)(2,1)S(1)} %hidden_rows.6.refs_1_, bf16[512,256]{1,0:T(8,128)(2,1)S(1)} %hidden_rows.7.refs_2_, bf16[1,1792,4096]{2,1,0:T(8,128)(2,1)S(1)} %bitcast.33, ...), custom_call_target="tpu_custom_call" | custom-call | flops 3758096384 | bytes 3014656 | tf_op jit(solution)/shard_map/down_rows/pallas_call | solution.py:323
  127.5 3.9 %down_rows.6.kept_ref = bf16[256,4096]{1,0:T(8,128)(2,1)S(1)} custom-call(bf16[512,1024]{1,0:T(8,128)(2,1)S(1)} %hidden_rows.5.refs_0_, bf16[512,512]{1,0:T(8,128)(2,1)S(1)} %hidden_rows.6.refs_1_, bf16[512,256]{1,0:T(8,128)(2,1)S(1)} %hidden_rows.7.refs_2_, bf16[1,1792,4096]{2,1,0:T(8,128)(2,1)S(1)} %bitcast.33, bf16[16,4096]{1,0:T(8,128)(2,1)S(1)} %final_rows.2.refs_4_.refs_0_), custom_call_target="tpu_custom_call" | custom-call | flops 3758096384 | bytes 3014656 | tf_op jit(solution)/shard_map/down_rows/pallas_call | solution.py:323
  138.5 2.6 %collective-permute-done.22.refs_0_.refs_1_ = bf16[16,4096]{1,0:T(8,128)(2,1)S(1)} collective-permute-done((bf16[16,4096]{1,0:T(8,128)(2,1)S(1)}, bf16[16,4096]{1,0:T(8,128)(2,1)S(1)}, u32[]{:S(2)}, u32[]{:S(2)}) %collective-permute-start.22) | collective-permute-done | bytes 131104 | tf_op jit(solution)/shard_map/ppermute | solution.py:31
  141.2 7.7 %collective-permute-done.23.refs_1_.refs_2_ = bf16[16,4096]{1,0:T(8,128)(2,1)S(1)} collective-permute-done((bf16[16,4096]{1,0:T(8,128)(2,1)S(1)}, bf16[16,4096]{1,0:T(8,128)(2,1)S(1)}, u32[]{:S(2)}, u32[]{:S(2)}) %collective-permute-start.23) | collective-permute-done | bytes 131104 | tf_op jit(solution)/shard_map/ppermute | solution.py:31
  151.1 4.3 %collective-permute-done.32.last_one_ref = bf16[32,4096]{1,0:T(8,128)(2,1)S(1)} collective-permute-done((bf16[32,4096]{1,0:T(8,128)(2,1)S(1)}, bf16[32,4096]{1,0:T(8,128)(2,1)S(1)}, u32[]{:S(2)}, u32[]{:S(2)}) %collective-permute-start.32) | collective-permute-done | bytes 262176 | tf_op jit(solution)/shard_map/ppermute | solution.py:31
  165.3 7.5 %collective-permute-done.39.refs_2_ = bf16[16,4096]{1,0:T(8,128)(2,1)S(1)} collective-permute-done((bf16[16,4096]{1,0:T(8,128)(2,1)S(1)}, bf16[16,4096]{1,0:T(8,128)(2,1)S(1)}, u32[]{:S(2)}, u32[]{:S(2)}) %collective-permute-start.39) | collective-permute-done | bytes 131104 | tf_op jit(solution)/shard_map/ppermute | solution.py:31
  181.7 6.0 %collective-permute-done.42.refs_2_ = bf16[16,4096]{1,0:T(8,128)(2,1)S(1)} collective-permute-done((bf16[16,4096]{1,0:T(8,128)(2,1)S(1)}, bf16[16,4096]{1,0:T(8,128)(2,1)S(1)}, u32[]{:S(2)}, u32[]{:S(2)}) %collective-permute-start.42) | collective-permute-done | bytes 131104 | tf_op jit(solution)/shard_map/ppermute | solution.py:31
  191.0 9.5 %head_terms.2.refs_2_ = f32[8,256]{1,0:T(8,128)S(1)} custom-call(bf16[64,4096]{1,0:T(8,128)(2,1)S(1)} %move_rows.16.refs_0_, bf16[64,4096]{1,0:T(8,128)(2,1)S(1)} %collective-permute-done.34.refs_1_, bf16[64,4096]{1,0:T(8,128)(2,1)S(1)} %collective-permute-done.35.refs_0_.refs_2_, bf16[32,4096]{1,0:T(8,128)(2,1)S(1)} %collective-permute-done.36.refs_3_, ...), custom_call_target="tpu_custom_call" | custom-call | flops 4194304000 | bytes 18481152 | tf_op jit(solution)/shard_map/head_terms/pallas_call | solution.py:462
  202.6 4.3 %collective-permute-done.46.refs_3_ = bf16[32,4096]{1,0:T(8,128)(2,1)S(1)} collective-permute-done((bf16[32,4096]{1,0:T(8,128)(2,1)S(1)}, bf16[32,4096]{1,0:T(8,128)(2,1)S(1)}, u32[]{:S(2)}, u32[]{:S(2)}) %collective-permute-start.46) | collective-permute-done | bytes 262176 | tf_op jit(solution)/shard_map/ppermute | solution.py:31
  207.7 9.6 %head_terms.3 = f32[8,256]{1,0:T(8,128)S(1)} custom-call(bf16[64,4096]{1,0:T(8,128)(2,1)S(1)} %move_rows.18.refs_0_, bf16[64,4096]{1,0:T(8,128)(2,1)S(1)} %collective-permute-done.44.refs_1_, bf16[64,4096]{1,0:T(8,128)(2,1)S(1)} %collective-permute-done.45.refs_0_.refs_2_, bf16[32,4096]{1,0:T(8,128)(2,1)S(1)} %collective-permute-done.46.refs_3_, ...), custom_call_target="tpu_custom_call" | custom-call | flops 4194304000 | bytes 18481152 | tf_op jit(solution)/shard_map/head_terms/pallas_call | solution.py:462
  217.5 3.3 %collective-permute-start.50 = (f32[3,4,2,16]{3,2,1,0:T(2,128)S(1)}, f32[3,4,2,16]{3,2,1,0:T(2,128)S(1)}, u32[]{:S(2)}, u32[]{:S(2)}) collective-permute-start(f32[3,4,2,16]{3,2,1,0:T(2,128)S(1)} %get-tuple-element.83), channel_id=1, source_target_pairs={{0,3},{1,2},{2,1},{3,0},{4,7},{5,6},{6,5},{7,4},{8,11},{9,10},{10,... | collective-permute-start | bytes 4616 | tf_op jit(solution)/shard_map/ppermute | solution.py:31
  (165 shorter events, 83.4 us)
Async XLA Ops:
  5.5 14.0 %collective-permute-start.1 = (bf16[72,1024]{1,0:T(8,128)(2,1)S(1)}, bf16[72,1024]{1,0:T(8,128)(2,1)S(1)}, u32[]{:S(2)}, u32[]{:S(2)}) collective-permute-start(bf16[72,1024]{1,0:T(8,128)(2,1)S(1)} %get-tuple-element.40.refs_0_), channel_id=1, source_target_pairs={{0,2},{1,3},{2,0},{3,1},{4,6},{5,7},{6,4},{7,5},{8,10},{9,11},{10,... | collective-permute-start | bytes 442376 | tf_op jit(solution)/shard_map/ppermute | solution.py:31
  8.1 11.4 %collective-permute-start.2 = (bf16[72,1024]{1,0:T(8,128)(2,1)S(1)}, bf16[72,1024]{1,0:T(8,128)(2,1)S(1)}, u32[]{:S(2)}, u32[]{:S(2)}) collective-permute-start(bf16[72,1024]{1,0:T(8,128)(2,1)S(1)} %get-tuple-element.40.refs_0_), channel_id=1, source_target_pairs={{0,3},{1,2},{2,1},{3,0},{4,7},{5,6},{6,5},{7,4},{8,11},{9,10},{10,... | collective-permute-start | bytes 442376 | tf_op jit(solution)/shard_map/ppermute | solution.py:31
  19.8 16.6 %collective-permute-start.3 = (bf16[64,4224]{1,0:T(8,128)(2,1)S(1)}, bf16[64,4224]{1,0:T(8,128)(2,1)S(1)}, u32[]{:S(2)}, u32[]{:S(2)}) collective-permute-start(bf16[64,4224]{1,0:T(8,128)(2,1)S(1)} %get-tuple-element.41.refs_0_), channel_id=1, source_target_pairs={{0,4},{4,0},{8,12},{12,8},{1,5},{5,1},{9,13},{13,9},{2,6},{6,2},{1... | collective-permute-start | bytes 1622024 | tf_op jit(solution)/shard_map/ppermute | solution.py:31
  21.4 15.0 %collective-permute-start.4 = (bf16[64,4224]{1,0:T(8,128)(2,1)S(1)}, bf16[64,4224]{1,0:T(8,128)(2,1)S(1)}, u32[]{:S(2)}, u32[]{:S(2)}) collective-permute-start(bf16[64,4224]{1,0:T(8,128)(2,1)S(1)} %get-tuple-element.41.refs_0_), channel_id=1, source_target_pairs={{0,8},{4,12},{8,0},{12,4},{1,9},{5,13},{9,1},{13,5},{2,10},{6,14},... | collective-permute-start | bytes 1622024 | tf_op jit(solution)/shard_map/ppermute | solution.py:31
  25.2 11.2 %collective-permute-start.8 = (bf16[64,1024]{1,0:T(8,128)(2,1)S(1)}, bf16[64,1024]{1,0:T(8,128)(2,1)S(1)}, u32[]{:S(2)}, u32[]{:S(2)}) collective-permute-start(bf16[64,1024]{1,0:T(8,128)(2,1)S(1)} %get-tuple-element.44.refs_0_), channel_id=1, source_target_pairs={{0,2},{1,3},{2,0},{3,1},{4,6},{5,7},{6,4},{7,5},{8,10},{9,11},{10,... | collective-permute-start | bytes 393224 | tf_op jit(solution)/shard_map/ppermute | solution.py:31
  36.6 12.0 %collective-permute-start.10 = (bf16[192,4224]{1,0:T(8,128)(2,1)S(1)}, bf16[192,4224]{1,0:T(8,128)(2,1)S(1)}, u32[]{:S(2)}, u32[]{:S(2)}) collective-permute-start(bf16[192,4224]{1,0:T(8,128)(2,1)S(1)} %move_rows.11), channel_id=1, source_target_pairs={{0,16},{16,0},{1,17},{17,1},{2,18},{18,2},{3,19},{19,3},{4,20},{20... | collective-permute-start | bytes 4866056 | tf_op jit(solution)/shard_map/ppermute | solution.py:31
  46.5 21.6 %collective-permute-start.12 = (bf16[64,4224]{1,0:T(8,128)(2,1)S(1)}, bf16[64,4224]{1,0:T(8,128)(2,1)S(1)}, u32[]{:S(2)}, u32[]{:S(2)}) collective-permute-start(bf16[64,4224]{1,0:T(8,128)(2,1)S(1)} %get-tuple-element.46.refs_0_), channel_id=1, source_target_pairs={{0,4},{4,0},{8,12},{12,8},{1,5},{5,1},{9,13},{13,9},{2,6},{6,2},{1... | collective-permute-start | bytes 1622024 | tf_op jit(solution)/shard_map/ppermute | solution.py:31
  48.1 20.1 %collective-permute-start.13 = (bf16[64,4224]{1,0:T(8,128)(2,1)S(1)}, bf16[64,4224]{1,0:T(8,128)(2,1)S(1)}, u32[]{:S(2)}, u32[]{:S(2)}) collective-permute-start(bf16[64,4224]{1,0:T(8,128)(2,1)S(1)} %get-tuple-element.46.refs_0_), channel_id=1, source_target_pairs={{0,8},{4,12},{8,0},{12,4},{1,9},{5,13},{9,1},{13,5},{2,10},{6,14},... | collective-permute-start | bytes 1622024 | tf_op jit(solution)/shard_map/ppermute | solution.py:31
  72.2 11.0 %collective-permute-start.14 = (bf16[256,4096]{1,0:T(8,128)(2,1)S(1)}, bf16[256,4096]{1,0:T(8,128)(2,1)S(1)}, u32[]{:S(2)}, u32[]{:S(2)}) collective-permute-start(bf16[256,4096]{1,0:T(8,128)(2,1)S(1)} %down_rows.5), channel_id=1, source_target_pairs={{0,16},{16,0},{1,17},{17,1},{2,18},{18,2},{3,19},{19,3},{4,20},{20... | collective-permute-start | bytes 6291464 | tf_op jit(solution)/shard_map/ppermute | solution.py:31
  72.9 12.6 %collective-permute-start.27 = (bf16[192,4224]{1,0:T(8,128)(2,1)S(1)}, bf16[192,4224]{1,0:T(8,128)(2,1)S(1)}, u32[]{:S(2)}, u32[]{:S(2)}) collective-permute-start(bf16[192,4224]{1,0:T(8,128)(2,1)S(1)} %move_rows.14), channel_id=1, source_target_pairs={{0,16},{16,0},{1,17},{17,1},{2,18},{18,2},{3,19},{19,3},{4,20},{20... | collective-permute-start | bytes 4866056 | tf_op jit(solution)/shard_map/ppermute | solution.py:31
  83.6 14.4 %collective-permute-start.15 = (bf16[64,4096]{1,0:T(8,128)(2,1)S(1)}, bf16[64,4096]{1,0:T(8,128)(2,1)S(1)}, u32[]{:S(2)}, u32[]{:S(2)}) collective-permute-start(bf16[64,4096]{1,0:T(8,128)(2,1)S(1)} %get-tuple-element.48.refs_9_), channel_id=1, source_target_pairs={{0,4},{4,0},{8,12},{12,8},{1,5},{5,1},{9,13},{13,9},{2,6},{6,2},{1... | collective-permute-start | bytes 1572872 | tf_op jit(solution)/shard_map/ppermute | solution.py:31
  84.4 14.0 %collective-permute-start.16 = (bf16[64,4096]{1,0:T(8,128)(2,1)S(1)}, bf16[64,4096]{1,0:T(8,128)(2,1)S(1)}, u32[]{:S(2)}, u32[]{:S(2)}) collective-permute-start(bf16[64,4096]{1,0:T(8,128)(2,1)S(1)} %get-tuple-element.49.refs_10_), channel_id=1, source_target_pairs={{0,8},{4,12},{8,0},{12,4},{1,9},{5,13},{9,1},{13,5},{2,10},{6,14},... | collective-permute-start | bytes 1572872 | tf_op jit(solution)/shard_map/ppermute | solution.py:31
  110.0 11.9 %collective-permute-start.20 = (bf16[16,4096]{1,0:T(8,128)(2,1)S(1)}, bf16[16,4096]{1,0:T(8,128)(2,1)S(1)}, u32[]{:S(2)}, u32[]{:S(2)}) collective-permute-start(bf16[16,4096]{1,0:T(8,128)(2,1)S(1)} %get-tuple-element.55.refs_11_), channel_id=1, source_target_pairs={{0,2},{1,3},{2,0},{3,1},{4,6},{5,7},{6,4},{7,5},{8,10},{9,11},{10,... | collective-permute-start | bytes 393224 | tf_op jit(solution)/shard_map/ppermute | solution.py:31
  131.9 17.0 %collective-permute-start.30 = (bf16[64,4096]{1,0:T(8,128)(2,1)S(1)}, bf16[64,4096]{1,0:T(8,128)(2,1)S(1)}, u32[]{:S(2)}, u32[]{:S(2)}) collective-permute-start(bf16[64,4096]{1,0:T(8,128)(2,1)S(1)} %get-tuple-element.61), channel_id=1, source_target_pairs={{0,4},{4,0},{8,12},{12,8},{1,5},{5,1},{9,13},{13,9},{2,6},{6,2},{1... | collective-permute-start | bytes 1572872 | tf_op jit(solution)/shard_map/ppermute | solution.py:31
  133.1 15.9 %collective-permute-start.31 = (bf16[64,4096]{1,0:T(8,128)(2,1)S(1)}, bf16[64,4096]{1,0:T(8,128)(2,1)S(1)}, u32[]{:S(2)}, u32[]{:S(2)}) collective-permute-start(bf16[64,4096]{1,0:T(8,128)(2,1)S(1)} %get-tuple-element.62), channel_id=1, source_target_pairs={{0,8},{4,12},{8,0},{12,4},{1,9},{5,13},{9,1},{13,5},{2,10},{6,14},... | collective-permute-start | bytes 1572872 | tf_op jit(solution)/shard_map/ppermute | solution.py:31
  136.0 12.9 %collective-permute-start.23 = (bf16[16,4096]{1,0:T(8,128)(2,1)S(1)}, bf16[16,4096]{1,0:T(8,128)(2,1)S(1)}, u32[]{:S(2)}, u32[]{:S(2)}) collective-permute-start(bf16[16,4096]{1,0:T(8,128)(2,1)S(1)} %final_rows.2.refs_4_.refs_0_), channel_id=1, source_target_pairs={{0,2},{1,3},{2,0},{3,1},{4,6},{5,7},{6,4},{7,5},{8,10},{9,11},{10,... | collective-permute-start | bytes 393224 | tf_op jit(solution)/shard_map/ppermute | solution.py:31
  137.1 11.9 %collective-permute-start.24 = (bf16[16,4096]{1,0:T(8,128)(2,1)S(1)}, bf16[16,4096]{1,0:T(8,128)(2,1)S(1)}, u32[]{:S(2)}, u32[]{:S(2)}) collective-permute-start(bf16[16,4096]{1,0:T(8,128)(2,1)S(1)} %final_rows.2.refs_4_.refs_0_), channel_id=1, source_target_pairs={{0,3},{1,2},{2,1},{3,0},{4,7},{5,6},{6,5},{7,4},{8,11},{9,10},{10,... | collective-permute-start | bytes 393224 | tf_op jit(solution)/shard_map/ppermute | solution.py:31
  157.8 20.7 %collective-permute-start.34 = (bf16[64,4096]{1,0:T(8,128)(2,1)S(1)}, bf16[64,4096]{1,0:T(8,128)(2,1)S(1)}, u32[]{:S(2)}, u32[]{:S(2)}) collective-permute-start(bf16[64,4096]{1,0:T(8,128)(2,1)S(1)} %move_rows.16.refs_0_), channel_id=1, source_target_pairs={{0,4},{4,0},{8,12},{12,8},{1,5},{5,1},{9,13},{13,9},{2,6},{6,2},{1... | collective-permute-start | bytes 1572872 | tf_op jit(solution)/shard_map/ppermute | solution.py:31
  158.6 19.9 %collective-permute-start.35 = (bf16[64,4096]{1,0:T(8,128)(2,1)S(1)}, bf16[64,4096]{1,0:T(8,128)(2,1)S(1)}, u32[]{:S(2)}, u32[]{:S(2)}) collective-permute-start(bf16[64,4096]{1,0:T(8,128)(2,1)S(1)} %move_rows.16.refs_0_), channel_id=1, source_target_pairs={{0,8},{4,12},{8,0},{12,4},{1,9},{5,13},{9,1},{13,5},{2,10},{6,14},... | collective-permute-start | bytes 1572872 | tf_op jit(solution)/shard_map/ppermute | solution.py:31
  162.0 10.8 %collective-permute-start.39 = (bf16[16,4096]{1,0:T(8,128)(2,1)S(1)}, bf16[16,4096]{1,0:T(8,128)(2,1)S(1)}, u32[]{:S(2)}, u32[]{:S(2)}) collective-permute-start(bf16[16,4096]{1,0:T(8,128)(2,1)S(1)} %get-tuple-element.70), channel_id=1, source_target_pairs={{0,2},{1,3},{2,0},{3,1},{4,6},{5,7},{6,4},{7,5},{8,10},{9,11},{10,... | collective-permute-start | bytes 393224 | tf_op jit(solution)/shard_map/ppermute | solution.py:31
  176.1 11.6 %collective-permute-start.42 = (bf16[16,4096]{1,0:T(8,128)(2,1)S(1)}, bf16[16,4096]{1,0:T(8,128)(2,1)S(1)}, u32[]{:S(2)}, u32[]{:S(2)}) collective-permute-start(bf16[16,4096]{1,0:T(8,128)(2,1)S(1)} %final_rows.3.refs_0_), channel_id=1, source_target_pairs={{0,2},{1,3},{2,0},{3,1},{4,6},{5,7},{6,4},{7,5},{8,10},{9,11},{10,... | collective-permute-start | bytes 393224 | tf_op jit(solution)/shard_map/ppermute | solution.py:31
  179.4 11.6 %collective-permute-start.36 = (bf16[32,4096]{1,0:T(8,128)(2,1)}, bf16[32,4096]{1,0:T(8,128)(2,1)S(1)}, u32[]{:S(2)}, u32[]{:S(2)}) collective-permute-start(bf16[32,4096]{1,0:T(8,128)(2,1)} %get-tuple-element.67.refs_4_), channel_id=1, source_target_pairs={{0,4},{4,0},{8,12},{12,8},{1,5},{5,1},{9,13},{13,9},{2,6},{6,2},{1... | collective-permute-start | bytes 786440 | tf_op jit(solution)/shard_map/ppermute | solution.py:31
  188.4 12.0 %collective-permute-start.44 = (bf16[64,4096]{1,0:T(8,128)(2,1)S(1)}, bf16[64,4096]{1,0:T(8,128)(2,1)S(1)}, u32[]{:S(2)}, u32[]{:S(2)}) collective-permute-start(bf16[64,4096]{1,0:T(8,128)(2,1)S(1)} %move_rows.18.refs_0_), channel_id=1, source_target_pairs={{0,4},{4,0},{8,12},{12,8},{1,5},{5,1},{9,13},{13,9},{2,6},{6,2},{1... | collective-permute-start | bytes 1572872 | tf_op jit(solution)/shard_map/ppermute | solution.py:31
  189.4 11.0 %collective-permute-start.45 = (bf16[64,4096]{1,0:T(8,128)(2,1)S(1)}, bf16[64,4096]{1,0:T(8,128)(2,1)S(1)}, u32[]{:S(2)}, u32[]{:S(2)}) collective-permute-start(bf16[64,4096]{1,0:T(8,128)(2,1)S(1)} %move_rows.18.refs_0_), channel_id=1, source_target_pairs={{0,8},{4,12},{8,0},{12,4},{1,9},{5,13},{9,1},{13,5},{2,10},{6,14},... | collective-permute-start | bytes 1572872 | tf_op jit(solution)/shard_map/ppermute | solution.py:31
  (38 other events, 333.0 us)

commit v8 on v7

--- a/solution.py
+++ b/solution.py
@@ -32,7 +32,15 @@
 
 
 def gather_near(x, axis):
-    return [x] + [swap(x, axis, d) for d in range(1, lax.axis_size(axis))]
+    return [x] + swap_each([x] * (lax.axis_size(axis) - 1), axis)
+
+
+def swap_each(pieces, axis):
+    return [swap(piece, axis, d + 1) for d, piece in enumerate(pieces)]
+
+
+def far_first(pieces):
+    return pieces[:1] + pieces[1:][::-1]
 
 
 def gather_plane(x, axis, after):
@@ -88,6 +96,12 @@
     return move_rows(arrays, moves, after)[0]
 
 
+def stack_line(pieces, after):
+    count, size = len(pieces), pieces[0].shape[0]
+    moves = [(i, 0, size, 0, (count - i if i else 0) * size) for i in range(count)]
+    return move_rows(far_first(pieces), moves, after)[0]
+
+
 def load_pieces(piece_refs, scratch, sems):
     copies = []
     start = 0
@@ -103,18 +117,24 @@
         copy.wait()
 
 
-def begin_kernel(count, tokens_ref, norm_ref, final_ref, *block_refs):
-    splits = len(block_refs)
-    own_rows = tokens_ref.shape[0] // (count * splits)
+def begin_kernel(count, splits, *refs):
+    block_refs, (tokens_scr, gains_scr, sems) = refs[3 : 3 + splits], refs[3 + splits :]
+    targets = [tokens_scr, gains_scr.at[0], gains_scr.at[1]]
+    copies = [pltpu.make_async_copy(refs[i], targets[i], sems.at[i]) for i in range(3)]
+    for copy in copies:
+        copy.start()
+    for copy in copies:
+        copy.wait()
+    own_rows = tokens_scr.shape[0] // (count * splits)
     for i in range(count):
         for h in range(splits):
             start = (i * splits + h) * own_rows
-            block_refs[h][i * own_rows : (i + 1) * own_rows, :] = tokens_ref[
+            block_refs[h][i * own_rows : (i + 1) * own_rows, :] = tokens_scr[
                 start : start + own_rows, :
             ]
     lines = []
-    for gain_ref in (norm_ref, final_ref):
-        gain = gain_ref[...]
+    for i in range(2):
+        gain = gains_scr[i]
         high = gain.astype(jnp.bfloat16).astype(jnp.float32)
         middle = (gain - high).astype(jnp.bfloat16).astype(jnp.float32)
         lines += [high, middle, gain - high - middle]
@@ -125,19 +145,27 @@
 def begin(tokens, norm_gain, final_gain, count, splits):
     rows, width = tokens.shape
     sizes = [rows // splits + (0 if h else 8) for h in range(splits)]
-    return small_call(
-        functools.partial(begin_kernel, count),
-        "begin",
-        [tokens, norm_gain.reshape(1, width), final_gain.reshape(1, width)],
-        [],
-        [((size, width), jnp.bfloat16) for size in sizes],
-        [],
-        4 * MIB,
+    return pl.pallas_call(
+        functools.partial(begin_kernel, count, splits),
+        out_shape=tuple(jax.ShapeDtypeStruct((size, width), jnp.bfloat16) for size in sizes),
+        in_specs=[anywhere()] * 3,
+        out_specs=(whole(),) * splits,
+        scratch_shapes=[
+            pltpu.VMEM((rows, width), jnp.bfloat16),
+            pltpu.VMEM((2, 1, width), jnp.float32),
+            pltpu.SemaphoreType.DMA((3,)),
+        ],
+        compiler_params=params(4 * MIB),
+        name="begin",
+    )(
+        pltpu.with_memory_space_constraint(tokens, pltpu.HBM),
+        pltpu.with_memory_space_constraint(norm_gain.reshape(1, width), pltpu.HBM),
+        pltpu.with_memory_space_constraint(final_gain.reshape(1, width), pltpu.HBM),
     )
 
 
 def norm_kernel(splits, part, count, after, *refs):
-    slices = refs[:count]
+    slices = refs[:1] + refs[1:count][::-1]
     routes_ref, weights_ref = refs[count : count + 2]
     rest = list(refs[count + 2 :])
     gains_in = rest.pop(0) if part else None
@@ -200,24 +228,23 @@
             flops=6 * rows * full_width, bytes_accessed=4 * rows * full_width, transcendentals=rows
         ),
         name="norm_rows",
-    )(*slices, routes, route_weights, *gains, *after)
+    )(*far_first(slices), routes, route_weights, *gains, *after)
 
 
 def hidden_kernel(pieces, after, tile, first, steps, *refs):
     piece_refs = refs[:pieces]
     weight_refs = refs[pieces : pieces + 2]
-    out_ref, rows_scr, route_scr, weight_scr, work, sems, weight_sems = refs[pieces + 2 + after :]
+    out_ref, rows_scr, route_scr, weight_scr, sems, weight_sems = refs[pieces + 2 + after :]
     full_width = weight_scr.shape[2]
 
     def fetch(i, act):
-        slot = lax.rem(i, 2)
-        columns = pl.ds(pl.multiple_of((first + i) * tile, tile), tile)
+        columns = pl.ds((first + i) * tile, tile)
         for j in range(2):
             act(
                 pltpu.make_async_copy(
                     weight_refs[j].at[0, :, columns],
-                    weight_scr.at[j, slot],
-                    weight_sems.at[j, slot],
+                    weight_scr.at[j, i % 2],
+                    weight_sems.at[j, i % 2],
                 )
             )
 
@@ -226,18 +253,6 @@
 
     def wait(copy):
         copy.wait()
-
-    def dots(i):
-        rows = rows_scr[:, :full_width]
-        slot = lax.rem(i, 2)
-        for j in range(2):
-            work[j] = jnp.dot(rows, weight_scr[j, slot], preferred_element_type=jnp.float32)
-
-    def finish(i):
-        gate, up = work[0], work[1]
-        hidden = gate * (1.0 + jnp.tanh(0.5 * gate)) * up * route_scr[:, :1]
-        columns = pl.ds(pl.multiple_of(i * tile, tile), tile)
-        out_ref[:, columns] = hidden.astype(jnp.bfloat16)
 
     fetch(0, start)
     load_pieces(piece_refs, rows_scr, sems)
@@ -247,23 +262,15 @@
     mine = (lane >= place) & (lane < place + 3)
     weight = jnp.sum(jnp.where(mine, small, 0.0), axis=1, keepdims=True)
     route_scr[...] = jnp.broadcast_to(0.5 * weight, route_scr.shape)
-    fetch(0, wait)
-    if steps > 1:
-        fetch(1, start)
-    dots(0)
-
-    @pl.loop(1, steps)
-    def _(i):
+    for i in range(steps):
         fetch(i, wait)
-
-        @pl.when(i + 1 < steps)
-        def _():
+        if i + 1 < steps:
             fetch(i + 1, start)
-
-        finish(i - 1)
-        dots(i)
-
-    finish(steps - 1)
+        rows = rows_scr[:, :full_width]
+        gate = jnp.dot(rows, weight_scr[0, i % 2], preferred_element_type=jnp.float32)
+        up = jnp.dot(rows, weight_scr[1, i % 2], preferred_element_type=jnp.float32)
+        hidden = gate * (1.0 + jnp.tanh(0.5 * gate)) * up * route_scr[:, :1]
+        out_ref[:, i * tile : (i + 1) * tile] = hidden.astype(jnp.bfloat16)
 
 
 def tile_of(weight):
@@ -284,7 +291,6 @@
             pltpu.VMEM((rows, full_width + LANES), jnp.bfloat16),
             pltpu.VMEM((rows, LANES), jnp.float32),
             pltpu.VMEM((2, 2, full_width, tile), jnp.bfloat16),
-            pltpu.VMEM((2, rows, tile), jnp.float32),
             pltpu.SemaphoreType.DMA((len(pieces),)),
             pltpu.SemaphoreType.DMA((2, 2)),
         ],
@@ -400,7 +406,7 @@
 
     def fetch(i):
         return pltpu.make_async_copy(
-            head_ref.at[pl.ds(pl.multiple_of(i * tile, tile), tile), :],
+            head_ref.at[pl.ds(i * tile, tile), :],
             head_scr.at[i],
             head_sems.at[i],
         )
@@ -418,8 +424,7 @@
                 )
             )
     ahead = min(2, steps)
-    for i in range(1):
-        fetch(i).start()
+    fetch(0).start()
     for copy in copies:
         copy.start()
     for i in range(1, ahead):
@@ -430,14 +435,10 @@
     out_ref[...] = jnp.where(lane == 0, -jnp.inf, 0.0)
     targets = target_ref[...] - (my_expert * n_tensor + my_tensor) * vocab_part
 
-    @pl.loop(0, steps)
-    def _(i):
+    for i in range(steps):
         fetch(i).wait()
-
-        @pl.when(i + ahead < steps)
-        def _():
+        if i + ahead < steps:
             fetch(i + ahead).start()
-
         logits = lax.dot_general(
             head_scr[i],
             rows_scr[...],
@@ -633,7 +634,7 @@
     before = {}
     for h in range(splits):
         if 2 * n_expert * rows <= LARGEST:
-            nearer = stack_rows(planes[h][:3], [] if before else sum((p[1:] for p in slices[1:2]), []))
+            nearer = stack_rows(planes[h][:3], [] if before else sum((p[:0:-1] for p in slices[1:2]), []))
             away = [swap(nearer, "seq", 1)]
             if planes[h][3:]:
                 away.append(swap(stack_rows(planes[h][3:], before.get("kept", [])), "seq", 1))
@@ -650,7 +651,7 @@
                 for i in range(len(cuts) - 1)
             ]
             later = planes[h + 1][1:3] if h + 1 < splits else []
-            other = down_rows(hidden, w_down, half, half, later + before.get("sums", []))
+            other = down_rows(hidden, w_down, half, half, later + before.get("sums", [])[::-1])
             kept = down_rows(hidden, w_down, 0, half, before.get("final", []))
         else:
             away = [swap(p, "seq", 1) for p in planes[h]]
@@ -658,15 +659,15 @@
                 away, w_gate, w_up, w_down
             )
         got = swap(other, "seq", 1)
-        totals, packed, passed = sum_plane(kept, got, rows, before.get("column", []))
-        sums = [swap(totals[d], "tensor", d) for d in range(1, n_tensor)]
+        totals, packed, passed = sum_plane(kept, got, rows, before.get("column", [])[::-1])
+        sums = swap_each(totals[1:], "tensor")
         cut = []
         if before:
-            column = stack_rows([before["final"][0]] + before["column"], totals[:1])
+            column = stack_line(before["final"] + before["column"], totals[:1])
             plane, cut = gather_plane(column, "expert", [])
             wanted = target_rows[:, :, h - 1].reshape(1, -1)
             terms.append(head_terms(plane, head_rows, wanted, sub))
-        final = final_rows(totals[:1] + sums, raws[h], gains, [])
+        final = final_rows(far_first(totals[:1] + sums), raws[h], gains, [])
         column = gather_near(final, "tensor")
         before = {
             "kept": [kept],
@@ -677,7 +678,7 @@
             "final": [final],
             "column": column[1:],
         }
-    column = stack_rows(column, cut)
+    column = stack_line(column, cut)
     plane, _ = gather_plane(column, "expert", terms[-1:])
     wanted = target_rows[:, :, splits - 1].reshape(1, -1)
     terms.append(head_terms(plane, head_rows, wanted, sub))

time: 234 us -> 236 us (level)
  Pallas kernels: 86.1 us -> 94.3 us
  waiting for transfers between devices: 76.7 us -> 73 us
  starting transfers between devices: 64.4 us -> 61.8 us
    pallas_call x2, Pallas kernels: 19.1 us -> 25.9 us  [head_terms(): pl.pallas_call(functools.partial(head_kernel, len(pieces), tile, sub), ou...]
    ppermute x54, waiting for transfers between devices: 76.7 us -> 73 us  [swap(): return lax.ppermute(x, axis, [(i, i ^ distance) for i in range(size)])]
    ppermute x54, starting transfers between devices: 64.4 us -> 61.8 us  [swap(): return lax.ppermute(x, axis, [(i, i ^ distance) for i in range(size)])]
  transfers between devices with their start and end apart: 54 -> 54, of which waited for: 25 -> 27; matrix products, arithmetic and copies ran while one was open for 1% -> 1% of each run, Pallas kernels for 28% -> 30%
where the time goes in v8:
time: 236 us; the launch traced here: 234 us
  Pallas kernels  94.3 us (40%)
  waiting for transfers between devices  73 us (31%)
  starting transfers between devices  61.8 us (26%)
  local copies, waits for them, and re-layouts  3.16 us (1%)
    ppermute x54, waiting for transfers between devices, swap(): return lax.ppermute(x, axis, [(i, i ^ distance) for i in range(size)])  73 us
    ppermute x54, starting transfers between devices, swap(): return lax.ppermute(x, axis, [(i, i ^ distance) for i in range(size)])  61.8 us
    pallas_call x4, Pallas kernels, hidden_rows(): pl.pallas_call(functools.partial(hidden_kernel, len(pieces), len(after),...  42.9 us
    pallas_call x2, Pallas kernels, head_terms(): pl.pallas_call(functools.partial(head_kernel, len(pieces), tile, sub), ou...  25.9 us
    pallas_call x4, Pallas kernels, down_rows(): pl.pallas_call(functools.partial(down_kernel, start, len(hidden)), out_sh...  16.3 us
  transfers between devices with their start and end apart: 54, of which 27 were waited for; matrix products, arithmetic and copies ran while one was open for 1% of the time, Pallas kernels for 30%

profile of v8, /device:TPU:0, one launch (start us, length us, event | category | flops | bytes accessed | tf_op | source)
XLA Modules:
  0.0 233.7 jit_solution(3613287334111991226)
XLA Ops:
  1.0 5.1 %collective-permute-start = (bf16[72,1024]{1,0:T(8,128)(2,1)S(1)}, bf16[72,1024]{1,0:T(8,128)(2,1)S(1)}, u32[]{:S(2)}, u32[]{:S(2)}) collective-permute-start(bf16[72,1024]{1,0:T(8,128)(2,1)S(1)} %get-tuple-element.40.refs_0_), channel_id=1, source_target_pairs={{0,3},{1,2},{2,1},{3,0},{4,7},{5,6},{6,5},{7,4},{8,11},{9,10},{10,... | collective-permute-start | bytes 442376 | tf_op jit(solution)/shard_map/ppermute | solution.py:31
  10.9 7.7 %collective-permute-done.1.refs_2_ = bf16[72,1024]{1,0:T(8,128)(2,1)S(1)} collective-permute-done((bf16[72,1024]{1,0:T(8,128)(2,1)S(1)}, bf16[72,1024]{1,0:T(8,128)(2,1)S(1)}, u32[]{:S(2)}, u32[]{:S(2)}) %collective-permute-start.1) | collective-permute-done | bytes 147488 | tf_op jit(solution)/shard_map/ppermute | solution.py:31
  26.4 3.8 %collective-permute-done.7.refs_3_.refs_1_ = bf16[64,1024]{1,0:T(8,128)(2,1)S(1)} collective-permute-done((bf16[64,1024]{1,0:T(8,128)(2,1)S(1)}, bf16[64,1024]{1,0:T(8,128)(2,1)S(1)}, u32[]{:S(2)}, u32[]{:S(2)}) %collective-permute-start.7) | collective-permute-done | bytes 131104 | tf_op jit(solution)/shard_map/ppermute | solution.py:31
  30.3 4.3 %collective-permute-done.8.refs_4_.refs_2_ = bf16[64,1024]{1,0:T(8,128)(2,1)S(1)} collective-permute-done((bf16[64,1024]{1,0:T(8,128)(2,1)S(1)}, bf16[64,1024]{1,0:T(8,128)(2,1)S(1)}, u32[]{:S(2)}, u32[]{:S(2)}) %collective-permute-start.8) | collective-permute-done | bytes 131104 | tf_op jit(solution)/shard_map/ppermute | solution.py:31
  36.1 7.8 %collective-permute-done.5.refs_0_.refs_3_.refs_7_ = bf16[32,4224]{1,0:T(8,128)(2,1)S(1)} collective-permute-done((bf16[32,4224]{1,0:T(8,128)(2,1)S(1)}, bf16[32,4224]{1,0:T(8,128)(2,1)S(1)}, u32[]{:S(2)}, u32[]{:S(2)}) %collective-permute-start.5) | collective-permute-done | bytes 270368 | tf_op jit(solution)/shard_map/ppermute | solution.py:31
  46.8 19.5 %hidden_rows.4.refs_0_ = bf16[512,1792]{1,0:T(8,128)(2,1)S(1)} custom-call(bf16[64,4224]{1,0:T(8,128)(2,1)S(1)} %get-tuple-element.41.refs_0_, bf16[64,4224]{1,0:T(8,128)(2,1)S(1)} %collective-permute-done.3.refs_1_, bf16[64,4224]{1,0:T(8,128)(2,1)S(1)} %collective-permute-done.4.refs_0_.refs_2_, ...), custom_call_target="tpu_custom_call" | custom-call | flops 15032385536 | bytes 35389440 | tf_op jit(solution)/shard_map/hidden_rows/pallas_call | solution.py:285
  66.4 4.5 %down_rows.5 = bf16[256,4096]{1,0:T(8,128)(2,1)S(1)} custom-call(bf16[512,1792]{1,0:T(8,128)(2,1)S(1)} %hidden_rows.4.refs_0_, bf16[1,1792,4096]{2,1,0:T(8,128)(2,1)S(1)} %bitcast.33, bf16[64,4224]{1,0:T(8,128)(2,1)S(1)} %collective-permute-done.12.refs_2_.refs_1_, bf16[64,4224]{1,0:T(8,128)(2,1)S(1)} %collective-permute-done.13.refs_3_.refs_0_.refs_2_), custom_call_target="tpu_custom_call" | custom-call | flops 3758096384 | bytes 3014656 | tf_op jit(solution)/shard_map/down_rows/pallas_call | solution.py:329
  73.9 3.9 %down_rows.4.kept_ref.refs_2_ = bf16[256,4096]{1,0:T(8,128)(2,1)S(1)} custom-call(bf16[512,1792]{1,0:T(8,128)(2,1)S(1)} %hidden_rows.4.refs_0_, bf16[1,1792,4096]{2,1,0:T(8,128)(2,1)S(1)} %bitcast.33), custom_call_target="tpu_custom_call" | custom-call | flops 3758096384 | bytes 3014656 | tf_op jit(solution)/shard_map/down_rows/pallas_call | solution.py:329
  84.2 11.7 %hidden_rows.5.refs_0_ = bf16[512,1024]{1,0:T(8,128)(2,1)S(1)} custom-call(bf16[64,4224]{1,0:T(8,128)(2,1)S(1)} %get-tuple-element.46.refs_0_, bf16[64,4224]{1,0:T(8,128)(2,1)S(1)} %collective-permute-done.12.refs_2_.refs_1_, bf16[64,4224]{1,0:T(8,128)(2,1)S(1)} %collective-permute-done.13.refs_3_.refs_0_.refs_2_, ...), custom_call_target="tpu_custom_call" | custom-call | flops 8589934592 | bytes 22020096 | tf_op jit(solution)/shard_map/hidden_rows/pallas_call | solution.py:285
  99.3 7.0 %hidden_rows.6.refs_1_ = bf16[512,512]{1,0:T(8,128)(2,1)S(1)} custom-call(bf16[64,4224]{1,0:T(8,128)(2,1)S(1)} %get-tuple-element.46.refs_0_, bf16[64,4224]{1,0:T(8,128)(2,1)S(1)} %collective-permute-done.12.refs_2_.refs_1_, bf16[64,4224]{1,0:T(8,128)(2,1)S(1)} %collective-permute-done.13.refs_3_.refs_0_.refs_2_, ...), custom_call_target="tpu_custom_call" | custom-call | flops 4294967296 | bytes 13107200 | tf_op jit(solution)/shard_map/hidden_rows/pallas_call | solution.py:285
  111.1 4.7 %hidden_rows.7.refs_2_ = bf16[512,256]{1,0:T(8,128)(2,1)S(1)} custom-call(bf16[64,4224]{1,0:T(8,128)(2,1)S(1)} %get-tuple-element.46.refs_0_, bf16[64,4224]{1,0:T(8,128)(2,1)S(1)} %collective-permute-done.12.refs_2_.refs_1_, bf16[64,4224]{1,0:T(8,128)(2,1)S(1)} %collective-permute-done.13.refs_3_.refs_0_.refs_2_, ...), custom_call_target="tpu_custom_call" | custom-call | flops 2147483648 | bytes 8650752 | tf_op jit(solution)/shard_map/hidden_rows/pallas_call | solution.py:285
  115.8 3.3 %collective-permute-done.20.refs_2_.refs_5_ = bf16[16,4096]{1,0:T(8,128)(2,1)S(1)} collective-permute-done((bf16[16,4096]{1,0:T(8,128)(2,1)S(1)}, bf16[16,4096]{1,0:T(8,128)(2,1)S(1)}, u32[]{:S(2)}, u32[]{:S(2)}) %collective-permute-start.20) | collective-permute-done | bytes 131104 | tf_op jit(solution)/shard_map/ppermute | solution.py:31
  119.1 3.9 %down_rows.7 = bf16[256,4096]{1,0:T(8,128)(2,1)S(1)} custom-call(bf16[512,1024]{1,0:T(8,128)(2,1)S(1)} %hidden_rows.5.refs_0_, bf16[512,512]{1,0:T(8,128)(2,1)S(1)} %hidden_rows.6.refs_1_, bf16[512,256]{1,0:T(8,128)(2,1)S(1)} %hidden_rows.7.refs_2_, bf16[1,1792,4096]{2,1,0:T(8,128)(2,1)S(1)} %bitcast.33, ...), custom_call_target="tpu_custom_call" | custom-call | flops 3758096384 | bytes 3014656 | tf_op jit(solution)/shard_map/down_rows/pallas_call | solution.py:329
  124.6 3.9 %down_rows.6.kept_ref = bf16[256,4096]{1,0:T(8,128)(2,1)S(1)} custom-call(bf16[512,1024]{1,0:T(8,128)(2,1)S(1)} %hidden_rows.5.refs_0_, bf16[512,512]{1,0:T(8,128)(2,1)S(1)} %hidden_rows.6.refs_1_, bf16[512,256]{1,0:T(8,128)(2,1)S(1)} %hidden_rows.7.refs_2_, bf16[1,1792,4096]{2,1,0:T(8,128)(2,1)S(1)} %bitcast.33, bf16[16,4096]{1,0:T(8,128)(2,1)S(1)} %final_rows.2.refs_4_.refs_0_), custom_call_target="tpu_custom_call" | custom-call | flops 3758096384 | bytes 3014656 | tf_op jit(solution)/shard_map/down_rows/pallas_call | solution.py:329
  132.7 2.8 %collective-permute-start.24 = (bf16[16,4096]{1,0:T(8,128)(2,1)S(1)}, bf16[16,4096]{1,0:T(8,128)(2,1)S(1)}, u32[]{:S(2)}, u32[]{:S(2)}) collective-permute-start(bf16[16,4096]{1,0:T(8,128)(2,1)S(1)} %final_rows.2.refs_4_.refs_0_), channel_id=1, source_target_pairs={{0,1},{1,0},{2,3},{3,2},{4,5},{5,4},{6,7},{7,6},{8,9},{9,8},{10,11... | collective-permute-start | bytes 393224 | tf_op jit(solution)/shard_map/ppermute | solution.py:31
  135.5 3.9 %collective-permute-done.22.refs_0_.refs_1_ = bf16[16,4096]{1,0:T(8,128)(2,1)S(1)} collective-permute-done((bf16[16,4096]{1,0:T(8,128)(2,1)S(1)}, bf16[16,4096]{1,0:T(8,128)(2,1)S(1)}, u32[]{:S(2)}, u32[]{:S(2)}) %collective-permute-start.22) | collective-permute-done | bytes 131104 | tf_op jit(solution)/shard_map/ppermute | solution.py:31
  139.4 4.4 %collective-permute-done.23.refs_1_.refs_2_ = bf16[16,4096]{1,0:T(8,128)(2,1)S(1)} collective-permute-done((bf16[16,4096]{1,0:T(8,128)(2,1)S(1)}, bf16[16,4096]{1,0:T(8,128)(2,1)S(1)}, u32[]{:S(2)}, u32[]{:S(2)}) %collective-permute-start.23) | collective-permute-done | bytes 131104 | tf_op jit(solution)/shard_map/ppermute | solution.py:31
  146.5 5.7 %collective-permute-done.32.last_one_ref = bf16[32,4096]{1,0:T(8,128)(2,1)S(1)} collective-permute-done((bf16[32,4096]{1,0:T(8,128)(2,1)S(1)}, bf16[32,4096]{1,0:T(8,128)(2,1)S(1)}, u32[]{:S(2)}, u32[]{:S(2)}) %collective-permute-start.32) | collective-permute-done | bytes 262176 | tf_op jit(solution)/shard_map/ppermute | solution.py:31
  160.6 3.8 %collective-permute-done.38.refs_1_ = bf16[16,4096]{1,0:T(8,128)(2,1)S(1)} collective-permute-done((bf16[16,4096]{1,0:T(8,128)(2,1)S(1)}, bf16[16,4096]{1,0:T(8,128)(2,1)S(1)}, u32[]{:S(2)}, u32[]{:S(2)}) %collective-permute-start.38) | collective-permute-done | bytes 131104 | tf_op jit(solution)/shard_map/ppermute | solution.py:31
  164.4 3.7 %collective-permute-done.39.refs_2_ = bf16[16,4096]{1,0:T(8,128)(2,1)S(1)} collective-permute-done((bf16[16,4096]{1,0:T(8,128)(2,1)S(1)}, bf16[16,4096]{1,0:T(8,128)(2,1)S(1)}, u32[]{:S(2)}, u32[]{:S(2)}) %collective-permute-start.39) | collective-permute-done | bytes 131104 | tf_op jit(solution)/shard_map/ppermute | solution.py:31
  177.7 3.8 %collective-permute-done.42.refs_2_ = bf16[16,4096]{1,0:T(8,128)(2,1)S(1)} collective-permute-done((bf16[16,4096]{1,0:T(8,128)(2,1)S(1)}, bf16[16,4096]{1,0:T(8,128)(2,1)S(1)}, u32[]{:S(2)}, u32[]{:S(2)}) %collective-permute-start.42) | collective-permute-done | bytes 131104 | tf_op jit(solution)/shard_map/ppermute | solution.py:31
  184.9 12.7 %head_terms.2.refs_2_ = f32[8,256]{1,0:T(8,128)S(1)} custom-call(bf16[64,4096]{1,0:T(8,128)(2,1)S(1)} %move_rows.16.refs_0_, bf16[64,4096]{1,0:T(8,128)(2,1)S(1)} %collective-permute-done.34.refs_1_, bf16[64,4096]{1,0:T(8,128)(2,1)S(1)} %collective-permute-done.35.refs_0_.refs_2_, bf16[32,4096]{1,0:T(8,128)(2,1)S(1)} %collective-permute-done.36.refs_3_, ...), custom_call_target="tpu_custom_call" | custom-call | flops 4194304000 | bytes 18481152 | tf_op jit(solution)/shard_map/head_terms/pallas_call | solution.py:463
  199.7 5.7 %collective-permute-done.46.refs_3_ = bf16[32,4096]{1,0:T(8,128)(2,1)S(1)} collective-permute-done((bf16[32,4096]{1,0:T(8,128)(2,1)S(1)}, bf16[32,4096]{1,0:T(8,128)(2,1)S(1)}, u32[]{:S(2)}, u32[]{:S(2)}) %collective-permute-start.46) | collective-permute-done | bytes 262176 | tf_op jit(solution)/shard_map/ppermute | solution.py:31
  205.8 13.2 %head_terms.3 = f32[8,256]{1,0:T(8,128)S(1)} custom-call(bf16[64,4096]{1,0:T(8,128)(2,1)S(1)} %move_rows.18.refs_0_, bf16[64,4096]{1,0:T(8,128)(2,1)S(1)} %collective-permute-done.44.refs_1_, bf16[64,4096]{1,0:T(8,128)(2,1)S(1)} %collective-permute-done.45.refs_0_.refs_2_, bf16[32,4096]{1,0:T(8,128)(2,1)S(1)} %collective-permute-done.46.refs_3_, ...), custom_call_target="tpu_custom_call" | custom-call | flops 4194304000 | bytes 18481152 | tf_op jit(solution)/shard_map/head_terms/pallas_call | solution.py:463
  (159 shorter events, 82.0 us)
Async XLA Ops:
  6.2 12.5 %collective-permute-start.1 = (bf16[72,1024]{1,0:T(8,128)(2,1)S(1)}, bf16[72,1024]{1,0:T(8,128)(2,1)S(1)}, u32[]{:S(2)}, u32[]{:S(2)}) collective-permute-start(bf16[72,1024]{1,0:T(8,128)(2,1)S(1)} %get-tuple-element.40.refs_0_), channel_id=1, source_target_pairs={{0,2},{1,3},{2,0},{3,1},{4,6},{5,7},{6,4},{7,5},{8,10},{9,11},{10,... | collective-permute-start | bytes 442376 | tf_op jit(solution)/shard_map/ppermute | solution.py:31
  6.2 12.5 %collective-permute-start.2 = (bf16[72,1024]{1,0:T(8,128)(2,1)S(1)}, bf16[72,1024]{1,0:T(8,128)(2,1)S(1)}, u32[]{:S(2)}, u32[]{:S(2)}) collective-permute-start(bf16[72,1024]{1,0:T(8,128)(2,1)S(1)} %get-tuple-element.40.refs_0_), channel_id=1, source_target_pairs={{0,1},{1,0},{2,3},{3,2},{4,5},{5,4},{6,7},{7,6},{8,9},{9,8},{10,11... | collective-permute-start | bytes 442376 | tf_op jit(solution)/shard_map/ppermute | solution.py:31
  19.0 15.6 %collective-permute-start.3 = (bf16[64,4224]{1,0:T(8,128)(2,1)S(1)}, bf16[64,4224]{1,0:T(8,128)(2,1)S(1)}, u32[]{:S(2)}, u32[]{:S(2)}) collective-permute-start(bf16[64,4224]{1,0:T(8,128)(2,1)S(1)} %get-tuple-element.41.refs_0_), channel_id=1, source_target_pairs={{0,4},{4,0},{8,12},{12,8},{1,5},{5,1},{9,13},{13,9},{2,6},{6,2},{1... | collective-permute-start | bytes 1622024 | tf_op jit(solution)/shard_map/ppermute | solution.py:31
  20.5 14.1 %collective-permute-start.4 = (bf16[64,4224]{1,0:T(8,128)(2,1)S(1)}, bf16[64,4224]{1,0:T(8,128)(2,1)S(1)}, u32[]{:S(2)}, u32[]{:S(2)}) collective-permute-start(bf16[64,4224]{1,0:T(8,128)(2,1)S(1)} %get-tuple-element.41.refs_0_), channel_id=1, source_target_pairs={{0,8},{4,12},{8,0},{12,4},{1,9},{5,13},{9,1},{13,5},{2,10},{6,14},... | collective-permute-start | bytes 1622024 | tf_op jit(solution)/shard_map/ppermute | solution.py:31
  34.8 12.0 %collective-permute-start.10 = (bf16[192,4224]{1,0:T(8,128)(2,1)S(1)}, bf16[192,4224]{1,0:T(8,128)(2,1)S(1)}, u32[]{:S(2)}, u32[]{:S(2)}) collective-permute-start(bf16[192,4224]{1,0:T(8,128)(2,1)S(1)} %move_rows.11), channel_id=1, source_target_pairs={{0,16},{16,0},{1,17},{17,1},{2,18},{18,2},{3,19},{19,3},{4,20},{20... | collective-permute-start | bytes 4866056 | tf_op jit(solution)/shard_map/ppermute | solution.py:31
  44.7 21.6 %collective-permute-start.12 = (bf16[64,4224]{1,0:T(8,128)(2,1)S(1)}, bf16[64,4224]{1,0:T(8,128)(2,1)S(1)}, u32[]{:S(2)}, u32[]{:S(2)}) collective-permute-start(bf16[64,4224]{1,0:T(8,128)(2,1)S(1)} %get-tuple-element.46.refs_0_), channel_id=1, source_target_pairs={{0,4},{4,0},{8,12},{12,8},{1,5},{5,1},{9,13},{13,9},{2,6},{6,2},{1... | collective-permute-start | bytes 1622024 | tf_op jit(solution)/shard_map/ppermute | solution.py:31
  46.3 20.0 %collective-permute-start.13 = (bf16[64,4224]{1,0:T(8,128)(2,1)S(1)}, bf16[64,4224]{1,0:T(8,128)(2,1)S(1)}, u32[]{:S(2)}, u32[]{:S(2)}) collective-permute-start(bf16[64,4224]{1,0:T(8,128)(2,1)S(1)} %get-tuple-element.46.refs_0_), channel_id=1, source_target_pairs={{0,8},{4,12},{8,0},{12,4},{1,9},{5,13},{9,1},{13,5},{2,10},{6,14},... | collective-permute-start | bytes 1622024 | tf_op jit(solution)/shard_map/ppermute | solution.py:31
  70.9 11.0 %collective-permute-start.14 = (bf16[256,4096]{1,0:T(8,128)(2,1)S(1)}, bf16[256,4096]{1,0:T(8,128)(2,1)S(1)}, u32[]{:S(2)}, u32[]{:S(2)}) collective-permute-start(bf16[256,4096]{1,0:T(8,128)(2,1)S(1)} %down_rows.5), channel_id=1, source_target_pairs={{0,16},{16,0},{1,17},{17,1},{2,18},{18,2},{3,19},{19,3},{4,20},{20... | collective-permute-start | bytes 6291464 | tf_op jit(solution)/shard_map/ppermute | solution.py:31
  71.6 12.6 %collective-permute-start.27 = (bf16[192,4224]{1,0:T(8,128)(2,1)S(1)}, bf16[192,4224]{1,0:T(8,128)(2,1)S(1)}, u32[]{:S(2)}, u32[]{:S(2)}) collective-permute-start(bf16[192,4224]{1,0:T(8,128)(2,1)S(1)} %move_rows.14), channel_id=1, source_target_pairs={{0,16},{16,0},{1,17},{17,1},{2,18},{18,2},{3,19},{19,3},{4,20},{20... | collective-permute-start | bytes 4866056 | tf_op jit(solution)/shard_map/ppermute | solution.py:31
  82.3 14.4 %collective-permute-start.15 = (bf16[64,4096]{1,0:T(8,128)(2,1)S(1)}, bf16[64,4096]{1,0:T(8,128)(2,1)S(1)}, u32[]{:S(2)}, u32[]{:S(2)}) collective-permute-start(bf16[64,4096]{1,0:T(8,128)(2,1)S(1)} %get-tuple-element.48.refs_9_), channel_id=1, source_target_pairs={{0,4},{4,0},{8,12},{12,8},{1,5},{5,1},{9,13},{13,9},{2,6},{6,2},{1... | collective-permute-start | bytes 1572872 | tf_op jit(solution)/shard_map/ppermute | solution.py:31
  83.1 14.0 %collective-permute-start.16 = (bf16[64,4096]{1,0:T(8,128)(2,1)S(1)}, bf16[64,4096]{1,0:T(8,128)(2,1)S(1)}, u32[]{:S(2)}, u32[]{:S(2)}) collective-permute-start(bf16[64,4096]{1,0:T(8,128)(2,1)S(1)} %get-tuple-element.49.refs_10_), channel_id=1, source_target_pairs={{0,8},{4,12},{8,0},{12,4},{1,9},{5,13},{9,1},{13,5},{2,10},{6,14},... | collective-permute-start | bytes 1572872 | tf_op jit(solution)/shard_map/ppermute | solution.py:31
  108.8 10.2 %collective-permute-start.20 = (bf16[16,4096]{1,0:T(8,128)(2,1)S(1)}, bf16[16,4096]{1,0:T(8,128)(2,1)S(1)}, u32[]{:S(2)}, u32[]{:S(2)}) collective-permute-start(bf16[16,4096]{1,0:T(8,128)(2,1)S(1)} %get-tuple-element.55.refs_11_), channel_id=1, source_target_pairs={{0,2},{1,3},{2,0},{3,1},{4,6},{5,7},{6,4},{7,5},{8,10},{9,11},{10,... | collective-permute-start | bytes 393224 | tf_op jit(solution)/shard_map/ppermute | solution.py:31
  108.8 10.2 %collective-permute-start.21 = (bf16[16,4096]{1,0:T(8,128)(2,1)S(1)}, bf16[16,4096]{1,0:T(8,128)(2,1)S(1)}, u32[]{:S(2)}, u32[]{:S(2)}) collective-permute-start(bf16[16,4096]{1,0:T(8,128)(2,1)S(1)} %get-tuple-element.56.refs_10_), channel_id=1, source_target_pairs={{0,1},{1,0},{2,3},{3,2},{4,5},{5,4},{6,7},{7,6},{8,9},{9,8},{10,11... | collective-permute-start | bytes 393224 | tf_op jit(solution)/shard_map/ppermute | solution.py:31
  129.0 14.8 %collective-permute-start.30 = (bf16[64,4096]{1,0:T(8,128)(2,1)S(1)}, bf16[64,4096]{1,0:T(8,128)(2,1)S(1)}, u32[]{:S(2)}, u32[]{:S(2)}) collective-permute-start(bf16[64,4096]{1,0:T(8,128)(2,1)S(1)} %get-tuple-element.61), channel_id=1, source_target_pairs={{0,4},{4,0},{8,12},{12,8},{1,5},{5,1},{9,13},{13,9},{2,6},{6,2},{1... | collective-permute-start | bytes 1572872 | tf_op jit(solution)/shard_map/ppermute | solution.py:31
  130.2 14.0 %collective-permute-start.31 = (bf16[64,4096]{1,0:T(8,128)(2,1)S(1)}, bf16[64,4096]{1,0:T(8,128)(2,1)S(1)}, u32[]{:S(2)}, u32[]{:S(2)}) collective-permute-start(bf16[64,4096]{1,0:T(8,128)(2,1)S(1)} %get-tuple-element.62), channel_id=1, source_target_pairs={{0,8},{4,12},{8,0},{12,4},{1,9},{5,13},{9,1},{13,5},{2,10},{6,14},... | collective-permute-start | bytes 1572872 | tf_op jit(solution)/shard_map/ppermute | solution.py:31
  132.7 11.2 %collective-permute-start.23 = (bf16[16,4096]{1,0:T(8,128)(2,1)S(1)}, bf16[16,4096]{1,0:T(8,128)(2,1)S(1)}, u32[]{:S(2)}, u32[]{:S(2)}) collective-permute-start(bf16[16,4096]{1,0:T(8,128)(2,1)S(1)} %final_rows.2.refs_4_.refs_0_), channel_id=1, source_target_pairs={{0,2},{1,3},{2,0},{3,1},{4,6},{5,7},{6,4},{7,5},{8,10},{9,11},{10,... | collective-permute-start | bytes 393224 | tf_op jit(solution)/shard_map/ppermute | solution.py:31
  132.7 11.2 %collective-permute-start.24 = (bf16[16,4096]{1,0:T(8,128)(2,1)S(1)}, bf16[16,4096]{1,0:T(8,128)(2,1)S(1)}, u32[]{:S(2)}, u32[]{:S(2)}) collective-permute-start(bf16[16,4096]{1,0:T(8,128)(2,1)S(1)} %final_rows.2.refs_4_.refs_0_), channel_id=1, source_target_pairs={{0,1},{1,0},{2,3},{3,2},{4,5},{5,4},{6,7},{7,6},{8,9},{9,8},{10,11... | collective-permute-start | bytes 393224 | tf_op jit(solution)/shard_map/ppermute | solution.py:31
  154.3 19.5 %collective-permute-start.34 = (bf16[64,4096]{1,0:T(8,128)(2,1)S(1)}, bf16[64,4096]{1,0:T(8,128)(2,1)S(1)}, u32[]{:S(2)}, u32[]{:S(2)}) collective-permute-start(bf16[64,4096]{1,0:T(8,128)(2,1)S(1)} %move_rows.16.refs_0_), channel_id=1, source_target_pairs={{0,4},{4,0},{8,12},{12,8},{1,5},{5,1},{9,13},{13,9},{2,6},{6,2},{1... | collective-permute-start | bytes 1572872 | tf_op jit(solution)/shard_map/ppermute | solution.py:31
  155.1 18.7 %collective-permute-start.35 = (bf16[64,4096]{1,0:T(8,128)(2,1)S(1)}, bf16[64,4096]{1,0:T(8,128)(2,1)S(1)}, u32[]{:S(2)}, u32[]{:S(2)}) collective-permute-start(bf16[64,4096]{1,0:T(8,128)(2,1)S(1)} %move_rows.16.refs_0_), channel_id=1, source_target_pairs={{0,8},{4,12},{8,0},{12,4},{1,9},{5,13},{9,1},{13,5},{2,10},{6,14},... | collective-permute-start | bytes 1572872 | tf_op jit(solution)/shard_map/ppermute | solution.py:31
  171.5 10.1 %collective-permute-start.42 = (bf16[16,4096]{1,0:T(8,128)(2,1)S(1)}, bf16[16,4096]{1,0:T(8,128)(2,1)S(1)}, u32[]{:S(2)}, u32[]{:S(2)}) collective-permute-start(bf16[16,4096]{1,0:T(8,128)(2,1)S(1)} %final_rows.3.refs_0_), channel_id=1, source_target_pairs={{0,2},{1,3},{2,0},{3,1},{4,6},{5,7},{6,4},{7,5},{8,10},{9,11},{10,... | collective-permute-start | bytes 393224 | tf_op jit(solution)/shard_map/ppermute | solution.py:31
  171.5 10.1 %collective-permute-start.43 = (bf16[16,4096]{1,0:T(8,128)(2,1)S(1)}, bf16[16,4096]{1,0:T(8,128)(2,1)S(1)}, u32[]{:S(2)}, u32[]{:S(2)}) collective-permute-start(bf16[16,4096]{1,0:T(8,128)(2,1)S(1)} %final_rows.3.refs_0_), channel_id=1, source_target_pairs={{0,1},{1,0},{2,3},{3,2},{4,5},{5,4},{6,7},{7,6},{8,9},{9,8},{10,11... | collective-permute-start | bytes 393224 | tf_op jit(solution)/shard_map/ppermute | solution.py:31
  174.7 10.2 %collective-permute-start.36 = (bf16[32,4096]{1,0:T(8,128)(2,1)}, bf16[32,4096]{1,0:T(8,128)(2,1)S(1)}, u32[]{:S(2)}, u32[]{:S(2)}) collective-permute-start(bf16[32,4096]{1,0:T(8,128)(2,1)} %get-tuple-element.67.refs_4_), channel_id=1, source_target_pairs={{0,4},{4,0},{8,12},{12,8},{1,5},{5,1},{9,13},{13,9},{2,6},{6,2},{1... | collective-permute-start | bytes 786440 | tf_op jit(solution)/shard_map/ppermute | solution.py:31
  182.3 15.4 %collective-permute-start.44 = (bf16[64,4096]{1,0:T(8,128)(2,1)S(1)}, bf16[64,4096]{1,0:T(8,128)(2,1)S(1)}, u32[]{:S(2)}, u32[]{:S(2)}) collective-permute-start(bf16[64,4096]{1,0:T(8,128)(2,1)S(1)} %move_rows.18.refs_0_), channel_id=1, source_target_pairs={{0,4},{4,0},{8,12},{12,8},{1,5},{5,1},{9,13},{13,9},{2,6},{6,2},{1... | collective-permute-start | bytes 1572872 | tf_op jit(solution)/shard_map/ppermute | solution.py:31
  183.3 14.4 %collective-permute-start.45 = (bf16[64,4096]{1,0:T(8,128)(2,1)S(1)}, bf16[64,4096]{1,0:T(8,128)(2,1)S(1)}, u32[]{:S(2)}, u32[]{:S(2)}) collective-permute-start(bf16[64,4096]{1,0:T(8,128)(2,1)S(1)} %move_rows.18.refs_0_), channel_id=1, source_target_pairs={{0,8},{4,12},{8,0},{12,4},{1,9},{5,13},{9,1},{13,5},{2,10},{6,14},... | collective-permute-start | bytes 1572872 | tf_op jit(solution)/shard_map/ppermute | solution.py:31
  (35 other events, 339.1 us)

commit v9 on v8

--- a/solution.py
+++ b/solution.py
@@ -9,6 +9,7 @@
 
 epsilon = 1e-05
 LANES = 128
+SLOTS = 3
 LARGEST = 512
 MIB = 1024 * 1024
 VMEM_BYTES = 56 * 1024 * 1024
@@ -243,8 +244,8 @@
             act(
                 pltpu.make_async_copy(
                     weight_refs[j].at[0, :, columns],
-                    weight_scr.at[j, i % 2],
-                    weight_sems.at[j, i % 2],
+                    weight_scr.at[j, i % SLOTS],
+                    weight_sems.at[j, i % SLOTS],
                 )
             )
 
@@ -256,6 +257,8 @@
 
     fetch(0, start)
     load_pieces(piece_refs, rows_scr, sems)
+    for i in range(1, min(SLOTS - 1, steps)):
+        fetch(i, start)
     small = rows_scr[:, full_width:].astype(jnp.float32)
     lane = lax.broadcasted_iota(jnp.int32, small.shape, 1)
     place = lax.axis_index("expert") * 3
@@ -264,11 +267,11 @@
     route_scr[...] = jnp.broadcast_to(0.5 * weight, route_scr.shape)
     for i in range(steps):
         fetch(i, wait)
-        if i + 1 < steps:
-            fetch(i + 1, start)
+        if i + SLOTS - 1 < steps:
+            fetch(i + SLOTS - 1, start)
         rows = rows_scr[:, :full_width]
-        gate = jnp.dot(rows, weight_scr[0, i % 2], preferred_element_type=jnp.float32)
-        up = jnp.dot(rows, weight_scr[1, i % 2], preferred_element_type=jnp.float32)
+        gate = jnp.dot(rows, weight_scr[0, i % SLOTS], preferred_element_type=jnp.float32)
+        up = jnp.dot(rows, weight_scr[1, i % SLOTS], preferred_element_type=jnp.float32)
         hidden = gate * (1.0 + jnp.tanh(0.5 * gate)) * up * route_scr[:, :1]
         out_ref[:, i * tile : (i + 1) * tile] = hidden.astype(jnp.bfloat16)
 
@@ -290,11 +293,11 @@
         scratch_shapes=[
             pltpu.VMEM((rows, full_width + LANES), jnp.bfloat16),
             pltpu.VMEM((rows, LANES), jnp.float32),
-            pltpu.VMEM((2, 2, full_width, tile), jnp.bfloat16),
+            pltpu.VMEM((2, SLOTS, full_width, tile), jnp.bfloat16),
             pltpu.SemaphoreType.DMA((len(pieces),)),
-            pltpu.SemaphoreType.DMA((2, 2)),
+            pltpu.SemaphoreType.DMA((2, SLOTS)),
         ],
-        compiler_params=params((14 + rows // 64) * MIB),
+        compiler_params=params((18 + rows // 64) * MIB),
         cost_estimate=pl.CostEstimate(
             flops=4 * rows * full_width * hidden,
             bytes_accessed=4 * full_width * hidden + 2 * rows * (full_width + hidden),
@@ -406,7 +409,7 @@
 
     def fetch(i):
         return pltpu.make_async_copy(
-            head_ref.at[pl.ds(i * tile, tile), :],
+            head_ref.at[pl.ds(pl.multiple_of(i * tile, tile), tile), :],
             head_scr.at[i],
             head_sems.at[i],
         )
@@ -423,11 +426,9 @@
                     sems.at[len(copies)],
                 )
             )
-    ahead = min(2, steps)
-    fetch(0).start()
     for copy in copies:
         copy.start()
-    for i in range(1, ahead):
+    for i in range(steps):
         fetch(i).start()
     for copy in copies:
         copy.wait()
@@ -435,10 +436,9 @@
     out_ref[...] = jnp.where(lane == 0, -jnp.inf, 0.0)
     targets = target_ref[...] - (my_expert * n_tensor + my_tensor) * vocab_part
 
-    for i in range(steps):
+    @pl.loop(0, steps)
+    def _(i):
         fetch(i).wait()
-        if i + ahead < steps:
-            fetch(i + ahead).start()
         logits = lax.dot_general(
             head_scr[i],
             rows_scr[...],

time: 236 us -> 233 us (0.987)
  transfers between devices with their start and end apart: 54 -> 54, of which waited for: 27 -> 26; matrix products, arithmetic and copies ran while one was open for 1% -> 1% of each run, Pallas kernels for 30% -> 30%
where the time goes in v9:
time: 233 us; the launch traced here: 231 us
  Pallas kernels  92.1 us (40%)
  waiting for transfers between devices  72.2 us (31%)
  starting transfers between devices  61.9 us (27%)
  local copies, waits for them, and re-layouts  3.16 us (1%)
    ppermute x54, waiting for transfers between devices, swap(): return lax.ppermute(x, axis, [(i, i ^ distance) for i in range(size)])  72.2 us
    ppermute x54, starting transfers between devices, swap(): return lax.ppermute(x, axis, [(i, i ^ distance) for i in range(size)])  61.9 us
    pallas_call x4, Pallas kernels, hidden_rows(): pl.pallas_call(functools.partial(hidden_kernel, len(pieces), len(after),...  43 us
    pallas_call x2, Pallas kernels, head_terms(): pl.pallas_call(functools.partial(head_kernel, len(pieces), tile, sub), ou...  24 us
    pallas_call x4, Pallas kernels, down_rows(): pl.pallas_call(functools.partial(down_kernel, start, len(hidden)), out_sh...  16 us
  transfers between devices with their start and end apart: 54, of which 26 were waited for; matrix products, arithmetic and copies ran while one was open for 1% of the time, Pallas kernels for 30%

profile of v9, /device:TPU:0, one launch (start us, length us, event | category | flops | bytes accessed | tf_op | source)
XLA Modules:
  0.0 230.8 jit_solution(8306120919800389522)
XLA Ops:
  1.0 5.1 %collective-permute-start = (bf16[72,1024]{1,0:T(8,128)(2,1)S(1)}, bf16[72,1024]{1,0:T(8,128)(2,1)S(1)}, u32[]{:S(2)}, u32[]{:S(2)}) collective-permute-start(bf16[72,1024]{1,0:T(8,128)(2,1)S(1)} %get-tuple-element.40.refs_0_), channel_id=1, source_target_pairs={{0,3},{1,2},{2,1},{3,0},{4,7},{5,6},{6,5},{7,4},{8,11},{9,10},{10,... | collective-permute-start | bytes 442376 | tf_op jit(solution)/shard_map/ppermute | solution.py:32
  10.9 7.7 %collective-permute-done.1.refs_2_ = bf16[72,1024]{1,0:T(8,128)(2,1)S(1)} collective-permute-done((bf16[72,1024]{1,0:T(8,128)(2,1)S(1)}, bf16[72,1024]{1,0:T(8,128)(2,1)S(1)}, u32[]{:S(2)}, u32[]{:S(2)}) %collective-permute-start.1) | collective-permute-done | bytes 147488 | tf_op jit(solution)/shard_map/ppermute | solution.py:32
  26.4 3.8 %collective-permute-done.7.refs_3_.refs_1_ = bf16[64,1024]{1,0:T(8,128)(2,1)S(1)} collective-permute-done((bf16[64,1024]{1,0:T(8,128)(2,1)S(1)}, bf16[64,1024]{1,0:T(8,128)(2,1)S(1)}, u32[]{:S(2)}, u32[]{:S(2)}) %collective-permute-start.7) | collective-permute-done | bytes 131104 | tf_op jit(solution)/shard_map/ppermute | solution.py:32
  30.3 4.3 %collective-permute-done.8.refs_4_.refs_2_ = bf16[64,1024]{1,0:T(8,128)(2,1)S(1)} collective-permute-done((bf16[64,1024]{1,0:T(8,128)(2,1)S(1)}, bf16[64,1024]{1,0:T(8,128)(2,1)S(1)}, u32[]{:S(2)}, u32[]{:S(2)}) %collective-permute-start.8) | collective-permute-done | bytes 131104 | tf_op jit(solution)/shard_map/ppermute | solution.py:32
  36.1 7.8 %collective-permute-done.5.refs_0_.refs_3_.refs_7_ = bf16[32,4224]{1,0:T(8,128)(2,1)S(1)} collective-permute-done((bf16[32,4224]{1,0:T(8,128)(2,1)S(1)}, bf16[32,4224]{1,0:T(8,128)(2,1)S(1)}, u32[]{:S(2)}, u32[]{:S(2)}) %collective-permute-start.5) | collective-permute-done | bytes 270368 | tf_op jit(solution)/shard_map/ppermute | solution.py:32
  46.8 19.5 %hidden_rows.4.refs_0_ = bf16[512,1792]{1,0:T(8,128)(2,1)S(1)} custom-call(bf16[64,4224]{1,0:T(8,128)(2,1)S(1)} %get-tuple-element.41.refs_0_, bf16[64,4224]{1,0:T(8,128)(2,1)S(1)} %collective-permute-done.3.refs_1_, bf16[64,4224]{1,0:T(8,128)(2,1)S(1)} %collective-permute-done.4.refs_0_.refs_2_, ...), custom_call_target="tpu_custom_call" | custom-call | flops 15032385536 | bytes 35389440 | tf_op jit(solution)/shard_map/hidden_rows/pallas_call | solution.py:288
  66.4 4.1 %down_rows.5 = bf16[256,4096]{1,0:T(8,128)(2,1)S(1)} custom-call(bf16[512,1792]{1,0:T(8,128)(2,1)S(1)} %hidden_rows.4.refs_0_, bf16[1,1792,4096]{2,1,0:T(8,128)(2,1)S(1)} %bitcast.33, bf16[64,4224]{1,0:T(8,128)(2,1)S(1)} %collective-permute-done.12.refs_2_.refs_1_, bf16[64,4224]{1,0:T(8,128)(2,1)S(1)} %collective-permute-done.13.refs_3_.refs_0_.refs_2_), custom_call_target="tpu_custom_call" | custom-call | flops 3758096384 | bytes 3014656 | tf_op jit(solution)/shard_map/down_rows/pallas_call | solution.py:332
  73.6 3.9 %down_rows.4.kept_ref.refs_2_ = bf16[256,4096]{1,0:T(8,128)(2,1)S(1)} custom-call(bf16[512,1792]{1,0:T(8,128)(2,1)S(1)} %hidden_rows.4.refs_0_, bf16[1,1792,4096]{2,1,0:T(8,128)(2,1)S(1)} %bitcast.33), custom_call_target="tpu_custom_call" | custom-call | flops 3758096384 | bytes 3014656 | tf_op jit(solution)/shard_map/down_rows/pallas_call | solution.py:332
  84.3 11.7 %hidden_rows.5.refs_0_ = bf16[512,1024]{1,0:T(8,128)(2,1)S(1)} custom-call(bf16[64,4224]{1,0:T(8,128)(2,1)S(1)} %get-tuple-element.46.refs_0_, bf16[64,4224]{1,0:T(8,128)(2,1)S(1)} %collective-permute-done.12.refs_2_.refs_1_, bf16[64,4224]{1,0:T(8,128)(2,1)S(1)} %collective-permute-done.13.refs_3_.refs_0_.refs_2_, ...), custom_call_target="tpu_custom_call" | custom-call | flops 8589934592 | bytes 22020096 | tf_op jit(solution)/shard_map/hidden_rows/pallas_call | solution.py:288
  98.9 7.0 %hidden_rows.6.refs_1_ = bf16[512,512]{1,0:T(8,128)(2,1)S(1)} custom-call(bf16[64,4224]{1,0:T(8,128)(2,1)S(1)} %get-tuple-element.46.refs_0_, bf16[64,4224]{1,0:T(8,128)(2,1)S(1)} %collective-permute-done.12.refs_2_.refs_1_, bf16[64,4224]{1,0:T(8,128)(2,1)S(1)} %collective-permute-done.13.refs_3_.refs_0_.refs_2_, ...), custom_call_target="tpu_custom_call" | custom-call | flops 4294967296 | bytes 13107200 | tf_op jit(solution)/shard_map/hidden_rows/pallas_call | solution.py:288
  107.8 2.9 %collective-permute-start.21 = (bf16[16,4096]{1,0:T(8,128)(2,1)S(1)}, bf16[16,4096]{1,0:T(8,128)(2,1)S(1)}, u32[]{:S(2)}, u32[]{:S(2)}) collective-permute-start(bf16[16,4096]{1,0:T(8,128)(2,1)S(1)} %get-tuple-element.56.refs_10_), channel_id=1, source_target_pairs={{0,1},{1,0},{2,3},{3,2},{4,5},{5,4},{6,7},{7,6},{8,9},{9,8},{10,11... | collective-permute-start | bytes 393224 | tf_op jit(solution)/shard_map/ppermute | solution.py:32
  110.7 4.7 %hidden_rows.7.refs_2_ = bf16[512,256]{1,0:T(8,128)(2,1)S(1)} custom-call(bf16[64,4224]{1,0:T(8,128)(2,1)S(1)} %get-tuple-element.46.refs_0_, bf16[64,4224]{1,0:T(8,128)(2,1)S(1)} %collective-permute-done.12.refs_2_.refs_1_, bf16[64,4224]{1,0:T(8,128)(2,1)S(1)} %collective-permute-done.13.refs_3_.refs_0_.refs_2_, ...), custom_call_target="tpu_custom_call" | custom-call | flops 2147483648 | bytes 8650752 | tf_op jit(solution)/shard_map/hidden_rows/pallas_call | solution.py:288
  115.4 2.9 %collective-permute-done.20.refs_2_.refs_5_ = bf16[16,4096]{1,0:T(8,128)(2,1)S(1)} collective-permute-done((bf16[16,4096]{1,0:T(8,128)(2,1)S(1)}, bf16[16,4096]{1,0:T(8,128)(2,1)S(1)}, u32[]{:S(2)}, u32[]{:S(2)}) %collective-permute-start.20) | collective-permute-done | bytes 131104 | tf_op jit(solution)/shard_map/ppermute | solution.py:32
  118.3 3.9 %down_rows.7 = bf16[256,4096]{1,0:T(8,128)(2,1)S(1)} custom-call(bf16[512,1024]{1,0:T(8,128)(2,1)S(1)} %hidden_rows.5.refs_0_, bf16[512,512]{1,0:T(8,128)(2,1)S(1)} %hidden_rows.6.refs_1_, bf16[512,256]{1,0:T(8,128)(2,1)S(1)} %hidden_rows.7.refs_2_, bf16[1,1792,4096]{2,1,0:T(8,128)(2,1)S(1)} %bitcast.33, ...), custom_call_target="tpu_custom_call" | custom-call | flops 3758096384 | bytes 3014656 | tf_op jit(solution)/shard_map/down_rows/pallas_call | solution.py:332
  124.0 3.9 %down_rows.6.kept_ref = bf16[256,4096]{1,0:T(8,128)(2,1)S(1)} custom-call(bf16[512,1024]{1,0:T(8,128)(2,1)S(1)} %hidden_rows.5.refs_0_, bf16[512,512]{1,0:T(8,128)(2,1)S(1)} %hidden_rows.6.refs_1_, bf16[512,256]{1,0:T(8,128)(2,1)S(1)} %hidden_rows.7.refs_2_, bf16[1,1792,4096]{2,1,0:T(8,128)(2,1)S(1)} %bitcast.33, bf16[16,4096]{1,0:T(8,128)(2,1)S(1)} %final_rows.2.refs_4_.refs_0_), custom_call_target="tpu_custom_call" | custom-call | flops 3758096384 | bytes 3014656 | tf_op jit(solution)/shard_map/down_rows/pallas_call | solution.py:332
  134.9 3.9 %collective-permute-done.22.refs_0_.refs_1_ = bf16[16,4096]{1,0:T(8,128)(2,1)S(1)} collective-permute-done((bf16[16,4096]{1,0:T(8,128)(2,1)S(1)}, bf16[16,4096]{1,0:T(8,128)(2,1)S(1)}, u32[]{:S(2)}, u32[]{:S(2)}) %collective-permute-start.22) | collective-permute-done | bytes 131104 | tf_op jit(solution)/shard_map/ppermute | solution.py:32
  138.7 4.8 %collective-permute-done.23.refs_1_.refs_2_ = bf16[16,4096]{1,0:T(8,128)(2,1)S(1)} collective-permute-done((bf16[16,4096]{1,0:T(8,128)(2,1)S(1)}, bf16[16,4096]{1,0:T(8,128)(2,1)S(1)}, u32[]{:S(2)}, u32[]{:S(2)}) %collective-permute-start.23) | collective-permute-done | bytes 131104 | tf_op jit(solution)/shard_map/ppermute | solution.py:32
  145.6 6.3 %collective-permute-done.32.last_one_ref = bf16[32,4096]{1,0:T(8,128)(2,1)S(1)} collective-permute-done((bf16[32,4096]{1,0:T(8,128)(2,1)S(1)}, bf16[32,4096]{1,0:T(8,128)(2,1)S(1)}, u32[]{:S(2)}, u32[]{:S(2)}) %collective-permute-start.32) | collective-permute-done | bytes 262176 | tf_op jit(solution)/shard_map/ppermute | solution.py:32
  160.4 3.8 %collective-permute-done.38.refs_1_ = bf16[16,4096]{1,0:T(8,128)(2,1)S(1)} collective-permute-done((bf16[16,4096]{1,0:T(8,128)(2,1)S(1)}, bf16[16,4096]{1,0:T(8,128)(2,1)S(1)}, u32[]{:S(2)}, u32[]{:S(2)}) %collective-permute-start.38) | collective-permute-done | bytes 131104 | tf_op jit(solution)/shard_map/ppermute | solution.py:32
  164.2 4.0 %collective-permute-done.39.refs_2_ = bf16[16,4096]{1,0:T(8,128)(2,1)S(1)} collective-permute-done((bf16[16,4096]{1,0:T(8,128)(2,1)S(1)}, bf16[16,4096]{1,0:T(8,128)(2,1)S(1)}, u32[]{:S(2)}, u32[]{:S(2)}) %collective-permute-start.39) | collective-permute-done | bytes 131104 | tf_op jit(solution)/shard_map/ppermute | solution.py:32
  177.9 3.8 %collective-permute-done.42.refs_2_ = bf16[16,4096]{1,0:T(8,128)(2,1)S(1)} collective-permute-done((bf16[16,4096]{1,0:T(8,128)(2,1)S(1)}, bf16[16,4096]{1,0:T(8,128)(2,1)S(1)}, u32[]{:S(2)}, u32[]{:S(2)}) %collective-permute-start.42) | collective-permute-done | bytes 131104 | tf_op jit(solution)/shard_map/ppermute | solution.py:32
  183.9 13.2 %head_terms.2.refs_2_ = f32[8,256]{1,0:T(8,128)S(1)} custom-call(bf16[64,4096]{1,0:T(8,128)(2,1)S(1)} %move_rows.16.refs_0_, bf16[64,4096]{1,0:T(8,128)(2,1)S(1)} %collective-permute-done.34.refs_1_, bf16[64,4096]{1,0:T(8,128)(2,1)S(1)} %collective-permute-done.35.refs_0_.refs_2_, bf16[32,4096]{1,0:T(8,128)(2,1)S(1)} %collective-permute-done.36.refs_3_, ...), custom_call_target="tpu_custom_call" | custom-call | flops 4194304000 | bytes 18481152 | tf_op jit(solution)/shard_map/head_terms/pallas_call | solution.py:463
  200.3 4.7 %collective-permute-done.46.refs_3_ = bf16[32,4096]{1,0:T(8,128)(2,1)S(1)} collective-permute-done((bf16[32,4096]{1,0:T(8,128)(2,1)S(1)}, bf16[32,4096]{1,0:T(8,128)(2,1)S(1)}, u32[]{:S(2)}, u32[]{:S(2)}) %collective-permute-start.46) | collective-permute-done | bytes 262176 | tf_op jit(solution)/shard_map/ppermute | solution.py:32
  205.9 10.7 %head_terms.3 = f32[8,256]{1,0:T(8,128)S(1)} custom-call(bf16[64,4096]{1,0:T(8,128)(2,1)S(1)} %move_rows.18.refs_0_, bf16[64,4096]{1,0:T(8,128)(2,1)S(1)} %collective-permute-done.44.refs_1_, bf16[64,4096]{1,0:T(8,128)(2,1)S(1)} %collective-permute-done.45.refs_0_.refs_2_, bf16[32,4096]{1,0:T(8,128)(2,1)S(1)} %collective-permute-done.46.refs_3_, ...), custom_call_target="tpu_custom_call" | custom-call | flops 4194304000 | bytes 18481152 | tf_op jit(solution)/shard_map/head_terms/pallas_call | solution.py:463
  (159 shorter events, 81.2 us)
Async XLA Ops:
  6.2 12.5 %collective-permute-start.1 = (bf16[72,1024]{1,0:T(8,128)(2,1)S(1)}, bf16[72,1024]{1,0:T(8,128)(2,1)S(1)}, u32[]{:S(2)}, u32[]{:S(2)}) collective-permute-start(bf16[72,1024]{1,0:T(8,128)(2,1)S(1)} %get-tuple-element.40.refs_0_), channel_id=1, source_target_pairs={{0,2},{1,3},{2,0},{3,1},{4,6},{5,7},{6,4},{7,5},{8,10},{9,11},{10,... | collective-permute-start | bytes 442376 | tf_op jit(solution)/shard_map/ppermute | solution.py:32
  6.2 12.5 %collective-permute-start.2 = (bf16[72,1024]{1,0:T(8,128)(2,1)S(1)}, bf16[72,1024]{1,0:T(8,128)(2,1)S(1)}, u32[]{:S(2)}, u32[]{:S(2)}) collective-permute-start(bf16[72,1024]{1,0:T(8,128)(2,1)S(1)} %get-tuple-element.40.refs_0_), channel_id=1, source_target_pairs={{0,1},{1,0},{2,3},{3,2},{4,5},{5,4},{6,7},{7,6},{8,9},{9,8},{10,11... | collective-permute-start | bytes 442376 | tf_op jit(solution)/shard_map/ppermute | solution.py:32
  19.0 15.6 %collective-permute-start.3 = (bf16[64,4224]{1,0:T(8,128)(2,1)S(1)}, bf16[64,4224]{1,0:T(8,128)(2,1)S(1)}, u32[]{:S(2)}, u32[]{:S(2)}) collective-permute-start(bf16[64,4224]{1,0:T(8,128)(2,1)S(1)} %get-tuple-element.41.refs_0_), channel_id=1, source_target_pairs={{0,4},{4,0},{8,12},{12,8},{1,5},{5,1},{9,13},{13,9},{2,6},{6,2},{1... | collective-permute-start | bytes 1622024 | tf_op jit(solution)/shard_map/ppermute | solution.py:32
  20.5 14.1 %collective-permute-start.4 = (bf16[64,4224]{1,0:T(8,128)(2,1)S(1)}, bf16[64,4224]{1,0:T(8,128)(2,1)S(1)}, u32[]{:S(2)}, u32[]{:S(2)}) collective-permute-start(bf16[64,4224]{1,0:T(8,128)(2,1)S(1)} %get-tuple-element.41.refs_0_), channel_id=1, source_target_pairs={{0,8},{4,12},{8,0},{12,4},{1,9},{5,13},{9,1},{13,5},{2,10},{6,14},... | collective-permute-start | bytes 1622024 | tf_op jit(solution)/shard_map/ppermute | solution.py:32
  34.8 12.0 %collective-permute-start.10 = (bf16[192,4224]{1,0:T(8,128)(2,1)S(1)}, bf16[192,4224]{1,0:T(8,128)(2,1)S(1)}, u32[]{:S(2)}, u32[]{:S(2)}) collective-permute-start(bf16[192,4224]{1,0:T(8,128)(2,1)S(1)} %move_rows.11), channel_id=1, source_target_pairs={{0,16},{16,0},{1,17},{17,1},{2,18},{18,2},{3,19},{19,3},{4,20},{20... | collective-permute-start | bytes 4866056 | tf_op jit(solution)/shard_map/ppermute | solution.py:32
  44.7 21.6 %collective-permute-start.12 = (bf16[64,4224]{1,0:T(8,128)(2,1)S(1)}, bf16[64,4224]{1,0:T(8,128)(2,1)S(1)}, u32[]{:S(2)}, u32[]{:S(2)}) collective-permute-start(bf16[64,4224]{1,0:T(8,128)(2,1)S(1)} %get-tuple-element.46.refs_0_), channel_id=1, source_target_pairs={{0,4},{4,0},{8,12},{12,8},{1,5},{5,1},{9,13},{13,9},{2,6},{6,2},{1... | collective-permute-start | bytes 1622024 | tf_op jit(solution)/shard_map/ppermute | solution.py:32
  46.3 20.1 %collective-permute-start.13 = (bf16[64,4224]{1,0:T(8,128)(2,1)S(1)}, bf16[64,4224]{1,0:T(8,128)(2,1)S(1)}, u32[]{:S(2)}, u32[]{:S(2)}) collective-permute-start(bf16[64,4224]{1,0:T(8,128)(2,1)S(1)} %get-tuple-element.46.refs_0_), channel_id=1, source_target_pairs={{0,8},{4,12},{8,0},{12,4},{1,9},{5,13},{9,1},{13,5},{2,10},{6,14},... | collective-permute-start | bytes 1622024 | tf_op jit(solution)/shard_map/ppermute | solution.py:32
  70.5 10.3 %collective-permute-start.14 = (bf16[256,4096]{1,0:T(8,128)(2,1)S(1)}, bf16[256,4096]{1,0:T(8,128)(2,1)S(1)}, u32[]{:S(2)}, u32[]{:S(2)}) collective-permute-start(bf16[256,4096]{1,0:T(8,128)(2,1)S(1)} %down_rows.5), channel_id=1, source_target_pairs={{0,16},{16,0},{1,17},{17,1},{2,18},{18,2},{3,19},{19,3},{4,20},{20... | collective-permute-start | bytes 6291464 | tf_op jit(solution)/shard_map/ppermute | solution.py:32
  70.8 13.5 %collective-permute-start.27 = (bf16[192,4224]{1,0:T(8,128)(2,1)S(1)}, bf16[192,4224]{1,0:T(8,128)(2,1)S(1)}, u32[]{:S(2)}, u32[]{:S(2)}) collective-permute-start(bf16[192,4224]{1,0:T(8,128)(2,1)S(1)} %move_rows.14), channel_id=1, source_target_pairs={{0,16},{16,0},{1,17},{17,1},{2,18},{18,2},{3,19},{19,3},{4,20},{20... | collective-permute-start | bytes 4866056 | tf_op jit(solution)/shard_map/ppermute | solution.py:32
  81.3 14.8 %collective-permute-start.15 = (bf16[64,4096]{1,0:T(8,128)(2,1)S(1)}, bf16[64,4096]{1,0:T(8,128)(2,1)S(1)}, u32[]{:S(2)}, u32[]{:S(2)}) collective-permute-start(bf16[64,4096]{1,0:T(8,128)(2,1)S(1)} %get-tuple-element.48.refs_9_), channel_id=1, source_target_pairs={{0,4},{4,0},{8,12},{12,8},{1,5},{5,1},{9,13},{13,9},{2,6},{6,2},{1... | collective-permute-start | bytes 1572872 | tf_op jit(solution)/shard_map/ppermute | solution.py:32
  82.6 14.0 %collective-permute-start.16 = (bf16[64,4096]{1,0:T(8,128)(2,1)S(1)}, bf16[64,4096]{1,0:T(8,128)(2,1)S(1)}, u32[]{:S(2)}, u32[]{:S(2)}) collective-permute-start(bf16[64,4096]{1,0:T(8,128)(2,1)S(1)} %get-tuple-element.49.refs_10_), channel_id=1, source_target_pairs={{0,8},{4,12},{8,0},{12,4},{1,9},{5,13},{9,1},{13,5},{2,10},{6,14},... | collective-permute-start | bytes 1572872 | tf_op jit(solution)/shard_map/ppermute | solution.py:32
  107.8 10.5 %collective-permute-start.20 = (bf16[16,4096]{1,0:T(8,128)(2,1)S(1)}, bf16[16,4096]{1,0:T(8,128)(2,1)S(1)}, u32[]{:S(2)}, u32[]{:S(2)}) collective-permute-start(bf16[16,4096]{1,0:T(8,128)(2,1)S(1)} %get-tuple-element.55.refs_11_), channel_id=1, source_target_pairs={{0,2},{1,3},{2,0},{3,1},{4,6},{5,7},{6,4},{7,5},{8,10},{9,11},{10,... | collective-permute-start | bytes 393224 | tf_op jit(solution)/shard_map/ppermute | solution.py:32
  107.8 10.5 %collective-permute-start.21 = (bf16[16,4096]{1,0:T(8,128)(2,1)S(1)}, bf16[16,4096]{1,0:T(8,128)(2,1)S(1)}, u32[]{:S(2)}, u32[]{:S(2)}) collective-permute-start(bf16[16,4096]{1,0:T(8,128)(2,1)S(1)} %get-tuple-element.56.refs_10_), channel_id=1, source_target_pairs={{0,1},{1,0},{2,3},{3,2},{4,5},{5,4},{6,7},{7,6},{8,9},{9,8},{10,11... | collective-permute-start | bytes 393224 | tf_op jit(solution)/shard_map/ppermute | solution.py:32
  128.4 15.2 %collective-permute-start.30 = (bf16[64,4096]{1,0:T(8,128)(2,1)S(1)}, bf16[64,4096]{1,0:T(8,128)(2,1)S(1)}, u32[]{:S(2)}, u32[]{:S(2)}) collective-permute-start(bf16[64,4096]{1,0:T(8,128)(2,1)S(1)} %get-tuple-element.61), channel_id=1, source_target_pairs={{0,4},{4,0},{8,12},{12,8},{1,5},{5,1},{9,13},{13,9},{2,6},{6,2},{1... | collective-permute-start | bytes 1572872 | tf_op jit(solution)/shard_map/ppermute | solution.py:32
  129.9 14.0 %collective-permute-start.31 = (bf16[64,4096]{1,0:T(8,128)(2,1)S(1)}, bf16[64,4096]{1,0:T(8,128)(2,1)S(1)}, u32[]{:S(2)}, u32[]{:S(2)}) collective-permute-start(bf16[64,4096]{1,0:T(8,128)(2,1)S(1)} %get-tuple-element.62), channel_id=1, source_target_pairs={{0,8},{4,12},{8,0},{12,4},{1,9},{5,13},{9,1},{13,5},{2,10},{6,14},... | collective-permute-start | bytes 1572872 | tf_op jit(solution)/shard_map/ppermute | solution.py:32
  132.3 11.3 %collective-permute-start.23 = (bf16[16,4096]{1,0:T(8,128)(2,1)S(1)}, bf16[16,4096]{1,0:T(8,128)(2,1)S(1)}, u32[]{:S(2)}, u32[]{:S(2)}) collective-permute-start(bf16[16,4096]{1,0:T(8,128)(2,1)S(1)} %final_rows.2.refs_4_.refs_0_), channel_id=1, source_target_pairs={{0,2},{1,3},{2,0},{3,1},{4,6},{5,7},{6,4},{7,5},{8,10},{9,11},{10,... | collective-permute-start | bytes 393224 | tf_op jit(solution)/shard_map/ppermute | solution.py:32
  132.3 11.3 %collective-permute-start.24 = (bf16[16,4096]{1,0:T(8,128)(2,1)S(1)}, bf16[16,4096]{1,0:T(8,128)(2,1)S(1)}, u32[]{:S(2)}, u32[]{:S(2)}) collective-permute-start(bf16[16,4096]{1,0:T(8,128)(2,1)S(1)} %final_rows.2.refs_4_.refs_0_), channel_id=1, source_target_pairs={{0,1},{1,0},{2,3},{3,2},{4,5},{5,4},{6,7},{7,6},{8,9},{9,8},{10,11... | collective-permute-start | bytes 393224 | tf_op jit(solution)/shard_map/ppermute | solution.py:32
  153.4 20.6 %collective-permute-start.34 = (bf16[64,4096]{1,0:T(8,128)(2,1)S(1)}, bf16[64,4096]{1,0:T(8,128)(2,1)S(1)}, u32[]{:S(2)}, u32[]{:S(2)}) collective-permute-start(bf16[64,4096]{1,0:T(8,128)(2,1)S(1)} %move_rows.16.refs_0_), channel_id=1, source_target_pairs={{0,4},{4,0},{8,12},{12,8},{1,5},{5,1},{9,13},{13,9},{2,6},{6,2},{1... | collective-permute-start | bytes 1572872 | tf_op jit(solution)/shard_map/ppermute | solution.py:32
  154.7 19.2 %collective-permute-start.35 = (bf16[64,4096]{1,0:T(8,128)(2,1)S(1)}, bf16[64,4096]{1,0:T(8,128)(2,1)S(1)}, u32[]{:S(2)}, u32[]{:S(2)}) collective-permute-start(bf16[64,4096]{1,0:T(8,128)(2,1)S(1)} %move_rows.16.refs_0_), channel_id=1, source_target_pairs={{0,8},{4,12},{8,0},{12,4},{1,9},{5,13},{9,1},{13,5},{2,10},{6,14},... | collective-permute-start | bytes 1572872 | tf_op jit(solution)/shard_map/ppermute | solution.py:32
  158.2 10.0 %collective-permute-start.39 = (bf16[16,4096]{1,0:T(8,128)(2,1)S(1)}, bf16[16,4096]{1,0:T(8,128)(2,1)S(1)}, u32[]{:S(2)}, u32[]{:S(2)}) collective-permute-start(bf16[16,4096]{1,0:T(8,128)(2,1)S(1)} %get-tuple-element.70), channel_id=1, source_target_pairs={{0,2},{1,3},{2,0},{3,1},{4,6},{5,7},{6,4},{7,5},{8,10},{9,11},{10,... | collective-permute-start | bytes 393224 | tf_op jit(solution)/shard_map/ppermute | solution.py:32
  171.2 10.4 %collective-permute-start.42 = (bf16[16,4096]{1,0:T(8,128)(2,1)S(1)}, bf16[16,4096]{1,0:T(8,128)(2,1)S(1)}, u32[]{:S(2)}, u32[]{:S(2)}) collective-permute-start(bf16[16,4096]{1,0:T(8,128)(2,1)S(1)} %final_rows.3.refs_0_), channel_id=1, source_target_pairs={{0,2},{1,3},{2,0},{3,1},{4,6},{5,7},{6,4},{7,5},{8,10},{9,11},{10,... | collective-permute-start | bytes 393224 | tf_op jit(solution)/shard_map/ppermute | solution.py:32
  171.2 10.4 %collective-permute-start.43 = (bf16[16,4096]{1,0:T(8,128)(2,1)S(1)}, bf16[16,4096]{1,0:T(8,128)(2,1)S(1)}, u32[]{:S(2)}, u32[]{:S(2)}) collective-permute-start(bf16[16,4096]{1,0:T(8,128)(2,1)S(1)} %final_rows.3.refs_0_), channel_id=1, source_target_pairs={{0,1},{1,0},{2,3},{3,2},{4,5},{5,4},{6,7},{7,6},{8,9},{9,8},{10,11... | collective-permute-start | bytes 393224 | tf_op jit(solution)/shard_map/ppermute | solution.py:32
  182.4 14.8 %collective-permute-start.44 = (bf16[64,4096]{1,0:T(8,128)(2,1)S(1)}, bf16[64,4096]{1,0:T(8,128)(2,1)S(1)}, u32[]{:S(2)}, u32[]{:S(2)}) collective-permute-start(bf16[64,4096]{1,0:T(8,128)(2,1)S(1)} %move_rows.18.refs_0_), channel_id=1, source_target_pairs={{0,4},{4,0},{8,12},{12,8},{1,5},{5,1},{9,13},{13,9},{2,6},{6,2},{1... | collective-permute-start | bytes 1572872 | tf_op jit(solution)/shard_map/ppermute | solution.py:32
  183.0 14.2 %collective-permute-start.45 = (bf16[64,4096]{1,0:T(8,128)(2,1)S(1)}, bf16[64,4096]{1,0:T(8,128)(2,1)S(1)}, u32[]{:S(2)}, u32[]{:S(2)}) collective-permute-start(bf16[64,4096]{1,0:T(8,128)(2,1)S(1)} %move_rows.18.refs_0_), channel_id=1, source_target_pairs={{0,8},{4,12},{8,0},{12,4},{1,9},{5,13},{9,1},{13,5},{2,10},{6,14},... | collective-permute-start | bytes 1572872 | tf_op jit(solution)/shard_map/ppermute | solution.py:32
  (35 other events, 338.5 us)

commit v10 on v9

--- a/solution.py
+++ b/solution.py
@@ -399,9 +399,14 @@
     )(*parts, raw, gains, *after)
 
 
-def head_kernel(pieces, tile, sub, *refs):
+def head_kernel(pieces, tile, sub, earlier, *refs):
     piece_refs = refs[:pieces]
-    head_ref, target_ref, out_ref, rows_scr, head_scr, sems, head_sems = refs[pieces:]
+    head_ref, target_ref = refs[pieces : pieces + 2]
+    earlier_refs = refs[pieces + 2 : pieces + 2 + earlier]
+    out_refs, rows_scr, head_scr, sems, head_sems = refs[pieces + 2 + earlier :]
+    for earlier_ref in earlier_refs:
+        out_refs[: earlier_ref.shape[0], :] = earlier_ref[...]
+    out_ref = out_refs.at[pl.ds(out_refs.shape[0] - 8, 8), :]
     vocab_part = head_ref.shape[0]
     steps = vocab_part // tile
     my_expert, my_tensor = lax.axis_index("expert"), lax.axis_index("tensor")
@@ -426,9 +431,11 @@
                     sems.at[len(copies)],
                 )
             )
+    ahead = min(2, steps)
+    fetch(0).start()
     for copy in copies:
         copy.start()
-    for i in range(steps):
+    for i in range(1, ahead):
         fetch(i).start()
     for copy in copies:
         copy.wait()
@@ -439,6 +446,11 @@
     @pl.loop(0, steps)
     def _(i):
         fetch(i).wait()
+
+        @pl.when(i + ahead < steps)
+        def _():
+            fetch(i + ahead).start()
+
         logits = lax.dot_general(
             head_scr[i],
             rows_scr[...],
@@ -456,14 +468,14 @@
         out_ref[2:3, :] += jnp.sum(jnp.where(hit, logits, 0.0), axis=0, keepdims=True)
 
 
-def head_terms(pieces, head_rows, targets, sub):
+def head_terms(pieces, head_rows, targets, sub, earlier):
     rows = sum(p.shape[0] for p in pieces)
     vocab_part, full_width = head_rows.shape
     tile = next(t for t in (400, 200, 80, 8, vocab_part) if vocab_part % t == 0)
     return pl.pallas_call(
-        functools.partial(head_kernel, len(pieces), tile, sub),
-        out_shape=jax.ShapeDtypeStruct((8, rows), jnp.float32),
-        in_specs=[anywhere()] * (len(pieces) + 1) + [whole()],
+        functools.partial(head_kernel, len(pieces), tile, sub, len(earlier)),
+        out_shape=jax.ShapeDtypeStruct((8 + sum(e.shape[0] for e in earlier), rows), jnp.float32),
+        in_specs=[anywhere()] * (len(pieces) + 1) + [whole()] * (1 + len(earlier)),
         out_specs=whole(),
         scratch_shapes=[
             pltpu.VMEM((rows, full_width), jnp.bfloat16),
@@ -478,21 +490,42 @@
             transcendentals=rows * vocab_part,
         ),
         name="head_terms",
-    )(*pieces, head_rows, targets)
-
-
-def join_terms(parts):
-    top = functools.reduce(jnp.maximum, [p[0] for p in parts])
-    total = sum(p[1] * jnp.exp(p[0] - top) for p in parts)
-    target = sum(p[2] for p in parts)
-    return jnp.stack([top, total, target])
-
-
-def join_axis(terms, axis, place, me):
-    def of(d):
-        return lax.dynamic_index_in_dim(terms, me ^ d, place, False)
-
-    return join_terms([of(0)] + [swap(of(d), axis, d) for d in range(1, lax.axis_size(axis))])
+    )(*pieces, head_rows, targets, *earlier)
+
+
+def join_kernel(last, mine_ref, got_ref, out_ref):
+    for line in range(0, mine_ref.shape[0], 8):
+        top_one, top_two = mine_ref[line : line + 1, :], got_ref[line : line + 1, :]
+        top = jnp.maximum(top_one, top_two)
+        total = mine_ref[line + 1 : line + 2, :] * jnp.exp(top_one - top)
+        total = total + got_ref[line + 1 : line + 2, :] * jnp.exp(top_two - top)
+        target = mine_ref[line + 2 : line + 3, :] + got_ref[line + 2 : line + 3, :]
+        if last:
+            out_ref[line : line + 1, :] = top + jnp.log(total) - target
+        else:
+            out_ref[line : line + 1, :] = top
+            out_ref[line + 1 : line + 2, :] = total
+            out_ref[line + 2 : line + 3, :] = target
+
+
+def join_all(terms):
+    hops = []
+    for axis in ("tensor", "expert"):
+        distance = 1
+        while distance < lax.axis_size(axis):
+            hops.append((axis, distance))
+            distance *= 2
+    for i, (axis, distance) in enumerate(hops):
+        (terms,) = small_call(
+            functools.partial(join_kernel, i == len(hops) - 1),
+            "join",
+            [terms, swap(terms, axis, distance)],
+            [],
+            [(terms.shape, jnp.float32)],
+            [],
+            2 * MIB,
+        )
+    return terms
 
 
 def pack_kernel(kept_ref, got_ref, one_ref, two_ref, home_ref, side_ref):
@@ -520,11 +553,22 @@
     pass_two_ref[...] = (side_ref[1] + one_ref[half:, :].astype(jnp.float32)).astype(jnp.bfloat16)
 
 
-def total_kernel(count, home_ref, one_ref, two_ref, last_one_ref, last_two_ref, *refs):
-    outs, work = refs[-count - 1 : -1], refs[-1]
+def total_kernel(count, column, *refs):
+    home_ref, one_ref, two_ref, last_one_ref, last_two_ref = refs[:5]
+    column_refs = refs[5 : 5 + column]
+    outs = refs[5 + column : 5 + column + count]
+    work, sems = refs[-2:]
     half = last_one_ref.shape[0]
     sub = outs[0].shape[0]
     me = lax.axis_index("tensor")
+    copies = [
+        pltpu.make_async_copy(
+            column_refs[i], refs[-3].at[pl.ds(i * sub, sub), :], sems.at[i]
+        )
+        for i in range(column)
+    ]
+    for copy in copies:
+        copy.start()
     upper = one_ref[:half, :].astype(jnp.float32) + last_two_ref[...].astype(jnp.float32)
     lower = two_ref[:half, :].astype(jnp.float32) + last_one_ref[...].astype(jnp.float32)
     work[:half, :] = home_ref[:half, :] + upper
@@ -532,6 +576,30 @@
     for d in range(count):
         block = pl.ds(pl.multiple_of((me ^ d) * sub, sub), sub)
         outs[d][...] = work[block, :].astype(jnp.bfloat16)
+    for copy in copies:
+        copy.wait()
+
+
+def totals_of(home, ones, lasts, count, sub, column):
+    rows, full_width = home.shape
+    piece = jax.ShapeDtypeStruct((sub, full_width), jnp.bfloat16)
+    stacked = jax.ShapeDtypeStruct((sub * len(column), full_width), jnp.bfloat16)
+    outs = pl.pallas_call(
+        functools.partial(total_kernel, count, len(column)),
+        out_shape=(piece,) * count + ((stacked,) if column else ()),
+        in_specs=[whole()] * 5 + [anywhere()] * len(column),
+        out_specs=(whole(),) * count + ((anywhere(),) if column else ()),
+        scratch_shapes=[
+            pltpu.VMEM((rows, full_width), jnp.float32),
+            pltpu.SemaphoreType.DMA((max(1, len(column)),)),
+        ],
+        compiler_params=params(8 * MIB),
+        cost_estimate=pl.CostEstimate(
+            flops=4 * home.size, bytes_accessed=20 * home.size, transcendentals=0
+        ),
+        name="total",
+    )(home, *ones, *lasts, *column)
+    return list(outs[:count]), list(outs[count:])
 
 
 def small_call(kernel, name, inputs, after, outs, scratch, limit):
@@ -548,7 +616,7 @@
     )(*inputs, *after)
 
 
-def sum_plane(kept, got, rows, after_pass):
+def sum_plane(kept, got, rows, column):
     f32, b16 = jnp.float32, jnp.bfloat16
     n_tensor = lax.axis_size("tensor")
     count, full_width = kept.shape[0] // rows, kept.shape[1]
@@ -570,22 +638,16 @@
             pass_kernel,
             "pass_on",
             [side, from_one, from_two],
-            after_pass,
+            column[:0:-1],
             [((half, full_width), b16)] * 2,
             [],
             6 * MIB,
         )
         last_one, last_two = swap(pass_one, "expert", 1), swap(pass_two, "expert", 2)
-        pieces = small_call(
-            functools.partial(total_kernel, n_tensor),
-            "total",
-            [home, from_one, from_two, last_one, last_two],
-            [],
-            [((sub, full_width), b16)] * n_tensor,
-            [pltpu.VMEM((rows, full_width), f32)],
-            8 * MIB,
-        )
-        return list(pieces), [one, two], [pass_one, pass_two]
+        pieces, stacked = totals_of(
+            home, [from_one, from_two], [last_one, last_two], n_tensor, sub, column
+        )
+        return pieces, [one, two], [pass_one, pass_two], stacked
     both = (kept.astype(f32) + got.astype(f32)).reshape(count, rows, full_width)
     total = both[0]
     for d in range(1, count):
@@ -593,7 +655,7 @@
     total = total.astype(b16).reshape(n_tensor, sub, full_width)
     me = lax.axis_index("tensor")
     pieces = [lax.dynamic_index_in_dim(total, me ^ d, 0, False) for d in range(n_tensor)]
-    return pieces, [], []
+    return pieces, [], [], []
 
 
 def on_device(
@@ -659,14 +721,13 @@
                 away, w_gate, w_up, w_down
             )
         got = swap(other, "seq", 1)
-        totals, packed, passed = sum_plane(kept, got, rows, before.get("column", [])[::-1])
+        totals, packed, passed, stacked = sum_plane(kept, got, rows, before.get("column", []))
         sums = swap_each(totals[1:], "tensor")
         cut = []
         if before:
-            column = stack_line(before["final"] + before["column"], totals[:1])
-            plane, cut = gather_plane(column, "expert", [])
+            plane, cut = gather_plane(stacked[0], "expert", [])
             wanted = target_rows[:, :, h - 1].reshape(1, -1)
-            terms.append(head_terms(plane, head_rows, wanted, sub))
+            terms = [head_terms(plane, head_rows, wanted, sub, terms)]
         final = final_rows(far_first(totals[:1] + sums), raws[h], gains, [])
         column = gather_near(final, "tensor")
         before = {
@@ -676,17 +737,15 @@
             "totals": totals,
             "sums": sums,
             "final": [final],
-            "column": column[1:],
+            "column": column,
         }
     column = stack_line(column, cut)
-    plane, _ = gather_plane(column, "expert", terms[-1:])
+    plane, _ = gather_plane(column, "expert", terms)
     wanted = target_rows[:, :, splits - 1].reshape(1, -1)
-    terms.append(head_terms(plane, head_rows, wanted, sub))
-    terms = [term[:3].reshape(3, n_expert, n_tensor, sub) for term in terms]
-    terms = jnp.stack(terms, axis=3)
-    joined = join_axis(terms, "tensor", 2, my_tensor)
-    joined = join_axis(joined, "expert", 1, my_expert)
-    return (joined[0] + jnp.log(joined[1]) - joined[2]).reshape(own)
+    terms = [head_terms(plane, head_rows, wanted, sub, terms)]
+    losses = join_all(terms[0])[::8]
+    start = (my_expert * n_tensor + my_tensor) * sub
+    return lax.dynamic_slice_in_dim(losses, start, sub, 1).reshape(own)
 
 
 def solution(mesh):

time: 233 us -> 234 us (level)
  waiting for transfers between devices: 72.2 us -> 85.2 us
  starting transfers between devices: 61.9 us -> 55.6 us
  Pallas kernels: 92.1 us -> 87.2 us
    ppermute x54 -> x52, waiting for transfers between devices: 72.2 us -> 85.2 us  [swap(): return lax.ppermute(x, axis, [(i, i ^ distance) for i in range(size)])]
    ppermute x54 -> x52, starting transfers between devices: 61.9 us -> 55.6 us  [swap(): return lax.ppermute(x, axis, [(i, i ^ distance) for i in range(size)])]
    pallas_call x2 -> x4, Pallas kernels: 24 us -> 20.6 us  [the longest x2 19.1 us: head_terms(): pl.pallas_call(functools.partial(head_kernel, len(pieces), tile, sub, len...]
  transfers between devices with their start and end apart: 54 -> 52, of which waited for: 26 -> 27; matrix products, arithmetic and copies ran while one was open for 1% -> 1% of each run, Pallas kernels for 30% -> 28%
where the time goes in v10:
time: 234 us; the launch traced here: 231 us
  Pallas kernels  87.2 us (37%)
  waiting for transfers between devices  85.2 us (36%)
  starting transfers between devices  55.6 us (24%)
  local copies, waits for them, and re-layouts  2.61 us (1%)
    ppermute x52, waiting for transfers between devices, swap(): return lax.ppermute(x, axis, [(i, i ^ distance) for i in range(size)])  85.2 us
    ppermute x52, starting transfers between devices, swap(): return lax.ppermute(x, axis, [(i, i ^ distance) for i in range(size)])  55.6 us
    pallas_call x4, Pallas kernels, hidden_rows(): pl.pallas_call(functools.partial(hidden_kernel, len(pieces), len(after),...  43 us
    pallas_call x2, Pallas kernels, head_terms(): pl.pallas_call(functools.partial(head_kernel, len(pieces), tile, sub, len...  19.1 us
    pallas_call x4, Pallas kernels, down_rows(): pl.pallas_call(functools.partial(down_kernel, start, len(hidden)), out_sh...  16 us
  transfers between devices with their start and end apart: 52, of which 27 were waited for; matrix products, arithmetic and copies ran while one was open for 1% of the time, Pallas kernels for 28%

profile of v10, /device:TPU:0, one launch (start us, length us, event | category | flops | bytes accessed | tf_op | source)
XLA Modules:
  0.0 231.4 jit_solution(11528856173131050790)
XLA Ops:
  1.0 5.1 %collective-permute-start.3 = (bf16[72,1024]{1,0:T(8,128)(2,1)S(1)}, bf16[72,1024]{1,0:T(8,128)(2,1)S(1)}, u32[]{:S(2)}, u32[]{:S(2)}) collective-permute-start(bf16[72,1024]{1,0:T(8,128)(2,1)S(1)} %get-tuple-element.42.refs_0_), channel_id=1, source_target_pairs={{0,3},{1,2},{2,1},{3,0},{4,7},{5,6},{6,5},{7,4},{8,11},{9,10},{10,... | collective-permute-start | bytes 442376 | tf_op jit(solution)/shard_map/ppermute | solution.py:32
  10.9 7.7 %collective-permute-done.4.refs_2_ = bf16[72,1024]{1,0:T(8,128)(2,1)S(1)} collective-permute-done((bf16[72,1024]{1,0:T(8,128)(2,1)S(1)}, bf16[72,1024]{1,0:T(8,128)(2,1)S(1)}, u32[]{:S(2)}, u32[]{:S(2)}) %collective-permute-start.4) | collective-permute-done | bytes 147488 | tf_op jit(solution)/shard_map/ppermute | solution.py:32
  26.4 3.8 %collective-permute-done.refs_1_.refs_3_ = bf16[64,1024]{1,0:T(8,128)(2,1)S(1)} collective-permute-done((bf16[64,1024]{1,0:T(8,128)(2,1)S(1)}, bf16[64,1024]{1,0:T(8,128)(2,1)S(1)}, u32[]{:S(2)}, u32[]{:S(2)}) %collective-permute-start) | collective-permute-done | bytes 131104 | tf_op jit(solution)/shard_map/ppermute | solution.py:32
  30.3 4.3 %collective-permute-done.1.refs_2_.refs_4_ = bf16[64,1024]{1,0:T(8,128)(2,1)S(1)} collective-permute-done((bf16[64,1024]{1,0:T(8,128)(2,1)S(1)}, bf16[64,1024]{1,0:T(8,128)(2,1)S(1)}, u32[]{:S(2)}, u32[]{:S(2)}) %collective-permute-start.1) | collective-permute-done | bytes 131104 | tf_op jit(solution)/shard_map/ppermute | solution.py:32
  36.1 7.8 %collective-permute-done.8.refs_7_.refs_0_.refs_3_ = bf16[32,4224]{1,0:T(8,128)(2,1)S(1)} collective-permute-done((bf16[32,4224]{1,0:T(8,128)(2,1)S(1)}, bf16[32,4224]{1,0:T(8,128)(2,1)S(1)}, u32[]{:S(2)}, u32[]{:S(2)}) %collective-permute-start.8) | collective-permute-done | bytes 270368 | tf_op jit(solution)/shard_map/ppermute | solution.py:32
  46.8 19.5 %hidden_rows.4.refs_0_ = bf16[512,1792]{1,0:T(8,128)(2,1)S(1)} custom-call(bf16[64,4224]{1,0:T(8,128)(2,1)S(1)} %get-tuple-element.44.refs_0_, bf16[64,4224]{1,0:T(8,128)(2,1)S(1)} %collective-permute-done.7.refs_1_, bf16[64,4224]{1,0:T(8,128)(2,1)S(1)} %collective-permute-done.6.refs_0_.refs_2_, ...), custom_call_target="tpu_custom_call" | custom-call | flops 15032385536 | bytes 35389440 | tf_op jit(solution)/shard_map/hidden_rows/pallas_call | solution.py:288
  66.4 4.2 %down_rows.5 = bf16[256,4096]{1,0:T(8,128)(2,1)S(1)} custom-call(bf16[512,1792]{1,0:T(8,128)(2,1)S(1)} %hidden_rows.4.refs_0_, bf16[1,1792,4096]{2,1,0:T(8,128)(2,1)S(1)} %bitcast.4, bf16[64,4224]{1,0:T(8,128)(2,1)S(1)} %collective-permute-done.10.refs_1_.refs_2_, bf16[64,4224]{1,0:T(8,128)(2,1)S(1)} %collective-permute-done.11.refs_0_.refs_2_.refs_3_), custom_call_target="tpu_custom_call" | custom-call | flops 3758096384 | bytes 3014656 | tf_op jit(solution)/shard_map/down_rows/pallas_call | solution.py:332
  73.6 3.9 %down_rows.4.refs_2_.kept_ref = bf16[256,4096]{1,0:T(8,128)(2,1)S(1)} custom-call(bf16[512,1792]{1,0:T(8,128)(2,1)S(1)} %hidden_rows.4.refs_0_, bf16[1,1792,4096]{2,1,0:T(8,128)(2,1)S(1)} %bitcast.4), custom_call_target="tpu_custom_call" | custom-call | flops 3758096384 | bytes 3014656 | tf_op jit(solution)/shard_map/down_rows/pallas_call | solution.py:332
  83.9 11.7 %hidden_rows.5.refs_0_ = bf16[512,1024]{1,0:T(8,128)(2,1)S(1)} custom-call(bf16[64,4224]{1,0:T(8,128)(2,1)S(1)} %get-tuple-element.47.refs_0_, bf16[64,4224]{1,0:T(8,128)(2,1)S(1)} %collective-permute-done.10.refs_1_.refs_2_, bf16[64,4224]{1,0:T(8,128)(2,1)S(1)} %collective-permute-done.11.refs_0_.refs_2_.refs_3_, ...), custom_call_target="tpu_custom_call" | custom-call | flops 8589934592 | bytes 22020096 | tf_op jit(solution)/shard_map/hidden_rows/pallas_call | solution.py:288
  98.7 7.0 %hidden_rows.6.refs_1_ = bf16[512,512]{1,0:T(8,128)(2,1)S(1)} custom-call(bf16[64,4224]{1,0:T(8,128)(2,1)S(1)} %get-tuple-element.47.refs_0_, bf16[64,4224]{1,0:T(8,128)(2,1)S(1)} %collective-permute-done.10.refs_1_.refs_2_, bf16[64,4224]{1,0:T(8,128)(2,1)S(1)} %collective-permute-done.11.refs_0_.refs_2_.refs_3_, ...), custom_call_target="tpu_custom_call" | custom-call | flops 4294967296 | bytes 13107200 | tf_op jit(solution)/shard_map/hidden_rows/pallas_call | solution.py:288
  110.5 4.7 %hidden_rows.7.refs_2_ = bf16[512,256]{1,0:T(8,128)(2,1)S(1)} custom-call(bf16[64,4224]{1,0:T(8,128)(2,1)S(1)} %get-tuple-element.47.refs_0_, bf16[64,4224]{1,0:T(8,128)(2,1)S(1)} %collective-permute-done.10.refs_1_.refs_2_, bf16[64,4224]{1,0:T(8,128)(2,1)S(1)} %collective-permute-done.11.refs_0_.refs_2_.refs_3_, ...), custom_call_target="tpu_custom_call" | custom-call | flops 2147483648 | bytes 8650752 | tf_op jit(solution)/shard_map/hidden_rows/pallas_call | solution.py:288
  118.4 3.9 %down_rows.7 = bf16[256,4096]{1,0:T(8,128)(2,1)S(1)} custom-call(bf16[512,1024]{1,0:T(8,128)(2,1)S(1)} %hidden_rows.5.refs_0_, bf16[512,512]{1,0:T(8,128)(2,1)S(1)} %hidden_rows.6.refs_1_, bf16[512,256]{1,0:T(8,128)(2,1)S(1)} %hidden_rows.7.refs_2_, bf16[1,1792,4096]{2,1,0:T(8,128)(2,1)S(1)} %bitcast.4, ...), custom_call_target="tpu_custom_call" | custom-call | flops 3758096384 | bytes 3014656 | tf_op jit(solution)/shard_map/down_rows/pallas_call | solution.py:332
  123.8 3.9 %down_rows.6.kept_ref = bf16[256,4096]{1,0:T(8,128)(2,1)S(1)} custom-call(bf16[512,1024]{1,0:T(8,128)(2,1)S(1)} %hidden_rows.5.refs_0_, bf16[512,512]{1,0:T(8,128)(2,1)S(1)} %hidden_rows.6.refs_1_, bf16[512,256]{1,0:T(8,128)(2,1)S(1)} %hidden_rows.7.refs_2_, bf16[1,1792,4096]{2,1,0:T(8,128)(2,1)S(1)} %bitcast.4, bf16[16,4096]{1,0:T(8,128)(2,1)S(1)} %final_rows.2.refs_4_.refs_5_), custom_call_target="tpu_custom_call" | custom-call | flops 3758096384 | bytes 3014656 | tf_op jit(solution)/shard_map/down_rows/pallas_call | solution.py:332
  134.6 3.9 %collective-permute-done.29.refs_0_.refs_8_ = bf16[16,4096]{1,0:T(8,128)(2,1)S(1)} collective-permute-done((bf16[16,4096]{1,0:T(8,128)(2,1)S(1)}, bf16[16,4096]{1,0:T(8,128)(2,1)S(1)}, u32[]{:S(2)}, u32[]{:S(2)}) %collective-permute-start.29) | collective-permute-done | bytes 131104 | tf_op jit(solution)/shard_map/ppermute | solution.py:32
  138.5 4.4 %collective-permute-done.30.refs_1_.refs_7_ = bf16[16,4096]{1,0:T(8,128)(2,1)S(1)} collective-permute-done((bf16[16,4096]{1,0:T(8,128)(2,1)S(1)}, bf16[16,4096]{1,0:T(8,128)(2,1)S(1)}, u32[]{:S(2)}, u32[]{:S(2)}) %collective-permute-start.30) | collective-permute-done | bytes 131104 | tf_op jit(solution)/shard_map/ppermute | solution.py:32
  145.5 5.9 %collective-permute-done.32.refs_3_ = bf16[32,4096]{1,0:T(8,128)(2,1)S(1)} collective-permute-done((bf16[32,4096]{1,0:T(8,128)(2,1)S(1)}, bf16[32,4096]{1,0:T(8,128)(2,1)S(1)}, u32[]{:S(2)}, u32[]{:S(2)}) %collective-permute-start.32) | collective-permute-done | bytes 262176 | tf_op jit(solution)/shard_map/ppermute | solution.py:32
  160.3 3.9 %collective-permute-done.34.refs_1_ = bf16[16,4096]{1,0:T(8,128)(2,1)S(1)} collective-permute-done((bf16[16,4096]{1,0:T(8,128)(2,1)S(1)}, bf16[16,4096]{1,0:T(8,128)(2,1)S(1)}, u32[]{:S(2)}, u32[]{:S(2)}) %collective-permute-start.34) | collective-permute-done | bytes 131104 | tf_op jit(solution)/shard_map/ppermute | solution.py:32
  164.1 3.5 %collective-permute-done.35.refs_2_ = bf16[16,4096]{1,0:T(8,128)(2,1)S(1)} collective-permute-done((bf16[16,4096]{1,0:T(8,128)(2,1)S(1)}, bf16[16,4096]{1,0:T(8,128)(2,1)S(1)}, u32[]{:S(2)}, u32[]{:S(2)}) %collective-permute-start.35) | collective-permute-done | bytes 131104 | tf_op jit(solution)/shard_map/ppermute | solution.py:32
  177.3 4.1 %collective-permute-done.38.refs_2_ = bf16[16,4096]{1,0:T(8,128)(2,1)S(1)} collective-permute-done((bf16[16,4096]{1,0:T(8,128)(2,1)S(1)}, bf16[16,4096]{1,0:T(8,128)(2,1)S(1)}, u32[]{:S(2)}, u32[]{:S(2)}) %collective-permute-start.38) | collective-permute-done | bytes 131104 | tf_op jit(solution)/shard_map/ppermute | solution.py:32
  183.8 9.5 %head_terms.2.refs_2_.refs_7_ = f32[8,256]{1,0:T(8,128)S(1)} custom-call(bf16[64,4096]{1,0:T(8,128)(2,1)S(1)} %get-tuple-element.72.refs_0_, bf16[64,4096]{1,0:T(8,128)(2,1)S(1)} %collective-permute-done.41.refs_1_, bf16[64,4096]{1,0:T(8,128)(2,1)S(1)} %collective-permute-done.40.refs_0_.refs_2_, bf16[32,4096]{1,0:T(8,128)(2,1)S(1)} %collective-permute-done.44.refs_3_, ...), custom_call_target="tpu_custom_call" | custom-call | flops 4194304000 | bytes 18481152 | tf_op jit(solution)/shard_map/head_terms/pallas_call | solution.py:475
  198.4 5.2 %collective-permute-done.46.refs_3_ = bf16[32,4096]{1,0:T(8,128)(2,1)S(1)} collective-permute-done((bf16[32,4096]{1,0:T(8,128)(2,1)S(1)}, bf16[32,4096]{1,0:T(8,128)(2,1)S(1)}, u32[]{:S(2)}, u32[]{:S(2)}) %collective-permute-start.46) | collective-permute-done | bytes 262176 | tf_op jit(solution)/shard_map/ppermute | solution.py:32
  204.7 9.6 %head_terms.3.mine_ref = f32[16,256]{1,0:T(8,128)S(1)} custom-call(bf16[64,4096]{1,0:T(8,128)(2,1)S(1)} %move_rows.16.refs_0_, bf16[64,4096]{1,0:T(8,128)(2,1)S(1)} %collective-permute-done.42.refs_1_, bf16[64,4096]{1,0:T(8,128)(2,1)S(1)} %collective-permute-done.43.refs_0_.refs_2_, bf16[32,4096]{1,0:T(8,128)(2,1)S(1)} %collective-permute-done.46.refs_3_, ...), custom_call_target="tpu_custom_call" | custom-call | flops 4194304000 | bytes 18481152 | tf_op jit(solution)/shard_map/head_terms/pallas_call | solution.py:475
  214.4 3.7 %collective-permute-done.48.got_ref = f32[16,256]{1,0:T(8,128)S(1)} collective-permute-done((f32[16,256]{1,0:T(8,128)S(1)}, f32[16,256]{1,0:T(8,128)S(1)}, u32[]{:S(2)}, u32[]{:S(2)}) %collective-permute-start.48) | collective-permute-done | bytes 16416 | tf_op jit(solution)/shard_map/ppermute | solution.py:32
  218.9 3.9 %collective-permute-done.49.got_ref = f32[16,256]{1,0:T(8,128)S(1)} collective-permute-done((f32[16,256]{1,0:T(8,128)S(1)}, f32[16,256]{1,0:T(8,128)S(1)}, u32[]{:S(2)}, u32[]{:S(2)}) %collective-permute-start.49) | collective-permute-done | bytes 16416 | tf_op jit(solution)/shard_map/ppermute | solution.py:32
  (134 shorter events, 85.2 us)
Async XLA Ops:
  6.2 12.5 %collective-permute-start.4 = (bf16[72,1024]{1,0:T(8,128)(2,1)S(1)}, bf16[72,1024]{1,0:T(8,128)(2,1)S(1)}, u32[]{:S(2)}, u32[]{:S(2)}) collective-permute-start(bf16[72,1024]{1,0:T(8,128)(2,1)S(1)} %get-tuple-element.42.refs_0_), channel_id=1, source_target_pairs={{0,2},{1,3},{2,0},{3,1},{4,6},{5,7},{6,4},{7,5},{8,10},{9,11},{10,... | collective-permute-start | bytes 442376 | tf_op jit(solution)/shard_map/ppermute | solution.py:32
  6.2 12.5 %collective-permute-start.5 = (bf16[72,1024]{1,0:T(8,128)(2,1)S(1)}, bf16[72,1024]{1,0:T(8,128)(2,1)S(1)}, u32[]{:S(2)}, u32[]{:S(2)}) collective-permute-start(bf16[72,1024]{1,0:T(8,128)(2,1)S(1)} %get-tuple-element.42.refs_0_), channel_id=1, source_target_pairs={{0,1},{1,0},{2,3},{3,2},{4,5},{5,4},{6,7},{7,6},{8,9},{9,8},{10,11... | collective-permute-start | bytes 442376 | tf_op jit(solution)/shard_map/ppermute | solution.py:32
  19.0 15.6 %collective-permute-start.6 = (bf16[64,4224]{1,0:T(8,128)(2,1)S(1)}, bf16[64,4224]{1,0:T(8,128)(2,1)S(1)}, u32[]{:S(2)}, u32[]{:S(2)}) collective-permute-start(bf16[64,4224]{1,0:T(8,128)(2,1)S(1)} %get-tuple-element.44.refs_0_), channel_id=1, source_target_pairs={{0,8},{4,12},{8,0},{12,4},{1,9},{5,13},{9,1},{13,5},{2,10},{6,14},... | collective-permute-start | bytes 1622024 | tf_op jit(solution)/shard_map/ppermute | solution.py:32
  20.6 14.0 %collective-permute-start.7 = (bf16[64,4224]{1,0:T(8,128)(2,1)S(1)}, bf16[64,4224]{1,0:T(8,128)(2,1)S(1)}, u32[]{:S(2)}, u32[]{:S(2)}) collective-permute-start(bf16[64,4224]{1,0:T(8,128)(2,1)S(1)} %get-tuple-element.44.refs_0_), channel_id=1, source_target_pairs={{0,4},{4,0},{8,12},{12,8},{1,5},{5,1},{9,13},{13,9},{2,6},{6,2},{1... | collective-permute-start | bytes 1622024 | tf_op jit(solution)/shard_map/ppermute | solution.py:32
  24.6 10.0 %collective-permute-start.2 = (bf16[64,1024]{1,0:T(8,128)(2,1)S(1)}, bf16[64,1024]{1,0:T(8,128)(2,1)S(1)}, u32[]{:S(2)}, u32[]{:S(2)}) collective-permute-start(bf16[64,1024]{1,0:T(8,128)(2,1)S(1)} %get-tuple-element.41.refs_0_), channel_id=1, source_target_pairs={{0,1},{1,0},{2,3},{3,2},{4,5},{5,4},{6,7},{7,6},{8,9},{9,8},{10,11... | collective-permute-start | bytes 393224 | tf_op jit(solution)/shard_map/ppermute | solution.py:32
  34.8 12.0 %collective-permute-start.15 = (bf16[192,4224]{1,0:T(8,128)(2,1)S(1)}, bf16[192,4224]{1,0:T(8,128)(2,1)S(1)}, u32[]{:S(2)}, u32[]{:S(2)}) collective-permute-start(bf16[192,4224]{1,0:T(8,128)(2,1)S(1)} %move_rows.12), channel_id=1, source_target_pairs={{0,16},{16,0},{1,17},{17,1},{2,18},{18,2},{3,19},{19,3},{4,20},{20... | collective-permute-start | bytes 4866056 | tf_op jit(solution)/shard_map/ppermute | solution.py:32
  44.7 21.6 %collective-permute-start.10 = (bf16[64,4224]{1,0:T(8,128)(2,1)S(1)}, bf16[64,4224]{1,0:T(8,128)(2,1)S(1)}, u32[]{:S(2)}, u32[]{:S(2)}) collective-permute-start(bf16[64,4224]{1,0:T(8,128)(2,1)S(1)} %get-tuple-element.47.refs_0_), channel_id=1, source_target_pairs={{0,4},{4,0},{8,12},{12,8},{1,5},{5,1},{9,13},{13,9},{2,6},{6,2},{1... | collective-permute-start | bytes 1622024 | tf_op jit(solution)/shard_map/ppermute | solution.py:32
  46.3 20.1 %collective-permute-start.11 = (bf16[64,4224]{1,0:T(8,128)(2,1)S(1)}, bf16[64,4224]{1,0:T(8,128)(2,1)S(1)}, u32[]{:S(2)}, u32[]{:S(2)}) collective-permute-start(bf16[64,4224]{1,0:T(8,128)(2,1)S(1)} %get-tuple-element.47.refs_0_), channel_id=1, source_target_pairs={{0,8},{4,12},{8,0},{12,4},{1,9},{5,13},{9,1},{13,5},{2,10},{6,14},... | collective-permute-start | bytes 1622024 | tf_op jit(solution)/shard_map/ppermute | solution.py:32
  70.6 10.3 %collective-permute-start.18 = (bf16[256,4096]{1,0:T(8,128)(2,1)S(1)}, bf16[256,4096]{1,0:T(8,128)(2,1)S(1)}, u32[]{:S(2)}, u32[]{:S(2)}) collective-permute-start(bf16[256,4096]{1,0:T(8,128)(2,1)S(1)} %down_rows.5), channel_id=1, source_target_pairs={{0,16},{16,0},{1,17},{17,1},{2,18},{18,2},{3,19},{19,3},{4,20},{20... | collective-permute-start | bytes 6291464 | tf_op jit(solution)/shard_map/ppermute | solution.py:32
  70.9 13.1 %collective-permute-start.14 = (bf16[192,4224]{1,0:T(8,128)(2,1)S(1)}, bf16[192,4224]{1,0:T(8,128)(2,1)S(1)}, u32[]{:S(2)}, u32[]{:S(2)}) collective-permute-start(bf16[192,4224]{1,0:T(8,128)(2,1)S(1)} %move_rows.11), channel_id=1, source_target_pairs={{0,16},{16,0},{1,17},{17,1},{2,18},{18,2},{3,19},{19,3},{4,20},{20... | collective-permute-start | bytes 4866056 | tf_op jit(solution)/shard_map/ppermute | solution.py:32
  81.3 14.4 %collective-permute-start.19 = (bf16[64,4096]{1,0:T(8,128)(2,1)S(1)}, bf16[64,4096]{1,0:T(8,128)(2,1)S(1)}, u32[]{:S(2)}, u32[]{:S(2)}) collective-permute-start(bf16[64,4096]{1,0:T(8,128)(2,1)S(1)} %get-tuple-element.50.refs_9_), channel_id=1, source_target_pairs={{0,4},{4,0},{8,12},{12,8},{1,5},{5,1},{9,13},{13,9},{2,6},{6,2},{1... | collective-permute-start | bytes 1572872 | tf_op jit(solution)/shard_map/ppermute | solution.py:32
  82.4 14.0 %collective-permute-start.20 = (bf16[64,4096]{1,0:T(8,128)(2,1)S(1)}, bf16[64,4096]{1,0:T(8,128)(2,1)S(1)}, u32[]{:S(2)}, u32[]{:S(2)}) collective-permute-start(bf16[64,4096]{1,0:T(8,128)(2,1)S(1)} %get-tuple-element.51.refs_10_), channel_id=1, source_target_pairs={{0,8},{4,12},{8,0},{12,4},{1,9},{5,13},{9,1},{13,5},{2,10},{6,14},... | collective-permute-start | bytes 1572872 | tf_op jit(solution)/shard_map/ppermute | solution.py:32
  128.2 14.8 %collective-permute-start.27 = (bf16[64,4096]{1,0:T(8,128)(2,1)S(1)}, bf16[64,4096]{1,0:T(8,128)(2,1)S(1)}, u32[]{:S(2)}, u32[]{:S(2)}) collective-permute-start(bf16[64,4096]{1,0:T(8,128)(2,1)S(1)} %get-tuple-element.62), channel_id=1, source_target_pairs={{0,4},{4,0},{8,12},{12,8},{1,5},{5,1},{9,13},{13,9},{2,6},{6,2},{1... | collective-permute-start | bytes 1572872 | tf_op jit(solution)/shard_map/ppermute | solution.py:32
  129.7 14.0 %collective-permute-start.28 = (bf16[64,4096]{1,0:T(8,128)(2,1)S(1)}, bf16[64,4096]{1,0:T(8,128)(2,1)S(1)}, u32[]{:S(2)}, u32[]{:S(2)}) collective-permute-start(bf16[64,4096]{1,0:T(8,128)(2,1)S(1)} %get-tuple-element.63), channel_id=1, source_target_pairs={{0,8},{4,12},{8,0},{12,4},{1,9},{5,13},{9,1},{13,5},{2,10},{6,14},... | collective-permute-start | bytes 1572872 | tf_op jit(solution)/shard_map/ppermute | solution.py:32
  131.8 11.2 %collective-permute-start.30 = (bf16[16,4096]{1,0:T(8,128)(2,1)S(1)}, bf16[16,4096]{1,0:T(8,128)(2,1)S(1)}, u32[]{:S(2)}, u32[]{:S(2)}) collective-permute-start(bf16[16,4096]{1,0:T(8,128)(2,1)S(1)} %final_rows.2.refs_4_.refs_5_), channel_id=1, source_target_pairs={{0,2},{1,3},{2,0},{3,1},{4,6},{5,7},{6,4},{7,5},{8,10},{9,11},{10,... | collective-permute-start | bytes 393224 | tf_op jit(solution)/shard_map/ppermute | solution.py:32
  131.8 11.2 %collective-permute-start.31 = (bf16[16,4096]{1,0:T(8,128)(2,1)S(1)}, bf16[16,4096]{1,0:T(8,128)(2,1)S(1)}, u32[]{:S(2)}, u32[]{:S(2)}) collective-permute-start(bf16[16,4096]{1,0:T(8,128)(2,1)S(1)} %final_rows.2.refs_4_.refs_5_), channel_id=1, source_target_pairs={{0,1},{1,0},{2,3},{3,2},{4,5},{5,4},{6,7},{7,6},{8,9},{9,8},{10,11... | collective-permute-start | bytes 393224 | tf_op jit(solution)/shard_map/ppermute | solution.py:32
  153.2 20.2 %collective-permute-start.40 = (bf16[64,4096]{1,0:T(8,128)(2,1)S(1)}, bf16[64,4096]{1,0:T(8,128)(2,1)S(1)}, u32[]{:S(2)}, u32[]{:S(2)}) collective-permute-start(bf16[64,4096]{1,0:T(8,128)(2,1)S(1)} %get-tuple-element.72.refs_0_), channel_id=1, source_target_pairs={{0,8},{4,12},{8,0},{12,4},{1,9},{5,13},{9,1},{13,5},{2,10},{6,14},... | collective-permute-start | bytes 1572872 | tf_op jit(solution)/shard_map/ppermute | solution.py:32
  154.7 18.8 %collective-permute-start.41 = (bf16[64,4096]{1,0:T(8,128)(2,1)S(1)}, bf16[64,4096]{1,0:T(8,128)(2,1)S(1)}, u32[]{:S(2)}, u32[]{:S(2)}) collective-permute-start(bf16[64,4096]{1,0:T(8,128)(2,1)S(1)} %get-tuple-element.72.refs_0_), channel_id=1, source_target_pairs={{0,4},{4,0},{8,12},{12,8},{1,5},{5,1},{9,13},{13,9},{2,6},{6,2},{1... | collective-permute-start | bytes 1572872 | tf_op jit(solution)/shard_map/ppermute | solution.py:32
  157.7 10.0 %collective-permute-start.35 = (bf16[16,4096]{1,0:T(8,128)(2,1)S(1)}, bf16[16,4096]{1,0:T(8,128)(2,1)S(1)}, u32[]{:S(2)}, u32[]{:S(2)}) collective-permute-start(bf16[16,4096]{1,0:T(8,128)(2,1)S(1)} %get-tuple-element.69), channel_id=1, source_target_pairs={{0,2},{1,3},{2,0},{3,1},{4,6},{5,7},{6,4},{7,5},{8,10},{9,11},{10,... | collective-permute-start | bytes 393224 | tf_op jit(solution)/shard_map/ppermute | solution.py:32
  157.7 10.0 %collective-permute-start.36 = (bf16[16,4096]{1,0:T(8,128)(2,1)S(1)}, bf16[16,4096]{1,0:T(8,128)(2,1)S(1)}, u32[]{:S(2)}, u32[]{:S(2)}) collective-permute-start(bf16[16,4096]{1,0:T(8,128)(2,1)S(1)} %get-tuple-element.70), channel_id=1, source_target_pairs={{0,1},{1,0},{2,3},{3,2},{4,5},{5,4},{6,7},{7,6},{8,9},{9,8},{10,11... | collective-permute-start | bytes 393224 | tf_op jit(solution)/shard_map/ppermute | solution.py:32
  171.1 10.3 %collective-permute-start.38 = (bf16[16,4096]{1,0:T(8,128)(2,1)S(1)}, bf16[16,4096]{1,0:T(8,128)(2,1)S(1)}, u32[]{:S(2)}, u32[]{:S(2)}) collective-permute-start(bf16[16,4096]{1,0:T(8,128)(2,1)S(1)} %final_rows.3.refs_0_), channel_id=1, source_target_pairs={{0,2},{1,3},{2,0},{3,1},{4,6},{5,7},{6,4},{7,5},{8,10},{9,11},{10,... | collective-permute-start | bytes 393224 | tf_op jit(solution)/shard_map/ppermute | solution.py:32
  171.1 10.3 %collective-permute-start.39 = (bf16[16,4096]{1,0:T(8,128)(2,1)S(1)}, bf16[16,4096]{1,0:T(8,128)(2,1)S(1)}, u32[]{:S(2)}, u32[]{:S(2)}) collective-permute-start(bf16[16,4096]{1,0:T(8,128)(2,1)S(1)} %final_rows.3.refs_0_), channel_id=1, source_target_pairs={{0,1},{1,0},{2,3},{3,2},{4,5},{5,4},{6,7},{7,6},{8,9},{9,8},{10,11... | collective-permute-start | bytes 393224 | tf_op jit(solution)/shard_map/ppermute | solution.py:32
  182.1 13.9 %collective-permute-start.42 = (bf16[64,4096]{1,0:T(8,128)(2,1)S(1)}, bf16[64,4096]{1,0:T(8,128)(2,1)S(1)}, u32[]{:S(2)}, u32[]{:S(2)}) collective-permute-start(bf16[64,4096]{1,0:T(8,128)(2,1)S(1)} %move_rows.16.refs_0_), channel_id=1, source_target_pairs={{0,4},{4,0},{8,12},{12,8},{1,5},{5,1},{9,13},{13,9},{2,6},{6,2},{1... | collective-permute-start | bytes 1572872 | tf_op jit(solution)/shard_map/ppermute | solution.py:32
  182.9 13.6 %collective-permute-start.43 = (bf16[64,4096]{1,0:T(8,128)(2,1)S(1)}, bf16[64,4096]{1,0:T(8,128)(2,1)S(1)}, u32[]{:S(2)}, u32[]{:S(2)}) collective-permute-start(bf16[64,4096]{1,0:T(8,128)(2,1)S(1)} %move_rows.16.refs_0_), channel_id=1, source_target_pairs={{0,8},{4,12},{8,0},{12,4},{1,9},{5,13},{9,1},{13,5},{2,10},{6,14},... | collective-permute-start | bytes 1572872 | tf_op jit(solution)/shard_map/ppermute | solution.py:32
  (33 other events, 325.6 us)

commit v11 on v10

--- a/solution.py
+++ b/solution.py
@@ -493,13 +493,17 @@
     )(*pieces, head_rows, targets, *earlier)
 
 
-def join_kernel(last, mine_ref, got_ref, out_ref):
-    for line in range(0, mine_ref.shape[0], 8):
-        top_one, top_two = mine_ref[line : line + 1, :], got_ref[line : line + 1, :]
-        top = jnp.maximum(top_one, top_two)
-        total = mine_ref[line + 1 : line + 2, :] * jnp.exp(top_one - top)
-        total = total + got_ref[line + 1 : line + 2, :] * jnp.exp(top_two - top)
-        target = mine_ref[line + 2 : line + 3, :] + got_ref[line + 2 : line + 3, :]
+def join_kernel(last, *refs):
+    out_ref = refs[-1]
+    for line in range(0, out_ref.shape[0], 8):
+
+        def each(offset):
+            return [ref[line + offset : line + offset + 1, :] for ref in refs[:-1]]
+
+        tops = each(0)
+        top = functools.reduce(jnp.maximum, tops)
+        total = sum(t * jnp.exp(m - top) for m, t in zip(tops, each(1)))
+        target = sum(each(2))
         if last:
             out_ref[line : line + 1, :] = top + jnp.log(total) - target
         else:
@@ -509,17 +513,11 @@
 
 
 def join_all(terms):
-    hops = []
     for axis in ("tensor", "expert"):
-        distance = 1
-        while distance < lax.axis_size(axis):
-            hops.append((axis, distance))
-            distance *= 2
-    for i, (axis, distance) in enumerate(hops):
         (terms,) = small_call(
-            functools.partial(join_kernel, i == len(hops) - 1),
+            functools.partial(join_kernel, axis == "expert"),
             "join",
-            [terms, swap(terms, axis, distance)],
+            far_first(gather_near(terms, axis)),
             [],
             [(terms.shape, jnp.float32)],
             [],

time: 234 us -> 231 us (0.987)
  waiting for transfers between devices: 85.2 us -> 76 us
  starting transfers between devices: 55.6 us -> 61.3 us
    ppermute x52 -> x54, waiting for transfers between devices: 85.2 us -> 76 us  [swap(): return lax.ppermute(x, axis, [(i, i ^ distance) for i in range(size)])]
    ppermute x52 -> x54, starting transfers between devices: 55.6 us -> 61.3 us  [swap(): return lax.ppermute(x, axis, [(i, i ^ distance) for i in range(size)])]
  transfers between devices with their start and end apart: 52 -> 54, of which waited for: 27 -> 27; matrix products, arithmetic and copies ran while one was open for 1% -> 1% of each run, Pallas kernels for 28% -> 29%
where the time goes in v11:
time: 231 us; the launch traced here: 228 us
  Pallas kernels  87.2 us (38%)
  waiting for transfers between devices  76 us (33%)
  starting transfers between devices  61.3 us (27%)
  local copies, waits for them, and re-layouts  2.61 us (1%)
    ppermute x54, waiting for transfers between devices, swap(): return lax.ppermute(x, axis, [(i, i ^ distance) for i in range(size)])  76 us
    ppermute x54, starting transfers between devices, swap(): return lax.ppermute(x, axis, [(i, i ^ distance) for i in range(size)])  61.3 us
    pallas_call x4, Pallas kernels, hidden_rows(): pl.pallas_call(functools.partial(hidden_kernel, len(pieces), len(after),...  43 us
    pallas_call x2, Pallas kernels, head_terms(): pl.pallas_call(functools.partial(head_kernel, len(pieces), tile, sub, len...  19.1 us
    pallas_call x4, Pallas kernels, down_rows(): pl.pallas_call(functools.partial(down_kernel, start, len(hidden)), out_sh...  16 us
  transfers between devices with their start and end apart: 54, of which 27 were waited for; matrix products, arithmetic and copies ran while one was open for 1% of the time, Pallas kernels for 29%

profile of v11, /device:TPU:0, one launch (start us, length us, event | category | flops | bytes accessed | tf_op | source)
XLA Modules:
  0.0 227.9 jit_solution(6395221525554539814)
XLA Ops:
  1.0 5.1 %collective-permute-start.3 = (bf16[72,1024]{1,0:T(8,128)(2,1)S(1)}, bf16[72,1024]{1,0:T(8,128)(2,1)S(1)}, u32[]{:S(2)}, u32[]{:S(2)}) collective-permute-start(bf16[72,1024]{1,0:T(8,128)(2,1)S(1)} %get-tuple-element.42.refs_0_), channel_id=1, source_target_pairs={{0,3},{1,2},{2,1},{3,0},{4,7},{5,6},{6,5},{7,4},{8,11},{9,10},{10,... | collective-permute-start | bytes 442376 | tf_op jit(solution)/shard_map/ppermute | solution.py:32
  10.9 7.7 %collective-permute-done.4.refs_2_ = bf16[72,1024]{1,0:T(8,128)(2,1)S(1)} collective-permute-done((bf16[72,1024]{1,0:T(8,128)(2,1)S(1)}, bf16[72,1024]{1,0:T(8,128)(2,1)S(1)}, u32[]{:S(2)}, u32[]{:S(2)}) %collective-permute-start.4) | collective-permute-done | bytes 147488 | tf_op jit(solution)/shard_map/ppermute | solution.py:32
  26.4 3.8 %collective-permute-done.refs_1_.refs_3_ = bf16[64,1024]{1,0:T(8,128)(2,1)S(1)} collective-permute-done((bf16[64,1024]{1,0:T(8,128)(2,1)S(1)}, bf16[64,1024]{1,0:T(8,128)(2,1)S(1)}, u32[]{:S(2)}, u32[]{:S(2)}) %collective-permute-start) | collective-permute-done | bytes 131104 | tf_op jit(solution)/shard_map/ppermute | solution.py:32
  30.3 4.3 %collective-permute-done.1.refs_2_.refs_4_ = bf16[64,1024]{1,0:T(8,128)(2,1)S(1)} collective-permute-done((bf16[64,1024]{1,0:T(8,128)(2,1)S(1)}, bf16[64,1024]{1,0:T(8,128)(2,1)S(1)}, u32[]{:S(2)}, u32[]{:S(2)}) %collective-permute-start.1) | collective-permute-done | bytes 131104 | tf_op jit(solution)/shard_map/ppermute | solution.py:32
  36.1 7.8 %collective-permute-done.8.refs_7_.refs_0_.refs_3_ = bf16[32,4224]{1,0:T(8,128)(2,1)S(1)} collective-permute-done((bf16[32,4224]{1,0:T(8,128)(2,1)S(1)}, bf16[32,4224]{1,0:T(8,128)(2,1)S(1)}, u32[]{:S(2)}, u32[]{:S(2)}) %collective-permute-start.8) | collective-permute-done | bytes 270368 | tf_op jit(solution)/shard_map/ppermute | solution.py:32
  46.8 19.5 %hidden_rows.4.refs_0_ = bf16[512,1792]{1,0:T(8,128)(2,1)S(1)} custom-call(bf16[64,4224]{1,0:T(8,128)(2,1)S(1)} %get-tuple-element.44.refs_0_, bf16[64,4224]{1,0:T(8,128)(2,1)S(1)} %collective-permute-done.7.refs_1_, bf16[64,4224]{1,0:T(8,128)(2,1)S(1)} %collective-permute-done.6.refs_0_.refs_2_, ...), custom_call_target="tpu_custom_call" | custom-call | flops 15032385536 | bytes 35389440 | tf_op jit(solution)/shard_map/hidden_rows/pallas_call | solution.py:288
  66.4 4.2 %down_rows.5 = bf16[256,4096]{1,0:T(8,128)(2,1)S(1)} custom-call(bf16[512,1792]{1,0:T(8,128)(2,1)S(1)} %hidden_rows.4.refs_0_, bf16[1,1792,4096]{2,1,0:T(8,128)(2,1)S(1)} %bitcast.4, bf16[64,4224]{1,0:T(8,128)(2,1)S(1)} %collective-permute-done.10.refs_1_.refs_2_, bf16[64,4224]{1,0:T(8,128)(2,1)S(1)} %collective-permute-done.11.refs_0_.refs_2_.refs_3_), custom_call_target="tpu_custom_call" | custom-call | flops 3758096384 | bytes 3014656 | tf_op jit(solution)/shard_map/down_rows/pallas_call | solution.py:332
  73.6 3.9 %down_rows.4.refs_2_.kept_ref = bf16[256,4096]{1,0:T(8,128)(2,1)S(1)} custom-call(bf16[512,1792]{1,0:T(8,128)(2,1)S(1)} %hidden_rows.4.refs_0_, bf16[1,1792,4096]{2,1,0:T(8,128)(2,1)S(1)} %bitcast.4), custom_call_target="tpu_custom_call" | custom-call | flops 3758096384 | bytes 3014656 | tf_op jit(solution)/shard_map/down_rows/pallas_call | solution.py:332
  83.9 11.7 %hidden_rows.5.refs_0_ = bf16[512,1024]{1,0:T(8,128)(2,1)S(1)} custom-call(bf16[64,4224]{1,0:T(8,128)(2,1)S(1)} %get-tuple-element.47.refs_0_, bf16[64,4224]{1,0:T(8,128)(2,1)S(1)} %collective-permute-done.10.refs_1_.refs_2_, bf16[64,4224]{1,0:T(8,128)(2,1)S(1)} %collective-permute-done.11.refs_0_.refs_2_.refs_3_, ...), custom_call_target="tpu_custom_call" | custom-call | flops 8589934592 | bytes 22020096 | tf_op jit(solution)/shard_map/hidden_rows/pallas_call | solution.py:288
  98.7 7.0 %hidden_rows.6.refs_1_ = bf16[512,512]{1,0:T(8,128)(2,1)S(1)} custom-call(bf16[64,4224]{1,0:T(8,128)(2,1)S(1)} %get-tuple-element.47.refs_0_, bf16[64,4224]{1,0:T(8,128)(2,1)S(1)} %collective-permute-done.10.refs_1_.refs_2_, bf16[64,4224]{1,0:T(8,128)(2,1)S(1)} %collective-permute-done.11.refs_0_.refs_2_.refs_3_, ...), custom_call_target="tpu_custom_call" | custom-call | flops 4294967296 | bytes 13107200 | tf_op jit(solution)/shard_map/hidden_rows/pallas_call | solution.py:288
  110.5 4.7 %hidden_rows.7.refs_2_ = bf16[512,256]{1,0:T(8,128)(2,1)S(1)} custom-call(bf16[64,4224]{1,0:T(8,128)(2,1)S(1)} %get-tuple-element.47.refs_0_, bf16[64,4224]{1,0:T(8,128)(2,1)S(1)} %collective-permute-done.10.refs_1_.refs_2_, bf16[64,4224]{1,0:T(8,128)(2,1)S(1)} %collective-permute-done.11.refs_0_.refs_2_.refs_3_, ...), custom_call_target="tpu_custom_call" | custom-call | flops 2147483648 | bytes 8650752 | tf_op jit(solution)/shard_map/hidden_rows/pallas_call | solution.py:288
  115.2 3.2 %collective-permute-done.24.refs_2_.refs_5_ = bf16[16,4096]{1,0:T(8,128)(2,1)S(1)} collective-permute-done((bf16[16,4096]{1,0:T(8,128)(2,1)S(1)}, bf16[16,4096]{1,0:T(8,128)(2,1)S(1)}, u32[]{:S(2)}, u32[]{:S(2)}) %collective-permute-start.24) | collective-permute-done | bytes 131104 | tf_op jit(solution)/shard_map/ppermute | solution.py:32
  118.4 3.9 %down_rows.7 = bf16[256,4096]{1,0:T(8,128)(2,1)S(1)} custom-call(bf16[512,1024]{1,0:T(8,128)(2,1)S(1)} %hidden_rows.5.refs_0_, bf16[512,512]{1,0:T(8,128)(2,1)S(1)} %hidden_rows.6.refs_1_, bf16[512,256]{1,0:T(8,128)(2,1)S(1)} %hidden_rows.7.refs_2_, bf16[1,1792,4096]{2,1,0:T(8,128)(2,1)S(1)} %bitcast.4, ...), custom_call_target="tpu_custom_call" | custom-call | flops 3758096384 | bytes 3014656 | tf_op jit(solution)/shard_map/down_rows/pallas_call | solution.py:332
  123.8 3.9 %down_rows.6.kept_ref = bf16[256,4096]{1,0:T(8,128)(2,1)S(1)} custom-call(bf16[512,1024]{1,0:T(8,128)(2,1)S(1)} %hidden_rows.5.refs_0_, bf16[512,512]{1,0:T(8,128)(2,1)S(1)} %hidden_rows.6.refs_1_, bf16[512,256]{1,0:T(8,128)(2,1)S(1)} %hidden_rows.7.refs_2_, bf16[1,1792,4096]{2,1,0:T(8,128)(2,1)S(1)} %bitcast.4, bf16[16,4096]{1,0:T(8,128)(2,1)S(1)} %final_rows.2.refs_4_.refs_5_), custom_call_target="tpu_custom_call" | custom-call | flops 3758096384 | bytes 3014656 | tf_op jit(solution)/shard_map/down_rows/pallas_call | solution.py:332
  131.8 2.8 %collective-permute-start.31 = (bf16[16,4096]{1,0:T(8,128)(2,1)S(1)}, bf16[16,4096]{1,0:T(8,128)(2,1)S(1)}, u32[]{:S(2)}, u32[]{:S(2)}) collective-permute-start(bf16[16,4096]{1,0:T(8,128)(2,1)S(1)} %final_rows.2.refs_4_.refs_5_), channel_id=1, source_target_pairs={{0,1},{1,0},{2,3},{3,2},{4,5},{5,4},{6,7},{7,6},{8,9},{9,8},{10,11... | collective-permute-start | bytes 393224 | tf_op jit(solution)/shard_map/ppermute | solution.py:32
  134.6 3.9 %collective-permute-done.29.refs_0_.refs_8_ = bf16[16,4096]{1,0:T(8,128)(2,1)S(1)} collective-permute-done((bf16[16,4096]{1,0:T(8,128)(2,1)S(1)}, bf16[16,4096]{1,0:T(8,128)(2,1)S(1)}, u32[]{:S(2)}, u32[]{:S(2)}) %collective-permute-start.29) | collective-permute-done | bytes 131104 | tf_op jit(solution)/shard_map/ppermute | solution.py:32
  138.5 4.4 %collective-permute-done.30.refs_1_.refs_7_ = bf16[16,4096]{1,0:T(8,128)(2,1)S(1)} collective-permute-done((bf16[16,4096]{1,0:T(8,128)(2,1)S(1)}, bf16[16,4096]{1,0:T(8,128)(2,1)S(1)}, u32[]{:S(2)}, u32[]{:S(2)}) %collective-permute-start.30) | collective-permute-done | bytes 131104 | tf_op jit(solution)/shard_map/ppermute | solution.py:32
  145.5 5.9 %collective-permute-done.32.refs_3_ = bf16[32,4096]{1,0:T(8,128)(2,1)S(1)} collective-permute-done((bf16[32,4096]{1,0:T(8,128)(2,1)S(1)}, bf16[32,4096]{1,0:T(8,128)(2,1)S(1)}, u32[]{:S(2)}, u32[]{:S(2)}) %collective-permute-start.32) | collective-permute-done | bytes 262176 | tf_op jit(solution)/shard_map/ppermute | solution.py:32
  160.3 3.9 %collective-permute-done.34.refs_1_ = bf16[16,4096]{1,0:T(8,128)(2,1)S(1)} collective-permute-done((bf16[16,4096]{1,0:T(8,128)(2,1)S(1)}, bf16[16,4096]{1,0:T(8,128)(2,1)S(1)}, u32[]{:S(2)}, u32[]{:S(2)}) %collective-permute-start.34) | collective-permute-done | bytes 131104 | tf_op jit(solution)/shard_map/ppermute | solution.py:32
  164.1 3.5 %collective-permute-done.35.refs_2_ = bf16[16,4096]{1,0:T(8,128)(2,1)S(1)} collective-permute-done((bf16[16,4096]{1,0:T(8,128)(2,1)S(1)}, bf16[16,4096]{1,0:T(8,128)(2,1)S(1)}, u32[]{:S(2)}, u32[]{:S(2)}) %collective-permute-start.35) | collective-permute-done | bytes 131104 | tf_op jit(solution)/shard_map/ppermute | solution.py:32
  177.3 4.1 %collective-permute-done.38.refs_2_ = bf16[16,4096]{1,0:T(8,128)(2,1)S(1)} collective-permute-done((bf16[16,4096]{1,0:T(8,128)(2,1)S(1)}, bf16[16,4096]{1,0:T(8,128)(2,1)S(1)}, u32[]{:S(2)}, u32[]{:S(2)}) %collective-permute-start.38) | collective-permute-done | bytes 131104 | tf_op jit(solution)/shard_map/ppermute | solution.py:32
  183.8 9.5 %head_terms.2.refs_2_.refs_7_ = f32[8,256]{1,0:T(8,128)S(1)} custom-call(bf16[64,4096]{1,0:T(8,128)(2,1)S(1)} %get-tuple-element.72.refs_0_, bf16[64,4096]{1,0:T(8,128)(2,1)S(1)} %collective-permute-done.41.refs_1_, bf16[64,4096]{1,0:T(8,128)(2,1)S(1)} %collective-permute-done.40.refs_0_.refs_2_, bf16[32,4096]{1,0:T(8,128)(2,1)S(1)} %collective-permute-done.44.refs_3_, ...), custom_call_target="tpu_custom_call" | custom-call | flops 4194304000 | bytes 18481152 | tf_op jit(solution)/shard_map/head_terms/pallas_call | solution.py:475
  198.4 5.2 %collective-permute-done.46.refs_3_ = bf16[32,4096]{1,0:T(8,128)(2,1)S(1)} collective-permute-done((bf16[32,4096]{1,0:T(8,128)(2,1)S(1)}, bf16[32,4096]{1,0:T(8,128)(2,1)S(1)}, u32[]{:S(2)}, u32[]{:S(2)}) %collective-permute-start.46) | collective-permute-done | bytes 262176 | tf_op jit(solution)/shard_map/ppermute | solution.py:32
  204.7 9.6 %head_terms.3.refs_0_ = f32[16,256]{1,0:T(8,128)S(1)} custom-call(bf16[64,4096]{1,0:T(8,128)(2,1)S(1)} %move_rows.16.refs_0_, bf16[64,4096]{1,0:T(8,128)(2,1)S(1)} %collective-permute-done.42.refs_1_, bf16[64,4096]{1,0:T(8,128)(2,1)S(1)} %collective-permute-done.43.refs_0_.refs_2_, bf16[32,4096]{1,0:T(8,128)(2,1)S(1)} %collective-permute-done.46.refs_3_, ...), custom_call_target="tpu_custom_call" | custom-call | flops 4194304000 | bytes 18481152 | tf_op jit(solution)/shard_map/head_terms/pallas_call | solution.py:475
  (136 shorter events, 83.3 us)
Async XLA Ops:
  6.2 12.5 %collective-permute-start.4 = (bf16[72,1024]{1,0:T(8,128)(2,1)S(1)}, bf16[72,1024]{1,0:T(8,128)(2,1)S(1)}, u32[]{:S(2)}, u32[]{:S(2)}) collective-permute-start(bf16[72,1024]{1,0:T(8,128)(2,1)S(1)} %get-tuple-element.42.refs_0_), channel_id=1, source_target_pairs={{0,2},{1,3},{2,0},{3,1},{4,6},{5,7},{6,4},{7,5},{8,10},{9,11},{10,... | collective-permute-start | bytes 442376 | tf_op jit(solution)/shard_map/ppermute | solution.py:32
  6.2 12.5 %collective-permute-start.5 = (bf16[72,1024]{1,0:T(8,128)(2,1)S(1)}, bf16[72,1024]{1,0:T(8,128)(2,1)S(1)}, u32[]{:S(2)}, u32[]{:S(2)}) collective-permute-start(bf16[72,1024]{1,0:T(8,128)(2,1)S(1)} %get-tuple-element.42.refs_0_), channel_id=1, source_target_pairs={{0,1},{1,0},{2,3},{3,2},{4,5},{5,4},{6,7},{7,6},{8,9},{9,8},{10,11... | collective-permute-start | bytes 442376 | tf_op jit(solution)/shard_map/ppermute | solution.py:32
  19.0 15.6 %collective-permute-start.6 = (bf16[64,4224]{1,0:T(8,128)(2,1)S(1)}, bf16[64,4224]{1,0:T(8,128)(2,1)S(1)}, u32[]{:S(2)}, u32[]{:S(2)}) collective-permute-start(bf16[64,4224]{1,0:T(8,128)(2,1)S(1)} %get-tuple-element.44.refs_0_), channel_id=1, source_target_pairs={{0,8},{4,12},{8,0},{12,4},{1,9},{5,13},{9,1},{13,5},{2,10},{6,14},... | collective-permute-start | bytes 1622024 | tf_op jit(solution)/shard_map/ppermute | solution.py:32
  20.6 14.0 %collective-permute-start.7 = (bf16[64,4224]{1,0:T(8,128)(2,1)S(1)}, bf16[64,4224]{1,0:T(8,128)(2,1)S(1)}, u32[]{:S(2)}, u32[]{:S(2)}) collective-permute-start(bf16[64,4224]{1,0:T(8,128)(2,1)S(1)} %get-tuple-element.44.refs_0_), channel_id=1, source_target_pairs={{0,4},{4,0},{8,12},{12,8},{1,5},{5,1},{9,13},{13,9},{2,6},{6,2},{1... | collective-permute-start | bytes 1622024 | tf_op jit(solution)/shard_map/ppermute | solution.py:32
  24.6 10.0 %collective-permute-start.1 = (bf16[64,1024]{1,0:T(8,128)(2,1)S(1)}, bf16[64,1024]{1,0:T(8,128)(2,1)S(1)}, u32[]{:S(2)}, u32[]{:S(2)}) collective-permute-start(bf16[64,1024]{1,0:T(8,128)(2,1)S(1)} %get-tuple-element.41.refs_0_), channel_id=1, source_target_pairs={{0,2},{1,3},{2,0},{3,1},{4,6},{5,7},{6,4},{7,5},{8,10},{9,11},{10,... | collective-permute-start | bytes 393224 | tf_op jit(solution)/shard_map/ppermute | solution.py:32
  34.8 12.0 %collective-permute-start.15 = (bf16[192,4224]{1,0:T(8,128)(2,1)S(1)}, bf16[192,4224]{1,0:T(8,128)(2,1)S(1)}, u32[]{:S(2)}, u32[]{:S(2)}) collective-permute-start(bf16[192,4224]{1,0:T(8,128)(2,1)S(1)} %move_rows.12), channel_id=1, source_target_pairs={{0,16},{16,0},{1,17},{17,1},{2,18},{18,2},{3,19},{19,3},{4,20},{20... | collective-permute-start | bytes 4866056 | tf_op jit(solution)/shard_map/ppermute | solution.py:32
  44.7 21.6 %collective-permute-start.10 = (bf16[64,4224]{1,0:T(8,128)(2,1)S(1)}, bf16[64,4224]{1,0:T(8,128)(2,1)S(1)}, u32[]{:S(2)}, u32[]{:S(2)}) collective-permute-start(bf16[64,4224]{1,0:T(8,128)(2,1)S(1)} %get-tuple-element.47.refs_0_), channel_id=1, source_target_pairs={{0,4},{4,0},{8,12},{12,8},{1,5},{5,1},{9,13},{13,9},{2,6},{6,2},{1... | collective-permute-start | bytes 1622024 | tf_op jit(solution)/shard_map/ppermute | solution.py:32
  46.3 20.1 %collective-permute-start.11 = (bf16[64,4224]{1,0:T(8,128)(2,1)S(1)}, bf16[64,4224]{1,0:T(8,128)(2,1)S(1)}, u32[]{:S(2)}, u32[]{:S(2)}) collective-permute-start(bf16[64,4224]{1,0:T(8,128)(2,1)S(1)} %get-tuple-element.47.refs_0_), channel_id=1, source_target_pairs={{0,8},{4,12},{8,0},{12,4},{1,9},{5,13},{9,1},{13,5},{2,10},{6,14},... | collective-permute-start | bytes 1622024 | tf_op jit(solution)/shard_map/ppermute | solution.py:32
  70.6 10.3 %collective-permute-start.18 = (bf16[256,4096]{1,0:T(8,128)(2,1)S(1)}, bf16[256,4096]{1,0:T(8,128)(2,1)S(1)}, u32[]{:S(2)}, u32[]{:S(2)}) collective-permute-start(bf16[256,4096]{1,0:T(8,128)(2,1)S(1)} %down_rows.5), channel_id=1, source_target_pairs={{0,16},{16,0},{1,17},{17,1},{2,18},{18,2},{3,19},{19,3},{4,20},{20... | collective-permute-start | bytes 6291464 | tf_op jit(solution)/shard_map/ppermute | solution.py:32
  70.9 13.1 %collective-permute-start.14 = (bf16[192,4224]{1,0:T(8,128)(2,1)S(1)}, bf16[192,4224]{1,0:T(8,128)(2,1)S(1)}, u32[]{:S(2)}, u32[]{:S(2)}) collective-permute-start(bf16[192,4224]{1,0:T(8,128)(2,1)S(1)} %move_rows.11), channel_id=1, source_target_pairs={{0,16},{16,0},{1,17},{17,1},{2,18},{18,2},{3,19},{19,3},{4,20},{20... | collective-permute-start | bytes 4866056 | tf_op jit(solution)/shard_map/ppermute | solution.py:32
  81.3 14.4 %collective-permute-start.19 = (bf16[64,4096]{1,0:T(8,128)(2,1)S(1)}, bf16[64,4096]{1,0:T(8,128)(2,1)S(1)}, u32[]{:S(2)}, u32[]{:S(2)}) collective-permute-start(bf16[64,4096]{1,0:T(8,128)(2,1)S(1)} %get-tuple-element.50.refs_9_), channel_id=1, source_target_pairs={{0,4},{4,0},{8,12},{12,8},{1,5},{5,1},{9,13},{13,9},{2,6},{6,2},{1... | collective-permute-start | bytes 1572872 | tf_op jit(solution)/shard_map/ppermute | solution.py:32
  82.4 14.0 %collective-permute-start.20 = (bf16[64,4096]{1,0:T(8,128)(2,1)S(1)}, bf16[64,4096]{1,0:T(8,128)(2,1)S(1)}, u32[]{:S(2)}, u32[]{:S(2)}) collective-permute-start(bf16[64,4096]{1,0:T(8,128)(2,1)S(1)} %get-tuple-element.51.refs_10_), channel_id=1, source_target_pairs={{0,8},{4,12},{8,0},{12,4},{1,9},{5,13},{9,1},{13,5},{2,10},{6,14},... | collective-permute-start | bytes 1572872 | tf_op jit(solution)/shard_map/ppermute | solution.py:32
  128.2 14.8 %collective-permute-start.27 = (bf16[64,4096]{1,0:T(8,128)(2,1)S(1)}, bf16[64,4096]{1,0:T(8,128)(2,1)S(1)}, u32[]{:S(2)}, u32[]{:S(2)}) collective-permute-start(bf16[64,4096]{1,0:T(8,128)(2,1)S(1)} %get-tuple-element.62), channel_id=1, source_target_pairs={{0,4},{4,0},{8,12},{12,8},{1,5},{5,1},{9,13},{13,9},{2,6},{6,2},{1... | collective-permute-start | bytes 1572872 | tf_op jit(solution)/shard_map/ppermute | solution.py:32
  129.7 14.0 %collective-permute-start.28 = (bf16[64,4096]{1,0:T(8,128)(2,1)S(1)}, bf16[64,4096]{1,0:T(8,128)(2,1)S(1)}, u32[]{:S(2)}, u32[]{:S(2)}) collective-permute-start(bf16[64,4096]{1,0:T(8,128)(2,1)S(1)} %get-tuple-element.63), channel_id=1, source_target_pairs={{0,8},{4,12},{8,0},{12,4},{1,9},{5,13},{9,1},{13,5},{2,10},{6,14},... | collective-permute-start | bytes 1572872 | tf_op jit(solution)/shard_map/ppermute | solution.py:32
  131.8 11.2 %collective-permute-start.30 = (bf16[16,4096]{1,0:T(8,128)(2,1)S(1)}, bf16[16,4096]{1,0:T(8,128)(2,1)S(1)}, u32[]{:S(2)}, u32[]{:S(2)}) collective-permute-start(bf16[16,4096]{1,0:T(8,128)(2,1)S(1)} %final_rows.2.refs_4_.refs_5_), channel_id=1, source_target_pairs={{0,2},{1,3},{2,0},{3,1},{4,6},{5,7},{6,4},{7,5},{8,10},{9,11},{10,... | collective-permute-start | bytes 393224 | tf_op jit(solution)/shard_map/ppermute | solution.py:32
  131.8 11.2 %collective-permute-start.31 = (bf16[16,4096]{1,0:T(8,128)(2,1)S(1)}, bf16[16,4096]{1,0:T(8,128)(2,1)S(1)}, u32[]{:S(2)}, u32[]{:S(2)}) collective-permute-start(bf16[16,4096]{1,0:T(8,128)(2,1)S(1)} %final_rows.2.refs_4_.refs_5_), channel_id=1, source_target_pairs={{0,1},{1,0},{2,3},{3,2},{4,5},{5,4},{6,7},{7,6},{8,9},{9,8},{10,11... | collective-permute-start | bytes 393224 | tf_op jit(solution)/shard_map/ppermute | solution.py:32
  153.2 20.2 %collective-permute-start.40 = (bf16[64,4096]{1,0:T(8,128)(2,1)S(1)}, bf16[64,4096]{1,0:T(8,128)(2,1)S(1)}, u32[]{:S(2)}, u32[]{:S(2)}) collective-permute-start(bf16[64,4096]{1,0:T(8,128)(2,1)S(1)} %get-tuple-element.72.refs_0_), channel_id=1, source_target_pairs={{0,8},{4,12},{8,0},{12,4},{1,9},{5,13},{9,1},{13,5},{2,10},{6,14},... | collective-permute-start | bytes 1572872 | tf_op jit(solution)/shard_map/ppermute | solution.py:32
  154.7 18.8 %collective-permute-start.41 = (bf16[64,4096]{1,0:T(8,128)(2,1)S(1)}, bf16[64,4096]{1,0:T(8,128)(2,1)S(1)}, u32[]{:S(2)}, u32[]{:S(2)}) collective-permute-start(bf16[64,4096]{1,0:T(8,128)(2,1)S(1)} %get-tuple-element.72.refs_0_), channel_id=1, source_target_pairs={{0,4},{4,0},{8,12},{12,8},{1,5},{5,1},{9,13},{13,9},{2,6},{6,2},{1... | collective-permute-start | bytes 1572872 | tf_op jit(solution)/shard_map/ppermute | solution.py:32
  157.7 10.0 %collective-permute-start.35 = (bf16[16,4096]{1,0:T(8,128)(2,1)S(1)}, bf16[16,4096]{1,0:T(8,128)(2,1)S(1)}, u32[]{:S(2)}, u32[]{:S(2)}) collective-permute-start(bf16[16,4096]{1,0:T(8,128)(2,1)S(1)} %get-tuple-element.69), channel_id=1, source_target_pairs={{0,2},{1,3},{2,0},{3,1},{4,6},{5,7},{6,4},{7,5},{8,10},{9,11},{10,... | collective-permute-start | bytes 393224 | tf_op jit(solution)/shard_map/ppermute | solution.py:32
  157.7 10.0 %collective-permute-start.36 = (bf16[16,4096]{1,0:T(8,128)(2,1)S(1)}, bf16[16,4096]{1,0:T(8,128)(2,1)S(1)}, u32[]{:S(2)}, u32[]{:S(2)}) collective-permute-start(bf16[16,4096]{1,0:T(8,128)(2,1)S(1)} %get-tuple-element.70), channel_id=1, source_target_pairs={{0,1},{1,0},{2,3},{3,2},{4,5},{5,4},{6,7},{7,6},{8,9},{9,8},{10,11... | collective-permute-start | bytes 393224 | tf_op jit(solution)/shard_map/ppermute | solution.py:32
  171.1 10.3 %collective-permute-start.38 = (bf16[16,4096]{1,0:T(8,128)(2,1)S(1)}, bf16[16,4096]{1,0:T(8,128)(2,1)S(1)}, u32[]{:S(2)}, u32[]{:S(2)}) collective-permute-start(bf16[16,4096]{1,0:T(8,128)(2,1)S(1)} %final_rows.3.refs_0_), channel_id=1, source_target_pairs={{0,2},{1,3},{2,0},{3,1},{4,6},{5,7},{6,4},{7,5},{8,10},{9,11},{10,... | collective-permute-start | bytes 393224 | tf_op jit(solution)/shard_map/ppermute | solution.py:32
  171.1 10.3 %collective-permute-start.39 = (bf16[16,4096]{1,0:T(8,128)(2,1)S(1)}, bf16[16,4096]{1,0:T(8,128)(2,1)S(1)}, u32[]{:S(2)}, u32[]{:S(2)}) collective-permute-start(bf16[16,4096]{1,0:T(8,128)(2,1)S(1)} %final_rows.3.refs_0_), channel_id=1, source_target_pairs={{0,1},{1,0},{2,3},{3,2},{4,5},{5,4},{6,7},{7,6},{8,9},{9,8},{10,11... | collective-permute-start | bytes 393224 | tf_op jit(solution)/shard_map/ppermute | solution.py:32
  182.1 13.9 %collective-permute-start.42 = (bf16[64,4096]{1,0:T(8,128)(2,1)S(1)}, bf16[64,4096]{1,0:T(8,128)(2,1)S(1)}, u32[]{:S(2)}, u32[]{:S(2)}) collective-permute-start(bf16[64,4096]{1,0:T(8,128)(2,1)S(1)} %move_rows.16.refs_0_), channel_id=1, source_target_pairs={{0,4},{4,0},{8,12},{12,8},{1,5},{5,1},{9,13},{13,9},{2,6},{6,2},{1... | collective-permute-start | bytes 1572872 | tf_op jit(solution)/shard_map/ppermute | solution.py:32
  182.9 13.6 %collective-permute-start.43 = (bf16[64,4096]{1,0:T(8,128)(2,1)S(1)}, bf16[64,4096]{1,0:T(8,128)(2,1)S(1)}, u32[]{:S(2)}, u32[]{:S(2)}) collective-permute-start(bf16[64,4096]{1,0:T(8,128)(2,1)S(1)} %move_rows.16.refs_0_), channel_id=1, source_target_pairs={{0,8},{4,12},{8,0},{12,4},{1,9},{5,13},{9,1},{13,5},{2,10},{6,14},... | collective-permute-start | bytes 1572872 | tf_op jit(solution)/shard_map/ppermute | solution.py:32
  (35 other events, 336.8 us)

commit v12 on v11

--- a/solution.py
+++ b/solution.py
@@ -101,21 +101,6 @@
     count, size = len(pieces), pieces[0].shape[0]
     moves = [(i, 0, size, 0, (count - i if i else 0) * size) for i in range(count)]
     return move_rows(far_first(pieces), moves, after)[0]
-
-
-def load_pieces(piece_refs, scratch, sems):
-    copies = []
-    start = 0
-    for i in range(len(piece_refs)):
-        count = piece_refs[i].shape[0]
-        copies.append(
-            pltpu.make_async_copy(piece_refs[i], scratch.at[pl.ds(start, count), :], sems.at[i])
-        )
-        start += count
-    for copy in copies:
-        copy.start()
-    for copy in copies:
-        copy.wait()
 
 
 def begin_kernel(count, splits, *refs):
@@ -256,24 +241,53 @@
         copy.wait()
 
     fetch(0, start)
-    load_pieces(piece_refs, rows_scr, sems)
+    total_rows = rows_scr.shape[0]
+    copies, ends = [], []
+    for i in range(pieces):
+        place = ends[-1] if ends else 0
+        ends.append(place + piece_refs[i].shape[0])
+        block = rows_scr.at[pl.ds(place, piece_refs[i].shape[0]), :]
+        copies.append(pltpu.make_async_copy(piece_refs[i], block, sems.at[i]))
+    for copy in copies:
+        copy.start()
     for i in range(1, min(SLOTS - 1, steps)):
         fetch(i, start)
-    small = rows_scr[:, full_width:].astype(jnp.float32)
-    lane = lax.broadcasted_iota(jnp.int32, small.shape, 1)
-    place = lax.axis_index("expert") * 3
-    mine = (lane >= place) & (lane < place + 3)
-    weight = jnp.sum(jnp.where(mine, small, 0.0), axis=1, keepdims=True)
-    route_scr[...] = jnp.broadcast_to(0.5 * weight, route_scr.shape)
-    for i in range(steps):
+
+    def route_weights_of(block):
+        small = rows_scr[block, full_width:].astype(jnp.float32)
+        lane = lax.broadcasted_iota(jnp.int32, small.shape, 1)
+        place = lax.axis_index("expert") * 3
+        mine = (lane >= place) & (lane < place + 3)
+        weight = jnp.sum(jnp.where(mine, small, 0.0), axis=1, keepdims=True)
+        route_scr[block, :] = jnp.broadcast_to(0.5 * weight, small.shape)
+
+    def work(i, block):
+        rows = rows_scr[block, :full_width]
+        gate = jnp.dot(rows, weight_scr[0, i % SLOTS], preferred_element_type=jnp.float32)
+        up = jnp.dot(rows, weight_scr[1, i % SLOTS], preferred_element_type=jnp.float32)
+        hidden = gate * (1.0 + jnp.tanh(0.5 * gate)) * up * route_scr[block, :1]
+        out_ref[block, i * tile : (i + 1) * tile] = hidden.astype(jnp.bfloat16)
+
+    cut = ends.index(total_rows // 2) + 1 if total_rows // 2 in ends else pieces
+    for copy in copies[:cut]:
+        copy.wait()
+    first_rows = slice(0, ends[cut - 1])
+    route_weights_of(first_rows)
+    fetch(0, wait)
+    if SLOTS - 1 < steps:
+        fetch(SLOTS - 1, start)
+    work(0, first_rows)
+    if cut < pieces:
+        for copy in copies[cut:]:
+            copy.wait()
+        other_rows = slice(ends[cut - 1], total_rows)
+        route_weights_of(other_rows)
+        work(0, other_rows)
+    for i in range(1, steps):
         fetch(i, wait)
         if i + SLOTS - 1 < steps:
             fetch(i + SLOTS - 1, start)
-        rows = rows_scr[:, :full_width]
-        gate = jnp.dot(rows, weight_scr[0, i % SLOTS], preferred_element_type=jnp.float32)
-        up = jnp.dot(rows, weight_scr[1, i % SLOTS], preferred_element_type=jnp.float32)
-        hidden = gate * (1.0 + jnp.tanh(0.5 * gate)) * up * route_scr[:, :1]
-        out_ref[:, i * tile : (i + 1) * tile] = hidden.astype(jnp.bfloat16)
+        work(i, slice(0, total_rows))
 
 
 def tile_of(weight):

time: 231 us -> 231 us (level)
  no operation moved by 1% of the time
where the time goes in v12:
time: 231 us; the launch traced here: 229 us
  Pallas kernels  88 us (38%)
  waiting for transfers between devices  75.5 us (33%)
  starting transfers between devices  62 us (27%)
  local copies, waits for them, and re-layouts  2.61 us (1%)
    ppermute x54, waiting for transfers between devices, swap(): return lax.ppermute(x, axis, [(i, i ^ distance) for i in range(size)])  75.5 us
    ppermute x54, starting transfers between devices, swap(): return lax.ppermute(x, axis, [(i, i ^ distance) for i in range(size)])  62 us
    pallas_call x4, Pallas kernels, hidden_rows(): pl.pallas_call(functools.partial(hidden_kernel, len(pieces), len(after),...  43.7 us
    pallas_call x2, Pallas kernels, head_terms(): pl.pallas_call(functools.partial(head_kernel, len(pieces), tile, sub, len...  19.1 us
    pallas_call x4, Pallas kernels, down_rows(): pl.pallas_call(functools.partial(down_kernel, start, len(hidden)), out_sh...  16 us
  transfers between devices with their start and end apart: 54, of which 27 were waited for; matrix products, arithmetic and copies ran while one was open for 1% of the time, Pallas kernels for 29%

profile of v12, /device:TPU:0, one launch (start us, length us, event | category | flops | bytes accessed | tf_op | source)
XLA Modules:
  0.0 228.8 jit_solution(7977720571785257153)
XLA Ops:
  1.0 5.1 %collective-permute-start.3 = (bf16[72,1024]{1,0:T(8,128)(2,1)S(1)}, bf16[72,1024]{1,0:T(8,128)(2,1)S(1)}, u32[]{:S(2)}, u32[]{:S(2)}) collective-permute-start(bf16[72,1024]{1,0:T(8,128)(2,1)S(1)} %get-tuple-element.42.refs_0_), channel_id=1, source_target_pairs={{0,3},{1,2},{2,1},{3,0},{4,7},{5,6},{6,5},{7,4},{8,11},{9,10},{10,... | collective-permute-start | bytes 442376 | tf_op jit(solution)/shard_map/ppermute | solution.py:32
  10.9 7.7 %collective-permute-done.4.refs_2_ = bf16[72,1024]{1,0:T(8,128)(2,1)S(1)} collective-permute-done((bf16[72,1024]{1,0:T(8,128)(2,1)S(1)}, bf16[72,1024]{1,0:T(8,128)(2,1)S(1)}, u32[]{:S(2)}, u32[]{:S(2)}) %collective-permute-start.4) | collective-permute-done | bytes 147488 | tf_op jit(solution)/shard_map/ppermute | solution.py:32
  26.4 3.8 %collective-permute-done.refs_1_.refs_3_ = bf16[64,1024]{1,0:T(8,128)(2,1)S(1)} collective-permute-done((bf16[64,1024]{1,0:T(8,128)(2,1)S(1)}, bf16[64,1024]{1,0:T(8,128)(2,1)S(1)}, u32[]{:S(2)}, u32[]{:S(2)}) %collective-permute-start) | collective-permute-done | bytes 131104 | tf_op jit(solution)/shard_map/ppermute | solution.py:32
  30.3 4.3 %collective-permute-done.1.refs_2_.refs_4_ = bf16[64,1024]{1,0:T(8,128)(2,1)S(1)} collective-permute-done((bf16[64,1024]{1,0:T(8,128)(2,1)S(1)}, bf16[64,1024]{1,0:T(8,128)(2,1)S(1)}, u32[]{:S(2)}, u32[]{:S(2)}) %collective-permute-start.1) | collective-permute-done | bytes 131104 | tf_op jit(solution)/shard_map/ppermute | solution.py:32
  36.1 7.8 %collective-permute-done.8.refs_7_.refs_0_.refs_3_ = bf16[32,4224]{1,0:T(8,128)(2,1)S(1)} collective-permute-done((bf16[32,4224]{1,0:T(8,128)(2,1)S(1)}, bf16[32,4224]{1,0:T(8,128)(2,1)S(1)}, u32[]{:S(2)}, u32[]{:S(2)}) %collective-permute-start.8) | collective-permute-done | bytes 270368 | tf_op jit(solution)/shard_map/ppermute | solution.py:32
  46.8 19.7 %hidden_rows.4.refs_0_ = bf16[512,1792]{1,0:T(8,128)(2,1)S(1)} custom-call(bf16[64,4224]{1,0:T(8,128)(2,1)S(1)} %get-tuple-element.44.refs_0_, bf16[64,4224]{1,0:T(8,128)(2,1)S(1)} %collective-permute-done.7.refs_1_, bf16[64,4224]{1,0:T(8,128)(2,1)S(1)} %collective-permute-done.6.refs_0_.refs_2_, ...), custom_call_target="tpu_custom_call" | custom-call | flops 15032385536 | bytes 35389440 | tf_op jit(solution)/shard_map/hidden_rows/pallas_call | solution.py:302
  66.6 4.1 %down_rows.5 = bf16[256,4096]{1,0:T(8,128)(2,1)S(1)} custom-call(bf16[512,1792]{1,0:T(8,128)(2,1)S(1)} %hidden_rows.4.refs_0_, bf16[1,1792,4096]{2,1,0:T(8,128)(2,1)S(1)} %bitcast.4, bf16[64,4224]{1,0:T(8,128)(2,1)S(1)} %collective-permute-done.10.refs_1_.refs_2_, bf16[64,4224]{1,0:T(8,128)(2,1)S(1)} %collective-permute-done.11.refs_0_.refs_2_.refs_3_), custom_call_target="tpu_custom_call" | custom-call | flops 3758096384 | bytes 3014656 | tf_op jit(solution)/shard_map/down_rows/pallas_call | solution.py:346
  73.8 3.9 %down_rows.4.refs_2_.kept_ref = bf16[256,4096]{1,0:T(8,128)(2,1)S(1)} custom-call(bf16[512,1792]{1,0:T(8,128)(2,1)S(1)} %hidden_rows.4.refs_0_, bf16[1,1792,4096]{2,1,0:T(8,128)(2,1)S(1)} %bitcast.4), custom_call_target="tpu_custom_call" | custom-call | flops 3758096384 | bytes 3014656 | tf_op jit(solution)/shard_map/down_rows/pallas_call | solution.py:346
  84.5 11.9 %hidden_rows.5.refs_0_ = bf16[512,1024]{1,0:T(8,128)(2,1)S(1)} custom-call(bf16[64,4224]{1,0:T(8,128)(2,1)S(1)} %get-tuple-element.47.refs_0_, bf16[64,4224]{1,0:T(8,128)(2,1)S(1)} %collective-permute-done.10.refs_1_.refs_2_, bf16[64,4224]{1,0:T(8,128)(2,1)S(1)} %collective-permute-done.11.refs_0_.refs_2_.refs_3_, ...), custom_call_target="tpu_custom_call" | custom-call | flops 8589934592 | bytes 22020096 | tf_op jit(solution)/shard_map/hidden_rows/pallas_call | solution.py:302
  99.1 7.2 %hidden_rows.6.refs_1_ = bf16[512,512]{1,0:T(8,128)(2,1)S(1)} custom-call(bf16[64,4224]{1,0:T(8,128)(2,1)S(1)} %get-tuple-element.47.refs_0_, bf16[64,4224]{1,0:T(8,128)(2,1)S(1)} %collective-permute-done.10.refs_1_.refs_2_, bf16[64,4224]{1,0:T(8,128)(2,1)S(1)} %collective-permute-done.11.refs_0_.refs_2_.refs_3_, ...), custom_call_target="tpu_custom_call" | custom-call | flops 4294967296 | bytes 13107200 | tf_op jit(solution)/shard_map/hidden_rows/pallas_call | solution.py:302
  111.1 4.9 %hidden_rows.7.refs_2_ = bf16[512,256]{1,0:T(8,128)(2,1)S(1)} custom-call(bf16[64,4224]{1,0:T(8,128)(2,1)S(1)} %get-tuple-element.47.refs_0_, bf16[64,4224]{1,0:T(8,128)(2,1)S(1)} %collective-permute-done.10.refs_1_.refs_2_, bf16[64,4224]{1,0:T(8,128)(2,1)S(1)} %collective-permute-done.11.refs_0_.refs_2_.refs_3_, ...), custom_call_target="tpu_custom_call" | custom-call | flops 2147483648 | bytes 8650752 | tf_op jit(solution)/shard_map/hidden_rows/pallas_call | solution.py:302
  116.0 3.0 %collective-permute-done.24.refs_2_.refs_5_ = bf16[16,4096]{1,0:T(8,128)(2,1)S(1)} collective-permute-done((bf16[16,4096]{1,0:T(8,128)(2,1)S(1)}, bf16[16,4096]{1,0:T(8,128)(2,1)S(1)}, u32[]{:S(2)}, u32[]{:S(2)}) %collective-permute-start.24) | collective-permute-done | bytes 131104 | tf_op jit(solution)/shard_map/ppermute | solution.py:32
  119.1 3.9 %down_rows.7 = bf16[256,4096]{1,0:T(8,128)(2,1)S(1)} custom-call(bf16[512,1024]{1,0:T(8,128)(2,1)S(1)} %hidden_rows.5.refs_0_, bf16[512,512]{1,0:T(8,128)(2,1)S(1)} %hidden_rows.6.refs_1_, bf16[512,256]{1,0:T(8,128)(2,1)S(1)} %hidden_rows.7.refs_2_, bf16[1,1792,4096]{2,1,0:T(8,128)(2,1)S(1)} %bitcast.4, ...), custom_call_target="tpu_custom_call" | custom-call | flops 3758096384 | bytes 3014656 | tf_op jit(solution)/shard_map/down_rows/pallas_call | solution.py:346
  124.6 3.9 %down_rows.6.kept_ref = bf16[256,4096]{1,0:T(8,128)(2,1)S(1)} custom-call(bf16[512,1024]{1,0:T(8,128)(2,1)S(1)} %hidden_rows.5.refs_0_, bf16[512,512]{1,0:T(8,128)(2,1)S(1)} %hidden_rows.6.refs_1_, bf16[512,256]{1,0:T(8,128)(2,1)S(1)} %hidden_rows.7.refs_2_, bf16[1,1792,4096]{2,1,0:T(8,128)(2,1)S(1)} %bitcast.4, bf16[16,4096]{1,0:T(8,128)(2,1)S(1)} %final_rows.2.refs_4_.refs_5_), custom_call_target="tpu_custom_call" | custom-call | flops 3758096384 | bytes 3014656 | tf_op jit(solution)/shard_map/down_rows/pallas_call | solution.py:346
  132.6 2.9 %collective-permute-start.31 = (bf16[16,4096]{1,0:T(8,128)(2,1)S(1)}, bf16[16,4096]{1,0:T(8,128)(2,1)S(1)}, u32[]{:S(2)}, u32[]{:S(2)}) collective-permute-start(bf16[16,4096]{1,0:T(8,128)(2,1)S(1)} %final_rows.2.refs_4_.refs_5_), channel_id=1, source_target_pairs={{0,1},{1,0},{2,3},{3,2},{4,5},{5,4},{6,7},{7,6},{8,9},{9,8},{10,11... | collective-permute-start | bytes 393224 | tf_op jit(solution)/shard_map/ppermute | solution.py:32
  135.5 3.9 %collective-permute-done.29.refs_0_.refs_8_ = bf16[16,4096]{1,0:T(8,128)(2,1)S(1)} collective-permute-done((bf16[16,4096]{1,0:T(8,128)(2,1)S(1)}, bf16[16,4096]{1,0:T(8,128)(2,1)S(1)}, u32[]{:S(2)}, u32[]{:S(2)}) %collective-permute-start.29) | collective-permute-done | bytes 131104 | tf_op jit(solution)/shard_map/ppermute | solution.py:32
  139.3 4.4 %collective-permute-done.30.refs_1_.refs_7_ = bf16[16,4096]{1,0:T(8,128)(2,1)S(1)} collective-permute-done((bf16[16,4096]{1,0:T(8,128)(2,1)S(1)}, bf16[16,4096]{1,0:T(8,128)(2,1)S(1)}, u32[]{:S(2)}, u32[]{:S(2)}) %collective-permute-start.30) | collective-permute-done | bytes 131104 | tf_op jit(solution)/shard_map/ppermute | solution.py:32
  146.6 5.9 %collective-permute-done.32.refs_3_ = bf16[32,4096]{1,0:T(8,128)(2,1)S(1)} collective-permute-done((bf16[32,4096]{1,0:T(8,128)(2,1)S(1)}, bf16[32,4096]{1,0:T(8,128)(2,1)S(1)}, u32[]{:S(2)}, u32[]{:S(2)}) %collective-permute-start.32) | collective-permute-done | bytes 262176 | tf_op jit(solution)/shard_map/ppermute | solution.py:32
  161.2 3.9 %collective-permute-done.34.refs_1_ = bf16[16,4096]{1,0:T(8,128)(2,1)S(1)} collective-permute-done((bf16[16,4096]{1,0:T(8,128)(2,1)S(1)}, bf16[16,4096]{1,0:T(8,128)(2,1)S(1)}, u32[]{:S(2)}, u32[]{:S(2)}) %collective-permute-start.34) | collective-permute-done | bytes 131104 | tf_op jit(solution)/shard_map/ppermute | solution.py:32
  165.0 3.5 %collective-permute-done.35.refs_2_ = bf16[16,4096]{1,0:T(8,128)(2,1)S(1)} collective-permute-done((bf16[16,4096]{1,0:T(8,128)(2,1)S(1)}, bf16[16,4096]{1,0:T(8,128)(2,1)S(1)}, u32[]{:S(2)}, u32[]{:S(2)}) %collective-permute-start.35) | collective-permute-done | bytes 131104 | tf_op jit(solution)/shard_map/ppermute | solution.py:32
  178.2 4.1 %collective-permute-done.38.refs_2_ = bf16[16,4096]{1,0:T(8,128)(2,1)S(1)} collective-permute-done((bf16[16,4096]{1,0:T(8,128)(2,1)S(1)}, bf16[16,4096]{1,0:T(8,128)(2,1)S(1)}, u32[]{:S(2)}, u32[]{:S(2)}) %collective-permute-start.38) | collective-permute-done | bytes 131104 | tf_op jit(solution)/shard_map/ppermute | solution.py:32
  184.6 9.5 %head_terms.2.refs_2_.refs_7_ = f32[8,256]{1,0:T(8,128)S(1)} custom-call(bf16[64,4096]{1,0:T(8,128)(2,1)S(1)} %get-tuple-element.72.refs_0_, bf16[64,4096]{1,0:T(8,128)(2,1)S(1)} %collective-permute-done.41.refs_1_, bf16[64,4096]{1,0:T(8,128)(2,1)S(1)} %collective-permute-done.40.refs_0_.refs_2_, bf16[32,4096]{1,0:T(8,128)(2,1)S(1)} %collective-permute-done.44.refs_3_, ...), custom_call_target="tpu_custom_call" | custom-call | flops 4194304000 | bytes 18481152 | tf_op jit(solution)/shard_map/head_terms/pallas_call | solution.py:489
  199.3 5.1 %collective-permute-done.46.refs_3_ = bf16[32,4096]{1,0:T(8,128)(2,1)S(1)} collective-permute-done((bf16[32,4096]{1,0:T(8,128)(2,1)S(1)}, bf16[32,4096]{1,0:T(8,128)(2,1)S(1)}, u32[]{:S(2)}, u32[]{:S(2)}) %collective-permute-start.46) | collective-permute-done | bytes 262176 | tf_op jit(solution)/shard_map/ppermute | solution.py:32
  205.6 9.6 %head_terms.3.refs_0_ = f32[16,256]{1,0:T(8,128)S(1)} custom-call(bf16[64,4096]{1,0:T(8,128)(2,1)S(1)} %move_rows.16.refs_0_, bf16[64,4096]{1,0:T(8,128)(2,1)S(1)} %collective-permute-done.42.refs_1_, bf16[64,4096]{1,0:T(8,128)(2,1)S(1)} %collective-permute-done.43.refs_0_.refs_2_, bf16[32,4096]{1,0:T(8,128)(2,1)S(1)} %collective-permute-done.46.refs_3_, ...), custom_call_target="tpu_custom_call" | custom-call | flops 4194304000 | bytes 18481152 | tf_op jit(solution)/shard_map/head_terms/pallas_call | solution.py:489
  (136 shorter events, 83.7 us)
Async XLA Ops:
  6.2 12.5 %collective-permute-start.4 = (bf16[72,1024]{1,0:T(8,128)(2,1)S(1)}, bf16[72,1024]{1,0:T(8,128)(2,1)S(1)}, u32[]{:S(2)}, u32[]{:S(2)}) collective-permute-start(bf16[72,1024]{1,0:T(8,128)(2,1)S(1)} %get-tuple-element.42.refs_0_), channel_id=1, source_target_pairs={{0,2},{1,3},{2,0},{3,1},{4,6},{5,7},{6,4},{7,5},{8,10},{9,11},{10,... | collective-permute-start | bytes 442376 | tf_op jit(solution)/shard_map/ppermute | solution.py:32
  6.2 12.5 %collective-permute-start.5 = (bf16[72,1024]{1,0:T(8,128)(2,1)S(1)}, bf16[72,1024]{1,0:T(8,128)(2,1)S(1)}, u32[]{:S(2)}, u32[]{:S(2)}) collective-permute-start(bf16[72,1024]{1,0:T(8,128)(2,1)S(1)} %get-tuple-element.42.refs_0_), channel_id=1, source_target_pairs={{0,1},{1,0},{2,3},{3,2},{4,5},{5,4},{6,7},{7,6},{8,9},{9,8},{10,11... | collective-permute-start | bytes 442376 | tf_op jit(solution)/shard_map/ppermute | solution.py:32
  19.0 15.6 %collective-permute-start.6 = (bf16[64,4224]{1,0:T(8,128)(2,1)S(1)}, bf16[64,4224]{1,0:T(8,128)(2,1)S(1)}, u32[]{:S(2)}, u32[]{:S(2)}) collective-permute-start(bf16[64,4224]{1,0:T(8,128)(2,1)S(1)} %get-tuple-element.44.refs_0_), channel_id=1, source_target_pairs={{0,8},{4,12},{8,0},{12,4},{1,9},{5,13},{9,1},{13,5},{2,10},{6,14},... | collective-permute-start | bytes 1622024 | tf_op jit(solution)/shard_map/ppermute | solution.py:32
  20.6 14.0 %collective-permute-start.7 = (bf16[64,4224]{1,0:T(8,128)(2,1)S(1)}, bf16[64,4224]{1,0:T(8,128)(2,1)S(1)}, u32[]{:S(2)}, u32[]{:S(2)}) collective-permute-start(bf16[64,4224]{1,0:T(8,128)(2,1)S(1)} %get-tuple-element.44.refs_0_), channel_id=1, source_target_pairs={{0,4},{4,0},{8,12},{12,8},{1,5},{5,1},{9,13},{13,9},{2,6},{6,2},{1... | collective-permute-start | bytes 1622024 | tf_op jit(solution)/shard_map/ppermute | solution.py:32
  24.6 10.0 %collective-permute-start.1 = (bf16[64,1024]{1,0:T(8,128)(2,1)S(1)}, bf16[64,1024]{1,0:T(8,128)(2,1)S(1)}, u32[]{:S(2)}, u32[]{:S(2)}) collective-permute-start(bf16[64,1024]{1,0:T(8,128)(2,1)S(1)} %get-tuple-element.41.refs_0_), channel_id=1, source_target_pairs={{0,2},{1,3},{2,0},{3,1},{4,6},{5,7},{6,4},{7,5},{8,10},{9,11},{10,... | collective-permute-start | bytes 393224 | tf_op jit(solution)/shard_map/ppermute | solution.py:32
  34.8 12.0 %collective-permute-start.15 = (bf16[192,4224]{1,0:T(8,128)(2,1)S(1)}, bf16[192,4224]{1,0:T(8,128)(2,1)S(1)}, u32[]{:S(2)}, u32[]{:S(2)}) collective-permute-start(bf16[192,4224]{1,0:T(8,128)(2,1)S(1)} %move_rows.12), channel_id=1, source_target_pairs={{0,16},{16,0},{1,17},{17,1},{2,18},{18,2},{3,19},{19,3},{4,20},{20... | collective-permute-start | bytes 4866056 | tf_op jit(solution)/shard_map/ppermute | solution.py:32
  44.7 21.8 %collective-permute-start.10 = (bf16[64,4224]{1,0:T(8,128)(2,1)S(1)}, bf16[64,4224]{1,0:T(8,128)(2,1)S(1)}, u32[]{:S(2)}, u32[]{:S(2)}) collective-permute-start(bf16[64,4224]{1,0:T(8,128)(2,1)S(1)} %get-tuple-element.47.refs_0_), channel_id=1, source_target_pairs={{0,4},{4,0},{8,12},{12,8},{1,5},{5,1},{9,13},{13,9},{2,6},{6,2},{1... | collective-permute-start | bytes 1622024 | tf_op jit(solution)/shard_map/ppermute | solution.py:32
  46.3 20.2 %collective-permute-start.11 = (bf16[64,4224]{1,0:T(8,128)(2,1)S(1)}, bf16[64,4224]{1,0:T(8,128)(2,1)S(1)}, u32[]{:S(2)}, u32[]{:S(2)}) collective-permute-start(bf16[64,4224]{1,0:T(8,128)(2,1)S(1)} %get-tuple-element.47.refs_0_), channel_id=1, source_target_pairs={{0,8},{4,12},{8,0},{12,4},{1,9},{5,13},{9,1},{13,5},{2,10},{6,14},... | collective-permute-start | bytes 1622024 | tf_op jit(solution)/shard_map/ppermute | solution.py:32
  70.7 10.3 %collective-permute-start.18 = (bf16[256,4096]{1,0:T(8,128)(2,1)S(1)}, bf16[256,4096]{1,0:T(8,128)(2,1)S(1)}, u32[]{:S(2)}, u32[]{:S(2)}) collective-permute-start(bf16[256,4096]{1,0:T(8,128)(2,1)S(1)} %down_rows.5), channel_id=1, source_target_pairs={{0,16},{16,0},{1,17},{17,1},{2,18},{18,2},{3,19},{19,3},{4,20},{20... | collective-permute-start | bytes 6291464 | tf_op jit(solution)/shard_map/ppermute | solution.py:32
  71.0 13.5 %collective-permute-start.14 = (bf16[192,4224]{1,0:T(8,128)(2,1)S(1)}, bf16[192,4224]{1,0:T(8,128)(2,1)S(1)}, u32[]{:S(2)}, u32[]{:S(2)}) collective-permute-start(bf16[192,4224]{1,0:T(8,128)(2,1)S(1)} %move_rows.11), channel_id=1, source_target_pairs={{0,16},{16,0},{1,17},{17,1},{2,18},{18,2},{3,19},{19,3},{4,20},{20... | collective-permute-start | bytes 4866056 | tf_op jit(solution)/shard_map/ppermute | solution.py:32
  81.5 15.0 %collective-permute-start.19 = (bf16[64,4096]{1,0:T(8,128)(2,1)S(1)}, bf16[64,4096]{1,0:T(8,128)(2,1)S(1)}, u32[]{:S(2)}, u32[]{:S(2)}) collective-permute-start(bf16[64,4096]{1,0:T(8,128)(2,1)S(1)} %get-tuple-element.50.refs_9_), channel_id=1, source_target_pairs={{0,4},{4,0},{8,12},{12,8},{1,5},{5,1},{9,13},{13,9},{2,6},{6,2},{1... | collective-permute-start | bytes 1572872 | tf_op jit(solution)/shard_map/ppermute | solution.py:32
  82.8 14.0 %collective-permute-start.20 = (bf16[64,4096]{1,0:T(8,128)(2,1)S(1)}, bf16[64,4096]{1,0:T(8,128)(2,1)S(1)}, u32[]{:S(2)}, u32[]{:S(2)}) collective-permute-start(bf16[64,4096]{1,0:T(8,128)(2,1)S(1)} %get-tuple-element.51.refs_10_), channel_id=1, source_target_pairs={{0,8},{4,12},{8,0},{12,4},{1,9},{5,13},{9,1},{13,5},{2,10},{6,14},... | collective-permute-start | bytes 1572872 | tf_op jit(solution)/shard_map/ppermute | solution.py:32
  129.1 14.7 %collective-permute-start.27 = (bf16[64,4096]{1,0:T(8,128)(2,1)S(1)}, bf16[64,4096]{1,0:T(8,128)(2,1)S(1)}, u32[]{:S(2)}, u32[]{:S(2)}) collective-permute-start(bf16[64,4096]{1,0:T(8,128)(2,1)S(1)} %get-tuple-element.62), channel_id=1, source_target_pairs={{0,4},{4,0},{8,12},{12,8},{1,5},{5,1},{9,13},{13,9},{2,6},{6,2},{1... | collective-permute-start | bytes 1572872 | tf_op jit(solution)/shard_map/ppermute | solution.py:32
  130.8 14.0 %collective-permute-start.28 = (bf16[64,4096]{1,0:T(8,128)(2,1)S(1)}, bf16[64,4096]{1,0:T(8,128)(2,1)S(1)}, u32[]{:S(2)}, u32[]{:S(2)}) collective-permute-start(bf16[64,4096]{1,0:T(8,128)(2,1)S(1)} %get-tuple-element.63), channel_id=1, source_target_pairs={{0,8},{4,12},{8,0},{12,4},{1,9},{5,13},{9,1},{13,5},{2,10},{6,14},... | collective-permute-start | bytes 1572872 | tf_op jit(solution)/shard_map/ppermute | solution.py:32
  132.6 11.2 %collective-permute-start.30 = (bf16[16,4096]{1,0:T(8,128)(2,1)S(1)}, bf16[16,4096]{1,0:T(8,128)(2,1)S(1)}, u32[]{:S(2)}, u32[]{:S(2)}) collective-permute-start(bf16[16,4096]{1,0:T(8,128)(2,1)S(1)} %final_rows.2.refs_4_.refs_5_), channel_id=1, source_target_pairs={{0,2},{1,3},{2,0},{3,1},{4,6},{5,7},{6,4},{7,5},{8,10},{9,11},{10,... | collective-permute-start | bytes 393224 | tf_op jit(solution)/shard_map/ppermute | solution.py:32
  132.6 11.2 %collective-permute-start.31 = (bf16[16,4096]{1,0:T(8,128)(2,1)S(1)}, bf16[16,4096]{1,0:T(8,128)(2,1)S(1)}, u32[]{:S(2)}, u32[]{:S(2)}) collective-permute-start(bf16[16,4096]{1,0:T(8,128)(2,1)S(1)} %final_rows.2.refs_4_.refs_5_), channel_id=1, source_target_pairs={{0,1},{1,0},{2,3},{3,2},{4,5},{5,4},{6,7},{7,6},{8,9},{9,8},{10,11... | collective-permute-start | bytes 393224 | tf_op jit(solution)/shard_map/ppermute | solution.py:32
  153.9 20.4 %collective-permute-start.40 = (bf16[64,4096]{1,0:T(8,128)(2,1)S(1)}, bf16[64,4096]{1,0:T(8,128)(2,1)S(1)}, u32[]{:S(2)}, u32[]{:S(2)}) collective-permute-start(bf16[64,4096]{1,0:T(8,128)(2,1)S(1)} %get-tuple-element.72.refs_0_), channel_id=1, source_target_pairs={{0,8},{4,12},{8,0},{12,4},{1,9},{5,13},{9,1},{13,5},{2,10},{6,14},... | collective-permute-start | bytes 1572872 | tf_op jit(solution)/shard_map/ppermute | solution.py:32
  155.4 18.9 %collective-permute-start.41 = (bf16[64,4096]{1,0:T(8,128)(2,1)S(1)}, bf16[64,4096]{1,0:T(8,128)(2,1)S(1)}, u32[]{:S(2)}, u32[]{:S(2)}) collective-permute-start(bf16[64,4096]{1,0:T(8,128)(2,1)S(1)} %get-tuple-element.72.refs_0_), channel_id=1, source_target_pairs={{0,4},{4,0},{8,12},{12,8},{1,5},{5,1},{9,13},{13,9},{2,6},{6,2},{1... | collective-permute-start | bytes 1572872 | tf_op jit(solution)/shard_map/ppermute | solution.py:32
  158.6 10.0 %collective-permute-start.35 = (bf16[16,4096]{1,0:T(8,128)(2,1)S(1)}, bf16[16,4096]{1,0:T(8,128)(2,1)S(1)}, u32[]{:S(2)}, u32[]{:S(2)}) collective-permute-start(bf16[16,4096]{1,0:T(8,128)(2,1)S(1)} %get-tuple-element.69), channel_id=1, source_target_pairs={{0,2},{1,3},{2,0},{3,1},{4,6},{5,7},{6,4},{7,5},{8,10},{9,11},{10,... | collective-permute-start | bytes 393224 | tf_op jit(solution)/shard_map/ppermute | solution.py:32
  158.6 10.0 %collective-permute-start.36 = (bf16[16,4096]{1,0:T(8,128)(2,1)S(1)}, bf16[16,4096]{1,0:T(8,128)(2,1)S(1)}, u32[]{:S(2)}, u32[]{:S(2)}) collective-permute-start(bf16[16,4096]{1,0:T(8,128)(2,1)S(1)} %get-tuple-element.70), channel_id=1, source_target_pairs={{0,1},{1,0},{2,3},{3,2},{4,5},{5,4},{6,7},{7,6},{8,9},{9,8},{10,11... | collective-permute-start | bytes 393224 | tf_op jit(solution)/shard_map/ppermute | solution.py:32
  172.0 10.3 %collective-permute-start.38 = (bf16[16,4096]{1,0:T(8,128)(2,1)S(1)}, bf16[16,4096]{1,0:T(8,128)(2,1)S(1)}, u32[]{:S(2)}, u32[]{:S(2)}) collective-permute-start(bf16[16,4096]{1,0:T(8,128)(2,1)S(1)} %final_rows.3.refs_0_), channel_id=1, source_target_pairs={{0,2},{1,3},{2,0},{3,1},{4,6},{5,7},{6,4},{7,5},{8,10},{9,11},{10,... | collective-permute-start | bytes 393224 | tf_op jit(solution)/shard_map/ppermute | solution.py:32
  172.0 10.3 %collective-permute-start.39 = (bf16[16,4096]{1,0:T(8,128)(2,1)S(1)}, bf16[16,4096]{1,0:T(8,128)(2,1)S(1)}, u32[]{:S(2)}, u32[]{:S(2)}) collective-permute-start(bf16[16,4096]{1,0:T(8,128)(2,1)S(1)} %final_rows.3.refs_0_), channel_id=1, source_target_pairs={{0,1},{1,0},{2,3},{3,2},{4,5},{5,4},{6,7},{7,6},{8,9},{9,8},{10,11... | collective-permute-start | bytes 393224 | tf_op jit(solution)/shard_map/ppermute | solution.py:32
  183.0 13.9 %collective-permute-start.42 = (bf16[64,4096]{1,0:T(8,128)(2,1)S(1)}, bf16[64,4096]{1,0:T(8,128)(2,1)S(1)}, u32[]{:S(2)}, u32[]{:S(2)}) collective-permute-start(bf16[64,4096]{1,0:T(8,128)(2,1)S(1)} %move_rows.16.refs_0_), channel_id=1, source_target_pairs={{0,4},{4,0},{8,12},{12,8},{1,5},{5,1},{9,13},{13,9},{2,6},{6,2},{1... | collective-permute-start | bytes 1572872 | tf_op jit(solution)/shard_map/ppermute | solution.py:32
  183.7 13.6 %collective-permute-start.43 = (bf16[64,4096]{1,0:T(8,128)(2,1)S(1)}, bf16[64,4096]{1,0:T(8,128)(2,1)S(1)}, u32[]{:S(2)}, u32[]{:S(2)}) collective-permute-start(bf16[64,4096]{1,0:T(8,128)(2,1)S(1)} %move_rows.16.refs_0_), channel_id=1, source_target_pairs={{0,8},{4,12},{8,0},{12,4},{1,9},{5,13},{9,1},{13,5},{2,10},{6,14},... | collective-permute-start | bytes 1572872 | tf_op jit(solution)/shard_map/ppermute | solution.py:32
  (35 other events, 338.8 us)

commit v13 on v11

--- a/solution.py
+++ b/solution.py
@@ -697,12 +697,12 @@
             nearer = stack_rows(planes[h][:3], [] if before else sum((p[:0:-1] for p in slices[1:2]), []))
             away = [swap(nearer, "seq", 1)]
             if planes[h][3:]:
-                away.append(swap(stack_rows(planes[h][3:], before.get("kept", [])), "seq", 1))
+                away.append(swap(stack_rows(planes[h][3:], before.get("packed", [])), "seq", 1))
             half = n_expert * rows
             everything = planes[h] + away
             tile = tile_of(w_gate)
             count = w_gate.shape[2] // tile
-            cuts = [0, (count + 1) // 2, count - 1, count] if h else [0, count]
+            cuts = [0, count // 2, count // 2 + (count + 1) // 4, count] if h else [0, count]
             ties = [before.get(key, []) for key in ("packed", "passed", "totals")]
             hidden = [
                 hidden_rows(

time: 231 us -> 240 us (1.039)
  waiting for transfers between devices: 76 us -> 84.5 us
    ppermute x54, waiting for transfers between devices: 76 us -> 84.5 us  [swap(): return lax.ppermute(x, axis, [(i, i ^ distance) for i in range(size)])]
  transfers between devices with their start and end apart: 54 -> 54, of which waited for: 27 -> 28; matrix products, arithmetic and copies ran while one was open for 1% -> 1% of each run, Pallas kernels for 29% -> 28%
where the time goes in v13:
time: 240 us; the launch traced here: 237 us
  Pallas kernels  87.3 us (36%)
  waiting for transfers between devices  84.5 us (35%)
  starting transfers between devices  62.1 us (26%)
  local copies, waits for them, and re-layouts  2.61 us (1%)
    ppermute x54, waiting for transfers between devices, swap(): return lax.ppermute(x, axis, [(i, i ^ distance) for i in range(size)])  84.5 us
    ppermute x54, starting transfers between devices, swap(): return lax.ppermute(x, axis, [(i, i ^ distance) for i in range(size)])  62.1 us
    pallas_call x4, Pallas kernels, hidden_rows(): pl.pallas_call(functools.partial(hidden_kernel, len(pieces), len(after),...  43 us
    pallas_call x2, Pallas kernels, head_terms(): pl.pallas_call(functools.partial(head_kernel, len(pieces), tile, sub, len...  19.1 us
    pallas_call x4, Pallas kernels, down_rows(): pl.pallas_call(functools.partial(down_kernel, start, len(hidden)), out_sh...  16 us
  transfers between devices with their start and end apart: 54, of which 28 were waited for; matrix products, arithmetic and copies ran while one was open for 1% of the time, Pallas kernels for 28%

profile of v13, /device:TPU:0, one launch (start us, length us, event | category | flops | bytes accessed | tf_op | source)
XLA Modules:
  0.0 237.3 jit_solution(13884191878931685635)
XLA Ops:
  1.0 5.1 %collective-permute-start.3 = (bf16[72,1024]{1,0:T(8,128)(2,1)S(1)}, bf16[72,1024]{1,0:T(8,128)(2,1)S(1)}, u32[]{:S(2)}, u32[]{:S(2)}) collective-permute-start(bf16[72,1024]{1,0:T(8,128)(2,1)S(1)} %get-tuple-element.42.refs_0_), channel_id=1, source_target_pairs={{0,3},{1,2},{2,1},{3,0},{4,7},{5,6},{6,5},{7,4},{8,11},{9,10},{10,... | collective-permute-start | bytes 442376 | tf_op jit(solution)/shard_map/ppermute | solution.py:32
  10.9 7.7 %collective-permute-done.4.refs_2_ = bf16[72,1024]{1,0:T(8,128)(2,1)S(1)} collective-permute-done((bf16[72,1024]{1,0:T(8,128)(2,1)S(1)}, bf16[72,1024]{1,0:T(8,128)(2,1)S(1)}, u32[]{:S(2)}, u32[]{:S(2)}) %collective-permute-start.4) | collective-permute-done | bytes 147488 | tf_op jit(solution)/shard_map/ppermute | solution.py:32
  26.4 3.8 %collective-permute-done.refs_1_.refs_3_ = bf16[64,1024]{1,0:T(8,128)(2,1)S(1)} collective-permute-done((bf16[64,1024]{1,0:T(8,128)(2,1)S(1)}, bf16[64,1024]{1,0:T(8,128)(2,1)S(1)}, u32[]{:S(2)}, u32[]{:S(2)}) %collective-permute-start) | collective-permute-done | bytes 131104 | tf_op jit(solution)/shard_map/ppermute | solution.py:32
  30.3 4.3 %collective-permute-done.1.refs_2_.refs_4_ = bf16[64,1024]{1,0:T(8,128)(2,1)S(1)} collective-permute-done((bf16[64,1024]{1,0:T(8,128)(2,1)S(1)}, bf16[64,1024]{1,0:T(8,128)(2,1)S(1)}, u32[]{:S(2)}, u32[]{:S(2)}) %collective-permute-start.1) | collective-permute-done | bytes 131104 | tf_op jit(solution)/shard_map/ppermute | solution.py:32
  36.1 7.8 %collective-permute-done.8.refs_7_.refs_0_.refs_3_ = bf16[32,4224]{1,0:T(8,128)(2,1)S(1)} collective-permute-done((bf16[32,4224]{1,0:T(8,128)(2,1)S(1)}, bf16[32,4224]{1,0:T(8,128)(2,1)S(1)}, u32[]{:S(2)}, u32[]{:S(2)}) %collective-permute-start.8) | collective-permute-done | bytes 270368 | tf_op jit(solution)/shard_map/ppermute | solution.py:32
  46.8 19.5 %hidden_rows.4.refs_0_ = bf16[512,1792]{1,0:T(8,128)(2,1)S(1)} custom-call(bf16[64,4224]{1,0:T(8,128)(2,1)S(1)} %get-tuple-element.44.refs_0_, bf16[64,4224]{1,0:T(8,128)(2,1)S(1)} %collective-permute-done.7.refs_1_, bf16[64,4224]{1,0:T(8,128)(2,1)S(1)} %collective-permute-done.6.refs_0_.refs_2_, ...), custom_call_target="tpu_custom_call" | custom-call | flops 15032385536 | bytes 35389440 | tf_op jit(solution)/shard_map/hidden_rows/pallas_call | solution.py:288
  66.4 4.1 %down_rows.5 = bf16[256,4096]{1,0:T(8,128)(2,1)S(1)} custom-call(bf16[512,1792]{1,0:T(8,128)(2,1)S(1)} %hidden_rows.4.refs_0_, bf16[1,1792,4096]{2,1,0:T(8,128)(2,1)S(1)} %bitcast.4, bf16[64,4224]{1,0:T(8,128)(2,1)S(1)} %collective-permute-done.10.refs_1_.refs_2_, bf16[64,4224]{1,0:T(8,128)(2,1)S(1)} %collective-permute-done.11.refs_0_.refs_2_.refs_3_), custom_call_target="tpu_custom_call" | custom-call | flops 3758096384 | bytes 3014656 | tf_op jit(solution)/shard_map/down_rows/pallas_call | solution.py:332
  73.6 3.9 %down_rows.4.kept_ref = bf16[256,4096]{1,0:T(8,128)(2,1)S(1)} custom-call(bf16[512,1792]{1,0:T(8,128)(2,1)S(1)} %hidden_rows.4.refs_0_, bf16[1,1792,4096]{2,1,0:T(8,128)(2,1)S(1)} %bitcast.4), custom_call_target="tpu_custom_call" | custom-call | flops 3758096384 | bytes 3014656 | tf_op jit(solution)/shard_map/down_rows/pallas_call | solution.py:332
  83.9 11.3 %collective-permute-done.19.one_ref.refs_1_ = bf16[64,4096]{1,0:T(8,128)(2,1)S(1)} collective-permute-done((bf16[64,4096]{1,0:T(8,128)(2,1)S(1)}, bf16[64,4096]{1,0:T(8,128)(2,1)S(1)}, u32[]{:S(2)}, u32[]{:S(2)}) %collective-permute-start.19) | collective-permute-done | bytes 524320 | tf_op jit(solution)/shard_map/ppermute | solution.py:32
  98.4 9.4 %hidden_rows.5.refs_0_ = bf16[512,768]{1,0:T(8,128)(2,1)S(1)} custom-call(bf16[64,4224]{1,0:T(8,128)(2,1)S(1)} %get-tuple-element.47.refs_0_, bf16[64,4224]{1,0:T(8,128)(2,1)S(1)} %collective-permute-done.10.refs_1_.refs_2_, bf16[64,4224]{1,0:T(8,128)(2,1)S(1)} %collective-permute-done.11.refs_0_.refs_2_.refs_3_, ...), custom_call_target="tpu_custom_call" | custom-call | flops 6442450944 | bytes 17563648 | tf_op jit(solution)/shard_map/hidden_rows/pallas_call | solution.py:288
  107.8 7.0 %hidden_rows.6.refs_1_ = bf16[512,512]{1,0:T(8,128)(2,1)S(1)} custom-call(bf16[64,4224]{1,0:T(8,128)(2,1)S(1)} %get-tuple-element.47.refs_0_, bf16[64,4224]{1,0:T(8,128)(2,1)S(1)} %collective-permute-done.10.refs_1_.refs_2_, bf16[64,4224]{1,0:T(8,128)(2,1)S(1)} %collective-permute-done.11.refs_0_.refs_2_.refs_3_, ...), custom_call_target="tpu_custom_call" | custom-call | flops 4294967296 | bytes 13107200 | tf_op jit(solution)/shard_map/hidden_rows/pallas_call | solution.py:288
  119.7 7.0 %hidden_rows.7.refs_2_ = bf16[512,512]{1,0:T(8,128)(2,1)S(1)} custom-call(bf16[64,4224]{1,0:T(8,128)(2,1)S(1)} %get-tuple-element.47.refs_0_, bf16[64,4224]{1,0:T(8,128)(2,1)S(1)} %collective-permute-done.10.refs_1_.refs_2_, bf16[64,4224]{1,0:T(8,128)(2,1)S(1)} %collective-permute-done.11.refs_0_.refs_2_.refs_3_, ...), custom_call_target="tpu_custom_call" | custom-call | flops 4294967296 | bytes 13107200 | tf_op jit(solution)/shard_map/hidden_rows/pallas_call | solution.py:288
  127.6 3.9 %down_rows.7 = bf16[256,4096]{1,0:T(8,128)(2,1)S(1)} custom-call(bf16[512,768]{1,0:T(8,128)(2,1)S(1)} %hidden_rows.5.refs_0_, bf16[512,512]{1,0:T(8,128)(2,1)S(1)} %hidden_rows.6.refs_1_, bf16[512,512]{1,0:T(8,128)(2,1)S(1)} %hidden_rows.7.refs_2_, bf16[1,1792,4096]{2,1,0:T(8,128)(2,1)S(1)} %bitcast.4, ...), custom_call_target="tpu_custom_call" | custom-call | flops 3758096384 | bytes 3014656 | tf_op jit(solution)/shard_map/down_rows/pallas_call | solution.py:332
  133.2 3.9 %down_rows.6.kept_ref = bf16[256,4096]{1,0:T(8,128)(2,1)S(1)} custom-call(bf16[512,768]{1,0:T(8,128)(2,1)S(1)} %hidden_rows.5.refs_0_, bf16[512,512]{1,0:T(8,128)(2,1)S(1)} %hidden_rows.6.refs_1_, bf16[512,512]{1,0:T(8,128)(2,1)S(1)} %hidden_rows.7.refs_2_, bf16[1,1792,4096]{2,1,0:T(8,128)(2,1)S(1)} %bitcast.4, bf16[16,4096]{1,0:T(8,128)(2,1)S(1)} %final_rows.2.refs_4_.refs_5_), custom_call_target="tpu_custom_call" | custom-call | flops 3758096384 | bytes 3014656 | tf_op jit(solution)/shard_map/down_rows/pallas_call | solution.py:332
  141.1 2.9 %collective-permute-start.31 = (bf16[16,4096]{1,0:T(8,128)(2,1)S(1)}, bf16[16,4096]{1,0:T(8,128)(2,1)S(1)}, u32[]{:S(2)}, u32[]{:S(2)}) collective-permute-start(bf16[16,4096]{1,0:T(8,128)(2,1)S(1)} %final_rows.2.refs_4_.refs_5_), channel_id=1, source_target_pairs={{0,1},{1,0},{2,3},{3,2},{4,5},{5,4},{6,7},{7,6},{8,9},{9,8},{10,11... | collective-permute-start | bytes 393224 | tf_op jit(solution)/shard_map/ppermute | solution.py:32
  144.0 3.9 %collective-permute-done.29.refs_0_.refs_8_ = bf16[16,4096]{1,0:T(8,128)(2,1)S(1)} collective-permute-done((bf16[16,4096]{1,0:T(8,128)(2,1)S(1)}, bf16[16,4096]{1,0:T(8,128)(2,1)S(1)}, u32[]{:S(2)}, u32[]{:S(2)}) %collective-permute-start.29) | collective-permute-done | bytes 131104 | tf_op jit(solution)/shard_map/ppermute | solution.py:32
  147.9 4.4 %collective-permute-done.30.refs_1_.refs_7_ = bf16[16,4096]{1,0:T(8,128)(2,1)S(1)} collective-permute-done((bf16[16,4096]{1,0:T(8,128)(2,1)S(1)}, bf16[16,4096]{1,0:T(8,128)(2,1)S(1)}, u32[]{:S(2)}, u32[]{:S(2)}) %collective-permute-start.30) | collective-permute-done | bytes 131104 | tf_op jit(solution)/shard_map/ppermute | solution.py:32
  155.1 6.0 %collective-permute-done.32.refs_3_ = bf16[32,4096]{1,0:T(8,128)(2,1)S(1)} collective-permute-done((bf16[32,4096]{1,0:T(8,128)(2,1)S(1)}, bf16[32,4096]{1,0:T(8,128)(2,1)S(1)}, u32[]{:S(2)}, u32[]{:S(2)}) %collective-permute-start.32) | collective-permute-done | bytes 262176 | tf_op jit(solution)/shard_map/ppermute | solution.py:32
  169.7 3.9 %collective-permute-done.34.refs_1_ = bf16[16,4096]{1,0:T(8,128)(2,1)S(1)} collective-permute-done((bf16[16,4096]{1,0:T(8,128)(2,1)S(1)}, bf16[16,4096]{1,0:T(8,128)(2,1)S(1)}, u32[]{:S(2)}, u32[]{:S(2)}) %collective-permute-start.34) | collective-permute-done | bytes 131104 | tf_op jit(solution)/shard_map/ppermute | solution.py:32
  173.6 3.5 %collective-permute-done.35.refs_2_ = bf16[16,4096]{1,0:T(8,128)(2,1)S(1)} collective-permute-done((bf16[16,4096]{1,0:T(8,128)(2,1)S(1)}, bf16[16,4096]{1,0:T(8,128)(2,1)S(1)}, u32[]{:S(2)}, u32[]{:S(2)}) %collective-permute-start.35) | collective-permute-done | bytes 131104 | tf_op jit(solution)/shard_map/ppermute | solution.py:32
  186.7 4.1 %collective-permute-done.38.refs_2_ = bf16[16,4096]{1,0:T(8,128)(2,1)S(1)} collective-permute-done((bf16[16,4096]{1,0:T(8,128)(2,1)S(1)}, bf16[16,4096]{1,0:T(8,128)(2,1)S(1)}, u32[]{:S(2)}, u32[]{:S(2)}) %collective-permute-start.38) | collective-permute-done | bytes 131104 | tf_op jit(solution)/shard_map/ppermute | solution.py:32
  193.2 9.5 %head_terms.2.refs_2_.refs_7_ = f32[8,256]{1,0:T(8,128)S(1)} custom-call(bf16[64,4096]{1,0:T(8,128)(2,1)S(1)} %get-tuple-element.72.refs_0_, bf16[64,4096]{1,0:T(8,128)(2,1)S(1)} %collective-permute-done.41.refs_1_, bf16[64,4096]{1,0:T(8,128)(2,1)S(1)} %collective-permute-done.40.refs_0_.refs_2_, bf16[32,4096]{1,0:T(8,128)(2,1)S(1)} %collective-permute-done.44.refs_3_, ...), custom_call_target="tpu_custom_call" | custom-call | flops 4194304000 | bytes 18481152 | tf_op jit(solution)/shard_map/head_terms/pallas_call | solution.py:475
  208.0 5.0 %collective-permute-done.46.refs_3_ = bf16[32,4096]{1,0:T(8,128)(2,1)S(1)} collective-permute-done((bf16[32,4096]{1,0:T(8,128)(2,1)S(1)}, bf16[32,4096]{1,0:T(8,128)(2,1)S(1)}, u32[]{:S(2)}, u32[]{:S(2)}) %collective-permute-start.46) | collective-permute-done | bytes 262176 | tf_op jit(solution)/shard_map/ppermute | solution.py:32
  214.1 9.6 %head_terms.3.refs_0_ = f32[16,256]{1,0:T(8,128)S(1)} custom-call(bf16[64,4096]{1,0:T(8,128)(2,1)S(1)} %move_rows.16.refs_0_, bf16[64,4096]{1,0:T(8,128)(2,1)S(1)} %collective-permute-done.42.refs_1_, bf16[64,4096]{1,0:T(8,128)(2,1)S(1)} %collective-permute-done.43.refs_0_.refs_2_, bf16[32,4096]{1,0:T(8,128)(2,1)S(1)} %collective-permute-done.46.refs_3_, ...), custom_call_target="tpu_custom_call" | custom-call | flops 4194304000 | bytes 18481152 | tf_op jit(solution)/shard_map/head_terms/pallas_call | solution.py:475
  (136 shorter events, 84.8 us)
Async XLA Ops:
  6.2 12.5 %collective-permute-start.4 = (bf16[72,1024]{1,0:T(8,128)(2,1)S(1)}, bf16[72,1024]{1,0:T(8,128)(2,1)S(1)}, u32[]{:S(2)}, u32[]{:S(2)}) collective-permute-start(bf16[72,1024]{1,0:T(8,128)(2,1)S(1)} %get-tuple-element.42.refs_0_), channel_id=1, source_target_pairs={{0,2},{1,3},{2,0},{3,1},{4,6},{5,7},{6,4},{7,5},{8,10},{9,11},{10,... | collective-permute-start | bytes 442376 | tf_op jit(solution)/shard_map/ppermute | solution.py:32
  6.2 12.5 %collective-permute-start.5 = (bf16[72,1024]{1,0:T(8,128)(2,1)S(1)}, bf16[72,1024]{1,0:T(8,128)(2,1)S(1)}, u32[]{:S(2)}, u32[]{:S(2)}) collective-permute-start(bf16[72,1024]{1,0:T(8,128)(2,1)S(1)} %get-tuple-element.42.refs_0_), channel_id=1, source_target_pairs={{0,1},{1,0},{2,3},{3,2},{4,5},{5,4},{6,7},{7,6},{8,9},{9,8},{10,11... | collective-permute-start | bytes 442376 | tf_op jit(solution)/shard_map/ppermute | solution.py:32
  19.0 15.6 %collective-permute-start.6 = (bf16[64,4224]{1,0:T(8,128)(2,1)S(1)}, bf16[64,4224]{1,0:T(8,128)(2,1)S(1)}, u32[]{:S(2)}, u32[]{:S(2)}) collective-permute-start(bf16[64,4224]{1,0:T(8,128)(2,1)S(1)} %get-tuple-element.44.refs_0_), channel_id=1, source_target_pairs={{0,8},{4,12},{8,0},{12,4},{1,9},{5,13},{9,1},{13,5},{2,10},{6,14},... | collective-permute-start | bytes 1622024 | tf_op jit(solution)/shard_map/ppermute | solution.py:32
  20.6 14.0 %collective-permute-start.7 = (bf16[64,4224]{1,0:T(8,128)(2,1)S(1)}, bf16[64,4224]{1,0:T(8,128)(2,1)S(1)}, u32[]{:S(2)}, u32[]{:S(2)}) collective-permute-start(bf16[64,4224]{1,0:T(8,128)(2,1)S(1)} %get-tuple-element.44.refs_0_), channel_id=1, source_target_pairs={{0,4},{4,0},{8,12},{12,8},{1,5},{5,1},{9,13},{13,9},{2,6},{6,2},{1... | collective-permute-start | bytes 1622024 | tf_op jit(solution)/shard_map/ppermute | solution.py:32
  34.8 12.0 %collective-permute-start.15 = (bf16[192,4224]{1,0:T(8,128)(2,1)S(1)}, bf16[192,4224]{1,0:T(8,128)(2,1)S(1)}, u32[]{:S(2)}, u32[]{:S(2)}) collective-permute-start(bf16[192,4224]{1,0:T(8,128)(2,1)S(1)} %move_rows.12), channel_id=1, source_target_pairs={{0,16},{16,0},{1,17},{17,1},{2,18},{18,2},{3,19},{19,3},{4,20},{20... | collective-permute-start | bytes 4866056 | tf_op jit(solution)/shard_map/ppermute | solution.py:32
  44.7 21.6 %collective-permute-start.10 = (bf16[64,4224]{1,0:T(8,128)(2,1)S(1)}, bf16[64,4224]{1,0:T(8,128)(2,1)S(1)}, u32[]{:S(2)}, u32[]{:S(2)}) collective-permute-start(bf16[64,4224]{1,0:T(8,128)(2,1)S(1)} %get-tuple-element.47.refs_0_), channel_id=1, source_target_pairs={{0,4},{4,0},{8,12},{12,8},{1,5},{5,1},{9,13},{13,9},{2,6},{6,2},{1... | collective-permute-start | bytes 1622024 | tf_op jit(solution)/shard_map/ppermute | solution.py:32
  46.3 20.0 %collective-permute-start.11 = (bf16[64,4224]{1,0:T(8,128)(2,1)S(1)}, bf16[64,4224]{1,0:T(8,128)(2,1)S(1)}, u32[]{:S(2)}, u32[]{:S(2)}) collective-permute-start(bf16[64,4224]{1,0:T(8,128)(2,1)S(1)} %get-tuple-element.47.refs_0_), channel_id=1, source_target_pairs={{0,8},{4,12},{8,0},{12,4},{1,9},{5,13},{9,1},{13,5},{2,10},{6,14},... | collective-permute-start | bytes 1622024 | tf_op jit(solution)/shard_map/ppermute | solution.py:32
  70.8 27.6 %collective-permute-start.14 = (bf16[192,4224]{1,0:T(8,128)(2,1)S(1)}, bf16[192,4224]{1,0:T(8,128)(2,1)S(1)}, u32[]{:S(2)}, u32[]{:S(2)}) collective-permute-start(bf16[192,4224]{1,0:T(8,128)(2,1)S(1)} %move_rows.11), channel_id=1, source_target_pairs={{0,16},{16,0},{1,17},{17,1},{2,18},{18,2},{3,19},{19,3},{4,20},{20... | collective-permute-start | bytes 4866056 | tf_op jit(solution)/shard_map/ppermute | solution.py:32
  80.7 17.7 %collective-permute-start.18 = (bf16[64,4224]{1,0:T(8,128)(2,1)S(1)}, bf16[64,4224]{1,0:T(8,128)(2,1)S(1)}, u32[]{:S(2)}, u32[]{:S(2)}) collective-permute-start(bf16[64,4224]{1,0:T(8,128)(2,1)S(1)} %move_rows.14), channel_id=1, source_target_pairs={{0,16},{16,0},{1,17},{17,1},{2,18},{18,2},{3,19},{19,3},{4,20},{20... | collective-permute-start | bytes 1622024 | tf_op jit(solution)/shard_map/ppermute | solution.py:32
  80.8 14.3 %collective-permute-start.19 = (bf16[64,4096]{1,0:T(8,128)(2,1)S(1)}, bf16[64,4096]{1,0:T(8,128)(2,1)S(1)}, u32[]{:S(2)}, u32[]{:S(2)}) collective-permute-start(bf16[64,4096]{1,0:T(8,128)(2,1)S(1)} %get-tuple-element.50.refs_2_.refs_9_), channel_id=1, source_target_pairs={{0,4},{4,0},{8,12},{12,8},{1,5},{5,1},{9,13},{13,9},{2,6},{6,2},{1... | collective-permute-start | bytes 1572872 | tf_op jit(solution)/shard_map/ppermute | solution.py:32
  82.1 14.0 %collective-permute-start.20 = (bf16[64,4096]{1,0:T(8,128)(2,1)S(1)}, bf16[64,4096]{1,0:T(8,128)(2,1)S(1)}, u32[]{:S(2)}, u32[]{:S(2)}) collective-permute-start(bf16[64,4096]{1,0:T(8,128)(2,1)S(1)} %get-tuple-element.51.refs_3_.refs_10_), channel_id=1, source_target_pairs={{0,8},{4,12},{8,0},{12,4},{1,9},{5,13},{9,1},{13,5},{2,10},{6,14},... | collective-permute-start | bytes 1572872 | tf_op jit(solution)/shard_map/ppermute | solution.py:32
  96.2 18.6 %collective-permute-start.21 = (bf16[32,4096]{1,0:T(8,128)(2,1)S(1)}, bf16[32,4096]{1,0:T(8,128)(2,1)S(1)}, u32[]{:S(2)}, u32[]{:S(2)}) collective-permute-start(bf16[32,4096]{1,0:T(8,128)(2,1)S(1)} %get-tuple-element.53.refs_9_), channel_id=1, source_target_pairs={{0,4},{4,0},{8,12},{12,8},{1,5},{5,1},{9,13},{13,9},{2,6},{6,2},{1... | collective-permute-start | bytes 786440 | tf_op jit(solution)/shard_map/ppermute | solution.py:32
  97.1 17.8 %collective-permute-start.22 = (bf16[32,4096]{1,0:T(8,128)(2,1)S(1)}, bf16[32,4096]{1,0:T(8,128)(2,1)S(1)}, u32[]{:S(2)}, u32[]{:S(2)}) collective-permute-start(bf16[32,4096]{1,0:T(8,128)(2,1)S(1)} %get-tuple-element.54.refs_10_), channel_id=1, source_target_pairs={{0,8},{4,12},{8,0},{12,4},{1,9},{5,13},{9,1},{13,5},{2,10},{6,14},... | collective-permute-start | bytes 786440 | tf_op jit(solution)/shard_map/ppermute | solution.py:32
  115.2 11.5 %collective-permute-start.23 = (bf16[16,4096]{1,0:T(8,128)(2,1)S(1)}, bf16[16,4096]{1,0:T(8,128)(2,1)S(1)}, u32[]{:S(2)}, u32[]{:S(2)}) collective-permute-start(bf16[16,4096]{1,0:T(8,128)(2,1)S(1)} %get-tuple-element.59.refs_12_), channel_id=1, source_target_pairs={{0,3},{1,2},{2,1},{3,0},{4,7},{5,6},{6,5},{7,4},{8,11},{9,10},{10,... | collective-permute-start | bytes 393224 | tf_op jit(solution)/shard_map/ppermute | solution.py:32
  137.6 14.7 %collective-permute-start.27 = (bf16[64,4096]{1,0:T(8,128)(2,1)S(1)}, bf16[64,4096]{1,0:T(8,128)(2,1)S(1)}, u32[]{:S(2)}, u32[]{:S(2)}) collective-permute-start(bf16[64,4096]{1,0:T(8,128)(2,1)S(1)} %get-tuple-element.62), channel_id=1, source_target_pairs={{0,4},{4,0},{8,12},{12,8},{1,5},{5,1},{9,13},{13,9},{2,6},{6,2},{1... | collective-permute-start | bytes 1572872 | tf_op jit(solution)/shard_map/ppermute | solution.py:32
  139.3 14.0 %collective-permute-start.28 = (bf16[64,4096]{1,0:T(8,128)(2,1)S(1)}, bf16[64,4096]{1,0:T(8,128)(2,1)S(1)}, u32[]{:S(2)}, u32[]{:S(2)}) collective-permute-start(bf16[64,4096]{1,0:T(8,128)(2,1)S(1)} %get-tuple-element.63), channel_id=1, source_target_pairs={{0,8},{4,12},{8,0},{12,4},{1,9},{5,13},{9,1},{13,5},{2,10},{6,14},... | collective-permute-start | bytes 1572872 | tf_op jit(solution)/shard_map/ppermute | solution.py:32
  141.1 11.2 %collective-permute-start.30 = (bf16[16,4096]{1,0:T(8,128)(2,1)S(1)}, bf16[16,4096]{1,0:T(8,128)(2,1)S(1)}, u32[]{:S(2)}, u32[]{:S(2)}) collective-permute-start(bf16[16,4096]{1,0:T(8,128)(2,1)S(1)} %final_rows.2.refs_4_.refs_5_), channel_id=1, source_target_pairs={{0,2},{1,3},{2,0},{3,1},{4,6},{5,7},{6,4},{7,5},{8,10},{9,11},{10,... | collective-permute-start | bytes 393224 | tf_op jit(solution)/shard_map/ppermute | solution.py:32
  141.1 11.2 %collective-permute-start.31 = (bf16[16,4096]{1,0:T(8,128)(2,1)S(1)}, bf16[16,4096]{1,0:T(8,128)(2,1)S(1)}, u32[]{:S(2)}, u32[]{:S(2)}) collective-permute-start(bf16[16,4096]{1,0:T(8,128)(2,1)S(1)} %final_rows.2.refs_4_.refs_5_), channel_id=1, source_target_pairs={{0,1},{1,0},{2,3},{3,2},{4,5},{5,4},{6,7},{7,6},{8,9},{9,8},{10,11... | collective-permute-start | bytes 393224 | tf_op jit(solution)/shard_map/ppermute | solution.py:32
  162.4 20.4 %collective-permute-start.40 = (bf16[64,4096]{1,0:T(8,128)(2,1)S(1)}, bf16[64,4096]{1,0:T(8,128)(2,1)S(1)}, u32[]{:S(2)}, u32[]{:S(2)}) collective-permute-start(bf16[64,4096]{1,0:T(8,128)(2,1)S(1)} %get-tuple-element.72.refs_0_), channel_id=1, source_target_pairs={{0,8},{4,12},{8,0},{12,4},{1,9},{5,13},{9,1},{13,5},{2,10},{6,14},... | collective-permute-start | bytes 1572872 | tf_op jit(solution)/shard_map/ppermute | solution.py:32
  163.9 19.0 %collective-permute-start.41 = (bf16[64,4096]{1,0:T(8,128)(2,1)S(1)}, bf16[64,4096]{1,0:T(8,128)(2,1)S(1)}, u32[]{:S(2)}, u32[]{:S(2)}) collective-permute-start(bf16[64,4096]{1,0:T(8,128)(2,1)S(1)} %get-tuple-element.72.refs_0_), channel_id=1, source_target_pairs={{0,4},{4,0},{8,12},{12,8},{1,5},{5,1},{9,13},{13,9},{2,6},{6,2},{1... | collective-permute-start | bytes 1572872 | tf_op jit(solution)/shard_map/ppermute | solution.py:32
  180.6 10.3 %collective-permute-start.38 = (bf16[16,4096]{1,0:T(8,128)(2,1)S(1)}, bf16[16,4096]{1,0:T(8,128)(2,1)S(1)}, u32[]{:S(2)}, u32[]{:S(2)}) collective-permute-start(bf16[16,4096]{1,0:T(8,128)(2,1)S(1)} %final_rows.3.refs_0_), channel_id=1, source_target_pairs={{0,2},{1,3},{2,0},{3,1},{4,6},{5,7},{6,4},{7,5},{8,10},{9,11},{10,... | collective-permute-start | bytes 393224 | tf_op jit(solution)/shard_map/ppermute | solution.py:32
  180.6 10.3 %collective-permute-start.39 = (bf16[16,4096]{1,0:T(8,128)(2,1)S(1)}, bf16[16,4096]{1,0:T(8,128)(2,1)S(1)}, u32[]{:S(2)}, u32[]{:S(2)}) collective-permute-start(bf16[16,4096]{1,0:T(8,128)(2,1)S(1)} %final_rows.3.refs_0_), channel_id=1, source_target_pairs={{0,1},{1,0},{2,3},{3,2},{4,5},{5,4},{6,7},{7,6},{8,9},{9,8},{10,11... | collective-permute-start | bytes 393224 | tf_op jit(solution)/shard_map/ppermute | solution.py:32
  191.5 13.9 %collective-permute-start.42 = (bf16[64,4096]{1,0:T(8,128)(2,1)S(1)}, bf16[64,4096]{1,0:T(8,128)(2,1)S(1)}, u32[]{:S(2)}, u32[]{:S(2)}) collective-permute-start(bf16[64,4096]{1,0:T(8,128)(2,1)S(1)} %move_rows.16.refs_0_), channel_id=1, source_target_pairs={{0,4},{4,0},{8,12},{12,8},{1,5},{5,1},{9,13},{13,9},{2,6},{6,2},{1... | collective-permute-start | bytes 1572872 | tf_op jit(solution)/shard_map/ppermute | solution.py:32
  192.2 13.6 %collective-permute-start.43 = (bf16[64,4096]{1,0:T(8,128)(2,1)S(1)}, bf16[64,4096]{1,0:T(8,128)(2,1)S(1)}, u32[]{:S(2)}, u32[]{:S(2)}) collective-permute-start(bf16[64,4096]{1,0:T(8,128)(2,1)S(1)} %move_rows.16.refs_0_), channel_id=1, source_target_pairs={{0,8},{4,12},{8,0},{12,4},{1,9},{5,13},{9,1},{13,5},{2,10},{6,14},... | collective-permute-start | bytes 1572872 | tf_op jit(solution)/shard_map/ppermute | solution.py:32
  (35 other events, 344.3 us)
